TPU v7x, 32 devices: a whole 2x2x4 slice. The times are simulated.
32 devices in a mesh: groups: 2 (over x), blk: 8 (over z, y), heads: 2 (over core).
Axes of the slice: x: 2, y: 2, z: 4, core: 2. Of those that a mesh axis runs over, the one named last changes fastest.
Arguments:
- image_feats: bfloat16 [4096, 8192], P(('groups', 'blk')), parts along dimension 0, may hold values from -6 to 6
- slot_image: int32 [4096], P(('groups', 'blk')), parts along dimension 0, may hold values from -1 to 3, as said below
- key_weight: bfloat16 [8192, 512], P('blk', 'heads'), may hold values from -0.0625 to 0.0625
- value_weight: bfloat16 [8192, 512], P('blk', 'heads'), may hold values from -0.0625 to 0.0625
- key_gain: float32 [128], replicated, may hold values from 0.25 to 1.75
- queries: bfloat16 [512, 4096], P(('groups', 'blk'), 'heads'), parts along dimension 0, may hold values from -60 to 60
- text_image: int32 [512], P('groups'), parts along dimension 0, may hold values from 0 to 3
- text_hidden: bfloat16 [512, 8192], P(('groups', 'heads'), 'blk'), parts along dimension 0, may hold values from -4 to 4
- out_weight: bfloat16 [4096, 8192], P('heads', 'blk'), may hold values from -0.09375 to 0.09375
- attn_gate: float32 [1], replicated, may hold values from 0.4 to 1.2
Outputs:
- mixed: bfloat16 [512, 8192], P(('groups', 'heads'), 'blk'), parts along dimension 0
There are 2 independent parts, one for each index of `groups`. A program takes and returns all parts, laid end to end along the dimension named above; an argument that names none is the same for every part. Nothing has to cross between parts.
Inputs may be any that keep to these rules, and one draw needn't show every extreme that they name: `slot_image`: slots come in tiles of 64; the live slots of a tile come first and carry one image id, -1 marks an empty slot; every image has live slots; the first 256 slots are all live.
All inputs are finite; a program needn't handle non-finite values.
Results may differ from a plain program's by a relative error of at most 0.008.
Values may be sent and summed in bfloat16 or wider, within the bound.
No kernel may reach another device: no remote copies, remote signals or barrier semaphores. Data moves between devices by JAX's collectives and lax.ppermute only.
A program may use at most 128 MiB of HBM per device.

v0:
```python
import math

import jax
import jax.numpy as jnp
from jax import lax
from jax.sharding import PartitionSpec as P

HD = 128


def body(
    image_feats,
    slot_image,
    key_weight,
    value_weight,
    key_gain,
    queries,
    text_image,
    text_hidden,
    out_weight,
    attn_gate,
):
    tok_rows = image_feats.shape[0]
    kv_cols = key_weight.shape[1]
    kv_local = kv_cols // HD
    q_cols = queries.shape[1]
    q_per_kv = q_cols // kv_cols
    text_rows = queries.shape[0]
    score_scale = 1.0 / math.sqrt(HD)
    keys_raw = jnp.dot(
        image_feats,
        lax.all_gather(key_weight, "blk", axis=0, tiled=True),
        preferred_element_type=jnp.float32,
    )
    values_raw = jnp.dot(
        image_feats,
        lax.all_gather(value_weight, "blk", axis=0, tiled=True),
        preferred_element_type=jnp.float32,
    )
    key_heads_raw = keys_raw.reshape(tok_rows, kv_local, HD)
    norm_scale = lax.rsqrt(jnp.mean(key_heads_raw * key_heads_raw, axis=-1, keepdims=True) + 1e-05)
    keys = (key_heads_raw * norm_scale * key_gain).astype(jnp.bfloat16).reshape(tok_rows, kv_cols)
    values = values_raw.astype(jnp.bfloat16)
    row_start = lax.axis_index("blk") * text_rows
    row_images = lax.dynamic_slice_in_dim(text_image, row_start, text_rows, 0).astype(jnp.float32)
    query_heads = queries.reshape(text_rows, kv_local, q_per_kv, HD)
    slot_code = slot_image.astype(jnp.bfloat16)
    row_top = jnp.full((text_rows, kv_local, q_per_kv), -1e30, jnp.float32)
    piece_keys = lax.all_gather(keys, "blk", axis=0, tiled=True)
    piece_values = lax.all_gather(values, "blk", axis=0, tiled=True)
    attend_slot_code = lax.all_gather(slot_code, "blk", axis=0, tiled=True)
    count_rows = piece_keys.shape[0]
    slot_float = attend_slot_code.astype(jnp.float32)
    visible = (slot_float[None, :] >= 0.0) & (slot_float[None, :] <= row_images[:, None])
    visible_four = visible[:, None, None, :]
    key_heads = piece_keys.reshape(count_rows, kv_local, HD)
    value_heads = piece_values.reshape(count_rows, kv_local, HD)
    scores = (
        jnp.einsum("rgjd,sgd->rgjs", query_heads, key_heads, preferred_element_type=jnp.float32)
        * score_scale
    )
    masked_scores = jnp.where(visible_four, scores, -1e30)
    next_top = jnp.maximum(row_top, jnp.max(masked_scores, axis=-1))
    expo = jnp.where(visible_four, jnp.exp(scores - next_top[..., None]), 0.0)
    next_total = jnp.sum(expo, axis=-1)
    next_acc = jnp.einsum(
        "rgjs,sgd->rgjd", expo.astype(jnp.bfloat16), value_heads, preferred_element_type=jnp.float32
    )
    attn = (next_acc / next_total[..., None]).astype(jnp.bfloat16).reshape(text_rows, q_cols)
    partial_out = jnp.dot(
        lax.all_gather(attn, "blk", axis=0, tiled=True),
        out_weight,
        preferred_element_type=jnp.float32,
    )
    head_total = lax.psum_scatter(
        partial_out.astype(jnp.bfloat16), "heads", scatter_dimension=0, tiled=True
    ).astype(jnp.float32)
    return (text_hidden.astype(jnp.float32) + jnp.tanh(attn_gate[0]) * head_total).astype(
        jnp.bfloat16
    )


def solution(mesh):
    placed = (
        P(("groups", "blk"), None),
        P(("groups", "blk")),
        P("blk", "heads"),
        P("blk", "heads"),
        P(),
        P(("groups", "blk"), "heads"),
        P("groups"),
        P(("groups", "heads"), "blk"),
        P("heads", "blk"),
        P(),
    )
    return jax.shard_map(
        body, mesh=mesh, in_specs=placed, out_specs=P(("groups", "heads"), "blk"), check_vma=False
    )
```

profile of v0, /device:TPU:0, one launch (start us, length us, event | category | flops | bytes accessed | tf_op | source)
XLA Modules:
  0.0 304.9 jit_solution(10362841615920033740)
XLA Ops:
  6.5 0.0 copy-start
  6.5 0.0 all-gather.11.cloned.1.call-start
  6.5 0.7 all-gather.11.cloned.1.call-update
  7.3 0.0 all-gather.7.cloned.1.call-start
  7.3 0.7 all-gather.7.cloned.1.call-update
  8.0 0.0 all-gather.13.cloned.1.call-start
  8.1 0.0 copy-done
  8.1 77.5 %all-gather.11.cloned.1.call-done = bf16[8192,256]{1,0:T(8,128)(2,1)} async-done(((bf16[1024,256]{1,0:T(8,128)(2,1)}), bf16[8192,256]{1,0:T(8,128)(2,1)}) %all-gather.11.cloned.1.call-update) | async-done | bytes 4194320 | tf_op jit(solution)/shard_map/all_gather | solution.py:32
  85.6 5.2 %bitcast_reduce_fusion = (f32[256,2]{0,1:T(2,128)S(1)}, f32[256,256]{0,1:T(8,128)S(1)}) fusion(bf16[256,8192]{1,0:T(8,128)(2,1)} %param.10, bf16[8192,256]{1,0:T(8,128)(2,1)} %all-gather.11.cloned.1.call-done), kind=kOutput, calls=%fused_computation.19 | convolution fusion | flops 1073872384 | bytes 8652800 | tf_op jit(solution)/shard_map/dot_general | solution.py:30
  90.9 0.8 fusion.19
  91.6 0.0 all-gather.13.cloned.1.call-update
  91.6 0.0 copy-start.4
  91.7 0.0 copy-start.3
  91.7 0.0 copy-start.5
  91.7 0.0 all-gather.9.cloned.1.call-start
  91.7 67.7 %all-gather.7.cloned.1.call-done = bf16[8192,256]{1,0:T(8,128)(2,1)} async-done(((bf16[1024,256]{1,0:T(8,128)(2,1)}), bf16[8192,256]{1,0:T(8,128)(2,1)}) %all-gather.7.cloned.1.call-update) | async-done | bytes 4194320 | tf_op jit(solution)/shard_map/all_gather | solution.py:37
  159.4 5.4 %convolution_convert_fusion.1 = bf16[256,256]{1,0:T(8,128)(2,1)} fusion(bf16[256,8192]{1,0:T(8,128)(2,1)} %param.10, bf16[8192,256]{1,0:T(8,128)(2,1)} %all-gather.7.cloned.1.call-done), kind=kOutput, calls=%fused_computation.11 | convolution fusion | flops 1073807360 | bytes 8519680 | tf_op jit(solution)/shard_map/dot_general | solution.py:35
  164.8 0.0 all-gather.9.cloned.1.call-update
  164.8 0.0 all-gather.15.cloned.1.call-start
  164.9 0.0 copy-done.4
  164.9 17.8 %all-gather = bf16[8,1,256]{2,1,0:T(2,128)(2,1)S(1)} all-gather(bf16[1,1,256]{2,1,0:T(2,128)(2,1)S(1)} %reshape.71), channel_id=1, replica_groups=mesh['groups'=2,'blk'=8,'heads'=2] {'blk'}, dimensions={0}, use_global_device_ids=true | all-gather | bytes 4608 | tf_op jit(solution)/shard_map/all_gather | solution.py:51
  182.8 0.0 copy-done.3
  182.8 0.0 copy-done.5
  182.8 0.1 dynamic-slice_convert_fusion
  182.9 0.1 compare_and_fusion
  183.0 16.5 %all-gather.13.cloned.1.call-done = bf16[2048,256]{0,1:T(8,128)(2,1)} async-done(((bf16[256,256]{0,1:T(8,128)(2,1)}), bf16[2048,256]{0,1:T(8,128)(2,1)}) %all-gather.13.cloned.1.call-update) | async-done | bytes 1048592 | tf_op jit(solution)/shard_map/all_gather | solution.py:49
  199.5 2.1 fusion
  201.6 0.0 copy-start.1
  201.7 1.9 copy-done.1
  203.6 1.1 fusion.3
  204.6 35.9 %all-gather.9.cloned.1.call-done = bf16[2048,256]{1,0:T(8,128)(2,1)} async-done(((bf16[256,256]{1,0:T(8,128)(2,1)}), bf16[2048,256]{1,0:T(8,128)(2,1)}) %all-gather.9.cloned.1.call-update) | async-done | bytes 1048592 | tf_op jit(solution)/shard_map/all_gather | solution.py:50
  240.6 1.3 reshape.67
  241.9 3.1 %fusion.14 = bf16[32,2,8,128]{3,0,2,1:T(8,128)(2,1)S(1)} fusion(f32[2,2048,32,8]{1,2,3,0:T(8,128)} %copy-done.1, f32[32,2,8]{0,2,1:T(8,128)S(1)} %broadcast_maximum_fusion, pred[32,2048]{1,0:T(8,128)(4,1)S(1)} %compare_and_fusion, bf16[2048,2,128,1]{2,1,0,3:T(2,128)(2,1)S(1)} %bitcast.60, f32[32,2,8]{0,2,1:T(8,128)S(1)} %fusion.3), kind=kOutput, calls=%fused_computation.13 | convolution fusion | flops 272760832 | bytes 5443584 | tf_op jit(solution)/shard_map/rgjs,sgd->rgjd/dot_general | solution.py:66
  245.0 0.1 copy.21
  245.0 0.0 copy-start.2
  245.1 0.7 copy.37
  245.7 0.0 all-gather.15.cloned.1.call-update
  245.8 0.0 reduce-scatter.2.cloned.1.call-start
  245.8 39.0 %all-gather.15.cloned.1.call-done = bf16[256,2048]{1,0:T(8,128)(2,1)} async-done(((bf16[32,2048]{1,0:T(8,128)(2,1)}), bf16[256,2048]{1,0:T(8,128)(2,1)}) %all-gather.15.cloned.1.call-update) | async-done | bytes 1048592 | tf_op jit(solution)/shard_map/all_gather | solution.py:71
  284.8 4.6 %convolution_convert_fusion = bf16[256,1024]{1,0:T(8,128)(2,1)} fusion(bf16[256,2048]{1,0:T(8,128)(2,1)} %all-gather.15.cloned.1.call-done, bf16[2048,1024]{1,0:T(8,128)(2,1)} %param.18), kind=kOutput, calls=%fused_computation.9 | convolution fusion | flops 1074003968 | bytes 5767168 | tf_op jit(solution)/shard_map/dot_general | solution.py:70
  289.4 0.0 reduce-scatter.2.cloned.1.call-update
  290.1 6.2 %reduce-scatter.2.cloned.1.call-done = bf16[128,1024]{1,0:T(8,128)(2,1)} async-done(((bf16[256,1024]{1,0:T(8,128)(2,1)}), bf16[128,1024]{1,0:T(8,128)(2,1)}) %reduce-scatter.2.cloned.1.call-update) | async-done | bytes 262160 | tf_op jit(solution)/shard_map/reduce_scatter | solution.py:75
  296.3 0.0 copy-done.2
  296.3 1.8 add_convert_fusion
  (8 shorter events, 0.1 us)
Async XLA Ops:
  6.5 1.5 copy-start
  6.5 79.1 %all-gather.11.cloned.1.call-start = ((), (), s32[]{:S(2)}) async-start(), calls=%async_computation.3 | async-start | bytes 4718592 | tf_op jit(solution)/shard_map/all_gather | solution.py:32
  7.3 152.2 %all-gather.7.cloned.1.call-start = ((), (), s32[]{:S(2)}) async-start(), calls=%async_computation.1 | async-start | bytes 4718592 | tf_op jit(solution)/shard_map/all_gather | solution.py:37
  8.0 191.5 %all-gather.13.cloned.1.call-start = ((), (), s32[]{:S(2)}) async-start(), calls=%async_computation.4 | async-start | bytes 1179648 | tf_op jit(solution)/shard_map/all_gather | solution.py:49
  91.6 73.2 %copy-start.4 = (s32[256]{0:T(256)S(1)}, s32[256]{0:T(256)}, u32[]{:S(2)}) copy-start(s32[256]{0:T(256)} %param.11) | copy-start | bytes 3076
  91.7 91.1 %copy-start.3 = (bf16[32,2048]{1,0:T(8,128)(2,1)S(1)}, bf16[32,2048]{1,0:T(8,128)(2,1)}, u32[]{:S(2)}) copy-start(bf16[32,2048]{1,0:T(8,128)(2,1)} %param.15) | copy-start | bytes 393220
  91.7 91.1 %copy-start.5 = (s32[256]{0:T(256)S(1)}, s32[256]{0:T(256)}, u32[]{:S(2)}) copy-start(s32[256]{0:T(256)} %param.16) | copy-start | bytes 3076
  91.7 148.9 %all-gather.9.cloned.1.call-start = ((), (), s32[]{:S(2)}) async-start(), calls=%async_computation.2 | async-start | bytes 1179648 | tf_op jit(solution)/shard_map/all_gather | solution.py:50
  164.8 120.0 %all-gather.15.cloned.1.call-start = ((), (), s32[]{:S(2)}) async-start(), calls=%async_computation.5 | async-start | bytes 1179648 | tf_op jit(solution)/shard_map/all_gather | solution.py:71
  201.6 2.0 copy-start.1
  245.0 51.3 %copy-start.2 = (bf16[128,1024]{1,0:T(8,128)(2,1)S(1)}, bf16[128,1024]{1,0:T(8,128)(2,1)}, u32[]{:S(2)}) copy-start(bf16[128,1024]{1,0:T(8,128)(2,1)} %param.17) | copy-start | bytes 786436
  245.8 50.5 %reduce-scatter.2.cloned.1.call-start = ((), (), s32[]{:S(2)}) async-start(), calls=%async_computation.6 | async-start | bytes 786432 | tf_op jit(solution)/shard_map/reduce_scatter | solution.py:75
Sparse Core Ops, SparseCore 0:
  9.5 76.0 all-gather.10
  87.7 71.6 all-gather.6
  161.5 37.9 all-gather.12
  201.5 39.0 all-gather.8
  245.9 38.8 all-gather.14
  289.6 6.7 reduce-scatter.1
where the time goes:
time: 305 us
  waiting for transfers between devices  244 us (80%)
  matrix products  20.4 us (7%)
  blocking collectives  17.8 us (6%)
  between operations  14.3 us (5%)
  local copies, waits for them, and re-layouts  4.08 us (1%)
  other arithmetic  3.81 us (1%)
    all_gather x1, waiting for transfers between devices, body(): lax.all_gather(key_weight, 'blk', axis=0, tiled=True)  77.5 us
    all_gather x1, waiting for transfers between devices, body(): lax.all_gather(value_weight, 'blk', axis=0, tiled=True)  67.7 us
    all_gather x1, waiting for transfers between devices, body(): lax.all_gather(attn, 'blk', axis=0, tiled=True)  39 us
    all_gather x1, waiting for transfers between devices, body(): piece_values = lax.all_gather(values, 'blk', axis=0, tiled=True)  35.9 us
    all_gather x1, blocking collectives, body(): attend_slot_code = lax.all_gather(slot_code, 'blk', axis=0, tiled=True)  17.8 us
    all_gather x1, waiting for transfers between devices, body(): piece_keys = lax.all_gather(keys, 'blk', axis=0, tiled=True)  16.5 us
    reduce_scatter x1, waiting for transfers between devices, body(): lax.psum_scatter(partial_out.astype(jnp.bfloat16), 'heads', scatter_dimen...  6.19 us
  transfers between devices with their start and end apart: 6, of which 6 were waited for; matrix products, arithmetic and copies ran while one was open for 5% of the time, Pallas kernels for 0%

commit v1 on v0

v1 whole, which is shorter than its diff:
```python
import functools
import math

import jax
import jax.numpy as jnp
from jax import lax
from jax.experimental import pallas as pl
from jax.experimental.pallas import tpu as pltpu
from jax.sharding import PartitionSpec as P

HD = 128
F32 = jnp.float32
BF16 = jnp.bfloat16
VMEM_BYTES = 48 * 1024 * 1024
PARAMS = pltpu.CompilerParams(vmem_limit_bytes=VMEM_BYTES)
WHOLE = pl.BlockSpec(memory_space=pltpu.VMEM)


def dot(a, b):
    return jnp.dot(a, b, preferred_element_type=F32)


def dot_nt(a, b):
    return lax.dot_general(a, b, (((1,), (1,)), ((), ())), preferred_element_type=F32)


def shard_kernel(n_w, first, idx_ref, own_m, own_o, par_m, par_o, *refs):
    rows = own_m.shape[0]
    w_m, w_o = refs[0][...], refs[1][...]
    if n_w == 2:
        take_up = idx_ref[3] > 0
        w_m = jnp.where(take_up, w_m, refs[2][...])
        w_o = jnp.where(take_up, w_o, refs[3][...])
    out = refs[-1]
    top = dot(own_m[...], w_m) + dot(own_o[...], w_o)
    low = dot(par_m[...], w_m) + dot(par_o[...], w_o)
    if not first:
        acc = refs[-2]
        top = top + acc[:rows, :]
        low = low + acc[rows:, :]
    out[:rows, :] = top
    out[rows:, :] = low


def shard_dot(idx, image, partner, weights, acc, own_weight):
    rows = image.shape[0]
    half = weights[0].shape[0] // (2 if own_weight else 1)
    cols = weights[0].shape[1]
    first = acc is None
    specs = [
        pl.BlockSpec((rows, half), lambda i, s: (0, 2 * s[0] + s[2])),
        pl.BlockSpec((rows, half), lambda i, s: (0, 2 * s[0] + 1 - s[2])),
        pl.BlockSpec((rows, half), lambda i, s: (0, 2 * s[1] + s[2])),
        pl.BlockSpec((rows, half), lambda i, s: (0, 2 * s[1] + 1 - s[2])),
    ]
    args = [image, image, partner, partner]
    if own_weight:
        specs += [
            pl.BlockSpec((half, cols), lambda i, s: (s[2], 0)),
            pl.BlockSpec((half, cols), lambda i, s: (1 - s[2], 0)),
        ]
        args += [weights[0], weights[0]]
        n_w = 1
    else:
        specs += [pl.BlockSpec((half, cols), lambda i, s: (0, 0))] * len(weights)
        args += list(weights)
        n_w = len(weights) // 2
    aliases = {}
    if not first:
        specs.append(pl.BlockSpec((2 * rows, cols), lambda i, s: (0, 0)))
        args.append(acc)
        aliases = {len(args): 0}
    return pl.pallas_call(
        functools.partial(shard_kernel, n_w, first),
        out_shape=jax.ShapeDtypeStruct((2 * rows, cols), F32),
        grid_spec=pltpu.PrefetchScalarGridSpec(
            num_scalar_prefetch=1,
            grid=(1,),
            in_specs=specs,
            out_specs=pl.BlockSpec((2 * rows, cols), lambda i, s: (0, 0)),
        ),
        input_output_aliases=aliases,
        compiler_params=PARAMS,
        cost_estimate=pl.CostEstimate(
            flops=8 * rows * half * cols, bytes_accessed=8 * rows * half + 4 * half * cols, transcendentals=0
        ),
    )(idx, *args)


def score_kernel(n, heads, q_ref, limit_ref, *refs):
    keys, slots = refs[:n], refs[n : 2 * n]
    expo_ref, total_ref, s_ref = refs[2 * n :]
    rows = limit_ref.shape[0]
    piece = keys[0].shape[0]
    scale = 1.0 / math.sqrt(HD)
    limit = limit_ref[...]
    top = jnp.full((heads * rows, 1), -1e30, F32)
    for i in range(n):
        slot = slots[i][...]
        visible = (slot >= 0.0) & (slot <= limit)
        bias = jnp.where(visible, 0.0, -1e30)
        s = dot_nt(q_ref[...], keys[i][...]) * scale
        s = jnp.where(bias[None] < 0.0, -1e30, s.reshape(heads, rows, piece)).reshape(heads * rows, piece)
        s_ref[:, i * piece : (i + 1) * piece] = s
        top = jnp.maximum(top, jnp.max(s, axis=1, keepdims=True))
    total = jnp.zeros((heads * rows, 1), F32)
    for i in range(n):
        s = s_ref[:, i * piece : (i + 1) * piece]
        e = jnp.where(s > -1e29, jnp.exp(s - top), 0.0)
        total = total + jnp.sum(e, axis=1, keepdims=True)
        expo_ref[:, i * piece : (i + 1) * piece] = e.astype(BF16)
    total_ref[...] = total


def value_kernel(n, heads, expo_ref, total_ref, *refs):
    values, out_ref = refs[:n], refs[n]
    rows = out_ref.shape[0]
    piece = values[0].shape[0]
    acc = jnp.zeros((heads * rows, HD), F32)
    for i in range(n):
        acc = acc + dot(expo_ref[:, i * piece : (i + 1) * piece], values[i][...])
    attn = (acc / total_ref[...]).astype(BF16)
    for j in range(heads):
        out_ref[:, j * HD : (j + 1) * HD] = attn[j * rows : (j + 1) * rows, :]


def proj_kernel(n, idx_ref, *refs):
    mine, other = refs[:n], refs[n : 2 * n]
    w_mine, w_other, keep_ref, send_ref, a_ref, p_ref = refs[2 * n :]
    rows, width = mine[0].shape
    for d in range(n):
        a_ref[d * rows : (d + 1) * rows, :width] = mine[d][...]
        a_ref[d * rows : (d + 1) * rows, width:] = other[d][...]
    p_ref[...] = dot(a_ref[:, :width], w_mine[...]) + dot(a_ref[:, width:], w_other[...])
    for k in range(n // 2):
        at_keep = pl.multiple_of(idx_ref[1 + k] * rows, rows)
        at_send = pl.multiple_of(idx_ref[1 + n // 2 + k] * rows, rows)
        keep_ref[k * rows : (k + 1) * rows, :] = p_ref[pl.ds(at_keep, rows), :]
        send_ref[k * rows : (k + 1) * rows, :] = p_ref[pl.ds(at_send, rows), :].astype(BF16)


def body(
    image_feats,
    slot_image,
    key_weight,
    value_weight,
    key_gain,
    queries,
    text_image,
    text_hidden,
    out_weight,
    attn_gate,
):
    groups, nblk, cores = (lax.axis_size(a) for a in ("groups", "blk", "heads"))
    lines = nblk // 2
    tok = image_feats.shape[0]
    depth = key_weight.shape[0]
    kv_cols = key_weight.shape[1]
    mine_cols = kv_cols // 2
    text_rows = queries.shape[0]
    q_half = queries.shape[1] // 2
    per_kv = q_half // mine_cols
    grp, blk, core = (lax.axis_index(a) for a in ("groups", "blk", "heads"))
    par = grp % 2
    y = blk % 2
    line = blk // 2

    swap_y = [(b, b ^ 1) for b in range(nblk)]
    swap_core = [(c, c ^ 1) for c in range(cores)]

    def shift(array, d):
        return lax.ppermute(array, "blk", [(b, b + 2 * d) for b in range(nblk) if 0 <= b + 2 * d < nblk])

    def turn(array, d):
        return lax.ppermute(array, "blk", [(b, (b - 2 * d) % nblk) for b in range(nblk)])

    def swap_x(array, ok):
        pairs = [(g * nblk + b, (g ^ 1) * nblk + b) for g in range(groups) for b in range(nblk) if ok(b // 2)]
        return lax.ppermute(array, ("groups", "blk"), pairs)

    def take_y(array, size, which):
        return lax.dynamic_slice_in_dim(array, which * size, size, 1)

    half_lines = lines // 2
    sends = [
        lax.dynamic_slice_in_dim(image_feats, (2 * (core * half_lines + l) + 1 - y) * depth, depth, 1)
        for l in range(half_lines)
    ]
    got = [lax.ppermute(s, "blk", swap_y) for s in sends]
    got_other = [lax.ppermute(s, "heads", swap_core) for s in got]
    got, got_other = jnp.concatenate(got, 1), jnp.concatenate(got_other, 1)
    low_core = core == 0
    partner = jnp.concatenate(
        [jnp.where(low_core, got, got_other), jnp.where(low_core, got_other, got)], 1
    )

    def project(weight):
        half = depth // 2
        up = dn = lax.dynamic_slice_in_dim(weight, par * half, half, 0)
        zero = jnp.int32(0)
        acc = shard_dot(
            jnp.stack([blk, line, par, zero]), image_feats, partner, [weight], None, True
        )
        for s in range(1, lines):
            up, dn = shift(up, 1), shift(dn, -1)
            up_x = swap_x(up, lambda l: l >= s)
            dn_x = swap_x(dn, lambda l: l + s < lines)
            low, high = jnp.maximum(line - s, 0), jnp.minimum(line + s, lines - 1)
            if 2 * s >= lines:
                is_up = line >= s
                at = jnp.where(is_up, low, high)
                acc = shard_dot(
                    jnp.stack([2 * at + y, at, par, is_up.astype(jnp.int32)]),
                    image_feats, partner, [up, up_x, dn, dn_x], acc, False,
                )
            else:
                acc = shard_dot(
                    jnp.stack([2 * low + y, low, par, zero]), image_feats, partner, [up, up_x], acc, False
                )
                acc = shard_dot(
                    jnp.stack([2 * high + y, high, par, zero]), image_feats, partner, [dn, dn_x], acc, False
                )
        keep = take_y(acc, mine_cols, y)
        send = take_y(acc, mine_cols, 1 - y)
        return keep, jnp.concatenate([send[tok:], send[:tok]], 0)

    keep, send = project(key_weight)
    raw = (keep + lax.ppermute(send, "blk", swap_y)).reshape(2 * tok, mine_cols // HD, HD)
    norm_scale = lax.rsqrt(jnp.mean(raw * raw, axis=-1, keepdims=True) + 1e-05)
    keys = (raw * norm_scale * key_gain).astype(BF16).reshape(2 * tok, mine_cols)

    slots = slot_image.astype(BF16)
    slots = jnp.concatenate([slots, lax.ppermute(slots, "blk", swap_y)]).reshape(2 * tok // HD, HD)
    pad = -slots.shape[0] % 16
    slots = jnp.pad(slots, ((0, pad), (0, 0)))
    packed = jnp.concatenate([keys, slots], 0)
    key_pieces, slot_pieces = [], []
    for d in range(lines):
        piece = packed if d == 0 else turn(packed, d)
        key_pieces.append(piece[: 2 * tok])
        slot_pieces.append(piece[2 * tok : 2 * tok + 2 * tok // HD].astype(F32).reshape(1, 2 * tok))

    q_mine = take_y(queries, q_half, y)
    q_got = lax.ppermute(take_y(queries, q_half, 1 - y), "blk", swap_y)
    is_low = y == 0
    q_rows = jnp.concatenate([jnp.where(is_low, q_mine, q_got), jnp.where(is_low, q_got, q_mine)], 0)
    rows = 2 * text_rows
    q_all = q_rows.reshape(rows, per_kv, HD).transpose(1, 0, 2).reshape(per_kv * rows, HD)
    limit = lax.dynamic_slice_in_dim(text_image, line * rows, rows, 0).astype(F32).reshape(rows, 1)

    tokens = 2 * tok * lines
    expo, total = pl.pallas_call(
        functools.partial(score_kernel, lines, per_kv),
        out_shape=(
            jax.ShapeDtypeStruct((per_kv * rows, tokens), BF16),
            jax.ShapeDtypeStruct((per_kv * rows, 1), F32),
        ),
        in_specs=[WHOLE] * (2 + 2 * lines),
        out_specs=(WHOLE, WHOLE),
        scratch_shapes=[pltpu.VMEM((per_kv * rows, tokens), F32)],
        compiler_params=PARAMS,
    )(q_all, limit, *key_pieces, *slot_pieces)

    keep, send = project(value_weight)
    values = (keep + lax.ppermute(send.astype(BF16), "blk", swap_y).astype(F32)).astype(BF16)
    value_pieces = [values if d == 0 else turn(values, d) for d in range(lines)]

    attn = pl.pallas_call(
        functools.partial(value_kernel, lines, per_kv),
        out_shape=jax.ShapeDtypeStruct((rows, q_half), BF16),
        in_specs=[WHOLE] * (2 + lines),
        out_specs=WHOLE,
        compiler_params=PARAMS,
    )(expo, total, *value_pieces)

    mine = [attn if d == 0 else turn(attn, d) for d in range(lines)]
    other = [lax.ppermute(m, "blk", swap_y) for m in mine]

    out_rows = lines * rows
    out_cols = out_weight.shape[1]
    keep_at = [(core * half_lines + k - line) % lines for k in range(half_lines)]
    send_at = [((1 - core) * half_lines + k - line) % lines for k in range(half_lines)]
    whole2 = lambda shape: pl.BlockSpec(shape, lambda i, s: (0, 0))
    keep, send = pl.pallas_call(
        functools.partial(proj_kernel, lines),
        out_shape=(
            jax.ShapeDtypeStruct((out_rows // 2, out_cols), F32),
            jax.ShapeDtypeStruct((out_rows // 2, out_cols), BF16),
        ),
        grid_spec=pltpu.PrefetchScalarGridSpec(
            num_scalar_prefetch=1,
            grid=(1,),
            in_specs=[whole2((rows, q_half))] * (2 * lines)
            + [
                pl.BlockSpec((q_half, out_cols), lambda i, s: (s[0], 0)),
                pl.BlockSpec((q_half, out_cols), lambda i, s: (1 - s[0], 0)),
            ],
            out_specs=(whole2((out_rows // 2, out_cols)), whole2((out_rows // 2, out_cols))),
            scratch_shapes=[
                pltpu.VMEM((out_rows, 2 * q_half), BF16),
                pltpu.VMEM((out_rows, out_cols), F32),
            ],
        ),
        compiler_params=PARAMS,
    )(jnp.stack([y] + keep_at + send_at), *mine, *other, out_weight, out_weight)
    head_total = keep + lax.ppermute(send, "heads", swap_core).astype(F32)
    return (text_hidden.astype(F32) + jnp.tanh(attn_gate[0]) * head_total).astype(BF16)


def solution(mesh):
    placed = (
        P(("groups", "blk"), None),
        P(("groups", "blk")),
        P("blk", "heads"),
        P("blk", "heads"),
        P(),
        P(("groups", "blk"), "heads"),
        P("groups"),
        P(("groups", "heads"), "blk"),
        P("heads", "blk"),
        P(),
    )
    return jax.shard_map(
        body, mesh=mesh, in_specs=placed, out_specs=P(("groups", "heads"), "blk"), check_vma=False
    )
```

time: 305 us -> 171 us (0.56)
  waiting for transfers between devices: 244 us -> 40.7 us
  starting transfers between devices: 0.21 us -> 90.9 us
  Pallas kernels: 0 us -> 24.7 us
  matrix products: 20.4 us -> 0 us
  blocking collectives: 17.8 us -> 0 us
  between operations: 14.3 us -> 1.44 us
  local copies, waits for them, and re-layouts: 4.08 us -> 7.38 us
    all_gather x5 -> x0, waiting for transfers between devices: 237 us -> none  [the longest x1 77.5 us: body(): lax.all_gather(key_weight, 'blk', axis=0, tiled=True)]
    ppermute x0 -> x46, starting transfers between devices: none -> 90.9 us  [the longest x12 37.7 us: shift(): lax.ppermute(array, 'blk', [(b, b + 2 * d) for b in range(nblk) if 0 <= b...]
    ppermute x0 -> x46, waiting for transfers between devices: none -> 40.7 us  [the longest x1 12.1 us: body(): lax.ppermute(slots, 'blk', swap_y)]
    pallas_call x0 -> x13, Pallas kernels: none -> 24.7 us  [the longest x10 20.3 us: shard_dot(): pl.pallas_call(functools.partial(shard_kernel, n_w, first), out_shape=jax...]
    dot_general x5 -> x0, matrix products: 20.4 us -> none  [the longest x1 5.35 us: body(): jnp.dot(image_feats, lax.all_gather(value_weight, 'blk', axis=0, tiled=Tr...]
    all_gather x1 -> x0, blocking collectives: 17.8 us -> none  [body(): attend_slot_code = lax.all_gather(slot_code, 'blk', axis=0, tiled=True)]
    reduce_scatter x1 -> x0, waiting for transfers between devices: 6.19 us -> none  [body(): lax.psum_scatter(partial_out.astype(jnp.bfloat16), 'heads', scatter_dimen...]
    dynamic_slice x0 -> x4, local copies, waits for them, and re-layouts: none -> 4.75 us  [the longest x2 2.64 us: project(): up = dn = lax.dynamic_slice_in_dim(weight, par * half, half, 0)]
  transfers between devices with their start and end apart: 6 -> 46, of which waited for: 6 -> 11; matrix products, arithmetic and copies ran while one was open for 5% -> 5% of each run, Pallas kernels for 0% -> 12%
where the time goes in v1:
time: 171 us; the launch traced here: 170 us
  starting transfers between devices  90.9 us (53%)
  waiting for transfers between devices  40.7 us (24%)
  Pallas kernels  24.7 us (14%)
  local copies, waits for them, and re-layouts  7.38 us (4%)
  other arithmetic  4.97 us (3%)
    ppermute x12, starting transfers between devices, shift(): lax.ppermute(array, 'blk', [(b, b + 2 * d) for b in range(nblk) if 0 <= b...  37.7 us
    ppermute x12, starting transfers between devices, swap_x(): return lax.ppermute(array, ('groups', 'blk'), pairs)  21.3 us
    pallas_call x10, Pallas kernels, shard_dot(): pl.pallas_call(functools.partial(shard_kernel, n_w, first), out_shape=jax...  20.3 us
    ppermute x9, starting transfers between devices, turn(): lax.ppermute(array, 'blk', [(b, (b - 2 * d) % nblk) for b in range(nblk)])  19.5 us
    ppermute x1, waiting for transfers between devices, body(): lax.ppermute(slots, 'blk', swap_y)  12.1 us
    ppermute x9, waiting for transfers between devices, turn(): lax.ppermute(array, 'blk', [(b, (b - 2 * d) % nblk) for b in range(nblk)])  10.5 us
    ppermute x12, waiting for transfers between devices, swap_x(): return lax.ppermute(array, ('groups', 'blk'), pairs)  7.19 us
    ppermute x4, starting transfers between devices, body(): other = [lax.ppermute(m, 'blk', swap_y) for m in mine]  4.61 us
  transfers between devices with their start and end apart: 46, of which 11 were waited for; matrix products, arithmetic and copies ran while one was open for 5% of the time, Pallas kernels for 12%

profile of v1, /device:TPU:0, one launch (start us, length us, event | category | flops | bytes accessed | tf_op | source)
XLA Modules:
  0.0 170.1 jit_solution(12268376193830046794)
XLA Ops:
  0.0 1.3 constant_dynamic-slice_fusion.3
  1.3 3.0 %collective-permute-start.1 = (bf16[256,1024]{1,0:T(8,128)(2,1)S(1)}, bf16[256,1024]{1,0:T(8,128)(2,1)S(1)}, u32[]{:S(2)}, u32[]{:S(2)}) collective-permute-start(bf16[256,1024]{1,0:T(8,128)(2,1)S(1)} %get-tuple-element.14), channel_id=1, source_target_pairs={{0,2},{2,0},{4,6},{6,4},{8,10},{10,8},{12,14},{14,12},{1,3},{3,1},... | collective-permute-start | bytes 1572872 | tf_op jit(solution)/shard_map/ppermute | solution.py:189
  4.4 1.0 constant_dynamic-slice_fusion
  5.4 3.9 %collective-permute-start.22 = (bf16[512,256]{1,0:T(8,128)(2,1)S(1)}, bf16[512,256]{1,0:T(8,128)(2,1)S(1)}, u32[]{:S(2)}, u32[]{:S(2)}) collective-permute-start(bf16[512,256]{1,0:T(8,128)(2,1)S(1)} %constant_dynamic-slice_fusion), channel_id=1, source_target_pairs={{0,4},{2,6},{4,8},{6,10},{8,12},{10,14},{1,5},{3,7},{5,9},{7,11},{... | collective-permute-start | bytes 786440 | tf_op jit(solution)/shard_map/ppermute | solution.py:172
  9.3 0.7 convert_element_type.51
  10.0 1.5 collective-permute-start.18
  11.5 0.8 constant_dynamic-slice_fusion.5
  13.8 1.7 constant_dynamic-slice_fusion.2
  15.4 0.8 convert_bitcast_fusion
  16.2 12.1 %collective-permute-done.18 = bf16[256]{0:T(256)(128)(2,1)S(1)} collective-permute-done((bf16[256]{0:T(256)(128)(2,1)S(1)}, bf16[256]{0:T(256)(128)(2,1)S(1)}, u32[]{:S(2)}, u32[]{:S(2)}) %collective-permute-start.18) | collective-permute-done | bytes 544 | tf_op jit(solution)/shard_map/ppermute | solution.py:233
  28.2 1.3 collective-permute-start.26
  29.5 4.6 %collective-permute-start.5 = (bf16[512,256]{1,0:T(8,128)(2,1)}, bf16[512,256]{1,0:T(8,128)(2,1)S(1)}, u32[]{:S(2)}, u32[]{:S(2)}) collective-permute-start(bf16[512,256]{1,0:T(8,128)(2,1)} %constant_dynamic-slice_fusion.2), channel_id=1, source_target_pairs={{0,4},{2,6},{4,8},{6,10},{8,12},{10,14},{1,5},{3,7},{5,9},{7,11},{... | collective-permute-start | bytes 786440 | tf_op jit(solution)/shard_map/ppermute | solution.py:172
  34.1 1.3 collective-permute-start.9
  37.5 0.8 collective-permute-done.5.refs_0_
  38.3 6.1 %collective-permute-start.23 = (bf16[512,256]{1,0:T(8,128)(2,1)S(1)}, bf16[512,256]{1,0:T(8,128)(2,1)S(1)}, u32[]{:S(2)}, u32[]{:S(2)}) collective-permute-start(bf16[512,256]{1,0:T(8,128)(2,1)S(1)} %collective-permute-done.22.refs_0_), channel_id=1, source_target_pairs={{0,4},{2,6},{4,8},{6,10},{8,12},{10,14},{1,5},{3,7},{5,9},{7,11},{... | collective-permute-start | bytes 786440 | tf_op jit(solution)/shard_map/ppermute | solution.py:172
  44.4 2.2 %collective-permute-start.32 = (bf16[512,256]{1,0:T(8,128)(2,1)S(1)}, bf16[512,256]{1,0:T(8,128)(2,1)S(1)}, u32[]{:S(2)}, u32[]{:S(2)}) collective-permute-start(bf16[512,256]{1,0:T(8,128)(2,1)S(1)} %collective-permute-done.26.refs_0_), channel_id=1, source_target_pairs={{0,16},{2,18},{4,20},{6,22},{8,24},{10,26},{16,0},{18,2},{20,4},{2... | collective-permute-start | bytes 786440 | tf_op jit(solution)/shard_map/ppermute | solution.py:179
  46.7 0.9 broadcast_select_fusion.3
  47.6 1.3 collective-permute-start.27
  48.9 5.1 %collective-permute-done.32.refs_1_ = bf16[512,256]{1,0:T(8,128)(2,1)S(1)} collective-permute-done((bf16[512,256]{1,0:T(8,128)(2,1)S(1)}, bf16[512,256]{1,0:T(8,128)(2,1)S(1)}, u32[]{:S(2)}, u32[]{:S(2)}) %collective-permute-start.32) | collective-permute-done | bytes 262176 | tf_op jit(solution)/shard_map/ppermute | solution.py:179
  54.7 5.5 %collective-permute-start.6 = (bf16[512,256]{1,0:T(8,128)(2,1)S(1)}, bf16[512,256]{1,0:T(8,128)(2,1)S(1)}, u32[]{:S(2)}, u32[]{:S(2)}) collective-permute-start(bf16[512,256]{1,0:T(8,128)(2,1)S(1)} %collective-permute-done.5.refs_0_), channel_id=1, source_target_pairs={{0,4},{2,6},{4,8},{6,10},{8,12},{10,14},{1,5},{3,7},{5,9},{7,11},{... | collective-permute-start | bytes 786440 | tf_op jit(solution)/shard_map/ppermute | solution.py:172
  60.2 3.2 %collective-permute-start.15 = (bf16[512,256]{1,0:T(8,128)(2,1)S(1)}, bf16[512,256]{1,0:T(8,128)(2,1)S(1)}, u32[]{:S(2)}, u32[]{:S(2)}) collective-permute-start(bf16[512,256]{1,0:T(8,128)(2,1)S(1)} %collective-permute-done.9.refs_0_), channel_id=1, source_target_pairs={{0,16},{2,18},{4,20},{6,22},{8,24},{10,26},{16,0},{18,2},{20,4},{2... | collective-permute-start | bytes 786440 | tf_op jit(solution)/shard_map/ppermute | solution.py:179
  63.4 1.3 collective-permute-start.10
  64.9 0.8 collective-permute-start.30
  65.7 4.6 %collective-permute-start.24 = (bf16[512,256]{1,0:T(8,128)(2,1)S(1)}, bf16[512,256]{1,0:T(8,128)(2,1)S(1)}, u32[]{:S(2)}, u32[]{:S(2)}) collective-permute-start(bf16[512,256]{1,0:T(8,128)(2,1)S(1)} %collective-permute-done.23.refs_0_), channel_id=1, source_target_pairs={{0,4},{2,6},{4,8},{6,10},{8,12},{10,14},{1,5},{3,7},{5,9},{7,11},{... | collective-permute-start | bytes 786440 | tf_op jit(solution)/shard_map/ppermute | solution.py:172
  70.3 2.7 %collective-permute-start.31 = (bf16[512,256]{1,0:T(8,128)(2,1)S(1)}, bf16[512,256]{1,0:T(8,128)(2,1)S(1)}, u32[]{:S(2)}, u32[]{:S(2)}) collective-permute-start(bf16[512,256]{1,0:T(8,128)(2,1)S(1)} %collective-permute-done.27.refs_2_), channel_id=1, source_target_pairs={{0,16},{2,18},{4,20},{6,22},{16,0},{18,2},{20,4},{22,6},{1,17},{3,... | collective-permute-start | bytes 786440 | tf_op jit(solution)/shard_map/ppermute | solution.py:179
  73.0 1.3 collective-permute-start.28
  75.1 3.2 %collective-permute-start.14 = (bf16[512,256]{1,0:T(8,128)(2,1)S(1)}, bf16[512,256]{1,0:T(8,128)(2,1)S(1)}, u32[]{:S(2)}, u32[]{:S(2)}) collective-permute-start(bf16[512,256]{1,0:T(8,128)(2,1)S(1)} %collective-permute-done.10.refs_2_), channel_id=1, source_target_pairs={{0,16},{2,18},{4,20},{6,22},{16,0},{18,2},{20,4},{22,6},{1,17},{3,... | collective-permute-start | bytes 786440 | tf_op jit(solution)/shard_map/ppermute | solution.py:179
  78.3 2.0 %collective-permute-done.31.refs_3_ = bf16[512,256]{1,0:T(8,128)(2,1)S(1)} collective-permute-done((bf16[512,256]{1,0:T(8,128)(2,1)S(1)}, bf16[512,256]{1,0:T(8,128)(2,1)S(1)}, u32[]{:S(2)}, u32[]{:S(2)}) %collective-permute-start.31) | collective-permute-done | bytes 262176 | tf_op jit(solution)/shard_map/ppermute | solution.py:179
  80.3 1.3 collective-permute-start.11
  81.6 5.4 %collective-permute-start.7 = (bf16[512,256]{1,0:T(8,128)(2,1)S(1)}, bf16[512,256]{1,0:T(8,128)(2,1)S(1)}, u32[]{:S(2)}, u32[]{:S(2)}) collective-permute-start(bf16[512,256]{1,0:T(8,128)(2,1)S(1)} %collective-permute-done.6.refs_0_), channel_id=1, source_target_pairs={{0,4},{2,6},{4,8},{6,10},{8,12},{10,14},{1,5},{3,7},{5,9},{7,11},{... | collective-permute-start | bytes 786440 | tf_op jit(solution)/shard_map/ppermute | solution.py:172
  87.7 3.6 %collective-permute-start.29 = (bf16[512,256]{1,0:T(8,128)(2,1)S(1)}, bf16[512,256]{1,0:T(8,128)(2,1)S(1)}, u32[]{:S(2)}, u32[]{:S(2)}) collective-permute-start(bf16[512,256]{1,0:T(8,128)(2,1)S(1)} %collective-permute-done.28.refs_2_), channel_id=1, source_target_pairs={{0,16},{2,18},{16,0},{18,2},{1,17},{3,19},{17,1},{19,3}} | collective-permute-start | bytes 786440 | tf_op jit(solution)/shard_map/ppermute | solution.py:179
  91.6 2.0 %shard_map.106.refs_2_ = f32[512,256]{1,0:T(8,128)S(1)} custom-call(s32[4]{0:T(128)S(1)} %pad_add_fusion.idx_ref, bf16[256,8192]{1,0:T(8,128)(2,1)} %own_o.19, bf16[256,8192]{1,0:T(8,128)(2,1)} %own_o.19, bf16[256,4096]{1,0:T(8,128)(2,1)S(1)} %pad_maximum_fusion.par_m.par_o, bf16[256,4096]{1,0:T(8,128)(2,1)S(1)} %pad_maximum_fusion.par_m.par_o, ...), custom_call_target="tpu_custom_call" | custom-call | flops 268435456 | bytes 1572864 | tf_op jit(solution)/shard_map/pallas_call | solution.py:73
  93.6 2.0 %shard_map.100.refs_2_ = f32[512,256]{1,0:T(8,128)S(1)} custom-call(s32[4]{0:T(128)S(1)} %pad_add_fusion.idx_ref, bf16[256,8192]{1,0:T(8,128)(2,1)} %own_o.19, bf16[256,8192]{1,0:T(8,128)(2,1)} %own_o.19, bf16[256,4096]{1,0:T(8,128)(2,1)S(1)} %pad_maximum_fusion.par_m.par_o, bf16[256,4096]{1,0:T(8,128)(2,1)S(1)} %pad_maximum_fusion.par_m.par_o, ...), custom_call_target="tpu_custom_call" | custom-call | flops 268435456 | bytes 1572864 | tf_op jit(solution)/shard_map/pallas_call | solution.py:73
  95.6 2.0 %shard_map.107.refs_2_ = f32[512,256]{1,0:T(8,128)S(1)} custom-call(s32[4]{0:T(128)S(1)} %pad_add_fusion.1.idx_ref, bf16[256,8192]{1,0:T(8,128)(2,1)} %own_o.19, bf16[256,8192]{1,0:T(8,128)(2,1)} %own_o.19, bf16[256,4096]{1,0:T(8,128)(2,1)S(1)} %pad_maximum_fusion.par_m.par_o, ...), custom_call_target="tpu_custom_call", output_to_operand_aliasing={{}: (7, {})} | custom-call | flops 268435456 | bytes 1572864 | tf_op jit(solution)/shard_map/pallas_call | solution.py:73
  97.6 2.2 %collective-permute-start.12 = (bf16[512,256]{1,0:T(8,128)(2,1)S(1)}, bf16[512,256]{1,0:T(8,128)(2,1)S(1)}, u32[]{:S(2)}, u32[]{:S(2)}) collective-permute-start(bf16[512,256]{1,0:T(8,128)(2,1)S(1)} %collective-permute-done.11.refs_2_), channel_id=1, source_target_pairs={{0,16},{2,18},{16,0},{18,2},{1,17},{3,19},{17,1},{19,3}} | collective-permute-start | bytes 786440 | tf_op jit(solution)/shard_map/ppermute | solution.py:179
  100.6 2.0 %shard_map.101.refs_2_ = f32[512,256]{1,0:T(8,128)S(1)} custom-call(s32[4]{0:T(128)S(1)} %pad_add_fusion.1.idx_ref, bf16[256,8192]{1,0:T(8,128)(2,1)} %own_o.19, bf16[256,8192]{1,0:T(8,128)(2,1)} %own_o.19, bf16[256,4096]{1,0:T(8,128)(2,1)S(1)} %pad_maximum_fusion.par_m.par_o, ...), custom_call_target="tpu_custom_call", output_to_operand_aliasing={{}: (7, {})} | custom-call | flops 268435456 | bytes 1572864 | tf_op jit(solution)/shard_map/pallas_call | solution.py:73
  102.6 2.0 %shard_map.108.refs_4_ = f32[512,256]{1,0:T(8,128)S(1)} custom-call(s32[4]{0:T(128)S(1)} %pad_add_fusion.2.idx_ref, bf16[256,8192]{1,0:T(8,128)(2,1)} %own_o.19, bf16[256,8192]{1,0:T(8,128)(2,1)} %own_o.19, bf16[256,4096]{1,0:T(8,128)(2,1)S(1)} %pad_maximum_fusion.par_m.par_o, ...), custom_call_target="tpu_custom_call", output_to_operand_aliasing={{}: (7, {})} | custom-call | flops 268435456 | bytes 1572864 | tf_op jit(solution)/shard_map/pallas_call | solution.py:73
  104.6 2.0 %shard_map.102.refs_4_ = f32[512,256]{1,0:T(8,128)S(1)} custom-call(s32[4]{0:T(128)S(1)} %pad_add_fusion.2.idx_ref, bf16[256,8192]{1,0:T(8,128)(2,1)} %own_o.19, bf16[256,8192]{1,0:T(8,128)(2,1)} %own_o.19, bf16[256,4096]{1,0:T(8,128)(2,1)S(1)} %pad_maximum_fusion.par_m.par_o, ...), custom_call_target="tpu_custom_call", output_to_operand_aliasing={{}: (7, {})} | custom-call | flops 268435456 | bytes 1572864 | tf_op jit(solution)/shard_map/pallas_call | solution.py:73
  106.7 2.0 %shard_map.109.refs_4_ = f32[512,256]{1,0:T(8,128)S(1)} custom-call(s32[4]{0:T(128)S(1)} %pad_add_fusion.4.idx_ref, bf16[256,8192]{1,0:T(8,128)(2,1)} %own_o.19, bf16[256,8192]{1,0:T(8,128)(2,1)} %own_o.19, bf16[256,4096]{1,0:T(8,128)(2,1)S(1)} %pad_maximum_fusion.par_m.par_o, ...), custom_call_target="tpu_custom_call", output_to_operand_aliasing={{}: (9, {})} | custom-call | flops 268435456 | bytes 1572864 | tf_op jit(solution)/shard_map/pallas_call | solution.py:73
  108.7 2.0 %shard_map.103.refs_4_ = f32[512,256]{1,0:T(8,128)S(1)} custom-call(s32[4]{0:T(128)S(1)} %pad_add_fusion.4.idx_ref, bf16[256,8192]{1,0:T(8,128)(2,1)} %own_o.19, bf16[256,8192]{1,0:T(8,128)(2,1)} %own_o.19, bf16[256,4096]{1,0:T(8,128)(2,1)S(1)} %pad_maximum_fusion.par_m.par_o, ...), custom_call_target="tpu_custom_call", output_to_operand_aliasing={{}: (9, {})} | custom-call | flops 268435456 | bytes 1572864 | tf_op jit(solution)/shard_map/pallas_call | solution.py:73
  110.8 2.0 %shard_map.110 = f32[512,256]{1,0:T(8,128)S(1)} custom-call(s32[4]{0:T(128)S(1)} %pad_add_fusion.3.idx_ref, bf16[256,8192]{1,0:T(8,128)(2,1)} %own_o.19, bf16[256,8192]{1,0:T(8,128)(2,1)} %own_o.19, bf16[256,4096]{1,0:T(8,128)(2,1)S(1)} %pad_maximum_fusion.par_m.par_o, ...), custom_call_target="tpu_custom_call", output_to_operand_aliasing={{}: (9, {})} | custom-call | flops 268435456 | bytes 1572864 | tf_op jit(solution)/shard_map/pallas_call | solution.py:73
  112.9 2.0 %shard_map.104 = f32[512,256]{1,0:T(8,128)S(1)} custom-call(s32[4]{0:T(128)S(1)} %pad_add_fusion.3.idx_ref, bf16[256,8192]{1,0:T(8,128)(2,1)} %own_o.19, bf16[256,8192]{1,0:T(8,128)(2,1)} %own_o.19, bf16[256,4096]{1,0:T(8,128)(2,1)S(1)} %pad_maximum_fusion.par_m.par_o, ...), custom_call_target="tpu_custom_call", output_to_operand_aliasing={{}: (9, {})} | custom-call | flops 268435456 | bytes 1572864 | tf_op jit(solution)/shard_map/pallas_call | solution.py:73
  115.0 1.6 collective-permute-start.17
  117.2 4.2 %collective-permute-done.17 = f32[512,128]{1,0:T(8,128)S(1)} collective-permute-done((f32[512,128]{1,0:T(8,128)S(1)}, f32[512,128]{1,0:T(8,128)S(1)}, u32[]{:S(2)}, u32[]{:S(2)}) %collective-permute-start.17) | collective-permute-done | bytes 262176 | tf_op jit(solution)/shard_map/ppermute | solution.py:228
  121.8 1.7 collective-permute-start.19
  123.5 1.0 collective-permute-start.35
  124.6 0.8 collective-permute-start.36
  125.6 2.9 %collective-permute-start.20 = (bf16[528,128]{1,0:T(8,128)(2,1)S(1)}, bf16[528,128]{1,0:T(8,128)(2,1)S(1)}, u32[]{:S(2)}, u32[]{:S(2)}) collective-permute-start(bf16[528,128]{1,0:T(8,128)(2,1)S(1)} %fusion.1), channel_id=1, source_target_pairs={{0,8},{2,10},{4,12},{6,14},{8,0},{10,2},{12,4},{14,6},{1,9},{3,11}... | collective-permute-start | bytes 405512 | tf_op jit(solution)/shard_map/ppermute | solution.py:175
  128.5 8.7 %collective-permute-start.21 = (bf16[528,128]{1,0:T(8,128)(2,1)S(1)}, bf16[528,128]{1,0:T(8,128)(2,1)S(1)}, u32[]{:S(2)}, u32[]{:S(2)}) collective-permute-start(bf16[528,128]{1,0:T(8,128)(2,1)S(1)} %fusion.1), channel_id=1, source_target_pairs={{0,4},{2,6},{4,8},{6,10},{8,12},{10,14},{12,0},{14,2},{1,5},{3,7},... | collective-permute-start | bytes 405512 | tf_op jit(solution)/shard_map/ppermute | solution.py:175
  137.2 4.8 %collective-permute-done.20 = bf16[528,128]{1,0:T(8,128)(2,1)S(1)} collective-permute-done((bf16[528,128]{1,0:T(8,128)(2,1)S(1)}, bf16[528,128]{1,0:T(8,128)(2,1)S(1)}, u32[]{:S(2)}, u32[]{:S(2)}) %collective-permute-start.20) | collective-permute-done | bytes 135200 | tf_op jit(solution)/shard_map/ppermute | solution.py:175
  142.1 1.9 %shard_map.105 = (bf16[512,2048]{1,0:T(8,128)(2,1)S(1)}, f32[512,1]{1,0:T(8,128)S(1)}) custom-call(bf16[512,128]{1,0:T(8,128)(2,1)S(1)} %bitcast.36, f32[64,1]{1,0:T(8,128)S(1)} %copy.20.limit_ref, bf16[512,128]{1,0:T(8,128)(2,1)S(1)} %multiply_convert_fusion.refs_0_, bf16[512,128]{1,0:T(8,128)(2,1)S(1)} %slice.43.refs_1_, ...), custom_call_target="tpu_custom_call" | custom-call | tf_op jit(solution)/shard_map/pallas_call | solution.py:252
  144.0 0.7 shard_map.111.refs_0_
  144.7 1.6 collective-permute-start.38
  146.9 1.9 %collective-permute-start.40 = (bf16[64,1024]{1,0:T(8,128)(2,1)S(1)}, bf16[64,1024]{1,0:T(8,128)(2,1)S(1)}, u32[]{:S(2)}, u32[]{:S(2)}) collective-permute-start(bf16[64,1024]{1,0:T(8,128)(2,1)S(1)} %shard_map.111.refs_0_), channel_id=1, source_target_pairs={{0,4},{2,6},{4,8},{6,10},{8,12},{10,14},{12,0},{14,2},{1,5},{3,7},... | collective-permute-start | bytes 393224 | tf_op jit(solution)/shard_map/ppermute | solution.py:175
  148.8 1.5 collective-permute-start.41
  150.4 1.1 collective-permute-start.42
  151.4 5.7 %collective-permute-done.39.refs_2_ = bf16[64,1024]{1,0:T(8,128)(2,1)S(1)} collective-permute-done((bf16[64,1024]{1,0:T(8,128)(2,1)S(1)}, bf16[64,1024]{1,0:T(8,128)(2,1)S(1)}, u32[]{:S(2)}, u32[]{:S(2)}) %collective-permute-start.39) | collective-permute-done | bytes 131104 | tf_op jit(solution)/shard_map/ppermute | solution.py:175
  157.2 1.5 collective-permute-start.43
  159.3 2.8 %collective-permute-done.43.refs_6_ = bf16[64,1024]{1,0:T(8,128)(2,1)S(1)} collective-permute-done((bf16[64,1024]{1,0:T(8,128)(2,1)S(1)}, bf16[64,1024]{1,0:T(8,128)(2,1)S(1)}, u32[]{:S(2)}, u32[]{:S(2)}) %collective-permute-start.43) | collective-permute-done | bytes 131104 | tf_op jit(solution)/shard_map/ppermute | solution.py:277
  162.1 1.5 collective-permute-done.44.refs_7_
  163.6 2.2 %copy-done = bf16[2048,1024]{1,0:T(8,128)(2,1)S(1)} copy-done((bf16[2048,1024]{1,0:T(8,128)(2,1)S(1)}, bf16[2048,1024]{1,0:T(8,128)(2,1)}, u32[]{:S(2)}) %copy-start) | copy-done | bytes 4194328
  165.8 1.8 %shard_map.112 = (f32[128,1024]{1,0:T(8,128)S(1)}, bf16[128,1024]{1,0:T(8,128)(2,1)S(1)}) custom-call(s32[5]{0:T(128)S(1)} %stack.109.idx_ref, bf16[64,1024]{1,0:T(8,128)(2,1)S(1)} %shard_map.111.refs_0_, bf16[64,1024]{1,0:T(8,128)(2,1)S(1)} %collective-permute-done.38.refs_1_, bf16[64,1024]{1,0:T(8,128)(2,1)S(1)} %collective-permute-done.39.refs_2_, ...), custom_call_target="tpu_custom_call" | custom-call | tf_op jit(solution)/shard_map/pallas_call | solution.py:284
  168.5 0.8 collective-permute-done.45
  169.3 0.8 add_convert_fusion
  (91 shorter events, 9.4 us)
Async XLA Ops:
  1.3 34.4 %collective-permute-start.1 = (bf16[256,1024]{1,0:T(8,128)(2,1)S(1)}, bf16[256,1024]{1,0:T(8,128)(2,1)S(1)}, u32[]{:S(2)}, u32[]{:S(2)}) collective-permute-start(bf16[256,1024]{1,0:T(8,128)(2,1)S(1)} %get-tuple-element.14), channel_id=1, source_target_pairs={{0,2},{2,0},{4,6},{6,4},{8,10},{10,8},{12,14},{14,12},{1,3},{3,1},... | collective-permute-start | bytes 1572872 | tf_op jit(solution)/shard_map/ppermute | solution.py:189
  4.3 31.4 %collective-permute-start.2 = (bf16[256,1024]{1,0:T(8,128)(2,1)S(1)}, bf16[256,1024]{1,0:T(8,128)(2,1)S(1)}, u32[]{:S(2)}, u32[]{:S(2)}) collective-permute-start(bf16[256,1024]{1,0:T(8,128)(2,1)S(1)} %get-tuple-element.13), channel_id=1, source_target_pairs={{0,2},{2,0},{4,6},{6,4},{8,10},{10,8},{12,14},{14,12},{1,3},{3,1},... | collective-permute-start | bytes 1572872 | tf_op jit(solution)/shard_map/ppermute | solution.py:189
  5.4 28.8 %collective-permute-start.22 = (bf16[512,256]{1,0:T(8,128)(2,1)S(1)}, bf16[512,256]{1,0:T(8,128)(2,1)S(1)}, u32[]{:S(2)}, u32[]{:S(2)}) collective-permute-start(bf16[512,256]{1,0:T(8,128)(2,1)S(1)} %constant_dynamic-slice_fusion), channel_id=1, source_target_pairs={{0,4},{2,6},{4,8},{6,10},{8,12},{10,14},{1,5},{3,7},{5,9},{7,11},{... | collective-permute-start | bytes 786440 | tf_op jit(solution)/shard_map/ppermute | solution.py:172
  10.0 18.3 %collective-permute-start.18 = (bf16[256]{0:T(256)(128)(2,1)S(1)}, bf16[256]{0:T(256)(128)(2,1)S(1)}, u32[]{:S(2)}, u32[]{:S(2)}) collective-permute-start(bf16[256]{0:T(256)(128)(2,1)S(1)} %convert_element_type.51), channel_id=1, source_target_pairs={{0,2},{2,0},{4,6},{6,4},{8,10},{10,8},{12,14},{14,12},{1,3},{3,1},... | collective-permute-start | bytes 1544 | tf_op jit(solution)/shard_map/ppermute | solution.py:233
  12.3 17.2 %collective-permute-start = (bf16[32,1024]{1,0:T(8,128)(2,1)S(1)}, bf16[32,1024]{1,0:T(8,128)(2,1)S(1)}, u32[]{:S(2)}, u32[]{:S(2)}) collective-permute-start(bf16[32,1024]{1,0:T(8,128)(2,1)S(1)} %constant_dynamic-slice_fusion.5), channel_id=1, source_target_pairs={{0,2},{2,0},{4,6},{6,4},{8,10},{10,8},{12,14},{14,12},{1,3},{3,1},... | collective-permute-start | bytes 196616 | tf_op jit(solution)/shard_map/ppermute | solution.py:244
  28.2 8.6 %collective-permute-start.26 = (bf16[512,256]{1,0:T(8,128)(2,1)S(1)}, bf16[512,256]{1,0:T(8,128)(2,1)S(1)}, u32[]{:S(2)}, u32[]{:S(2)}) collective-permute-start(bf16[512,256]{1,0:T(8,128)(2,1)S(1)} %constant_dynamic-slice_fusion), channel_id=1, source_target_pairs={{4,0},{6,2},{8,4},{10,6},{12,8},{14,10},{5,1},{7,3},{9,5},{11,7},{... | collective-permute-start | bytes 786440 | tf_op jit(solution)/shard_map/ppermute | solution.py:172
  29.5 8.8 %collective-permute-start.5 = (bf16[512,256]{1,0:T(8,128)(2,1)}, bf16[512,256]{1,0:T(8,128)(2,1)S(1)}, u32[]{:S(2)}, u32[]{:S(2)}) collective-permute-start(bf16[512,256]{1,0:T(8,128)(2,1)} %constant_dynamic-slice_fusion.2), channel_id=1, source_target_pairs={{0,4},{2,6},{4,8},{6,10},{8,12},{10,14},{1,5},{3,7},{5,9},{7,11},{... | collective-permute-start | bytes 786440 | tf_op jit(solution)/shard_map/ppermute | solution.py:172
  34.1 10.3 %collective-permute-start.9 = (bf16[512,256]{1,0:T(8,128)(2,1)}, bf16[512,256]{1,0:T(8,128)(2,1)S(1)}, u32[]{:S(2)}, u32[]{:S(2)}) collective-permute-start(bf16[512,256]{1,0:T(8,128)(2,1)} %constant_dynamic-slice_fusion.2), channel_id=1, source_target_pairs={{4,0},{6,2},{8,4},{10,6},{12,8},{14,10},{5,1},{7,3},{9,5},{11,7},{... | collective-permute-start | bytes 786440 | tf_op jit(solution)/shard_map/ppermute | solution.py:172
  35.7 24.5 %collective-permute-start.3 = (bf16[256,1024]{1,0:T(8,128)(2,1)S(1)}, bf16[256,1024]{1,0:T(8,128)(2,1)S(1)}, u32[]{:S(2)}, u32[]{:S(2)}) collective-permute-start(bf16[256,1024]{1,0:T(8,128)(2,1)S(1)} %collective-permute-done.1), channel_id=1, source_target_pairs={{0,1},{1,0},{2,3},{3,2},{4,5},{5,4},{6,7},{7,6},{8,9},{9,8},{10,11... | collective-permute-start | bytes 1572872 | tf_op jit(solution)/shard_map/ppermute | solution.py:190
  35.7 27.7 %collective-permute-start.4 = (bf16[256,1024]{1,0:T(8,128)(2,1)S(1)}, bf16[256,1024]{1,0:T(8,128)(2,1)S(1)}, u32[]{:S(2)}, u32[]{:S(2)}) collective-permute-start(bf16[256,1024]{1,0:T(8,128)(2,1)S(1)} %collective-permute-done.2), channel_id=1, source_target_pairs={{0,1},{1,0},{2,3},{3,2},{4,5},{5,4},{6,7},{7,6},{8,9},{9,8},{10,11... | collective-permute-start | bytes 1572872 | tf_op jit(solution)/shard_map/ppermute | solution.py:190
  36.9 10.8 %collective-permute-start.33 = (bf16[512,256]{1,0:T(8,128)(2,1)S(1)}, bf16[512,256]{1,0:T(8,128)(2,1)S(1)}, u32[]{:S(2)}, u32[]{:S(2)}) collective-permute-start(bf16[512,256]{1,0:T(8,128)(2,1)S(1)} %collective-permute-done.22.refs_0_), channel_id=1, source_target_pairs={{4,20},{6,22},{8,24},{10,26},{12,28},{14,30},{20,4},{22,6},{24,8},... | collective-permute-start | bytes 786440 | tf_op jit(solution)/shard_map/ppermute | solution.py:179
  38.3 16.4 %collective-permute-start.23 = (bf16[512,256]{1,0:T(8,128)(2,1)S(1)}, bf16[512,256]{1,0:T(8,128)(2,1)S(1)}, u32[]{:S(2)}, u32[]{:S(2)}) collective-permute-start(bf16[512,256]{1,0:T(8,128)(2,1)S(1)} %collective-permute-done.22.refs_0_), channel_id=1, source_target_pairs={{0,4},{2,6},{4,8},{6,10},{8,12},{10,14},{1,5},{3,7},{5,9},{7,11},{... | collective-permute-start | bytes 786440 | tf_op jit(solution)/shard_map/ppermute | solution.py:172
  44.4 9.6 %collective-permute-start.32 = (bf16[512,256]{1,0:T(8,128)(2,1)S(1)}, bf16[512,256]{1,0:T(8,128)(2,1)S(1)}, u32[]{:S(2)}, u32[]{:S(2)}) collective-permute-start(bf16[512,256]{1,0:T(8,128)(2,1)S(1)} %collective-permute-done.26.refs_0_), channel_id=1, source_target_pairs={{0,16},{2,18},{4,20},{6,22},{8,24},{10,26},{16,0},{18,2},{20,4},{2... | collective-permute-start | bytes 786440 | tf_op jit(solution)/shard_map/ppermute | solution.py:179
  47.6 17.2 %collective-permute-start.27 = (bf16[512,256]{1,0:T(8,128)(2,1)S(1)}, bf16[512,256]{1,0:T(8,128)(2,1)S(1)}, u32[]{:S(2)}, u32[]{:S(2)}) collective-permute-start(bf16[512,256]{1,0:T(8,128)(2,1)S(1)} %collective-permute-done.26.refs_0_), channel_id=1, source_target_pairs={{4,0},{6,2},{8,4},{10,6},{12,8},{14,10},{5,1},{7,3},{9,5},{11,7},{... | collective-permute-start | bytes 786440 | tf_op jit(solution)/shard_map/ppermute | solution.py:172
  54.1 11.6 %collective-permute-start.16 = (bf16[512,256]{1,0:T(8,128)(2,1)S(1)}, bf16[512,256]{1,0:T(8,128)(2,1)S(1)}, u32[]{:S(2)}, u32[]{:S(2)}) collective-permute-start(bf16[512,256]{1,0:T(8,128)(2,1)S(1)} %collective-permute-done.5.refs_0_), channel_id=1, source_target_pairs={{4,20},{6,22},{8,24},{10,26},{12,28},{14,30},{20,4},{22,6},{24,8},... | collective-permute-start | bytes 786440 | tf_op jit(solution)/shard_map/ppermute | solution.py:179
  54.7 18.2 %collective-permute-start.6 = (bf16[512,256]{1,0:T(8,128)(2,1)S(1)}, bf16[512,256]{1,0:T(8,128)(2,1)S(1)}, u32[]{:S(2)}, u32[]{:S(2)}) collective-permute-start(bf16[512,256]{1,0:T(8,128)(2,1)S(1)} %collective-permute-done.5.refs_0_), channel_id=1, source_target_pairs={{0,4},{2,6},{4,8},{6,10},{8,12},{10,14},{1,5},{3,7},{5,9},{7,11},{... | collective-permute-start | bytes 786440 | tf_op jit(solution)/shard_map/ppermute | solution.py:172
  60.2 10.1 %collective-permute-start.15 = (bf16[512,256]{1,0:T(8,128)(2,1)S(1)}, bf16[512,256]{1,0:T(8,128)(2,1)S(1)}, u32[]{:S(2)}, u32[]{:S(2)}) collective-permute-start(bf16[512,256]{1,0:T(8,128)(2,1)S(1)} %collective-permute-done.9.refs_0_), channel_id=1, source_target_pairs={{0,16},{2,18},{4,20},{6,22},{8,24},{10,26},{16,0},{18,2},{20,4},{2... | collective-permute-start | bytes 786440 | tf_op jit(solution)/shard_map/ppermute | solution.py:179
  63.4 10.9 %collective-permute-start.10 = (bf16[512,256]{1,0:T(8,128)(2,1)S(1)}, bf16[512,256]{1,0:T(8,128)(2,1)S(1)}, u32[]{:S(2)}, u32[]{:S(2)}) collective-permute-start(bf16[512,256]{1,0:T(8,128)(2,1)S(1)} %collective-permute-done.9.refs_0_), channel_id=1, source_target_pairs={{4,0},{6,2},{8,4},{10,6},{12,8},{14,10},{5,1},{7,3},{9,5},{11,7},{... | collective-permute-start | bytes 786440 | tf_op jit(solution)/shard_map/ppermute | solution.py:172
  64.8 26.7 %copy-start.1 = (bf16[1024,256]{1,0:T(8,128)(2,1)S(1)}, bf16[1024,256]{1,0:T(8,128)(2,1)}, u32[]{:S(2)}) copy-start(bf16[1024,256]{1,0:T(8,128)(2,1)} %refs_1_.3) | copy-start | bytes 1572868
  64.9 10.2 %collective-permute-start.30 = (bf16[512,256]{1,0:T(8,128)(2,1)S(1)}, bf16[512,256]{1,0:T(8,128)(2,1)S(1)}, u32[]{:S(2)}, u32[]{:S(2)}) collective-permute-start(bf16[512,256]{1,0:T(8,128)(2,1)S(1)} %collective-permute-done.23.refs_0_), channel_id=1, source_target_pairs={{8,24},{10,26},{12,28},{14,30},{24,8},{26,10},{28,12},{30,14},{9,2... | collective-permute-start | bytes 786440 | tf_op jit(solution)/shard_map/ppermute | solution.py:179
  65.7 15.9 %collective-permute-start.24 = (bf16[512,256]{1,0:T(8,128)(2,1)S(1)}, bf16[512,256]{1,0:T(8,128)(2,1)S(1)}, u32[]{:S(2)}, u32[]{:S(2)}) collective-permute-start(bf16[512,256]{1,0:T(8,128)(2,1)S(1)} %collective-permute-done.23.refs_0_), channel_id=1, source_target_pairs={{0,4},{2,6},{4,8},{6,10},{8,12},{10,14},{1,5},{3,7},{5,9},{7,11},{... | collective-permute-start | bytes 786440 | tf_op jit(solution)/shard_map/ppermute | solution.py:172
  70.3 10.0 %collective-permute-start.31 = (bf16[512,256]{1,0:T(8,128)(2,1)S(1)}, bf16[512,256]{1,0:T(8,128)(2,1)S(1)}, u32[]{:S(2)}, u32[]{:S(2)}) collective-permute-start(bf16[512,256]{1,0:T(8,128)(2,1)S(1)} %collective-permute-done.27.refs_2_), channel_id=1, source_target_pairs={{0,16},{2,18},{4,20},{6,22},{16,0},{18,2},{20,4},{22,6},{1,17},{3,... | collective-permute-start | bytes 786440 | tf_op jit(solution)/shard_map/ppermute | solution.py:179
  73.0 14.0 %collective-permute-start.28 = (bf16[512,256]{1,0:T(8,128)(2,1)S(1)}, bf16[512,256]{1,0:T(8,128)(2,1)S(1)}, u32[]{:S(2)}, u32[]{:S(2)}) collective-permute-start(bf16[512,256]{1,0:T(8,128)(2,1)S(1)} %collective-permute-done.27.refs_2_), channel_id=1, source_target_pairs={{4,0},{6,2},{8,4},{10,6},{12,8},{14,10},{5,1},{7,3},{9,5},{11,7},{... | collective-permute-start | bytes 786440 | tf_op jit(solution)/shard_map/ppermute | solution.py:172
  74.3 13.4 %collective-permute-start.13 = (bf16[512,256]{1,0:T(8,128)(2,1)S(1)}, bf16[512,256]{1,0:T(8,128)(2,1)S(1)}, u32[]{:S(2)}, u32[]{:S(2)}) collective-permute-start(bf16[512,256]{1,0:T(8,128)(2,1)S(1)} %collective-permute-done.6.refs_0_), channel_id=1, source_target_pairs={{8,24},{10,26},{12,28},{14,30},{24,8},{26,10},{28,12},{30,14},{9,2... | collective-permute-start | bytes 786440 | tf_op jit(solution)/shard_map/ppermute | solution.py:179
  75.1 33.6 %collective-permute-start.14 = (bf16[512,256]{1,0:T(8,128)(2,1)S(1)}, bf16[512,256]{1,0:T(8,128)(2,1)S(1)}, u32[]{:S(2)}, u32[]{:S(2)}) collective-permute-start(bf16[512,256]{1,0:T(8,128)(2,1)S(1)} %collective-permute-done.10.refs_2_), channel_id=1, source_target_pairs={{0,16},{2,18},{4,20},{6,22},{16,0},{18,2},{20,4},{22,6},{1,17},{3,... | collective-permute-start | bytes 786440 | tf_op jit(solution)/shard_map/ppermute | solution.py:179
  80.3 17.3 %collective-permute-start.11 = (bf16[512,256]{1,0:T(8,128)(2,1)S(1)}, bf16[512,256]{1,0:T(8,128)(2,1)S(1)}, u32[]{:S(2)}, u32[]{:S(2)}) collective-permute-start(bf16[512,256]{1,0:T(8,128)(2,1)S(1)} %collective-permute-done.10.refs_2_), channel_id=1, source_target_pairs={{4,0},{6,2},{8,4},{10,6},{12,8},{14,10},{5,1},{7,3},{9,5},{11,7},{... | collective-permute-start | bytes 786440 | tf_op jit(solution)/shard_map/ppermute | solution.py:172
  81.6 18.3 %collective-permute-start.7 = (bf16[512,256]{1,0:T(8,128)(2,1)S(1)}, bf16[512,256]{1,0:T(8,128)(2,1)S(1)}, u32[]{:S(2)}, u32[]{:S(2)}) collective-permute-start(bf16[512,256]{1,0:T(8,128)(2,1)S(1)} %collective-permute-done.6.refs_0_), channel_id=1, source_target_pairs={{0,4},{2,6},{4,8},{6,10},{8,12},{10,14},{1,5},{3,7},{5,9},{7,11},{... | collective-permute-start | bytes 786440 | tf_op jit(solution)/shard_map/ppermute | solution.py:172
  87.0 23.8 %collective-permute-start.25 = (bf16[512,256]{1,0:T(8,128)(2,1)S(1)}, bf16[512,256]{1,0:T(8,128)(2,1)S(1)}, u32[]{:S(2)}, u32[]{:S(2)}) collective-permute-start(bf16[512,256]{1,0:T(8,128)(2,1)S(1)} %collective-permute-done.24.refs_0_), channel_id=1, source_target_pairs={{12,28},{14,30},{28,12},{30,14},{13,29},{15,31},{29,13},{31,15}} | collective-permute-start | bytes 786440 | tf_op jit(solution)/shard_map/ppermute | solution.py:179
  87.7 23.1 %collective-permute-start.29 = (bf16[512,256]{1,0:T(8,128)(2,1)S(1)}, bf16[512,256]{1,0:T(8,128)(2,1)S(1)}, u32[]{:S(2)}, u32[]{:S(2)}) collective-permute-start(bf16[512,256]{1,0:T(8,128)(2,1)S(1)} %collective-permute-done.28.refs_2_), channel_id=1, source_target_pairs={{0,16},{2,18},{16,0},{18,2},{1,17},{3,19},{17,1},{19,3}} | collective-permute-start | bytes 786440 | tf_op jit(solution)/shard_map/ppermute | solution.py:179
  91.5 2.0 %copy-start.2 = (bf16[1024,256]{1,0:T(8,128)(2,1)S(1)}, bf16[1024,256]{1,0:T(8,128)(2,1)}, u32[]{:S(2)}) copy-start(bf16[1024,256]{1,0:T(8,128)(2,1)} %refs_1_.2) | copy-start | bytes 1572868
  97.6 15.2 %collective-permute-start.12 = (bf16[512,256]{1,0:T(8,128)(2,1)S(1)}, bf16[512,256]{1,0:T(8,128)(2,1)S(1)}, u32[]{:S(2)}, u32[]{:S(2)}) collective-permute-start(bf16[512,256]{1,0:T(8,128)(2,1)S(1)} %collective-permute-done.11.refs_2_), channel_id=1, source_target_pairs={{0,16},{2,18},{16,0},{18,2},{1,17},{3,19},{17,1},{19,3}} | collective-permute-start | bytes 786440 | tf_op jit(solution)/shard_map/ppermute | solution.py:179
  99.9 13.0 %collective-permute-start.8 = (bf16[512,256]{1,0:T(8,128)(2,1)S(1)}, bf16[512,256]{1,0:T(8,128)(2,1)S(1)}, u32[]{:S(2)}, u32[]{:S(2)}) collective-permute-start(bf16[512,256]{1,0:T(8,128)(2,1)S(1)} %collective-permute-done.7.refs_0_), channel_id=1, source_target_pairs={{12,28},{14,30},{28,12},{30,14},{13,29},{15,31},{29,13},{31,15}} | collective-permute-start | bytes 786440 | tf_op jit(solution)/shard_map/ppermute | solution.py:179
  112.9 8.8 %copy-start.4 = (f32[128]{0:T(128)S(1)}, f32[128]{0:T(128)}, u32[]{:S(2)}) copy-start(f32[128]{0:T(128)} %param.14) | copy-start | bytes 1540
  115.0 6.4 %collective-permute-start.17 = (f32[512,128]{1,0:T(8,128)S(1)}, f32[512,128]{1,0:T(8,128)S(1)}, u32[]{:S(2)}, u32[]{:S(2)}) collective-permute-start(f32[512,128]{1,0:T(8,128)S(1)} %pad_maximum_fusion.1), channel_id=1, source_target_pairs={{0,2},{2,0},{4,6},{6,4},{8,10},{10,8},{12,14},{14,12},{1,3},{3,1},... | collective-permute-start | bytes 786440 | tf_op jit(solution)/shard_map/ppermute | solution.py:228
  116.6 6.9 %collective-permute-start.34 = (bf16[512,128]{1,0:T(8,128)(2,1)S(1)}, bf16[512,128]{1,0:T(8,128)(2,1)S(1)}, u32[]{:S(2)}, u32[]{:S(2)}) collective-permute-start(bf16[512,128]{1,0:T(8,128)(2,1)S(1)} %pad_maximum_fusion.2), channel_id=1, source_target_pairs={{0,2},{2,0},{4,6},{6,4},{8,10},{10,8},{12,14},{14,12},{1,3},{3,1},... | collective-permute-start | bytes 393224 | tf_op jit(solution)/shard_map/ppermute | solution.py:265
  121.8 6.7 %collective-permute-start.19 = (bf16[528,128]{1,0:T(8,128)(2,1)S(1)}, bf16[528,128]{1,0:T(8,128)(2,1)S(1)}, u32[]{:S(2)}, u32[]{:S(2)}) collective-permute-start(bf16[528,128]{1,0:T(8,128)(2,1)S(1)} %fusion.1), channel_id=1, source_target_pairs={{0,12},{2,14},{4,0},{6,2},{8,4},{10,6},{12,8},{14,10},{1,13},{3,15... | collective-permute-start | bytes 405512 | tf_op jit(solution)/shard_map/ppermute | solution.py:175
  123.5 20.4 %collective-permute-start.35 = (bf16[512,128]{1,0:T(8,128)(2,1)S(1)}, bf16[512,128]{1,0:T(8,128)(2,1)S(1)}, u32[]{:S(2)}, u32[]{:S(2)}) collective-permute-start(bf16[512,128]{1,0:T(8,128)(2,1)S(1)} %add_convert_fusion.1.refs_0_), channel_id=1, source_target_pairs={{0,12},{2,14},{4,0},{6,2},{8,4},{10,6},{12,8},{14,10},{1,13},{3,15... | collective-permute-start | bytes 393224 | tf_op jit(solution)/shard_map/ppermute | solution.py:175
  124.6 19.4 %collective-permute-start.36 = (bf16[512,128]{1,0:T(8,128)(2,1)S(1)}, bf16[512,128]{1,0:T(8,128)(2,1)S(1)}, u32[]{:S(2)}, u32[]{:S(2)}) collective-permute-start(bf16[512,128]{1,0:T(8,128)(2,1)S(1)} %add_convert_fusion.1.refs_0_), channel_id=1, source_target_pairs={{0,8},{2,10},{4,12},{6,14},{8,0},{10,2},{12,4},{14,6},{1,9},{3,11}... | collective-permute-start | bytes 393224 | tf_op jit(solution)/shard_map/ppermute | solution.py:175
  125.4 18.6 %collective-permute-start.37 = (bf16[512,128]{1,0:T(8,128)(2,1)S(1)}, bf16[512,128]{1,0:T(8,128)(2,1)S(1)}, u32[]{:S(2)}, u32[]{:S(2)}) collective-permute-start(bf16[512,128]{1,0:T(8,128)(2,1)S(1)} %add_convert_fusion.1.refs_0_), channel_id=1, source_target_pairs={{0,4},{2,6},{4,8},{6,10},{8,12},{10,14},{12,0},{14,2},{1,5},{3,7},... | collective-permute-start | bytes 393224 | tf_op jit(solution)/shard_map/ppermute | solution.py:175
  125.6 16.4 %collective-permute-start.20 = (bf16[528,128]{1,0:T(8,128)(2,1)S(1)}, bf16[528,128]{1,0:T(8,128)(2,1)S(1)}, u32[]{:S(2)}, u32[]{:S(2)}) collective-permute-start(bf16[528,128]{1,0:T(8,128)(2,1)S(1)} %fusion.1), channel_id=1, source_target_pairs={{0,8},{2,10},{4,12},{6,14},{8,0},{10,2},{12,4},{14,6},{1,9},{3,11}... | collective-permute-start | bytes 405512 | tf_op jit(solution)/shard_map/ppermute | solution.py:175
  128.5 13.5 %collective-permute-start.21 = (bf16[528,128]{1,0:T(8,128)(2,1)S(1)}, bf16[528,128]{1,0:T(8,128)(2,1)S(1)}, u32[]{:S(2)}, u32[]{:S(2)}) collective-permute-start(bf16[528,128]{1,0:T(8,128)(2,1)S(1)} %fusion.1), channel_id=1, source_target_pairs={{0,4},{2,6},{4,8},{6,10},{8,12},{10,14},{12,0},{14,2},{1,5},{3,7},... | collective-permute-start | bytes 405512 | tf_op jit(solution)/shard_map/ppermute | solution.py:175
  144.7 5.6 %collective-permute-start.38 = (bf16[64,1024]{1,0:T(8,128)(2,1)S(1)}, bf16[64,1024]{1,0:T(8,128)(2,1)S(1)}, u32[]{:S(2)}, u32[]{:S(2)}) collective-permute-start(bf16[64,1024]{1,0:T(8,128)(2,1)S(1)} %shard_map.111.refs_0_), channel_id=1, source_target_pairs={{0,12},{2,14},{4,0},{6,2},{8,4},{10,6},{12,8},{14,10},{1,13},{3,15... | collective-permute-start | bytes 393224 | tf_op jit(solution)/shard_map/ppermute | solution.py:175
  146.3 10.9 %collective-permute-start.39 = (bf16[64,1024]{1,0:T(8,128)(2,1)S(1)}, bf16[64,1024]{1,0:T(8,128)(2,1)S(1)}, u32[]{:S(2)}, u32[]{:S(2)}) collective-permute-start(bf16[64,1024]{1,0:T(8,128)(2,1)S(1)} %shard_map.111.refs_0_), channel_id=1, source_target_pairs={{0,8},{2,10},{4,12},{6,14},{8,0},{10,2},{12,4},{14,6},{1,9},{3,11}... | collective-permute-start | bytes 393224 | tf_op jit(solution)/shard_map/ppermute | solution.py:175
  146.9 11.8 %collective-permute-start.40 = (bf16[64,1024]{1,0:T(8,128)(2,1)S(1)}, bf16[64,1024]{1,0:T(8,128)(2,1)S(1)}, u32[]{:S(2)}, u32[]{:S(2)}) collective-permute-start(bf16[64,1024]{1,0:T(8,128)(2,1)S(1)} %shard_map.111.refs_0_), channel_id=1, source_target_pairs={{0,4},{2,6},{4,8},{6,10},{8,12},{10,14},{12,0},{14,2},{1,5},{3,7},... | collective-permute-start | bytes 393224 | tf_op jit(solution)/shard_map/ppermute | solution.py:175
  148.8 10.4 %collective-permute-start.41 = (bf16[64,1024]{1,0:T(8,128)(2,1)S(1)}, bf16[64,1024]{1,0:T(8,128)(2,1)S(1)}, u32[]{:S(2)}, u32[]{:S(2)}) collective-permute-start(bf16[64,1024]{1,0:T(8,128)(2,1)S(1)} %shard_map.111.refs_0_), channel_id=1, source_target_pairs={{0,2},{2,0},{4,6},{6,4},{8,10},{10,8},{12,14},{14,12},{1,3},{3,1},... | collective-permute-start | bytes 393224 | tf_op jit(solution)/shard_map/ppermute | solution.py:277
  150.4 8.9 %collective-permute-start.42 = (bf16[64,1024]{1,0:T(8,128)(2,1)S(1)}, bf16[64,1024]{1,0:T(8,128)(2,1)S(1)}, u32[]{:S(2)}, u32[]{:S(2)}) collective-permute-start(bf16[64,1024]{1,0:T(8,128)(2,1)S(1)} %collective-permute-done.38.refs_1_), channel_id=1, source_target_pairs={{0,2},{2,0},{4,6},{6,4},{8,10},{10,8},{12,14},{14,12},{1,3},{3,1},... | collective-permute-start | bytes 393224 | tf_op jit(solution)/shard_map/ppermute | solution.py:277
  157.2 5.0 %collective-permute-start.43 = (bf16[64,1024]{1,0:T(8,128)(2,1)S(1)}, bf16[64,1024]{1,0:T(8,128)(2,1)S(1)}, u32[]{:S(2)}, u32[]{:S(2)}) collective-permute-start(bf16[64,1024]{1,0:T(8,128)(2,1)S(1)} %collective-permute-done.39.refs_2_), channel_id=1, source_target_pairs={{0,2},{2,0},{4,6},{6,4},{8,10},{10,8},{12,14},{14,12},{1,3},{3,1},... | collective-permute-start | bytes 393224 | tf_op jit(solution)/shard_map/ppermute | solution.py:277
  158.7 5.0 %collective-permute-start.44 = (bf16[64,1024]{1,0:T(8,128)(2,1)S(1)}, bf16[64,1024]{1,0:T(8,128)(2,1)S(1)}, u32[]{:S(2)}, u32[]{:S(2)}) collective-permute-start(bf16[64,1024]{1,0:T(8,128)(2,1)S(1)} %collective-permute-done.40.refs_3_), channel_id=1, source_target_pairs={{0,2},{2,0},{4,6},{6,4},{8,10},{10,8},{12,14},{14,12},{1,3},{3,1},... | collective-permute-start | bytes 393224 | tf_op jit(solution)/shard_map/ppermute | solution.py:277
  163.6 2.2 %copy-start = (bf16[2048,1024]{1,0:T(8,128)(2,1)S(1)}, bf16[2048,1024]{1,0:T(8,128)(2,1)}, u32[]{:S(2)}) copy-start(bf16[2048,1024]{1,0:T(8,128)(2,1)} %refs_9_.1) | copy-start | bytes 12582916
  165.8 3.5 %copy-start.3 = (bf16[128,1024]{1,0:T(8,128)(2,1)S(1)}, bf16[128,1024]{1,0:T(8,128)(2,1)}, u32[]{:S(2)}) copy-start(bf16[128,1024]{1,0:T(8,128)(2,1)} %param.17) | copy-start | bytes 786436
  167.7 1.6 collective-permute-start.45

commit v2 on v0

v2 whole, which is shorter than its diff:
```python
import functools
import math

import jax
import jax.numpy as jnp
from jax import lax
from jax.experimental import pallas as pl
from jax.experimental.pallas import tpu as pltpu
from jax.sharding import PartitionSpec as P

HD = 128
F32 = jnp.float32
BF16 = jnp.bfloat16
VMEM_BYTES = 20 * 1024 * 1024
PARAMS = pltpu.CompilerParams(vmem_limit_bytes=VMEM_BYTES)
BIG = pltpu.CompilerParams(vmem_limit_bytes=52 * 1024 * 1024)
WHOLE = pl.BlockSpec(memory_space=pltpu.VMEM)
FREE = pl.BlockSpec(memory_space=pltpu.HBM)


def dot(a, b):
    return jnp.dot(a, b, preferred_element_type=F32)


def dot_nt(a, b):
    return lax.dot_general(a, b, (((1,), (1,)), ((), ())), preferred_element_type=F32)


def share_kernel(idx_ref, image, key_weight, value_weight, to_y, to_x, to_both, own, sems):
    par, core, y = idx_ref[0], idx_ref[1], idx_ref[2]
    half = own.shape[0] // 2
    half_lines = to_y.shape[1] // half
    copies = []
    at_w = pl.multiple_of(par * half, half)
    copies.append((key_weight.at[pl.ds(at_w, half), :], own.at[pl.ds(0, half), :]))
    copies.append((value_weight.at[pl.ds(at_w, half), :], own.at[pl.ds(half, half), :]))
    for out, to_par, to_y_at in ((to_x, 1 - par, y), (to_y, par, 1 - y), (to_both, 1 - par, 1 - y)):
        for l in range(half_lines):
            at = pl.multiple_of(((2 * (core * half_lines + l) + to_y_at) * 2 + to_par) * half, half)
            copies.append((image.at[:, pl.ds(at, half)], out.at[:, pl.ds(l * half, half)]))
    copies = [pltpu.make_async_copy(src, dst, sems.at[i]) for i, (src, dst) in enumerate(copies)]
    for c in copies:
        c.start()
    for c in copies:
        c.wait()


def project_kernel(sources, extra, idx_ref, slots, image, *refs):
    par, core, y, inner = idx_ref[0], idx_ref[1], idx_ref[2], idx_ref[3]
    got, refs = refs[:6], refs[6:]
    weights, outs, (x_ref, w_ref, acc_ref, sems) = refs[:-8], refs[-8:-4], refs[-4:]
    rows = image.shape[0]
    half = w_ref.shape[1]
    half_lines = got[0].shape[1] // half

    def copy(src, dst, k, i):
        return pltpu.make_async_copy(src, dst, sems.at[k, i])

    waits = []
    for k, (in_src, out_src) in enumerate(sources):
        line = idx_ref[4 + k]
        own_at = pl.multiple_of(((2 * line + y) * 2 + par) * half, half)
        here = line // half_lines == core
        got_at = pl.multiple_of(lax.rem(line, half_lines) * half, half)
        own = copy(image.at[:, pl.ds(own_at, half)], x_ref.at[k, pl.ds(0, rows), :], k, 0)
        own.start()

        def from_core(which, k=k, got_at=got_at):
            return [
                copy(
                    got[2 * i + which].at[:, pl.ds(got_at, half)],
                    x_ref.at[k, pl.ds((i + 1) * rows, rows), :],
                    k,
                    1 + i,
                )
                for i in range(3)
            ]

        def from_weight(src, k=k):
            return copy(weights[src[0]].at[pl.ds(src[1], half), :], w_ref.at[k], k, 4)

        mine = from_core(0)
        weight = from_weight(in_src)

        @pl.when(here)
        def _(mine=mine):
            for c in mine:
                c.start()

        @pl.when(jnp.logical_not(here))
        def _(from_core=from_core):
            for c in from_core(1):
                c.start()

        if in_src == out_src:
            weight.start()
        else:

            @pl.when(inner > 0)
            def _(weight=weight):
                weight.start()

            @pl.when(inner <= 0)
            def _(from_weight=from_weight, out_src=out_src):
                from_weight(out_src).start()

        waits.append([own] + mine + [weight])
    for k in range(len(sources)):
        for c in waits[k]:
            c.wait()
        part = dot(x_ref[k], w_ref[k])
        if k == 0:
            acc_ref[...] = part
        else:
            acc_ref[...] += part
    keep, to_y, to_x, to_both = outs
    cols = keep.shape[1]
    mine = pl.ds(pl.multiple_of(y * cols, cols), cols)
    other = pl.ds(pl.multiple_of((1 - y) * cols, cols), cols)
    kind = to_y.dtype
    keep[...] = acc_ref[: 2 * rows, mine]
    to_y[:rows, :] = acc_ref[rows : 2 * rows, other].astype(kind)
    to_y[rows : 2 * rows, :] = acc_ref[:rows, other].astype(kind)
    to_x[...] = acc_ref[2 * rows :, mine].astype(kind)
    to_both[:rows, :] = acc_ref[3 * rows :, other].astype(kind)
    to_both[rows:, :] = acc_ref[2 * rows : 3 * rows, other].astype(kind)
    if extra:
        n = slots.shape[0]
        to_y[2 * rows : 2 * rows + n, :HD] = slots[...]
        to_y[2 * rows + n :, :] = jnp.zeros((extra - n, cols), kind)
        if cols > HD:
            to_y[2 * rows : 2 * rows + n, HD:] = jnp.zeros((n, cols - HD), kind)


def key_kernel(keep, got_y, got_x, got_both, gain, slots, out):
    rows = keep.shape[0]
    n = slots.shape[0]
    raw = (keep[...] + got_y[:rows, :]) + (got_x[...] + got_both[...])
    for c in range(0, raw.shape[1], HD):
        part = raw[:, c : c + HD]
        scale = lax.rsqrt(jnp.mean(part * part, axis=-1, keepdims=True) + 1e-05)
        out[:rows, c : c + HD] = (part * scale * gain[...]).astype(BF16)
    pad = jnp.zeros((out.shape[0] - rows - 2 * n, HD), F32)
    out[rows:, :HD] = jnp.concatenate([slots[...], got_y[rows : rows + n, :HD], pad], 0).astype(BF16)


def score_kernel(n, heads, q_ref, limit_ref, *refs):
    pieces = refs[:n]
    expo_ref, total_ref, s_ref = refs[n:]
    rows = limit_ref.shape[0]
    piece = s_ref.shape[1] // n
    scale = 1.0 / math.sqrt(HD)
    limit = limit_ref[...]
    top = jnp.full((heads * rows, 1), -1e30, F32)
    for i in range(n):
        slots = pieces[i][piece : piece + 16, :].astype(F32)
        seen = []
        for c in range(piece // HD):
            slot = slots[c : c + 1, :]
            seen.append(jnp.where((slot >= 0.0) & (slot <= limit), 1.0, 0.0))
        seen = jnp.concatenate(seen, 1)
        s = dot_nt(q_ref[...], pieces[i][:piece, :]) * scale
        s = jnp.where(seen[None] > 0.5, s.reshape(heads, rows, piece), -1e30).reshape(heads * rows, piece)
        s_ref[:, i * piece : (i + 1) * piece] = s
        top = jnp.maximum(top, jnp.max(s, axis=1, keepdims=True))
    total = jnp.zeros((heads * rows, 1), F32)
    for i in range(n):
        s = s_ref[:, i * piece : (i + 1) * piece]
        e = jnp.where(s > -1e29, jnp.exp(s - top), 0.0)
        total = total + jnp.sum(e, axis=1, keepdims=True)
        expo_ref[:, i * piece : (i + 1) * piece] = e.astype(BF16)
    total_ref[...] = total


def value_kernel(n, heads, expo_ref, total_ref, *refs):
    values, out_ref = refs[:n], refs[n]
    rows = out_ref.shape[0]
    piece = values[0].shape[0]
    acc = jnp.zeros((heads * rows, HD), F32)
    for i in range(n):
        acc = acc + dot(expo_ref[:, i * piece : (i + 1) * piece], values[i][...])
    attn = (acc / total_ref[...]).astype(BF16)
    for j in range(heads):
        out_ref[:, j * HD : (j + 1) * HD] = attn[j * rows : (j + 1) * rows, :]


def proj_kernel(n, idx_ref, *refs):
    pieces = refs[:n]
    w_ref, keep_ref, send_ref, a_ref, p_ref = refs[n:]
    rows, width = pieces[0].shape

    @pl.when(pl.program_id(0) == 0)
    def _():
        for k in range(n):
            at_row = pl.multiple_of(idx_ref[1 + 2 * k] * rows, rows)
            at_col = pl.multiple_of(idx_ref[2 + 2 * k] * width, width)
            a_ref[pl.ds(at_row, rows), pl.ds(at_col, width)] = pieces[k][...]

    p_ref[...] = dot(a_ref[...], w_ref[...])
    part = keep_ref.shape[0]
    core = idx_ref[0]
    keep_ref[...] = p_ref[pl.ds(pl.multiple_of(core * part, part), part), :]
    send_ref[...] = p_ref[pl.ds(pl.multiple_of((1 - core) * part, part), part), :].astype(BF16)


def body(
    image_feats,
    slot_image,
    key_weight,
    value_weight,
    key_gain,
    queries,
    text_image,
    text_hidden,
    out_weight,
    attn_gate,
):
    groups, nblk, cores = (lax.axis_size(a) for a in ("groups", "blk", "heads"))
    lines = nblk // 2
    tok = image_feats.shape[0]
    depth = key_weight.shape[0]
    kv_cols = key_weight.shape[1]
    mine_cols = kv_cols // 2
    text_rows = queries.shape[0]
    q_half = queries.shape[1] // 2
    per_kv = q_half // mine_cols
    grp, blk, core = (lax.axis_index(a) for a in ("groups", "blk", "heads"))
    par = grp % 2
    y = blk % 2
    line = blk // 2

    swap_y = [(b, b ^ 1) for b in range(nblk)]
    swap_core = [(c, c ^ 1) for c in range(cores)]
    half = depth // 2
    fast = lines == 4 and cores == 2 and kv_cols == 2 * HD

    def along(name, array, d, ok=lambda l: True):
        with jax.named_scope(f"{name}_z{d}"):
            return lax.ppermute(array, "blk", [(b, b ^ (2 * d)) for b in range(nblk) if ok(b // 2)])

    def over_y(name, array):
        with jax.named_scope(name + "_y"):
            return lax.ppermute(array, "blk", swap_y)

    def over_core(name, array):
        with jax.named_scope(name + "_core"):
            return lax.ppermute(array, "heads", swap_core)

    def over_x(name, array):
        with jax.named_scope(name + "_x"):
            return lax.ppermute(array, "groups", [(g, g ^ 1) for g in range(groups)])

    def over_both(name, array):
        pairs = [(g * nblk + b, (g ^ 1) * nblk + (b ^ 1)) for g in range(groups) for b in range(nblk)]
        with jax.named_scope(name + "_xy"):
            return lax.ppermute(array, ("groups", "blk"), pairs)

    def hold(*arrays):
        return lax.optimization_barrier(arrays)

    def take_y(array, size, which):
        return lax.dynamic_slice_in_dim(array, which * size, size, 1)

    def middle(l):
        return l in (1, 2)

    half_lines = lines // 2

    def share(to_x, to_y):
        return jnp.concatenate(
            [
                lax.dynamic_slice_in_dim(
                    image_feats, ((2 * (core * half_lines + l) + to_y) * 2 + to_x) * half, half, 1
                )
                for l in range(half_lines)
            ],
            1,
        )

    half_lines = lines // 2
    scalars = pl.BlockSpec(memory_space=pltpu.SMEM)
    share = jax.ShapeDtypeStruct((tok, half_lines * half), BF16)
    share_y, share_x, share_both, own = pl.pallas_call(
        share_kernel,
        out_shape=(share, share, share, jax.ShapeDtypeStruct((2 * half, kv_cols), BF16)),
        in_specs=[scalars, FREE, FREE, FREE],
        out_specs=(WHOLE,) * 4,
        scratch_shapes=[pltpu.SemaphoreType.DMA((2 + 3 * half_lines,))],
        compiler_params=pltpu.CompilerParams(vmem_limit_bytes=56 * 1024 * 1024),
    )(jnp.stack([par, core, y]), image_feats, key_weight, value_weight)
    if fast:
        z1, zm = along("w", own, 1), along("w", own, 3, middle)
        img_y, img_x = over_y("image", share_y), over_x("image", share_x)
        z1, zm, img_y, img_x, share_both = hold(z1, zm, img_y, img_x, share_both)
        fb, fa = along("w_across", z1, 3, middle), along("w_out", zm, 1, middle)
        img_both = over_both("image", share_both)
        core_y, core_x = over_core("image", img_y), over_core("image", img_x)
        fb, fa, img_both, core_y, core_x = hold(fb, fa, img_both, core_y, core_x)
        core_both = over_core("image", img_both)
        last_k, last_v = along("wk_end", fb[:half], 1, middle), along("wv_end", fb[half:], 1, middle)
        shared = [z1, fb, fa, zm]
        key_refs, value_refs = [own] + shared + [last_k], [own] + shared + [last_v]
        pairs = lambda at: (((0, at), (0, at)), ((1, at), (1, at)), ((2, at), (3, at)), ((4, at), (5, 0)))
        key_from, value_from = pairs(0), pairs(half)
    else:
        img_y, img_x, img_both = over_y("image", share_y), over_x("image", share_x), over_both("image", share_both)
        core_y, core_x, core_both = (over_core("image", i) for i in (img_y, img_x, img_both))
        shards = [own] + [along("w", own, d) for d in range(1, lines)]
        key_refs = value_refs = shards
        key_from = tuple(((d, 0), (d, 0)) for d in range(lines))
        value_from = tuple(((d, half), (d, half)) for d in range(lines))
    pieces = [img_y, core_y, img_x, core_x, img_both, core_both]
    slots = slot_image.astype(F32).reshape(tok // HD, HD)
    extra = 8 * (-(-(tok // HD) // 8))

    def project(weights, sources, extra, kind):
        idx = [par, core, y, ((line == 1) | (line == 2)).astype(jnp.int32)] + [line ^ d for d in range(lines)]
        out = lambda rows, dtype: jax.ShapeDtypeStruct((rows, mine_cols), dtype)
        macs = 4 * tok * half * kv_cols * lines
        return pl.pallas_call(
            functools.partial(project_kernel, sources, extra),
            out_shape=(out(2 * tok, F32), out(2 * tok + extra, kind), out(2 * tok, kind), out(2 * tok, kind)),
            in_specs=[scalars, WHOLE] + [FREE] * (7 + len(weights)),
            out_specs=(WHOLE,) * 4,
            scratch_shapes=[
                pltpu.VMEM((lines, 4 * tok, half), BF16),
                pltpu.VMEM((lines, half, kv_cols), BF16),
                pltpu.VMEM((4 * tok, kv_cols), F32),
                pltpu.SemaphoreType.DMA((lines, 5)),
            ],
            compiler_params=BIG,
            cost_estimate=pl.CostEstimate(flops=2 * macs, bytes_accessed=macs // 64, transcendentals=0),
        )(jnp.stack(idx), slots, image_feats, *pieces, *weights)

    keep, to_y, to_x, to_both = project(key_refs, key_from, extra, F32)
    key_parts = [over_y("key", to_y), over_x("key", to_x), over_both("key", to_both)]
    slot_rows = 2 * tok // HD
    packed = pl.pallas_call(
        key_kernel,
        out_shape=jax.ShapeDtypeStruct((2 * tok + slot_rows + (-slot_rows % 16), mine_cols), BF16),
        in_specs=[WHOLE] * 6,
        out_specs=WHOLE,
        compiler_params=PARAMS,
    )(keep, *key_parts, key_gain.reshape(1, HD), slots)

    rows = 2 * text_rows
    if fast:
        def to_head(name, tile):
            pairs = [
                ((2 * l + yy) * cores + c, (2 * (2 * c + yy) + l % 2) * cores + l // 2)
                for l in range(lines)
                for yy in range(2)
                for c in range(cores)
            ]
            with jax.named_scope(name + "_head"):
                tile = lax.ppermute(tile, ("blk", "heads"), pairs)
            there = over_y(name + "_tile", tile)
            return [tile, there, over_core(name + "_tile", tile), over_core(name + "_tile", there)]

        def query_round(r):
            pairs = [
                ((2 * l + yy) * cores + c, (2 * (2 * c + (r ^ yy)) + l % 2) * cores + l // 2)
                for l in range(lines)
                for yy in range(2)
                for c in range(cores)
            ]
            with jax.named_scope("q_head"):
                return lax.ppermute(take_y(queries, q_half, y ^ r), ("blk", "heads"), pairs)

        q_0, q_1 = query_round(0), query_round(1)
        is_low = line % 2 == 0
        row_at = 2 * core + y
    else:

        def to_head(name, tile):
            return [tile if d == 0 else along(name, tile, d) for d in range(lines)]

        q_0, q_1 = take_y(queries, q_half, y), over_y("q", take_y(queries, q_half, 1 - y))
        is_low = y == 0
        row_at = line
    q_rows = jnp.concatenate([jnp.where(is_low, q_0, q_1), jnp.where(is_low, q_1, q_0)], 0)
    q_all = q_rows.reshape(rows, per_kv, HD).transpose(1, 0, 2).reshape(per_kv * rows, HD)
    limit = lax.dynamic_slice_in_dim(text_image, row_at * rows, rows, 0).astype(F32).reshape(rows, 1)

    key_pieces = to_head("key", packed)

    tokens = 2 * tok * lines
    expo, total = pl.pallas_call(
        functools.partial(score_kernel, lines, per_kv),
        out_shape=(
            jax.ShapeDtypeStruct((per_kv * rows, tokens), BF16),
            jax.ShapeDtypeStruct((per_kv * rows, 1), F32),
        ),
        in_specs=[WHOLE] * (2 + lines),
        out_specs=(WHOLE, WHOLE),
        scratch_shapes=[pltpu.VMEM((per_kv * rows, tokens), F32)],
        compiler_params=PARAMS,
    )(q_all, limit, *key_pieces)

    keep, to_y, to_x, to_both = project(value_refs, value_from, 0, BF16)
    value_parts = [over_y("value", to_y), over_x("value", to_x), over_both("value", to_both)]
    value_y, value_x, value_both = (part.astype(F32) for part in value_parts)
    values = ((keep + value_y) + (value_x + value_both)).astype(BF16)
    value_pieces = to_head("value", values)

    attn = pl.pallas_call(
        functools.partial(value_kernel, lines, per_kv),
        out_shape=jax.ShapeDtypeStruct((rows, q_half), BF16),
        in_specs=[WHOLE] * (2 + lines),
        out_specs=WHOLE,
        compiler_params=PARAMS,
    )(expo, total, *value_pieces)

    where = []
    if fast:
        mine = []
        for k in range(lines):
            pairs = [
                ((2 * l + yy) * cores + c, (2 * ((2 * (l % 2) + c) ^ k) + yy) * cores + l // 2)
                for l in range(lines)
                for yy in range(2)
                for c in range(cores)
            ]
            with jax.named_scope(f"attn_out{k}"):
                mine.append(lax.ppermute(attn, ("blk", "heads"), pairs))
            where.append((2 * ((line ^ k) % 2), (line ^ k) // 2))
        where = [(at + y, col) for at, col in where] + [(at + 1 - y, col) for at, col in where]
    else:
        mine = [attn if d == 0 else along("attn", attn, d) for d in range(lines)]
        where = [(line ^ d, y) for d in range(lines)] + [(line ^ d, 1 - y) for d in range(lines)]
    other = [over_y(f"attn{d}", m) for d, m in enumerate(mine)]

    out_rows = lines * rows
    out_cols = out_weight.shape[1]
    tile = out_cols // max(1, out_cols // 256)
    out_spec = pl.BlockSpec((out_rows // 2, tile), lambda i, s: (0, i))
    keep, send = pl.pallas_call(
        functools.partial(proj_kernel, 2 * lines),
        out_shape=(
            jax.ShapeDtypeStruct((out_rows // 2, out_cols), F32),
            jax.ShapeDtypeStruct((out_rows // 2, out_cols), BF16),
        ),
        grid_spec=pltpu.PrefetchScalarGridSpec(
            num_scalar_prefetch=1,
            grid=(out_cols // tile,),
            in_specs=[pl.BlockSpec((rows, q_half), lambda i, s: (0, 0))] * (2 * lines)
            + [pl.BlockSpec((2 * q_half, tile), lambda i, s: (0, i))],
            out_specs=(out_spec, out_spec),
            scratch_shapes=[pltpu.VMEM((out_rows, 2 * q_half), BF16), pltpu.VMEM((out_rows, tile), F32)],
        ),
        compiler_params=BIG,
    )(jnp.stack([core] + [i for pair in where for i in pair]), *mine, *other, out_weight)
    head_total = keep + over_core("proj", send).astype(F32)
    return (text_hidden.astype(F32) + jnp.tanh(attn_gate[0]) * head_total).astype(BF16)


def solution(mesh):
    placed = (
        P(("groups", "blk"), None),
        P(("groups", "blk")),
        P("blk", "heads"),
        P("blk", "heads"),
        P(),
        P(("groups", "blk"), "heads"),
        P("groups"),
        P(("groups", "heads"), "blk"),
        P("heads", "blk"),
        P(),
    )
    return jax.shard_map(
        body, mesh=mesh, in_specs=placed, out_specs=P(("groups", "heads"), "blk"), check_vma=False
    )
```

time: 305 us -> 138 us (0.45)
  waiting for transfers between devices: 244 us -> 53 us
  starting transfers between devices: 0.21 us -> 58.9 us
  matrix products: 20.4 us -> 0 us
  Pallas kernels: 0 us -> 20 us
  blocking collectives: 17.8 us -> 0 us
  between operations: 14.3 us -> 1.02 us
    all_gather x5 -> x0, waiting for transfers between devices: 237 us -> none  [the longest x1 77.5 us: body(): lax.all_gather(key_weight, 'blk', axis=0, tiled=True)]
    ppermute x0 -> x37, starting transfers between devices: none -> 58.9 us  [the longest x9 16.8 us: over_y(): return lax.ppermute(array, 'blk', swap_y)]
    ppermute x0 -> x37, waiting for transfers between devices: none -> 53 us  [the longest x6 33 us: along(): lax.ppermute(array, 'blk', [(b, b ^ 2 * d) for b in range(nblk) if ok(b /...]
    dot_general x5 -> x0, matrix products: 20.4 us -> none  [the longest x1 5.35 us: body(): jnp.dot(image_feats, lax.all_gather(value_weight, 'blk', axis=0, tiled=Tr...]
    pallas_call x0 -> x7, Pallas kernels: none -> 20 us  [the longest x2 9.1 us: project(): pl.pallas_call(functools.partial(project_kernel, sources, extra), out_sha...]
    all_gather x1 -> x0, blocking collectives: 17.8 us -> none  [body(): attend_slot_code = lax.all_gather(slot_code, 'blk', axis=0, tiled=True)]
    reduce_scatter x1 -> x0, waiting for transfers between devices: 6.19 us -> none  [body(): lax.psum_scatter(partial_out.astype(jnp.bfloat16), 'heads', scatter_dimen...]
  transfers between devices with their start and end apart: 6 -> 37, of which waited for: 6 -> 15; matrix products, arithmetic and copies ran while one was open for 5% -> 1% of each run, Pallas kernels for 0% -> 8%
where the time goes in v2:
time: 138 us
  starting transfers between devices  58.9 us (43%)
  waiting for transfers between devices  53 us (38%)
  Pallas kernels  20 us (14%)
  local copies, waits for them, and re-layouts  3.07 us (2%)
  other arithmetic  1.58 us (1%)
    ppermute x6, waiting for transfers between devices, along(): lax.ppermute(array, 'blk', [(b, b ^ 2 * d) for b in range(nblk) if ok(b /...  33 us
    ppermute x9, starting transfers between devices, over_y(): return lax.ppermute(array, 'blk', swap_y)  16.8 us
    ppermute x9, waiting for transfers between devices, over_y(): return lax.ppermute(array, 'blk', swap_y)  12.5 us
    pallas_call x2, Pallas kernels, project(): pl.pallas_call(functools.partial(project_kernel, sources, extra), out_sha...  9.1 us
    ppermute x8, starting transfers between devices, over_core(): return lax.ppermute(array, 'heads', swap_core)  9.05 us
    ppermute x4, starting transfers between devices, body(): mine.append(lax.ppermute(attn, ('blk', 'heads'), pairs))  8.99 us
    ppermute x6, starting transfers between devices, along(): lax.ppermute(array, 'blk', [(b, b ^ 2 * d) for b in range(nblk) if ok(b /...  8.32 us
    ppermute x2, starting transfers between devices, query_round(): return lax.ppermute(take_y(queries, q_half, y ^ r), ('blk', 'heads'), pairs)  5.42 us
  transfers between devices with their start and end apart: 37, of which 15 were waited for; matrix products, arithmetic and copies ran while one was open for 1% of the time, Pallas kernels for 8%

profile of v2, /device:TPU:0, one launch (start us, length us, event | category | flops | bytes accessed | tf_op | source)
XLA Modules:
  0.0 137.5 jit_solution(3726233493527245320)
XLA Ops:
  0.0 0.6 pad_add_fusion.idx_ref
  0.6 3.5 %shard_map.100 = (bf16[256,1024]{1,0:T(8,128)(2,1)}, bf16[256,1024]{1,0:T(8,128)(2,1)}, bf16[256,1024]{1,0:T(8,128)(2,1)}, bf16[1024,256]{1,0:T(8,128)(2,1)}) custom-call(s32[3]{0:T(128)} %pad_add_fusion.idx_ref, bf16[256,8192]{1,0:T(8,128)(2,1)} %image.5, bf16[1024,256]{1,0:T(8,128)(2,1)} %key_weight.1, bf16[1024,256]{1,0:T(8,128)(2,1)} %value_weight.1), custom_call_target="tpu_custom_call" | custom-call | tf_op jit(solution)/shard_map/pallas_call | solution.py:283
  4.1 3.1 %collective-permute-start.2 = (bf16[1024,256]{1,0:T(8,128)(2,1)}, bf16[1024,256]{1,0:T(8,128)(2,1)S(1)}, u32[]{:S(2)}, u32[]{:S(2)}) collective-permute-start(bf16[1024,256]{1,0:T(8,128)(2,1)} %get-tuple-element.31.refs_6_), channel_id=1, source_target_pairs={{0,4},{2,6},{4,0},{6,2},{8,12},{10,14},{12,8},{14,10},{1,5},{3,7},... | collective-permute-start | bytes 1572872 | tf_op jit(solution)/shard_map/w_z1/ppermute | solution.py:239
  7.2 0.7 collective-permute-start.3
  7.9 1.6 %collective-permute-start.4 = (bf16[256,1024]{1,0:T(8,128)(2,1)}, bf16[256,1024]{1,0:T(8,128)(2,1)S(1)}, u32[]{:S(2)}, u32[]{:S(2)}) collective-permute-start(bf16[256,1024]{1,0:T(8,128)(2,1)} %get-tuple-element.32), channel_id=1, source_target_pairs={{0,2},{2,0},{4,6},{6,4},{8,10},{10,8},{12,14},{14,12},{1,3},{3,1},... | collective-permute-start | bytes 1572872 | tf_op jit(solution)/shard_map/image_y/ppermute | solution.py:243
  9.5 1.5 %collective-permute-start.5 = (bf16[256,1024]{1,0:T(8,128)(2,1)}, bf16[256,1024]{1,0:T(8,128)(2,1)S(1)}, u32[]{:S(2)}, u32[]{:S(2)}) collective-permute-start(bf16[256,1024]{1,0:T(8,128)(2,1)} %get-tuple-element.33), channel_id=1, source_target_pairs={{0,16},{16,0},{1,17},{17,1},{2,18},{18,2},{3,19},{19,3},{4,20},{20... | collective-permute-start | bytes 1572872 | tf_op jit(solution)/shard_map/image_x/ppermute | solution.py:251
  11.0 8.4 %collective-permute-done.2.refs_7_ = bf16[1024,256]{1,0:T(8,128)(2,1)S(1)} collective-permute-done((bf16[1024,256]{1,0:T(8,128)(2,1)}, bf16[1024,256]{1,0:T(8,128)(2,1)S(1)}, u32[]{:S(2)}, u32[]{:S(2)}) %collective-permute-start.2) | collective-permute-done | bytes 524320 | tf_op jit(solution)/shard_map/w_z1/ppermute | solution.py:239
  19.4 2.2 %collective-permute-done.4.refs_0_ = bf16[256,1024]{1,0:T(8,128)(2,1)S(1)} collective-permute-done((bf16[256,1024]{1,0:T(8,128)(2,1)}, bf16[256,1024]{1,0:T(8,128)(2,1)S(1)}, u32[]{:S(2)}, u32[]{:S(2)}) %collective-permute-start.4) | collective-permute-done | bytes 524320 | tf_op jit(solution)/shard_map/image_y/ppermute | solution.py:243
  21.6 1.2 collective-permute-done.5.refs_2_
  22.8 0.7 collective-permute-start.6
  23.5 1.3 collective-permute-start.7
  24.8 1.5 %collective-permute-start.8 = (bf16[256,1024]{1,0:T(8,128)(2,1)}, bf16[256,1024]{1,0:T(8,128)(2,1)}, u32[]{:S(2)}, u32[]{:S(2)}) collective-permute-start(bf16[256,1024]{1,0:T(8,128)(2,1)} %get-tuple-element.38), channel_id=1, source_target_pairs={{0,18},{2,16},{4,22},{6,20},{8,26},{10,24},{12,30},{14,28},{16,2},... | collective-permute-start | bytes 1572872 | tf_op jit(solution)/shard_map/image_xy/ppermute | solution.py:256
  26.3 0.2 collective-permute-start.9
  26.5 16.1 %collective-permute-done.7.refs_9_ = bf16[1024,256]{1,0:T(8,128)(2,1)S(1)} collective-permute-done((bf16[1024,256]{1,0:T(8,128)(2,1)S(1)}, bf16[1024,256]{1,0:T(8,128)(2,1)S(1)}, u32[]{:S(2)}, u32[]{:S(2)}) %collective-permute-start.7) | collective-permute-done | bytes 524320 | tf_op jit(solution)/shard_map/w_out_z1/ppermute | solution.py:239
  42.7 0.8 copy-done.8
  43.5 0.9 fusion
  44.4 1.3 collective-permute-start.12
  45.7 0.1 stack.111.idx_ref
  45.8 1.3 collective-permute-start.20
  47.1 8.5 %collective-permute-done.12.refs_11_ = bf16[512,256]{1,0:T(8,128)(2,1)S(1)} collective-permute-done((bf16[512,256]{1,0:T(8,128)(2,1)}, bf16[512,256]{1,0:T(8,128)(2,1)S(1)}, u32[]{:S(2)}, u32[]{:S(2)}) %collective-permute-start.12) | collective-permute-done | bytes 262176 | tf_op jit(solution)/shard_map/wk_end_z1/ppermute | solution.py:239
  55.7 4.6 %shard_map.101 = (f32[512,128]{1,0:T(8,128)S(1)}, f32[520,128]{1,0:T(8,128)S(1)}, f32[512,128]{1,0:T(8,128)S(1)}, f32[512,128]{1,0:T(8,128)S(1)}) custom-call(s32[8]{0:T(128)S(1)} %stack.111.idx_ref, f32[2,128]{1,0:T(2,128)S(1)} %convert_bitcast_fusion.slots, bf16[256,8192]{1,0:T(8,128)(2,1)} %image.5, bf16[256,1024]{1,0:T(8,128)(2,1)S(1)} %collective-permute-done.4.refs_0_, ...), custom_call_target="tpu_custom_call" | custom-call | flops 1073741824 | bytes 8388608 | tf_op jit(solution)/shard_map/pallas_call | solution.py:320
  60.2 1.6 %collective-permute-start.14 = (f32[512,128]{1,0:T(8,128)S(1)}, f32[512,128]{1,0:T(8,128)S(1)}, u32[]{:S(2)}, u32[]{:S(2)}) collective-permute-start(f32[512,128]{1,0:T(8,128)S(1)} %get-tuple-element.47), channel_id=1, source_target_pairs={{0,16},{16,0},{1,17},{17,1},{2,18},{18,2},{3,19},{19,3},{4,20},{20... | collective-permute-start | bytes 786440 | tf_op jit(solution)/shard_map/key_x/ppermute | solution.py:251
  61.8 0.5 collective-permute-start.13
  62.3 1.5 %collective-permute-start.15 = (f32[512,128]{1,0:T(8,128)S(1)}, f32[512,128]{1,0:T(8,128)S(1)}, u32[]{:S(2)}, u32[]{:S(2)}) collective-permute-start(f32[512,128]{1,0:T(8,128)S(1)} %get-tuple-element.48), channel_id=1, source_target_pairs={{0,18},{2,16},{4,22},{6,20},{8,26},{10,24},{12,30},{14,28},{16,2},... | collective-permute-start | bytes 786440 | tf_op jit(solution)/shard_map/key_xy/ppermute | solution.py:256
  63.8 1.0 copy-done.1
  64.8 4.5 %shard_map.104 = (f32[512,128]{1,0:T(8,128)S(1)}, bf16[512,128]{1,0:T(8,128)(2,1)S(1)}, bf16[512,128]{1,0:T(8,128)(2,1)S(1)}, bf16[512,128]{1,0:T(8,128)(2,1)S(1)}) custom-call(s32[8]{0:T(128)S(1)} %stack.111.idx_ref, f32[2,128]{1,0:T(2,128)S(1)} %convert_bitcast_fusion.slots, bf16[256,8192]{1,0:T(8,128)(2,1)} %image.5, ...), custom_call_target="tpu_custom_call" | custom-call | flops 1073741824 | bytes 8388608 | tf_op jit(solution)/shard_map/pallas_call | solution.py:320
  69.4 0.6 collective-permute-start.21
  70.0 1.5 %collective-permute-start.22 = (bf16[512,128]{1,0:T(8,128)(2,1)S(1)}, bf16[512,128]{1,0:T(8,128)(2,1)S(1)}, u32[]{:S(2)}, u32[]{:S(2)}) collective-permute-start(bf16[512,128]{1,0:T(8,128)(2,1)S(1)} %get-tuple-element.53), channel_id=1, source_target_pairs={{0,16},{16,0},{1,17},{17,1},{2,18},{18,2},{3,19},{19,3},{4,20},{20... | collective-permute-start | bytes 393224 | tf_op jit(solution)/shard_map/value_x/ppermute | solution.py:251
  71.4 1.5 %collective-permute-start.23 = (bf16[512,128]{1,0:T(8,128)(2,1)S(1)}, bf16[512,128]{1,0:T(8,128)(2,1)S(1)}, u32[]{:S(2)}, u32[]{:S(2)}) collective-permute-start(bf16[512,128]{1,0:T(8,128)(2,1)S(1)} %get-tuple-element.54), channel_id=1, source_target_pairs={{0,18},{2,16},{4,22},{6,20},{8,26},{10,24},{12,30},{14,28},{16,2},... | collective-permute-start | bytes 393224 | tf_op jit(solution)/shard_map/value_xy/ppermute | solution.py:256
  72.9 2.1 %collective-permute-done.15.got_both = f32[512,128]{1,0:T(8,128)S(1)} collective-permute-done((f32[512,128]{1,0:T(8,128)S(1)}, f32[512,128]{1,0:T(8,128)S(1)}, u32[]{:S(2)}, u32[]{:S(2)}) %collective-permute-start.15) | collective-permute-done | bytes 262176 | tf_op jit(solution)/shard_map/key_xy/ppermute | solution.py:256
  75.0 2.1 %collective-permute-done.13.got_y = f32[520,128]{1,0:T(8,128)S(1)} collective-permute-done((f32[520,128]{1,0:T(8,128)S(1)}, f32[520,128]{1,0:T(8,128)S(1)}, u32[]{:S(2)}, u32[]{:S(2)}) %collective-permute-start.13) | collective-permute-done | bytes 266272 | tf_op jit(solution)/shard_map/key_y/ppermute | solution.py:243
  77.2 0.2 shard_map.102
  77.4 0.7 collective-permute-start.16
  78.0 2.2 %collective-permute-done.21 = bf16[512,128]{1,0:T(8,128)(2,1)S(1)} collective-permute-done((bf16[512,128]{1,0:T(8,128)(2,1)S(1)}, bf16[512,128]{1,0:T(8,128)(2,1)S(1)}, u32[]{:S(2)}, u32[]{:S(2)}) %collective-permute-start.21) | collective-permute-done | bytes 131104 | tf_op jit(solution)/shard_map/value_y/ppermute | solution.py:243
  80.3 0.7 collective-permute-start.24
  81.0 10.4 %collective-permute-start.25 = (bf16[512,128]{1,0:T(8,128)(2,1)S(1)}, bf16[512,128]{1,0:T(8,128)(2,1)S(1)}, u32[]{:S(2)}, u32[]{:S(2)}) collective-permute-start(bf16[512,128]{1,0:T(8,128)(2,1)S(1)} %collective-permute-done.24.refs_0_), channel_id=1, source_target_pairs={{0,2},{2,0},{4,6},{6,4},{8,10},{10,8},{12,14},{14,12},{1,3},{3,1},... | collective-permute-start | bytes 393224 | tf_op jit(solution)/shard_map/value_tile_y/ppermute | solution.py:243
  91.5 0.7 collective-permute-start
  92.2 4.8 %collective-permute-start.1 = (bf16[32,1024]{1,0:T(8,128)(2,1)S(1)}, bf16[32,1024]{1,0:T(8,128)(2,1)S(1)}, u32[]{:S(2)}, u32[]{:S(2)}) collective-permute-start(bf16[32,1024]{1,0:T(8,128)(2,1)S(1)} %get-tuple-element.62), channel_id=1, source_target_pairs={{0,4},{1,12},{2,0},{3,8},{4,6},{5,14},{6,2},{7,10},{8,5},{9,13},{1... | collective-permute-start | bytes 196616 | tf_op jit(solution)/shard_map/q_head/ppermute | solution.py:368
  97.0 0.1 copy.12.limit_ref
  97.1 5.0 %collective-permute-start.26 = (bf16[512,128]{1,0:T(8,128)(2,1)S(1)}, bf16[512,128]{1,0:T(8,128)(2,1)S(1)}, u32[]{:S(2)}, u32[]{:S(2)}) collective-permute-start(bf16[512,128]{1,0:T(8,128)(2,1)S(1)} %collective-permute-done.24.refs_0_), channel_id=1, source_target_pairs={{0,1},{1,0},{2,3},{3,2},{4,5},{5,4},{6,7},{7,6},{8,9},{9,8},{10,11... | collective-permute-start | bytes 393224 | tf_op jit(solution)/shard_map/value_tile_core/ppermute | solution.py:247
  102.1 0.1 collective-permute-start.27
  102.2 0.4 collective-permute-start.18
  102.6 0.1 collective-permute-start.19
  102.8 0.9 collective-permute-done.18.refs_2_
  103.7 0.3 collective-permute-done.19.refs_3_
  104.0 1.8 %shard_map.103 = (bf16[512,2048]{1,0:T(8,128)(2,1)S(1)}, f32[512,1]{1,0:T(8,128)S(1)}) custom-call(bf16[512,128]{1,0:T(8,128)(2,1)S(1)} %bitcast.34, f32[64,1]{1,0:T(8,128)S(1)} %copy.12.limit_ref, bf16[528,128]{1,0:T(8,128)(2,1)S(1)} %collective-permute-done.16.refs_0_, bf16[528,128]{1,0:T(8,128)(2,1)S(1)} %collective-permute-done.17.refs_1_, ...), custom_call_target="tpu_custom_call" | custom-call | tf_op jit(solution)/shard_map/pallas_call | solution.py:388
  105.9 0.7 shard_map.105
  106.6 0.7 collective-permute-start.28
  107.3 3.2 %collective-permute-start.29 = (bf16[64,1024]{1,0:T(8,128)(2,1)S(1)}, bf16[64,1024]{1,0:T(8,128)(2,1)S(1)}, u32[]{:S(2)}, u32[]{:S(2)}) collective-permute-start(bf16[64,1024]{1,0:T(8,128)(2,1)S(1)} %shard_map.105), channel_id=1, source_target_pairs={{0,4},{1,0},{2,6},{3,2},{4,12},{5,8},{6,14},{7,10},{8,5},{9,1},{10... | collective-permute-start | bytes 393224 | tf_op jit(solution)/shard_map/attn_out1/ppermute | solution.py:425
  110.4 3.2 %collective-permute-start.30 = (bf16[64,1024]{1,0:T(8,128)(2,1)S(1)}, bf16[64,1024]{1,0:T(8,128)(2,1)S(1)}, u32[]{:S(2)}, u32[]{:S(2)}) collective-permute-start(bf16[64,1024]{1,0:T(8,128)(2,1)S(1)} %shard_map.105), channel_id=1, source_target_pairs={{0,8},{1,12},{2,10},{3,14},{4,0},{5,4},{6,2},{7,6},{8,9},{9,13},{1... | collective-permute-start | bytes 393224 | tf_op jit(solution)/shard_map/attn_out2/ppermute | solution.py:425
  113.7 1.9 %collective-permute-start.31 = (bf16[64,1024]{1,0:T(8,128)(2,1)S(1)}, bf16[64,1024]{1,0:T(8,128)(2,1)S(1)}, u32[]{:S(2)}, u32[]{:S(2)}) collective-permute-start(bf16[64,1024]{1,0:T(8,128)(2,1)S(1)} %shard_map.105), channel_id=1, source_target_pairs={{0,12},{1,8},{2,14},{3,10},{4,4},{5,0},{6,6},{7,2},{8,13},{9,9},{1... | collective-permute-start | bytes 393224 | tf_op jit(solution)/shard_map/attn_out3/ppermute | solution.py:425
  115.6 1.3 collective-permute-start.32
  116.8 0.8 collective-permute-start.33
  117.7 1.2 collective-permute-start.34
  118.9 2.4 %collective-permute-done.31.refs_3_ = bf16[64,1024]{1,0:T(8,128)(2,1)S(1)} collective-permute-done((bf16[64,1024]{1,0:T(8,128)(2,1)S(1)}, bf16[64,1024]{1,0:T(8,128)(2,1)S(1)}, u32[]{:S(2)}, u32[]{:S(2)}) %collective-permute-start.31) | collective-permute-done | bytes 131104 | tf_op jit(solution)/shard_map/attn_out3/ppermute | solution.py:425
  121.3 0.4 collective-permute-start.35
  121.7 0.1 stack.102.idx_ref
  121.8 0.2 collective-permute-done.33.refs_5_
  122.0 1.4 %collective-permute-done.34.refs_6_ = bf16[64,1024]{1,0:T(8,128)(2,1)S(1)} collective-permute-done((bf16[64,1024]{1,0:T(8,128)(2,1)S(1)}, bf16[64,1024]{1,0:T(8,128)(2,1)S(1)}, u32[]{:S(2)}, u32[]{:S(2)}) %collective-permute-start.34) | collective-permute-done | bytes 131104 | tf_op jit(solution)/shard_map/attn2_y/ppermute | solution.py:243
  123.4 4.2 %collective-permute-done.35.refs_7_ = bf16[64,1024]{1,0:T(8,128)(2,1)S(1)} collective-permute-done((bf16[64,1024]{1,0:T(8,128)(2,1)S(1)}, bf16[64,1024]{1,0:T(8,128)(2,1)S(1)}, u32[]{:S(2)}, u32[]{:S(2)}) %collective-permute-start.35) | collective-permute-done | bytes 131104 | tf_op jit(solution)/shard_map/attn3_y/ppermute | solution.py:243
  127.7 4.6 %shard_map.106 = (f32[128,1024]{1,0:T(8,128)S(1)}, bf16[128,1024]{1,0:T(8,128)(2,1)S(1)}) custom-call(s32[17]{0:T(128)S(1)} %stack.102.idx_ref, bf16[64,1024]{1,0:T(8,128)(2,1)S(1)} %collective-permute-done.28.refs_0_, bf16[64,1024]{1,0:T(8,128)(2,1)S(1)} %collective-permute-done.29.refs_1_, bf16[64,1024]{1,0:T(8,128)(2,1)S(1)} %collective-permute-done.30.refs_2_, ...), custom_call_target="tpu_custom_call" | custom-call | tf_op jit(solution)/shard_map/pallas_call | solution.py:437
  132.3 3.2 %collective-permute-start.36 = (bf16[128,1024]{1,0:T(8,128)(2,1)S(1)}, bf16[128,1024]{1,0:T(8,128)(2,1)S(1)}, u32[]{:S(2)}, u32[]{:S(2)}) collective-permute-start(bf16[128,1024]{1,0:T(8,128)(2,1)S(1)} %get-tuple-element.56), channel_id=1, source_target_pairs={{0,1},{1,0},{2,3},{3,2},{4,5},{5,4},{6,7},{7,6},{8,9},{9,8},{10,11... | collective-permute-start | bytes 786440 | tf_op jit(solution)/shard_map/proj_core/ppermute | solution.py:247
  136.2 0.5 collective-permute-done.36
  136.7 0.8 add_convert_fusion
  (55 shorter events, 0.3 us)
Async XLA Ops:
  0.0 45.8 %copy-start.11 = (s32[256]{0:T(256)S(1)}, s32[256]{0:T(256)}, u32[]{:S(2)}) copy-start(s32[256]{0:T(256)} %param.11) | copy-start | bytes 3076
  4.1 15.2 %collective-permute-start.2 = (bf16[1024,256]{1,0:T(8,128)(2,1)}, bf16[1024,256]{1,0:T(8,128)(2,1)S(1)}, u32[]{:S(2)}, u32[]{:S(2)}) collective-permute-start(bf16[1024,256]{1,0:T(8,128)(2,1)} %get-tuple-element.31.refs_6_), channel_id=1, source_target_pairs={{0,4},{2,6},{4,0},{6,2},{8,12},{10,14},{12,8},{14,10},{1,5},{3,7},... | collective-permute-start | bytes 1572872 | tf_op jit(solution)/shard_map/w_z1/ppermute | solution.py:239
  7.2 12.1 %collective-permute-start.3 = (bf16[1024,256]{1,0:T(8,128)(2,1)}, bf16[1024,256]{1,0:T(8,128)(2,1)S(1)}, u32[]{:S(2)}, u32[]{:S(2)}) collective-permute-start(bf16[1024,256]{1,0:T(8,128)(2,1)} %get-tuple-element.31.refs_6_), channel_id=1, source_target_pairs={{4,8},{6,10},{8,4},{10,6},{5,9},{7,11},{9,5},{11,7},{20,24},{22,26... | collective-permute-start | bytes 1572872 | tf_op jit(solution)/shard_map/w_z3/ppermute | solution.py:239
  7.9 13.7 %collective-permute-start.4 = (bf16[256,1024]{1,0:T(8,128)(2,1)}, bf16[256,1024]{1,0:T(8,128)(2,1)S(1)}, u32[]{:S(2)}, u32[]{:S(2)}) collective-permute-start(bf16[256,1024]{1,0:T(8,128)(2,1)} %get-tuple-element.32), channel_id=1, source_target_pairs={{0,2},{2,0},{4,6},{6,4},{8,10},{10,8},{12,14},{14,12},{1,3},{3,1},... | collective-permute-start | bytes 1572872 | tf_op jit(solution)/shard_map/image_y/ppermute | solution.py:243
  9.5 13.3 %collective-permute-start.5 = (bf16[256,1024]{1,0:T(8,128)(2,1)}, bf16[256,1024]{1,0:T(8,128)(2,1)S(1)}, u32[]{:S(2)}, u32[]{:S(2)}) collective-permute-start(bf16[256,1024]{1,0:T(8,128)(2,1)} %get-tuple-element.33), channel_id=1, source_target_pairs={{0,16},{16,0},{1,17},{17,1},{2,18},{18,2},{3,19},{19,3},{4,20},{20... | collective-permute-start | bytes 1572872 | tf_op jit(solution)/shard_map/image_x/ppermute | solution.py:251
  19.3 36.3 %copy-start.4 = (bf16[1024,256]{1,0:T(8,128)(2,1)}, bf16[1024,256]{1,0:T(8,128)(2,1)S(1)}, u32[]{:S(2)}) copy-start(bf16[1024,256]{1,0:T(8,128)(2,1)S(1)} %collective-permute-done.2.refs_7_) | copy-start | bytes 1572868
  19.4 36.3 %copy-start.5 = (bf16[1024,256]{1,0:T(8,128)(2,1)}, bf16[1024,256]{1,0:T(8,128)(2,1)S(1)}, u32[]{:S(2)}) copy-start(bf16[1024,256]{1,0:T(8,128)(2,1)S(1)} %collective-permute-done.3.refs_10_) | copy-start | bytes 1572868
  22.8 32.8 %copy-start.6 = (bf16[256,1024]{1,0:T(8,128)(2,1)}, bf16[256,1024]{1,0:T(8,128)(2,1)S(1)}, u32[]{:S(2)}) copy-start(bf16[256,1024]{1,0:T(8,128)(2,1)S(1)} %collective-permute-done.5.refs_2_) | copy-start | bytes 1572868
  22.8 3.7 %collective-permute-start.10 = (bf16[256,1024]{1,0:T(8,128)(2,1)S(1)}, bf16[256,1024]{1,0:T(8,128)(2,1)S(1)}, u32[]{:S(2)}, u32[]{:S(2)}) collective-permute-start(bf16[256,1024]{1,0:T(8,128)(2,1)S(1)} %collective-permute-done.5.refs_2_), channel_id=1, source_target_pairs={{0,1},{1,0},{2,3},{3,2},{4,5},{5,4},{6,7},{7,6},{8,9},{9,8},{10,11... | collective-permute-start | bytes 1572872 | tf_op jit(solution)/shard_map/image_core/ppermute | solution.py:247
  22.8 3.7 %collective-permute-start.6 = (bf16[1024,256]{1,0:T(8,128)(2,1)S(1)}, bf16[1024,256]{1,0:T(8,128)(2,1)S(1)}, u32[]{:S(2)}, u32[]{:S(2)}) collective-permute-start(bf16[1024,256]{1,0:T(8,128)(2,1)S(1)} %collective-permute-done.2.refs_7_), channel_id=1, source_target_pairs={{4,8},{6,10},{8,4},{10,6},{5,9},{7,11},{9,5},{11,7},{20,24},{22,26... | collective-permute-start | bytes 1572872 | tf_op jit(solution)/shard_map/w_across_z3/ppermute | solution.py:239
  23.5 19.2 %collective-permute-start.7 = (bf16[1024,256]{1,0:T(8,128)(2,1)S(1)}, bf16[1024,256]{1,0:T(8,128)(2,1)S(1)}, u32[]{:S(2)}, u32[]{:S(2)}) collective-permute-start(bf16[1024,256]{1,0:T(8,128)(2,1)S(1)} %collective-permute-done.3.refs_10_), channel_id=1, source_target_pairs={{4,0},{6,2},{8,12},{10,14},{5,1},{7,3},{9,13},{11,15},{20,16},{22,... | collective-permute-start | bytes 1572872 | tf_op jit(solution)/shard_map/w_out_z1/ppermute | solution.py:239
  24.8 17.9 %collective-permute-start.8 = (bf16[256,1024]{1,0:T(8,128)(2,1)}, bf16[256,1024]{1,0:T(8,128)(2,1)}, u32[]{:S(2)}, u32[]{:S(2)}) collective-permute-start(bf16[256,1024]{1,0:T(8,128)(2,1)} %get-tuple-element.38), channel_id=1, source_target_pairs={{0,18},{2,16},{4,22},{6,20},{8,26},{10,24},{12,30},{14,28},{16,2},... | collective-permute-start | bytes 1572872 | tf_op jit(solution)/shard_map/image_xy/ppermute | solution.py:256
  26.3 16.4 %collective-permute-start.9 = (bf16[256,1024]{1,0:T(8,128)(2,1)S(1)}, bf16[256,1024]{1,0:T(8,128)(2,1)S(1)}, u32[]{:S(2)}, u32[]{:S(2)}) collective-permute-start(bf16[256,1024]{1,0:T(8,128)(2,1)S(1)} %collective-permute-done.4.refs_0_), channel_id=1, source_target_pairs={{0,1},{1,0},{2,3},{3,2},{4,5},{5,4},{6,7},{7,6},{8,9},{9,8},{10,11... | collective-permute-start | bytes 1572872 | tf_op jit(solution)/shard_map/image_core/ppermute | solution.py:247
  26.5 16.2 %copy-start.7 = (bf16[256,1024]{1,0:T(8,128)(2,1)}, bf16[256,1024]{1,0:T(8,128)(2,1)S(1)}, u32[]{:S(2)}) copy-start(bf16[256,1024]{1,0:T(8,128)(2,1)S(1)} %collective-permute-done.10.refs_3_) | copy-start | bytes 1572868
  26.5 29.1 %copy-start.3 = (bf16[1024,256]{1,0:T(8,128)(2,1)}, bf16[1024,256]{1,0:T(8,128)(2,1)S(1)}, u32[]{:S(2)}) copy-start(bf16[1024,256]{1,0:T(8,128)(2,1)S(1)} %collective-permute-done.6.refs_8_) | copy-start | bytes 1572868
  42.7 0.8 copy-start.8
  43.5 12.2 %copy-start = (bf16[256,1024]{1,0:T(8,128)(2,1)}, bf16[256,1024]{1,0:T(8,128)(2,1)S(1)}, u32[]{:S(2)}) copy-start(bf16[256,1024]{1,0:T(8,128)(2,1)S(1)} %collective-permute-done.9.refs_1_) | copy-start | bytes 1572868
  43.5 12.1 %collective-permute-start.11 = (bf16[256,1024]{1,0:T(8,128)(2,1)}, bf16[256,1024]{1,0:T(8,128)(2,1)}, u32[]{:S(2)}, u32[]{:S(2)}) collective-permute-start(bf16[256,1024]{1,0:T(8,128)(2,1)} %collective-permute-done.8.refs_4_), channel_id=1, source_target_pairs={{0,1},{1,0},{2,3},{3,2},{4,5},{5,4},{6,7},{7,6},{8,9},{9,8},{10,11... | collective-permute-start | bytes 1572872 | tf_op jit(solution)/shard_map/image_core/ppermute | solution.py:247
  44.4 11.2 %collective-permute-start.12 = (bf16[512,256]{1,0:T(8,128)(2,1)}, bf16[512,256]{1,0:T(8,128)(2,1)S(1)}, u32[]{:S(2)}, u32[]{:S(2)}) collective-permute-start(bf16[512,256]{1,0:T(8,128)(2,1)} %get-tuple-element.58), channel_id=1, source_target_pairs={{4,0},{6,2},{8,12},{10,14},{5,1},{7,3},{9,13},{11,15},{20,16},{22,... | collective-permute-start | bytes 786440 | tf_op jit(solution)/shard_map/wk_end_z1/ppermute | solution.py:239
  45.8 18.0 %collective-permute-start.20 = (bf16[512,256]{1,0:T(8,128)(2,1)}, bf16[512,256]{1,0:T(8,128)(2,1)S(1)}, u32[]{:S(2)}, u32[]{:S(2)}) collective-permute-start(bf16[512,256]{1,0:T(8,128)(2,1)} %get-tuple-element.57), channel_id=1, source_target_pairs={{4,0},{6,2},{8,12},{10,14},{5,1},{7,3},{9,13},{11,15},{20,16},{22,... | collective-permute-start | bytes 786440 | tf_op jit(solution)/shard_map/wv_end_z1/ppermute | solution.py:239
  60.2 11.2 %collective-permute-start.14 = (f32[512,128]{1,0:T(8,128)S(1)}, f32[512,128]{1,0:T(8,128)S(1)}, u32[]{:S(2)}, u32[]{:S(2)}) collective-permute-start(f32[512,128]{1,0:T(8,128)S(1)} %get-tuple-element.47), channel_id=1, source_target_pairs={{0,16},{16,0},{1,17},{17,1},{2,18},{18,2},{3,19},{19,3},{4,20},{20... | collective-permute-start | bytes 786440 | tf_op jit(solution)/shard_map/key_x/ppermute | solution.py:251
  61.8 15.4 %collective-permute-start.13 = (f32[520,128]{1,0:T(8,128)S(1)}, f32[520,128]{1,0:T(8,128)S(1)}, u32[]{:S(2)}, u32[]{:S(2)}) collective-permute-start(f32[520,128]{1,0:T(8,128)S(1)} %get-tuple-element.46), channel_id=1, source_target_pairs={{0,2},{2,0},{4,6},{6,4},{8,10},{10,8},{12,14},{14,12},{1,3},{3,1},... | collective-permute-start | bytes 798728 | tf_op jit(solution)/shard_map/key_y/ppermute | solution.py:243
  62.3 14.9 %copy-start.2 = (f32[128]{0:T(128)S(1)}, f32[128]{0:T(128)}, u32[]{:S(2)}) copy-start(f32[128]{0:T(128)} %param.14) | copy-start | bytes 1540
  62.3 34.7 %copy-start.12 = (s32[256]{0:T(256)S(1)}, s32[256]{0:T(256)}, u32[]{:S(2)}) copy-start(s32[256]{0:T(256)} %param.16) | copy-start | bytes 3076
  62.3 12.8 %collective-permute-start.15 = (f32[512,128]{1,0:T(8,128)S(1)}, f32[512,128]{1,0:T(8,128)S(1)}, u32[]{:S(2)}, u32[]{:S(2)}) collective-permute-start(f32[512,128]{1,0:T(8,128)S(1)} %get-tuple-element.48), channel_id=1, source_target_pairs={{0,18},{2,16},{4,22},{6,20},{8,26},{10,24},{12,30},{14,28},{16,2},... | collective-permute-start | bytes 786440 | tf_op jit(solution)/shard_map/key_xy/ppermute | solution.py:256
  63.8 1.0 copy-start.1
  64.8 26.7 %copy-start.10 = (bf16[32,2048]{1,0:T(8,128)(2,1)S(1)}, bf16[32,2048]{1,0:T(8,128)(2,1)}, u32[]{:S(2)}) copy-start(bf16[32,2048]{1,0:T(8,128)(2,1)} %param.15) | copy-start | bytes 393220
  69.4 10.9 %collective-permute-start.21 = (bf16[512,128]{1,0:T(8,128)(2,1)S(1)}, bf16[512,128]{1,0:T(8,128)(2,1)S(1)}, u32[]{:S(2)}, u32[]{:S(2)}) collective-permute-start(bf16[512,128]{1,0:T(8,128)(2,1)S(1)} %get-tuple-element.52), channel_id=1, source_target_pairs={{0,2},{2,0},{4,6},{6,4},{8,10},{10,8},{12,14},{14,12},{1,3},{3,1},... | collective-permute-start | bytes 393224 | tf_op jit(solution)/shard_map/value_y/ppermute | solution.py:243
  70.0 10.3 %collective-permute-start.22 = (bf16[512,128]{1,0:T(8,128)(2,1)S(1)}, bf16[512,128]{1,0:T(8,128)(2,1)S(1)}, u32[]{:S(2)}, u32[]{:S(2)}) collective-permute-start(bf16[512,128]{1,0:T(8,128)(2,1)S(1)} %get-tuple-element.53), channel_id=1, source_target_pairs={{0,16},{16,0},{1,17},{17,1},{2,18},{18,2},{3,19},{19,3},{4,20},{20... | collective-permute-start | bytes 393224 | tf_op jit(solution)/shard_map/value_x/ppermute | solution.py:251
  71.4 8.8 %collective-permute-start.23 = (bf16[512,128]{1,0:T(8,128)(2,1)S(1)}, bf16[512,128]{1,0:T(8,128)(2,1)S(1)}, u32[]{:S(2)}, u32[]{:S(2)}) collective-permute-start(bf16[512,128]{1,0:T(8,128)(2,1)S(1)} %get-tuple-element.54), channel_id=1, source_target_pairs={{0,18},{2,16},{4,22},{6,20},{8,26},{10,24},{12,30},{14,28},{16,2},... | collective-permute-start | bytes 393224 | tf_op jit(solution)/shard_map/value_xy/ppermute | solution.py:256
  77.4 14.1 %collective-permute-start.16 = (bf16[528,128]{1,0:T(8,128)(2,1)S(1)}, bf16[528,128]{1,0:T(8,128)(2,1)S(1)}, u32[]{:S(2)}, u32[]{:S(2)}) collective-permute-start(bf16[528,128]{1,0:T(8,128)(2,1)S(1)} %shard_map.102), channel_id=1, source_target_pairs={{0,0},{1,8},{2,4},{3,12},{4,2},{5,10},{6,6},{7,14},{8,1},{9,9},{10... | collective-permute-start | bytes 405512 | tf_op jit(solution)/shard_map/key_head/ppermute | solution.py:356
  80.3 0.7 collective-permute-start.24
  81.0 21.1 %collective-permute-start.25 = (bf16[512,128]{1,0:T(8,128)(2,1)S(1)}, bf16[512,128]{1,0:T(8,128)(2,1)S(1)}, u32[]{:S(2)}, u32[]{:S(2)}) collective-permute-start(bf16[512,128]{1,0:T(8,128)(2,1)S(1)} %collective-permute-done.24.refs_0_), channel_id=1, source_target_pairs={{0,2},{2,0},{4,6},{6,4},{8,10},{10,8},{12,14},{14,12},{1,3},{3,1},... | collective-permute-start | bytes 393224 | tf_op jit(solution)/shard_map/value_tile_y/ppermute | solution.py:243
  91.5 11.2 %collective-permute-start.17 = (bf16[528,128]{1,0:T(8,128)(2,1)S(1)}, bf16[528,128]{1,0:T(8,128)(2,1)S(1)}, u32[]{:S(2)}, u32[]{:S(2)}) collective-permute-start(bf16[528,128]{1,0:T(8,128)(2,1)S(1)} %collective-permute-done.16.refs_0_), channel_id=1, source_target_pairs={{0,2},{2,0},{4,6},{6,4},{8,10},{10,8},{12,14},{14,12},{1,3},{3,1},... | collective-permute-start | bytes 405512 | tf_op jit(solution)/shard_map/key_tile_y/ppermute | solution.py:243
  91.5 10.7 %collective-permute-start = (bf16[32,1024]{1,0:T(8,128)(2,1)S(1)}, bf16[32,1024]{1,0:T(8,128)(2,1)S(1)}, u32[]{:S(2)}, u32[]{:S(2)}) collective-permute-start(bf16[32,1024]{1,0:T(8,128)(2,1)S(1)} %get-tuple-element.61), channel_id=1, source_target_pairs={{0,0},{1,8},{2,4},{3,12},{4,2},{5,10},{6,6},{7,14},{8,1},{9,9},{10... | collective-permute-start | bytes 196616 | tf_op jit(solution)/shard_map/q_head/ppermute | solution.py:368
  92.2 10.5 %collective-permute-start.1 = (bf16[32,1024]{1,0:T(8,128)(2,1)S(1)}, bf16[32,1024]{1,0:T(8,128)(2,1)S(1)}, u32[]{:S(2)}, u32[]{:S(2)}) collective-permute-start(bf16[32,1024]{1,0:T(8,128)(2,1)S(1)} %get-tuple-element.62), channel_id=1, source_target_pairs={{0,4},{1,12},{2,0},{3,8},{4,6},{5,14},{6,2},{7,10},{8,5},{9,13},{1... | collective-permute-start | bytes 196616 | tf_op jit(solution)/shard_map/q_head/ppermute | solution.py:368
  97.1 8.7 %collective-permute-start.26 = (bf16[512,128]{1,0:T(8,128)(2,1)S(1)}, bf16[512,128]{1,0:T(8,128)(2,1)S(1)}, u32[]{:S(2)}, u32[]{:S(2)}) collective-permute-start(bf16[512,128]{1,0:T(8,128)(2,1)S(1)} %collective-permute-done.24.refs_0_), channel_id=1, source_target_pairs={{0,1},{1,0},{2,3},{3,2},{4,5},{5,4},{6,7},{7,6},{8,9},{9,8},{10,11... | collective-permute-start | bytes 393224 | tf_op jit(solution)/shard_map/value_tile_core/ppermute | solution.py:247
  102.1 3.7 %collective-permute-start.27 = (bf16[512,128]{1,0:T(8,128)(2,1)S(1)}, bf16[512,128]{1,0:T(8,128)(2,1)S(1)}, u32[]{:S(2)}, u32[]{:S(2)}) collective-permute-start(bf16[512,128]{1,0:T(8,128)(2,1)S(1)} %collective-permute-done.25.refs_1_), channel_id=1, source_target_pairs={{0,1},{1,0},{2,3},{3,2},{4,5},{5,4},{6,7},{7,6},{8,9},{9,8},{10,11... | collective-permute-start | bytes 393224 | tf_op jit(solution)/shard_map/value_tile_core/ppermute | solution.py:247
  102.2 1.5 %collective-permute-start.18 = (bf16[528,128]{1,0:T(8,128)(2,1)S(1)}, bf16[528,128]{1,0:T(8,128)(2,1)S(1)}, u32[]{:S(2)}, u32[]{:S(2)}) collective-permute-start(bf16[528,128]{1,0:T(8,128)(2,1)S(1)} %collective-permute-done.16.refs_0_), channel_id=1, source_target_pairs={{0,1},{1,0},{2,3},{3,2},{4,5},{5,4},{6,7},{7,6},{8,9},{9,8},{10,11... | collective-permute-start | bytes 405512 | tf_op jit(solution)/shard_map/key_tile_core/ppermute | solution.py:247
  102.6 1.4 collective-permute-start.19
  105.8 30.8 %copy-start.9 = (bf16[128,1024]{1,0:T(8,128)(2,1)S(1)}, bf16[128,1024]{1,0:T(8,128)(2,1)}, u32[]{:S(2)}) copy-start(bf16[128,1024]{1,0:T(8,128)(2,1)} %param.17) | copy-start | bytes 786436
  106.6 9.0 %collective-permute-start.28 = (bf16[64,1024]{1,0:T(8,128)(2,1)S(1)}, bf16[64,1024]{1,0:T(8,128)(2,1)S(1)}, u32[]{:S(2)}, u32[]{:S(2)}) collective-permute-start(bf16[64,1024]{1,0:T(8,128)(2,1)S(1)} %shard_map.105), channel_id=1, source_target_pairs={{0,0},{1,4},{2,2},{3,6},{4,8},{5,12},{6,10},{7,14},{8,1},{9,5},{10... | collective-permute-start | bytes 393224 | tf_op jit(solution)/shard_map/attn_out0/ppermute | solution.py:425
  107.3 9.6 %collective-permute-start.29 = (bf16[64,1024]{1,0:T(8,128)(2,1)S(1)}, bf16[64,1024]{1,0:T(8,128)(2,1)S(1)}, u32[]{:S(2)}, u32[]{:S(2)}) collective-permute-start(bf16[64,1024]{1,0:T(8,128)(2,1)S(1)} %shard_map.105), channel_id=1, source_target_pairs={{0,4},{1,0},{2,6},{3,2},{4,12},{5,8},{6,14},{7,10},{8,5},{9,1},{10... | collective-permute-start | bytes 393224 | tf_op jit(solution)/shard_map/attn_out1/ppermute | solution.py:425
  110.4 7.3 %collective-permute-start.30 = (bf16[64,1024]{1,0:T(8,128)(2,1)S(1)}, bf16[64,1024]{1,0:T(8,128)(2,1)S(1)}, u32[]{:S(2)}, u32[]{:S(2)}) collective-permute-start(bf16[64,1024]{1,0:T(8,128)(2,1)S(1)} %shard_map.105), channel_id=1, source_target_pairs={{0,8},{1,12},{2,10},{3,14},{4,0},{5,4},{6,2},{7,6},{8,9},{9,13},{1... | collective-permute-start | bytes 393224 | tf_op jit(solution)/shard_map/attn_out2/ppermute | solution.py:425
  113.7 7.7 %collective-permute-start.31 = (bf16[64,1024]{1,0:T(8,128)(2,1)S(1)}, bf16[64,1024]{1,0:T(8,128)(2,1)S(1)}, u32[]{:S(2)}, u32[]{:S(2)}) collective-permute-start(bf16[64,1024]{1,0:T(8,128)(2,1)S(1)} %shard_map.105), channel_id=1, source_target_pairs={{0,12},{1,8},{2,14},{3,10},{4,4},{5,0},{6,6},{7,2},{8,13},{9,9},{1... | collective-permute-start | bytes 393224 | tf_op jit(solution)/shard_map/attn_out3/ppermute | solution.py:425
  115.6 6.2 %collective-permute-start.32 = (bf16[64,1024]{1,0:T(8,128)(2,1)S(1)}, bf16[64,1024]{1,0:T(8,128)(2,1)S(1)}, u32[]{:S(2)}, u32[]{:S(2)}) collective-permute-start(bf16[64,1024]{1,0:T(8,128)(2,1)S(1)} %collective-permute-done.28.refs_0_), channel_id=1, source_target_pairs={{0,2},{2,0},{4,6},{6,4},{8,10},{10,8},{12,14},{14,12},{1,3},{3,1},... | collective-permute-start | bytes 393224 | tf_op jit(solution)/shard_map/attn0_y/ppermute | solution.py:243
  116.8 5.2 %collective-permute-start.33 = (bf16[64,1024]{1,0:T(8,128)(2,1)S(1)}, bf16[64,1024]{1,0:T(8,128)(2,1)S(1)}, u32[]{:S(2)}, u32[]{:S(2)}) collective-permute-start(bf16[64,1024]{1,0:T(8,128)(2,1)S(1)} %collective-permute-done.29.refs_1_), channel_id=1, source_target_pairs={{0,2},{2,0},{4,6},{6,4},{8,10},{10,8},{12,14},{14,12},{1,3},{3,1},... | collective-permute-start | bytes 393224 | tf_op jit(solution)/shard_map/attn1_y/ppermute | solution.py:243
  117.7 5.7 %collective-permute-start.34 = (bf16[64,1024]{1,0:T(8,128)(2,1)S(1)}, bf16[64,1024]{1,0:T(8,128)(2,1)S(1)}, u32[]{:S(2)}, u32[]{:S(2)}) collective-permute-start(bf16[64,1024]{1,0:T(8,128)(2,1)S(1)} %collective-permute-done.30.refs_2_), channel_id=1, source_target_pairs={{0,2},{2,0},{4,6},{6,4},{8,10},{10,8},{12,14},{14,12},{1,3},{3,1},... | collective-permute-start | bytes 393224 | tf_op jit(solution)/shard_map/attn2_y/ppermute | solution.py:243
  121.3 6.4 %collective-permute-start.35 = (bf16[64,1024]{1,0:T(8,128)(2,1)S(1)}, bf16[64,1024]{1,0:T(8,128)(2,1)S(1)}, u32[]{:S(2)}, u32[]{:S(2)}) collective-permute-start(bf16[64,1024]{1,0:T(8,128)(2,1)S(1)} %collective-permute-done.31.refs_3_), channel_id=1, source_target_pairs={{0,2},{2,0},{4,6},{6,4},{8,10},{10,8},{12,14},{14,12},{1,3},{3,1},... | collective-permute-start | bytes 393224 | tf_op jit(solution)/shard_map/attn3_y/ppermute | solution.py:243
  132.3 4.4 %collective-permute-start.36 = (bf16[128,1024]{1,0:T(8,128)(2,1)S(1)}, bf16[128,1024]{1,0:T(8,128)(2,1)S(1)}, u32[]{:S(2)}, u32[]{:S(2)}) collective-permute-start(bf16[128,1024]{1,0:T(8,128)(2,1)S(1)} %get-tuple-element.56), channel_id=1, source_target_pairs={{0,1},{1,0},{2,3},{3,2},{4,5},{5,4},{6,7},{7,6},{8,9},{9,8},{10,11... | collective-permute-start | bytes 786440 | tf_op jit(solution)/shard_map/proj_core/ppermute | solution.py:247

commit v3 on v2

--- a/solution.py
+++ b/solution.py
@@ -26,17 +26,24 @@
     return lax.dot_general(a, b, (((1,), (1,)), ((), ())), preferred_element_type=F32)
 
 
-def share_kernel(idx_ref, image, key_weight, value_weight, to_y, to_x, to_both, own, sems):
+def share_kernel(flips, half_lines, idx_ref, image, *refs):
     par, core, y = idx_ref[0], idx_ref[1], idx_ref[2]
-    half = own.shape[0] // 2
-    half_lines = to_y.shape[1] // half
+    n = len(flips)
+    with_weights = len(refs) > n + 1
+    weights, outs, sems = refs[: 2 * with_weights], refs[2 * with_weights : -1], refs[-1]
     copies = []
-    at_w = pl.multiple_of(par * half, half)
-    copies.append((key_weight.at[pl.ds(at_w, half), :], own.at[pl.ds(0, half), :]))
-    copies.append((value_weight.at[pl.ds(at_w, half), :], own.at[pl.ds(half, half), :]))
-    for out, to_par, to_y_at in ((to_x, 1 - par, y), (to_y, par, 1 - y), (to_both, 1 - par, 1 - y)):
+    if with_weights:
+        own = outs[n]
+        half = own.shape[0] // 2
+        at_w = pl.multiple_of(par * half, half)
+        for i in range(2):
+            copies.append((weights[i].at[pl.ds(at_w, half), :], own.at[pl.ds(i * half, half), :]))
+    for (flip_x, flip_y), out in zip(flips, outs):
+        half = out.shape[1] // half_lines
+        to_par = 1 - par if flip_x else par
+        to_y = 1 - y if flip_y else y
         for l in range(half_lines):
-            at = pl.multiple_of(((2 * (core * half_lines + l) + to_y_at) * 2 + to_par) * half, half)
+            at = pl.multiple_of(((2 * (core * half_lines + l) + to_y) * 2 + to_par) * half, half)
             copies.append((image.at[:, pl.ds(at, half)], out.at[:, pl.ds(l * half, half)]))
     copies = [pltpu.make_async_copy(src, dst, sems.at[i]) for i, (src, dst) in enumerate(copies)]
     for c in copies:
@@ -45,20 +52,19 @@
         c.wait()
 
 
-def project_kernel(sources, extra, idx_ref, slots, image, *refs):
+def load_shards(first, sources, idx_ref, image, got, weights, x_ref, w_ref, sems):
     par, core, y, inner = idx_ref[0], idx_ref[1], idx_ref[2], idx_ref[3]
-    got, refs = refs[:6], refs[6:]
-    weights, outs, (x_ref, w_ref, acc_ref, sems) = refs[:-8], refs[-8:-4], refs[-4:]
     rows = image.shape[0]
-    half = w_ref.shape[1]
+    half = x_ref.shape[2]
     half_lines = got[0].shape[1] // half
+    cols = weights[0].shape[1]
 
     def copy(src, dst, k, i):
         return pltpu.make_async_copy(src, dst, sems.at[k, i])
 
     waits = []
-    for k, (in_src, out_src) in enumerate(sources):
-        line = idx_ref[4 + k]
+    for k, projections in enumerate(sources):
+        line = idx_ref[4 + first + k]
         own_at = pl.multiple_of(((2 * line + y) * 2 + par) * half, half)
         here = line // half_lines == core
         got_at = pl.multiple_of(lax.rem(line, half_lines) * half, half)
@@ -76,11 +82,7 @@
                 for i in range(3)
             ]
 
-        def from_weight(src, k=k):
-            return copy(weights[src[0]].at[pl.ds(src[1], half), :], w_ref.at[k], k, 4)
-
         mine = from_core(0)
-        weight = from_weight(in_src)
 
         @pl.when(here)
         def _(mine=mine):
@@ -92,38 +94,67 @@
             for c in from_core(1):
                 c.start()
 
-        if in_src == out_src:
-            weight.start()
-        else:
-
-            @pl.when(inner > 0)
-            def _(weight=weight):
+        waits.append([own] + mine)
+        for p, (in_src, out_src) in enumerate(projections):
+
+            def from_weight(src, k=k, p=p):
+                return copy(
+                    weights[src[0]].at[pl.ds(src[1], half), :], w_ref.at[k, :, pl.ds(p * cols, cols)], k, 4 + p
+                )
+
+            weight = from_weight(in_src)
+            if in_src == out_src:
                 weight.start()
-
-            @pl.when(inner <= 0)
-            def _(from_weight=from_weight, out_src=out_src):
-                from_weight(out_src).start()
-
-        waits.append([own] + mine + [weight])
-    for k in range(len(sources)):
-        for c in waits[k]:
+            else:
+
+                @pl.when(inner > 0)
+                def _(weight=weight):
+                    weight.start()
+
+                @pl.when(inner <= 0)
+                def _(from_weight=from_weight, out_src=out_src):
+                    from_weight(out_src).start()
+
+            waits[-1].append(weight)
+    return waits
+
+
+def partial_kernel(sources, idx_ref, image, *refs):
+    got, weights = refs[:6], refs[6:-5]
+    outs, (x_ref, w_ref, sems) = refs[-5:-3], refs[-3:]
+    cols = outs[0].shape[1]
+    waits = load_shards(0, sources, idx_ref, image, got, weights, x_ref, w_ref, sems)
+    for k, copies in enumerate(waits):
+        for c in copies:
             c.wait()
-        part = dot(x_ref[k], w_ref[k])
-        if k == 0:
-            acc_ref[...] = part
-        else:
-            acc_ref[...] += part
-    keep, to_y, to_x, to_both = outs
+        for p in range(2):
+            part = dot(x_ref[k], w_ref[k, :, p * cols : (p + 1) * cols])
+            if k == 0:
+                outs[p][...] = part
+            else:
+                outs[p][...] += part
+
+
+def finish_kernel(first, source, extra, idx_ref, slots, acc, image, *refs):
+    got, weights = refs[:6], refs[6:-7]
+    (keep, to_y, to_x, to_both), (x_ref, w_ref, sems) = refs[-7:-3], refs[-3:]
+    y = idx_ref[2]
+    rows = image.shape[0]
     cols = keep.shape[1]
-    mine = pl.ds(pl.multiple_of(y * cols, cols), cols)
-    other = pl.ds(pl.multiple_of((1 - y) * cols, cols), cols)
     kind = to_y.dtype
-    keep[...] = acc_ref[: 2 * rows, mine]
-    to_y[:rows, :] = acc_ref[rows : 2 * rows, other].astype(kind)
-    to_y[rows : 2 * rows, :] = acc_ref[:rows, other].astype(kind)
-    to_x[...] = acc_ref[2 * rows :, mine].astype(kind)
-    to_both[:rows, :] = acc_ref[3 * rows :, other].astype(kind)
-    to_both[rows:, :] = acc_ref[2 * rows : 3 * rows, other].astype(kind)
+    waits = load_shards(first, (source,), idx_ref, image, got, weights, x_ref, w_ref, sems)
+    for c in waits[0]:
+        c.wait()
+    total = acc[...] + dot(x_ref[0], w_ref[0])
+    low = y == 0
+    mine = jnp.where(low, total[:, :cols], total[:, cols:])
+    other = jnp.where(low, total[:, cols:], total[:, :cols]).astype(kind)
+    keep[...] = mine[: 2 * rows]
+    to_y[:rows, :] = other[rows : 2 * rows]
+    to_y[rows : 2 * rows, :] = other[:rows]
+    to_x[...] = mine[2 * rows :].astype(kind)
+    to_both[:rows, :] = other[3 * rows :]
+    to_both[rows:, :] = other[2 * rows : 3 * rows]
     if extra:
         n = slots.shape[0]
         to_y[2 * rows : 2 * rows + n, :HD] = slots[...]
@@ -188,19 +219,32 @@
     pieces = refs[:n]
     w_ref, keep_ref, send_ref, a_ref, p_ref = refs[n:]
     rows, width = pieces[0].shape
-
-    @pl.when(pl.program_id(0) == 0)
+    depth = w_ref.shape[0]
+    step = pl.program_id(0)
+
+    @pl.when(step == 0)
     def _():
         for k in range(n):
             at_row = pl.multiple_of(idx_ref[1 + 2 * k] * rows, rows)
             at_col = pl.multiple_of(idx_ref[2 + 2 * k] * width, width)
             a_ref[pl.ds(at_row, rows), pl.ds(at_col, width)] = pieces[k][...]
 
-    p_ref[...] = dot(a_ref[...], w_ref[...])
-    part = keep_ref.shape[0]
-    core = idx_ref[0]
-    keep_ref[...] = p_ref[pl.ds(pl.multiple_of(core * part, part), part), :]
-    send_ref[...] = p_ref[pl.ds(pl.multiple_of((1 - core) * part, part), part), :].astype(BF16)
+    part = dot(a_ref[:, pl.ds(pl.multiple_of(step * depth, depth), depth)], w_ref[...])
+
+    @pl.when(step == 0)
+    def _():
+        p_ref[...] = part
+
+    @pl.when(step > 0)
+    def _():
+        p_ref[...] += part
+
+    @pl.when(step == pl.num_programs(0) - 1)
+    def _():
+        size = keep_ref.shape[0]
+        core = idx_ref[0]
+        keep_ref[...] = p_ref[pl.ds(pl.multiple_of(core * size, size), size), :]
+        send_ref[...] = p_ref[pl.ds(pl.multiple_of((1 - core) * size, size), size), :].astype(BF16)
 
 
 def body(
@@ -280,15 +324,51 @@
     half_lines = lines // 2
     scalars = pl.BlockSpec(memory_space=pltpu.SMEM)
     share = jax.ShapeDtypeStruct((tok, half_lines * half), BF16)
-    share_y, share_x, share_both, own = pl.pallas_call(
-        share_kernel,
-        out_shape=(share, share, share, jax.ShapeDtypeStruct((2 * half, kv_cols), BF16)),
-        in_specs=[scalars, FREE, FREE, FREE],
-        out_specs=(WHOLE,) * 4,
-        scratch_shapes=[pltpu.SemaphoreType.DMA((2 + 3 * half_lines,))],
-        compiler_params=pltpu.CompilerParams(vmem_limit_bytes=56 * 1024 * 1024),
-    )(jnp.stack([par, core, y]), image_feats, key_weight, value_weight)
-    if fast:
+
+    def shares(flips, *weights):
+        out_shape = [share] * len(flips)
+        if weights:
+            out_shape.append(jax.ShapeDtypeStruct((2 * half, kv_cols), BF16))
+        return pl.pallas_call(
+            functools.partial(share_kernel, flips, half_lines),
+            out_shape=tuple(out_shape),
+            in_specs=[scalars, FREE] + [FREE] * len(weights),
+            out_specs=(WHOLE,) * len(out_shape),
+            scratch_shapes=[pltpu.SemaphoreType.DMA((2 + len(flips) * half_lines,))],
+            compiler_params=pltpu.CompilerParams(vmem_limit_bytes=56 * 1024 * 1024),
+        )(jnp.stack([par, core, y]), image_feats, *weights)
+
+    share_x, share_y, own = shares(((1, 0), (0, 1)), key_weight, value_weight)
+    (share_both,) = shares(((1, 1),))
+    if fast:
+        def devices(route):
+            pairs = []
+            for l in range(lines):
+                for yy in range(2):
+                    for c in range(cores):
+                        to_l, to_y, to_c = route(l, yy, c)
+                        pairs.append(((2 * l + yy) * cores + c, (2 * to_l + to_y) * cores + to_c))
+            return pairs
+
+        def to_head(name, tile):
+            tiles = []
+            for r in range(2):
+                with jax.named_scope(name + "_head"):
+                    tiles.append(
+                        lax.ppermute(
+                            tile, ("blk", "heads"), devices(lambda l, yy, c: (2 * c + yy, (l % 2) ^ r, l // 2))
+                        )
+                    )
+            return tiles + [over_core(name + "_tile", t) for t in tiles]
+
+        def query_round(queries, r):
+            with jax.named_scope("q_head"):
+                return lax.ppermute(
+                    take_y(queries, q_half, y ^ r),
+                    ("blk", "heads"),
+                    devices(lambda l, yy, c: (2 * c + (r ^ yy), l % 2, l // 2)),
+                )
+
         z1, zm = along("w", own, 1), along("w", own, 3, middle)
         img_y, img_x = over_y("image", share_y), over_x("image", share_x)
         z1, zm, img_y, img_x, share_both = hold(z1, zm, img_y, img_x, share_both)
@@ -297,43 +377,71 @@
         core_y, core_x = over_core("image", img_y), over_core("image", img_x)
         fb, fa, img_both, core_y, core_x = hold(fb, fa, img_both, core_y, core_x)
         core_both = over_core("image", img_both)
-        last_k, last_v = along("wk_end", fb[:half], 1, middle), along("wv_end", fb[half:], 1, middle)
-        shared = [z1, fb, fa, zm]
-        key_refs, value_refs = [own] + shared + [last_k], [own] + shared + [last_v]
-        pairs = lambda at: (((0, at), (0, at)), ((1, at), (1, at)), ((2, at), (3, at)), ((4, at), (5, 0)))
-        key_from, value_from = pairs(0), pairs(half)
+        last_k, last_v = along("wk_end", fb[:half], 1, middle), fb[half:]
+        refs = [own, z1, fb, fa]
+        both = lambda i, o: tuple(((i, at), (o, at)) for at in (0, half))
+        sources = (both(0, 0), both(1, 1), both(2, 3))
     else:
         img_y, img_x, img_both = over_y("image", share_y), over_x("image", share_x), over_both("image", share_both)
         core_y, core_x, core_both = (over_core("image", i) for i in (img_y, img_x, img_both))
-        shards = [own] + [along("w", own, d) for d in range(1, lines)]
-        key_refs = value_refs = shards
-        key_from = tuple(((d, 0), (d, 0)) for d in range(lines))
-        value_from = tuple(((d, half), (d, half)) for d in range(lines))
+        refs = [own] + [along("w", own, d) for d in range(1, lines)]
+        sources = tuple(tuple(((d, at), (d, at)) for at in (0, half)) for d in range(lines - 1))
     pieces = [img_y, core_y, img_x, core_x, img_both, core_both]
     slots = slot_image.astype(F32).reshape(tok // HD, HD)
     extra = 8 * (-(-(tok // HD) // 8))
 
-    def project(weights, sources, extra, kind):
-        idx = [par, core, y, ((line == 1) | (line == 2)).astype(jnp.int32)] + [line ^ d for d in range(lines)]
+    idx = jnp.stack([par, core, y, ((line == 1) | (line == 2)).astype(jnp.int32)] + [line ^ d for d in range(lines)])
+    macs = 4 * tok * half * kv_cols
+    acc = jax.ShapeDtypeStruct((4 * tok, kv_cols), F32)
+    key_acc, value_acc = pl.pallas_call(
+        functools.partial(partial_kernel, sources),
+        out_shape=(acc, acc),
+        in_specs=[scalars] + [FREE] * (7 + len(refs)),
+        out_specs=(WHOLE, WHOLE),
+        scratch_shapes=[
+            pltpu.VMEM((lines - 1, 4 * tok, half), BF16),
+            pltpu.VMEM((lines - 1, half, 2 * kv_cols), BF16),
+            pltpu.SemaphoreType.DMA((lines - 1, 6)),
+        ],
+        compiler_params=BIG,
+        cost_estimate=pl.CostEstimate(
+            flops=4 * macs * (lines - 1), bytes_accessed=macs // 16, transcendentals=0
+        ),
+    )(idx, image_feats, *pieces, *refs)
+
+    def finish(acc, weights, source, extra, kind):
         out = lambda rows, dtype: jax.ShapeDtypeStruct((rows, mine_cols), dtype)
-        macs = 4 * tok * half * kv_cols * lines
         return pl.pallas_call(
-            functools.partial(project_kernel, sources, extra),
+            functools.partial(finish_kernel, lines - 1, (source,), extra),
             out_shape=(out(2 * tok, F32), out(2 * tok + extra, kind), out(2 * tok, kind), out(2 * tok, kind)),
-            in_specs=[scalars, WHOLE] + [FREE] * (7 + len(weights)),
+            in_specs=[scalars, WHOLE, WHOLE] + [FREE] * (7 + len(weights)),
             out_specs=(WHOLE,) * 4,
             scratch_shapes=[
-                pltpu.VMEM((lines, 4 * tok, half), BF16),
-                pltpu.VMEM((lines, half, kv_cols), BF16),
-                pltpu.VMEM((4 * tok, kv_cols), F32),
-                pltpu.SemaphoreType.DMA((lines, 5)),
+                pltpu.VMEM((1, 4 * tok, half), BF16),
+                pltpu.VMEM((1, half, kv_cols), BF16),
+                pltpu.SemaphoreType.DMA((1, 5)),
             ],
             compiler_params=BIG,
-            cost_estimate=pl.CostEstimate(flops=2 * macs, bytes_accessed=macs // 64, transcendentals=0),
-        )(jnp.stack(idx), slots, image_feats, *pieces, *weights)
-
-    keep, to_y, to_x, to_both = project(key_refs, key_from, extra, F32)
+            cost_estimate=pl.CostEstimate(flops=2 * macs, bytes_accessed=macs // 32, transcendentals=0),
+        )(idx, slots, acc, image_feats, *pieces, *weights)
+
+    if fast:
+        key_last, value_last = [zm, last_k], None
+        key_src, value_src = ((0, 0), (1, 0)), ((0, half), (1, 0))
+    else:
+        key_last = value_last = refs[-1:]
+        key_src, value_src = ((0, 0), (0, 0)), ((0, half), (0, half))
+    if fast:
+        key_acc, last_k, last_v = hold(key_acc, last_k, last_v)
+        key_last = [zm, last_k]
+        value_last = [zm, along("wv_end", last_v, 1, middle)]
+    keep, to_y, to_x, to_both = finish(key_acc, key_last, key_src, extra, F32)
+    if fast:
+        to_y, to_x, to_both, queries = hold(to_y, to_x, to_both, queries)
     key_parts = [over_y("key", to_y), over_x("key", to_x), over_both("key", to_both)]
+    if fast:
+        q_0, q_1 = query_round(queries, 0), query_round(queries, 1)
+        *key_parts, q_0, q_1 = hold(*key_parts, q_0, q_1)
     slot_rows = 2 * tok // HD
     packed = pl.pallas_call(
         key_kernel,
@@ -345,29 +453,6 @@
 
     rows = 2 * text_rows
     if fast:
-        def to_head(name, tile):
-            pairs = [
-                ((2 * l + yy) * cores + c, (2 * (2 * c + yy) + l % 2) * cores + l // 2)
-                for l in range(lines)
-                for yy in range(2)
-                for c in range(cores)
-            ]
-            with jax.named_scope(name + "_head"):
-                tile = lax.ppermute(tile, ("blk", "heads"), pairs)
-            there = over_y(name + "_tile", tile)
-            return [tile, there, over_core(name + "_tile", tile), over_core(name + "_tile", there)]
-
-        def query_round(r):
-            pairs = [
-                ((2 * l + yy) * cores + c, (2 * (2 * c + (r ^ yy)) + l % 2) * cores + l // 2)
-                for l in range(lines)
-                for yy in range(2)
-                for c in range(cores)
-            ]
-            with jax.named_scope("q_head"):
-                return lax.ppermute(take_y(queries, q_half, y ^ r), ("blk", "heads"), pairs)
-
-        q_0, q_1 = query_round(0), query_round(1)
         is_low = line % 2 == 0
         row_at = 2 * core + y
     else:
@@ -397,7 +482,7 @@
         compiler_params=PARAMS,
     )(q_all, limit, *key_pieces)
 
-    keep, to_y, to_x, to_both = project(value_refs, value_from, 0, BF16)
+    keep, to_y, to_x, to_both = finish(value_acc, value_last, value_src, 0, BF16)
     value_parts = [over_y("value", to_y), over_x("value", to_x), over_both("value", to_both)]
     value_y, value_x, value_both = (part.astype(F32) for part in value_parts)
     values = ((keep + value_y) + (value_x + value_both)).astype(BF16)
@@ -415,12 +500,7 @@
     if fast:
         mine = []
         for k in range(lines):
-            pairs = [
-                ((2 * l + yy) * cores + c, (2 * ((2 * (l % 2) + c) ^ k) + yy) * cores + l // 2)
-                for l in range(lines)
-                for yy in range(2)
-                for c in range(cores)
-            ]
+            pairs = devices(lambda l, yy, c: ((2 * (l % 2) + c) ^ k, yy, l // 2))
             with jax.named_scope(f"attn_out{k}"):
                 mine.append(lax.ppermute(attn, ("blk", "heads"), pairs))
             where.append((2 * ((line ^ k) % 2), (line ^ k) // 2))
@@ -432,8 +512,8 @@
 
     out_rows = lines * rows
     out_cols = out_weight.shape[1]
-    tile = out_cols // max(1, out_cols // 256)
-    out_spec = pl.BlockSpec((out_rows // 2, tile), lambda i, s: (0, i))
+    steps = 4
+    out_spec = pl.BlockSpec((out_rows // 2, out_cols), lambda i, s: (0, 0))
     keep, send = pl.pallas_call(
         functools.partial(proj_kernel, 2 * lines),
         out_shape=(
@@ -442,11 +522,11 @@
         ),
         grid_spec=pltpu.PrefetchScalarGridSpec(
             num_scalar_prefetch=1,
-            grid=(out_cols // tile,),
+            grid=(steps,),
             in_specs=[pl.BlockSpec((rows, q_half), lambda i, s: (0, 0))] * (2 * lines)
-            + [pl.BlockSpec((2 * q_half, tile), lambda i, s: (0, i))],
+            + [pl.BlockSpec((2 * q_half // steps, out_cols), lambda i, s: (i, 0))],
             out_specs=(out_spec, out_spec),
-            scratch_shapes=[pltpu.VMEM((out_rows, 2 * q_half), BF16), pltpu.VMEM((out_rows, tile), F32)],
+            scratch_shapes=[pltpu.VMEM((out_rows, 2 * q_half), BF16), pltpu.VMEM((out_rows, out_cols), F32)],
         ),
         compiler_params=BIG,
     )(jnp.stack([core] + [i for pair in where for i in pair]), *mine, *other, out_weight)

time: 138 us -> 131 us (0.949)
  starting transfers between devices: 58.9 us -> 52.1 us
  Pallas kernels: 20 us -> 24.3 us
  waiting for transfers between devices: 53 us -> 50.7 us
  local copies, waits for them, and re-layouts: 3.07 us -> 1.08 us
    ppermute x4 -> x6, waiting for transfers between devices: 0.01 us -> 12.5 us  [the longest x4 9.04 us: to_head(): lax.ppermute(tile, ('blk', 'heads'), devices(lambda l, yy, c: (2 * c + yy...]
    ppermute x9 -> x7, starting transfers between devices: 16.8 us -> 7.14 us  [over_y(): return lax.ppermute(array, 'blk', swap_y)]
    ppermute x4 -> x6, starting transfers between devices: 6.76 us -> 16.1 us  [the longest x4 13 us: to_head(): lax.ppermute(tile, ('blk', 'heads'), devices(lambda l, yy, c: (2 * c + yy...]
    ppermute x6, waiting for transfers between devices: 33 us -> 25.7 us  [along(): lax.ppermute(array, 'blk', [(b, b ^ 2 * d) for b in range(nblk) if ok(b /...]
    ppermute x9 -> x7, waiting for transfers between devices: 12.5 us -> 8.02 us  [over_y(): return lax.ppermute(array, 'blk', swap_y)]
    pallas_call x3 -> x5, Pallas kernels: 12.6 us -> 16.8 us  [the longest x2 5.85 us: finish(): pl.pallas_call(functools.partial(finish_kernel, lines - 1, (source,), ext...]
    ppermute x8, starting transfers between devices: 9.05 us -> 5.67 us  [over_core(): return lax.ppermute(array, 'heads', swap_core)]
    ppermute x3, waiting for transfers between devices: 2.11 us -> 0.01 us  [over_both(): return lax.ppermute(array, ('groups', 'blk'), pairs)]
  transfers between devices with their start and end apart: 37 -> 37, of which waited for: 15 -> 14; matrix products, arithmetic and copies ran while one was open for 1% -> 1% of each run, Pallas kernels for 8% -> 12%
where the time goes in v3:
time: 131 us
  starting transfers between devices  52.1 us (40%)
  waiting for transfers between devices  50.7 us (39%)
  Pallas kernels  24.3 us (19%)
  other arithmetic  1.59 us (1%)
    ppermute x6, waiting for transfers between devices, along(): lax.ppermute(array, 'blk', [(b, b ^ 2 * d) for b in range(nblk) if ok(b /...  25.7 us
    ppermute x4, starting transfers between devices, to_head(): lax.ppermute(tile, ('blk', 'heads'), devices(lambda l, yy, c: (2 * c + yy...  13 us
    ppermute x4, waiting for transfers between devices, to_head(): lax.ppermute(tile, ('blk', 'heads'), devices(lambda l, yy, c: (2 * c + yy...  9.04 us
    ppermute x6, starting transfers between devices, along(): lax.ppermute(array, 'blk', [(b, b ^ 2 * d) for b in range(nblk) if ok(b /...  8.32 us
    ppermute x7, waiting for transfers between devices, over_y(): return lax.ppermute(array, 'blk', swap_y)  8.02 us
    ppermute x4, starting transfers between devices, body(): mine.append(lax.ppermute(attn, ('blk', 'heads'), pairs))  7.89 us
    ppermute x7, starting transfers between devices, over_y(): return lax.ppermute(array, 'blk', swap_y)  7.14 us
    pallas_call x2, Pallas kernels, finish(): pl.pallas_call(functools.partial(finish_kernel, lines - 1, (source,), ext...  5.85 us
  transfers between devices with their start and end apart: 37, of which 14 were waited for; matrix products, arithmetic and copies ran while one was open for 1% of the time, Pallas kernels for 12%

profile of v3, /device:TPU:0, one launch (start us, length us, event | category | flops | bytes accessed | tf_op | source)
XLA Modules:
  0.0 130.9 jit_solution(16131338068863286752)
XLA Ops:
  0.0 0.6 pad_add_fusion.idx_ref
  0.6 3.2 %shard_map.100 = (bf16[256,1024]{1,0:T(8,128)(2,1)}, bf16[256,1024]{1,0:T(8,128)(2,1)}, bf16[1024,256]{1,0:T(8,128)(2,1)}) custom-call(s32[3]{0:T(128)} %pad_add_fusion.idx_ref, bf16[256,8192]{1,0:T(8,128)(2,1)} %image.9, bf16[1024,256]{1,0:T(8,128)(2,1)} %refs_0_.1, bf16[1024,256]{1,0:T(8,128)(2,1)} %refs_1_.1), custom_call_target="tpu_custom_call" | custom-call | tf_op jit(solution)/shard_map/pallas_call | solution.py:332
  3.8 3.1 %collective-permute-start = (bf16[1024,256]{1,0:T(8,128)(2,1)}, bf16[1024,256]{1,0:T(8,128)(2,1)S(1)}, u32[]{:S(2)}, u32[]{:S(2)}) collective-permute-start(bf16[1024,256]{1,0:T(8,128)(2,1)} %get-tuple-element.44.refs_6_), channel_id=1, source_target_pairs={{0,4},{2,6},{4,0},{6,2},{8,12},{10,14},{12,8},{14,10},{1,5},{3,7},... | collective-permute-start | bytes 1572872 | tf_op jit(solution)/shard_map/w_z1/ppermute | solution.py:283
  6.9 0.7 collective-permute-start.1
  7.6 1.6 %collective-permute-start.2 = (bf16[256,1024]{1,0:T(8,128)(2,1)}, bf16[256,1024]{1,0:T(8,128)(2,1)S(1)}, u32[]{:S(2)}, u32[]{:S(2)}) collective-permute-start(bf16[256,1024]{1,0:T(8,128)(2,1)} %get-tuple-element.45), channel_id=1, source_target_pairs={{0,2},{2,0},{4,6},{6,4},{8,10},{10,8},{12,14},{14,12},{1,3},{3,1},... | collective-permute-start | bytes 1572872 | tf_op jit(solution)/shard_map/image_y/ppermute | solution.py:287
  9.2 1.5 %collective-permute-start.3 = (bf16[256,1024]{1,0:T(8,128)(2,1)}, bf16[256,1024]{1,0:T(8,128)(2,1)S(1)}, u32[]{:S(2)}, u32[]{:S(2)}) collective-permute-start(bf16[256,1024]{1,0:T(8,128)(2,1)} %get-tuple-element.46), channel_id=1, source_target_pairs={{0,16},{16,0},{1,17},{17,1},{2,18},{18,2},{3,19},{19,3},{4,20},{20... | collective-permute-start | bytes 1572872 | tf_op jit(solution)/shard_map/image_x/ppermute | solution.py:295
  10.7 2.5 %shard_map.101 = bf16[256,1024]{1,0:T(8,128)(2,1)} custom-call(s32[3]{0:T(128)} %pad_add_fusion.idx_ref, bf16[256,8192]{1,0:T(8,128)(2,1)} %image.9), custom_call_target="tpu_custom_call" | custom-call | tf_op jit(solution)/shard_map/pallas_call | solution.py:332
  13.2 5.8 %collective-permute-done.refs_7_ = bf16[1024,256]{1,0:T(8,128)(2,1)S(1)} collective-permute-done((bf16[1024,256]{1,0:T(8,128)(2,1)}, bf16[1024,256]{1,0:T(8,128)(2,1)S(1)}, u32[]{:S(2)}, u32[]{:S(2)}) %collective-permute-start) | collective-permute-done | bytes 524320 | tf_op jit(solution)/shard_map/w_z1/ppermute | solution.py:283
  19.0 2.2 %collective-permute-done.2.refs_0_ = bf16[256,1024]{1,0:T(8,128)(2,1)S(1)} collective-permute-done((bf16[256,1024]{1,0:T(8,128)(2,1)}, bf16[256,1024]{1,0:T(8,128)(2,1)S(1)}, u32[]{:S(2)}, u32[]{:S(2)}) %collective-permute-start.2) | collective-permute-done | bytes 524320 | tf_op jit(solution)/shard_map/image_y/ppermute | solution.py:287
  21.2 1.2 collective-permute-done.3.refs_2_
  22.5 0.7 collective-permute-start.4
  23.2 1.3 collective-permute-start.5
  24.5 1.5 %collective-permute-start.6 = (bf16[256,1024]{1,0:T(8,128)(2,1)}, bf16[256,1024]{1,0:T(8,128)(2,1)S(1)}, u32[]{:S(2)}, u32[]{:S(2)}) collective-permute-start(bf16[256,1024]{1,0:T(8,128)(2,1)} %shard_map.101), channel_id=1, source_target_pairs={{0,18},{2,16},{4,22},{6,20},{8,26},{10,24},{12,30},{14,28},{16,2},... | collective-permute-start | bytes 1572872 | tf_op jit(solution)/shard_map/image_xy/ppermute | solution.py:300
  26.0 0.5 collective-permute-start.8
  26.5 13.7 %collective-permute-done.5.refs_9_ = bf16[1024,256]{1,0:T(8,128)(2,1)S(1)} collective-permute-done((bf16[1024,256]{1,0:T(8,128)(2,1)S(1)}, bf16[1024,256]{1,0:T(8,128)(2,1)S(1)}, u32[]{:S(2)}, u32[]{:S(2)}) %collective-permute-start.5) | collective-permute-done | bytes 524320 | tf_op jit(solution)/shard_map/w_out_z1/ppermute | solution.py:283
  40.2 0.1 collective-permute-start.9
  40.3 0.7 fusion
  41.1 1.3 collective-permute-start.10
  42.4 0.1 stack.106.idx_ref
  42.5 5.2 %shard_map.102 = (f32[1024,256]{1,0:T(8,128)}, f32[1024,256]{1,0:T(8,128)}) custom-call(s32[8]{0:T(128)S(1)} %stack.106.idx_ref, bf16[256,8192]{1,0:T(8,128)(2,1)} %image.9, bf16[256,1024]{1,0:T(8,128)(2,1)S(1)} %collective-permute-done.2.refs_0_, bf16[256,1024]{1,0:T(8,128)(2,1)S(1)} %collective-permute-done.7.refs_1_, ...), custom_call_target="tpu_custom_call" | custom-call | flops 1610612736 | bytes 8388608 | tf_op jit(solution)/shard_map/pallas_call | solution.py:396
  47.7 4.6 %collective-permute-done.10.refs_7_ = bf16[512,256]{1,0:T(8,128)(2,1)S(1)} collective-permute-done((bf16[512,256]{1,0:T(8,128)(2,1)S(1)}, bf16[512,256]{1,0:T(8,128)(2,1)S(1)}, u32[]{:S(2)}, u32[]{:S(2)}) %collective-permute-start.10) | collective-permute-done | bytes 262176 | tf_op jit(solution)/shard_map/wk_end_z1/ppermute | solution.py:283
  52.3 1.3 collective-permute-start.20
  53.6 3.0 %shard_map.103 = (f32[512,128]{1,0:T(8,128)S(1)}, f32[520,128]{1,0:T(8,128)S(1)}, f32[512,128]{1,0:T(8,128)S(1)}, f32[512,128]{1,0:T(8,128)S(1)}) custom-call(s32[8]{0:T(128)S(1)} %stack.106.idx_ref, f32[2,128]{1,0:T(2,128)S(1)} %convert_bitcast_fusion.slots, f32[1024,256]{1,0:T(8,128)} %get-tuple-element.58.acc, bf16[256,8192]{1,0:T(8,128)(2,1)} %image.9, ...), custom_call_target="tpu_custom_call" | custom-call | flops 268435456 | bytes 4194304 | tf_op jit(solution)/shard_map/pallas_call | solution.py:414
  56.6 1.6 %collective-permute-start.12 = (f32[512,128]{1,0:T(8,128)S(1)}, f32[512,128]{1,0:T(8,128)S(1)}, u32[]{:S(2)}, u32[]{:S(2)}) collective-permute-start(f32[512,128]{1,0:T(8,128)S(1)} %get-tuple-element.64), channel_id=1, source_target_pairs={{0,16},{16,0},{1,17},{17,1},{2,18},{18,2},{3,19},{19,3},{4,20},{20... | collective-permute-start | bytes 786440 | tf_op jit(solution)/shard_map/key_x/ppermute | solution.py:295
  58.1 0.6 collective-permute-start.11
  58.7 1.4 %collective-permute-start.13 = (f32[512,128]{1,0:T(8,128)S(1)}, f32[512,128]{1,0:T(8,128)S(1)}, u32[]{:S(2)}, u32[]{:S(2)}) collective-permute-start(f32[512,128]{1,0:T(8,128)S(1)} %get-tuple-element.65), channel_id=1, source_target_pairs={{0,18},{2,16},{4,22},{6,20},{8,26},{10,24},{12,30},{14,28},{16,2},... | collective-permute-start | bytes 786440 | tf_op jit(solution)/shard_map/key_xy/ppermute | solution.py:300
  60.2 0.7 collective-permute-start.14
  60.8 1.6 %collective-permute-done.20.refs_7_ = bf16[512,256]{1,0:T(8,128)(2,1)S(1)} collective-permute-done((bf16[512,256]{1,0:T(8,128)(2,1)}, bf16[512,256]{1,0:T(8,128)(2,1)S(1)}, u32[]{:S(2)}, u32[]{:S(2)}) %collective-permute-start.20) | collective-permute-done | bytes 262176 | tf_op jit(solution)/shard_map/wv_end_z1/ppermute | solution.py:283
  62.4 2.5 %collective-permute-start.15 = (bf16[32,1024]{1,0:T(8,128)(2,1)S(1)}, bf16[32,1024]{1,0:T(8,128)(2,1)S(1)}, u32[]{:S(2)}, u32[]{:S(2)}) collective-permute-start(bf16[32,1024]{1,0:T(8,128)(2,1)S(1)} %get-tuple-element.87), channel_id=1, source_target_pairs={{0,4},{1,12},{2,0},{3,8},{4,6},{5,14},{6,2},{7,10},{8,5},{9,13},{1... | collective-permute-start | bytes 196616 | tf_op jit(solution)/shard_map/q_head/ppermute | solution.py:366
  64.9 2.9 %shard_map.106 = (f32[512,128]{1,0:T(8,128)S(1)}, bf16[512,128]{1,0:T(8,128)(2,1)S(1)}, bf16[512,128]{1,0:T(8,128)(2,1)S(1)}, bf16[512,128]{1,0:T(8,128)(2,1)S(1)}) custom-call(s32[8]{0:T(128)S(1)} %stack.106.idx_ref, f32[2,128]{1,0:T(2,128)S(1)} %convert_bitcast_fusion.slots, f32[1024,256]{1,0:T(8,128)} %get-tuple-element.75.acc, bf16[256,8192]{1,0:T(8,128)(2,1)} %image.9, ...), custom_call_target="tpu_custom_call" | custom-call | flops 268435456 | bytes 4194304 | tf_op jit(solution)/shard_map/pallas_call | solution.py:414
  67.8 2.7 %collective-permute-start.21 = (bf16[512,128]{1,0:T(8,128)(2,1)S(1)}, bf16[512,128]{1,0:T(8,128)(2,1)S(1)}, u32[]{:S(2)}, u32[]{:S(2)}) collective-permute-start(bf16[512,128]{1,0:T(8,128)(2,1)S(1)} %get-tuple-element.78), channel_id=1, source_target_pairs={{0,2},{2,0},{4,6},{6,4},{8,10},{10,8},{12,14},{14,12},{1,3},{3,1},... | collective-permute-start | bytes 393224 | tf_op jit(solution)/shard_map/value_y/ppermute | solution.py:287
  70.5 3.5 %collective-permute-done.15 = bf16[32,1024]{1,0:T(8,128)(2,1)S(1)} collective-permute-done((bf16[32,1024]{1,0:T(8,128)(2,1)S(1)}, bf16[32,1024]{1,0:T(8,128)(2,1)S(1)}, u32[]{:S(2)}, u32[]{:S(2)}) %collective-permute-start.15) | collective-permute-done | bytes 65568 | tf_op jit(solution)/shard_map/q_head/ppermute | solution.py:366
  74.0 1.0 collective-permute-start.23
  75.0 0.2 shard_map.104
  75.2 0.7 collective-permute-start.16
  75.9 7.5 %collective-permute-start.17 = (bf16[528,128]{1,0:T(8,128)(2,1)S(1)}, bf16[528,128]{1,0:T(8,128)(2,1)S(1)}, u32[]{:S(2)}, u32[]{:S(2)}) collective-permute-start(bf16[528,128]{1,0:T(8,128)(2,1)S(1)} %shard_map.104), channel_id=1, source_target_pairs={{0,2},{1,10},{2,6},{3,14},{4,0},{5,8},{6,4},{7,12},{8,3},{9,11},{1... | collective-permute-start | bytes 405512 | tf_op jit(solution)/shard_map/key_head/ppermute | solution.py:358
  83.4 0.1 add_convert_fusion.1
  83.5 0.7 collective-permute-start.24
  84.2 4.1 %collective-permute-start.25 = (bf16[512,128]{1,0:T(8,128)(2,1)S(1)}, bf16[512,128]{1,0:T(8,128)(2,1)S(1)}, u32[]{:S(2)}, u32[]{:S(2)}) collective-permute-start(bf16[512,128]{1,0:T(8,128)(2,1)S(1)} %add_convert_fusion.1), channel_id=1, source_target_pairs={{0,2},{1,10},{2,6},{3,14},{4,0},{5,8},{6,4},{7,12},{8,3},{9,11},{1... | collective-permute-start | bytes 393224 | tf_op jit(solution)/shard_map/value_head/ppermute | solution.py:358
  88.3 0.1 convert_bitcast_fusion.1
  88.4 0.1 copy.12.limit_ref
  88.5 0.1 collective-permute-start.18
  88.6 6.7 %collective-permute-done.17.refs_1_ = bf16[528,128]{1,0:T(8,128)(2,1)S(1)} collective-permute-done((bf16[528,128]{1,0:T(8,128)(2,1)S(1)}, bf16[528,128]{1,0:T(8,128)(2,1)S(1)}, u32[]{:S(2)}, u32[]{:S(2)}) %collective-permute-start.17) | collective-permute-done | bytes 135200 | tf_op jit(solution)/shard_map/key_head/ppermute | solution.py:358
  95.3 0.5 collective-permute-start.26
  95.8 2.3 %collective-permute-done.25.refs_1_ = bf16[512,128]{1,0:T(8,128)(2,1)S(1)} collective-permute-done((bf16[512,128]{1,0:T(8,128)(2,1)S(1)}, bf16[512,128]{1,0:T(8,128)(2,1)S(1)}, u32[]{:S(2)}, u32[]{:S(2)}) %collective-permute-start.25) | collective-permute-done | bytes 131104 | tf_op jit(solution)/shard_map/value_head/ppermute | solution.py:358
  98.2 1.8 %shard_map.105 = (bf16[512,2048]{1,0:T(8,128)(2,1)S(1)}, f32[512,1]{1,0:T(8,128)S(1)}) custom-call(bf16[512,128]{1,0:T(8,128)(2,1)S(1)} %bitcast.34, f32[64,1]{1,0:T(8,128)S(1)} %copy.12.limit_ref, bf16[528,128]{1,0:T(8,128)(2,1)S(1)} %collective-permute-done.16.refs_0_, bf16[528,128]{1,0:T(8,128)(2,1)S(1)} %collective-permute-done.17.refs_1_, ...), custom_call_target="tpu_custom_call" | custom-call | tf_op jit(solution)/shard_map/pallas_call | solution.py:473
  100.0 0.7 shard_map.107
  100.8 0.7 collective-permute-start.28
  101.4 0.9 collective-permute-start.29
  102.3 3.5 %collective-permute-start.30 = (bf16[64,1024]{1,0:T(8,128)(2,1)S(1)}, bf16[64,1024]{1,0:T(8,128)(2,1)S(1)}, u32[]{:S(2)}, u32[]{:S(2)}) collective-permute-start(bf16[64,1024]{1,0:T(8,128)(2,1)S(1)} %shard_map.107), channel_id=1, source_target_pairs={{0,8},{1,12},{2,10},{3,14},{4,0},{5,4},{6,2},{7,6},{8,9},{9,13},{1... | collective-permute-start | bytes 393224 | tf_op jit(solution)/shard_map/attn_out2/ppermute | solution.py:505
  105.9 2.8 %collective-permute-start.31 = (bf16[64,1024]{1,0:T(8,128)(2,1)S(1)}, bf16[64,1024]{1,0:T(8,128)(2,1)S(1)}, u32[]{:S(2)}, u32[]{:S(2)}) collective-permute-start(bf16[64,1024]{1,0:T(8,128)(2,1)S(1)} %shard_map.107), channel_id=1, source_target_pairs={{0,12},{1,8},{2,14},{3,10},{4,4},{5,0},{6,6},{7,2},{8,13},{9,9},{1... | collective-permute-start | bytes 393224 | tf_op jit(solution)/shard_map/attn_out3/ppermute | solution.py:505
  108.7 0.1 collective-permute-start.32
  108.8 2.0 %collective-permute-start.33 = (bf16[64,1024]{1,0:T(8,128)(2,1)S(1)}, bf16[64,1024]{1,0:T(8,128)(2,1)S(1)}, u32[]{:S(2)}, u32[]{:S(2)}) collective-permute-start(bf16[64,1024]{1,0:T(8,128)(2,1)S(1)} %collective-permute-done.29.refs_1_), channel_id=1, source_target_pairs={{0,2},{2,0},{4,6},{6,4},{8,10},{10,8},{12,14},{14,12},{1,3},{3,1},... | collective-permute-start | bytes 393224 | tf_op jit(solution)/shard_map/attn1_y/ppermute | solution.py:287
  110.8 0.1 collective-permute-start.34
  110.9 2.7 %collective-permute-done.31.refs_3_ = bf16[64,1024]{1,0:T(8,128)(2,1)S(1)} collective-permute-done((bf16[64,1024]{1,0:T(8,128)(2,1)S(1)}, bf16[64,1024]{1,0:T(8,128)(2,1)S(1)}, u32[]{:S(2)}, u32[]{:S(2)}) %collective-permute-start.31) | collective-permute-done | bytes 131104 | tf_op jit(solution)/shard_map/attn_out3/ppermute | solution.py:505
  113.6 0.1 collective-permute-start.35
  113.7 0.1 stack.97.idx_ref
  113.8 1.3 %collective-permute-done.33.refs_5_ = bf16[64,1024]{1,0:T(8,128)(2,1)S(1)} collective-permute-done((bf16[64,1024]{1,0:T(8,128)(2,1)S(1)}, bf16[64,1024]{1,0:T(8,128)(2,1)S(1)}, u32[]{:S(2)}, u32[]{:S(2)}) %collective-permute-start.33) | collective-permute-done | bytes 131104 | tf_op jit(solution)/shard_map/attn1_y/ppermute | solution.py:287
  115.1 1.4 %collective-permute-done.34.refs_6_ = bf16[64,1024]{1,0:T(8,128)(2,1)S(1)} collective-permute-done((bf16[64,1024]{1,0:T(8,128)(2,1)S(1)}, bf16[64,1024]{1,0:T(8,128)(2,1)S(1)}, u32[]{:S(2)}, u32[]{:S(2)}) %collective-permute-start.34) | collective-permute-done | bytes 131104 | tf_op jit(solution)/shard_map/attn2_y/ppermute | solution.py:287
  116.5 3.0 %collective-permute-done.35.refs_7_ = bf16[64,1024]{1,0:T(8,128)(2,1)S(1)} collective-permute-done((bf16[64,1024]{1,0:T(8,128)(2,1)S(1)}, bf16[64,1024]{1,0:T(8,128)(2,1)S(1)}, u32[]{:S(2)}, u32[]{:S(2)}) %collective-permute-start.35) | collective-permute-done | bytes 131104 | tf_op jit(solution)/shard_map/attn3_y/ppermute | solution.py:287
  119.6 4.8 %shard_map.108 = (f32[128,1024]{1,0:T(8,128)S(1)}, bf16[128,1024]{1,0:T(8,128)(2,1)S(1)}) custom-call(s32[17]{0:T(128)S(1)} %stack.97.idx_ref, bf16[64,1024]{1,0:T(8,128)(2,1)S(1)} %collective-permute-done.28.refs_0_, bf16[64,1024]{1,0:T(8,128)(2,1)S(1)} %collective-permute-done.29.refs_1_, bf16[64,1024]{1,0:T(8,128)(2,1)S(1)} %collective-permute-done.30.refs_2_, ...), custom_call_target="tpu_custom_call" | custom-call | tf_op jit(solution)/shard_map/pallas_call | solution.py:517
  124.4 4.5 %collective-permute-start.36 = (bf16[128,1024]{1,0:T(8,128)(2,1)S(1)}, bf16[128,1024]{1,0:T(8,128)(2,1)S(1)}, u32[]{:S(2)}, u32[]{:S(2)}) collective-permute-start(bf16[128,1024]{1,0:T(8,128)(2,1)S(1)} %get-tuple-element.82), channel_id=1, source_target_pairs={{0,1},{1,0},{2,3},{3,2},{4,5},{5,4},{6,7},{7,6},{8,9},{9,8},{10,11... | collective-permute-start | bytes 786440 | tf_op jit(solution)/shard_map/proj_core/ppermute | solution.py:291
  129.6 0.5 collective-permute-done.36
  130.1 0.8 add_convert_fusion
  (59 shorter events, 0.2 us)
Async XLA Ops:
  3.8 15.2 %collective-permute-start = (bf16[1024,256]{1,0:T(8,128)(2,1)}, bf16[1024,256]{1,0:T(8,128)(2,1)S(1)}, u32[]{:S(2)}, u32[]{:S(2)}) collective-permute-start(bf16[1024,256]{1,0:T(8,128)(2,1)} %get-tuple-element.44.refs_6_), channel_id=1, source_target_pairs={{0,4},{2,6},{4,0},{6,2},{8,12},{10,14},{12,8},{14,10},{1,5},{3,7},... | collective-permute-start | bytes 1572872 | tf_op jit(solution)/shard_map/w_z1/ppermute | solution.py:283
  6.9 12.1 %collective-permute-start.1 = (bf16[1024,256]{1,0:T(8,128)(2,1)}, bf16[1024,256]{1,0:T(8,128)(2,1)S(1)}, u32[]{:S(2)}, u32[]{:S(2)}) collective-permute-start(bf16[1024,256]{1,0:T(8,128)(2,1)} %get-tuple-element.44.refs_6_), channel_id=1, source_target_pairs={{4,8},{6,10},{8,4},{10,6},{5,9},{7,11},{9,5},{11,7},{20,24},{22,26... | collective-permute-start | bytes 1572872 | tf_op jit(solution)/shard_map/w_z3/ppermute | solution.py:283
  7.6 13.7 %collective-permute-start.2 = (bf16[256,1024]{1,0:T(8,128)(2,1)}, bf16[256,1024]{1,0:T(8,128)(2,1)S(1)}, u32[]{:S(2)}, u32[]{:S(2)}) collective-permute-start(bf16[256,1024]{1,0:T(8,128)(2,1)} %get-tuple-element.45), channel_id=1, source_target_pairs={{0,2},{2,0},{4,6},{6,4},{8,10},{10,8},{12,14},{14,12},{1,3},{3,1},... | collective-permute-start | bytes 1572872 | tf_op jit(solution)/shard_map/image_y/ppermute | solution.py:287
  9.2 13.3 %collective-permute-start.3 = (bf16[256,1024]{1,0:T(8,128)(2,1)}, bf16[256,1024]{1,0:T(8,128)(2,1)S(1)}, u32[]{:S(2)}, u32[]{:S(2)}) collective-permute-start(bf16[256,1024]{1,0:T(8,128)(2,1)} %get-tuple-element.46), channel_id=1, source_target_pairs={{0,16},{16,0},{1,17},{17,1},{2,18},{18,2},{3,19},{19,3},{4,20},{20... | collective-permute-start | bytes 1572872 | tf_op jit(solution)/shard_map/image_x/ppermute | solution.py:295
  19.0 22.0 %copy-start.8 = (bf16[1024,256]{1,0:T(8,128)(2,1)}, bf16[1024,256]{1,0:T(8,128)(2,1)S(1)}, u32[]{:S(2)}) copy-start(bf16[1024,256]{1,0:T(8,128)(2,1)S(1)} %collective-permute-done.refs_7_) | copy-start | bytes 1572868
  19.0 22.0 %copy-start.6 = (bf16[1024,256]{1,0:T(8,128)(2,1)}, bf16[1024,256]{1,0:T(8,128)(2,1)S(1)}, u32[]{:S(2)}) copy-start(bf16[1024,256]{1,0:T(8,128)(2,1)S(1)} %collective-permute-done.1.refs_6_) | copy-start | bytes 1572868
  22.5 25.2 %copy-start = (bf16[256,1024]{1,0:T(8,128)(2,1)}, bf16[256,1024]{1,0:T(8,128)(2,1)S(1)}, u32[]{:S(2)}) copy-start(bf16[256,1024]{1,0:T(8,128)(2,1)S(1)} %collective-permute-done.3.refs_2_) | copy-start | bytes 1572868
  22.5 4.0 %collective-permute-start.4 = (bf16[1024,256]{1,0:T(8,128)(2,1)S(1)}, bf16[1024,256]{1,0:T(8,128)(2,1)S(1)}, u32[]{:S(2)}, u32[]{:S(2)}) collective-permute-start(bf16[1024,256]{1,0:T(8,128)(2,1)S(1)} %collective-permute-done.refs_7_), channel_id=1, source_target_pairs={{4,8},{6,10},{8,4},{10,6},{5,9},{7,11},{9,5},{11,7},{20,24},{22,26... | collective-permute-start | bytes 1572872 | tf_op jit(solution)/shard_map/w_across_z3/ppermute | solution.py:283
  23.2 17.0 %collective-permute-start.5 = (bf16[1024,256]{1,0:T(8,128)(2,1)S(1)}, bf16[1024,256]{1,0:T(8,128)(2,1)S(1)}, u32[]{:S(2)}, u32[]{:S(2)}) collective-permute-start(bf16[1024,256]{1,0:T(8,128)(2,1)S(1)} %collective-permute-done.1.refs_6_), channel_id=1, source_target_pairs={{4,0},{6,2},{8,12},{10,14},{5,1},{7,3},{9,13},{11,15},{20,16},{22,... | collective-permute-start | bytes 1572872 | tf_op jit(solution)/shard_map/w_out_z1/ppermute | solution.py:283
  24.5 15.7 %collective-permute-start.6 = (bf16[256,1024]{1,0:T(8,128)(2,1)}, bf16[256,1024]{1,0:T(8,128)(2,1)S(1)}, u32[]{:S(2)}, u32[]{:S(2)}) collective-permute-start(bf16[256,1024]{1,0:T(8,128)(2,1)} %shard_map.101), channel_id=1, source_target_pairs={{0,18},{2,16},{4,22},{6,20},{8,26},{10,24},{12,30},{14,28},{16,2},... | collective-permute-start | bytes 1572872 | tf_op jit(solution)/shard_map/image_xy/ppermute | solution.py:300
  26.0 14.2 %collective-permute-start.7 = (bf16[256,1024]{1,0:T(8,128)(2,1)S(1)}, bf16[256,1024]{1,0:T(8,128)(2,1)S(1)}, u32[]{:S(2)}, u32[]{:S(2)}) collective-permute-start(bf16[256,1024]{1,0:T(8,128)(2,1)S(1)} %collective-permute-done.2.refs_0_), channel_id=1, source_target_pairs={{0,1},{1,0},{2,3},{3,2},{4,5},{5,4},{6,7},{7,6},{8,9},{9,8},{10,11... | collective-permute-start | bytes 1572872 | tf_op jit(solution)/shard_map/image_core/ppermute | solution.py:291
  26.0 14.2 %collective-permute-start.8 = (bf16[256,1024]{1,0:T(8,128)(2,1)S(1)}, bf16[256,1024]{1,0:T(8,128)(2,1)S(1)}, u32[]{:S(2)}, u32[]{:S(2)}) collective-permute-start(bf16[256,1024]{1,0:T(8,128)(2,1)S(1)} %collective-permute-done.3.refs_2_), channel_id=1, source_target_pairs={{0,1},{1,0},{2,3},{3,2},{4,5},{5,4},{6,7},{7,6},{8,9},{9,8},{10,11... | collective-permute-start | bytes 1572872 | tf_op jit(solution)/shard_map/image_core/ppermute | solution.py:291
  26.5 14.6 %copy-start.7 = (bf16[1024,256]{1,0:T(8,128)(2,1)}, bf16[1024,256]{1,0:T(8,128)(2,1)S(1)}, u32[]{:S(2)}) copy-start(bf16[1024,256]{1,0:T(8,128)(2,1)S(1)} %collective-permute-done.4.refs_8_) | copy-start | bytes 1572868
  40.2 0.9 copy-start.9
  40.2 2.3 %copy-start.4 = (bf16[256,1024]{1,0:T(8,128)(2,1)}, bf16[256,1024]{1,0:T(8,128)(2,1)S(1)}, u32[]{:S(2)}) copy-start(bf16[256,1024]{1,0:T(8,128)(2,1)S(1)} %collective-permute-done.6.refs_4_) | copy-start | bytes 1572868
  40.2 7.5 %copy-start.1 = (bf16[256,1024]{1,0:T(8,128)(2,1)}, bf16[256,1024]{1,0:T(8,128)(2,1)S(1)}, u32[]{:S(2)}) copy-start(bf16[256,1024]{1,0:T(8,128)(2,1)S(1)} %collective-permute-done.7.refs_1_) | copy-start | bytes 1572868
  40.2 2.3 %copy-start.5 = (bf16[256,1024]{1,0:T(8,128)(2,1)}, bf16[256,1024]{1,0:T(8,128)(2,1)S(1)}, u32[]{:S(2)}) copy-start(bf16[256,1024]{1,0:T(8,128)(2,1)S(1)} %collective-permute-done.8.refs_3_) | copy-start | bytes 1572868
  40.2 2.2 %collective-permute-start.9 = (bf16[256,1024]{1,0:T(8,128)(2,1)S(1)}, bf16[256,1024]{1,0:T(8,128)(2,1)}, u32[]{:S(2)}, u32[]{:S(2)}) collective-permute-start(bf16[256,1024]{1,0:T(8,128)(2,1)S(1)} %collective-permute-done.6.refs_4_), channel_id=1, source_target_pairs={{0,1},{1,0},{2,3},{3,2},{4,5},{5,4},{6,7},{7,6},{8,9},{9,8},{10,11... | collective-permute-start | bytes 1572872 | tf_op jit(solution)/shard_map/image_core/ppermute | solution.py:291
  41.1 11.2 %collective-permute-start.10 = (bf16[512,256]{1,0:T(8,128)(2,1)S(1)}, bf16[512,256]{1,0:T(8,128)(2,1)S(1)}, u32[]{:S(2)}, u32[]{:S(2)}) collective-permute-start(bf16[512,256]{1,0:T(8,128)(2,1)S(1)} %get-tuple-element.84), channel_id=1, source_target_pairs={{4,0},{6,2},{8,12},{10,14},{5,1},{7,3},{9,13},{11,15},{20,16},{22,... | collective-permute-start | bytes 786440 | tf_op jit(solution)/shard_map/wk_end_z1/ppermute | solution.py:283
  42.5 11.1 %copy-start.12 = (s32[256]{0:T(256)S(1)}, s32[256]{0:T(256)}, u32[]{:S(2)}) copy-start(s32[256]{0:T(256)} %param.11) | copy-start | bytes 3076
  52.3 10.1 %collective-permute-start.20 = (bf16[512,256]{1,0:T(8,128)(2,1)}, bf16[512,256]{1,0:T(8,128)(2,1)S(1)}, u32[]{:S(2)}, u32[]{:S(2)}) collective-permute-start(bf16[512,256]{1,0:T(8,128)(2,1)} %get-tuple-element.76), channel_id=1, source_target_pairs={{4,0},{6,2},{8,12},{10,14},{5,1},{7,3},{9,13},{11,15},{20,16},{22,... | collective-permute-start | bytes 786440 | tf_op jit(solution)/shard_map/wv_end_z1/ppermute | solution.py:283
  53.6 6.6 %copy-start.11 = (bf16[32,2048]{1,0:T(8,128)(2,1)S(1)}, bf16[32,2048]{1,0:T(8,128)(2,1)}, u32[]{:S(2)}) copy-start(bf16[32,2048]{1,0:T(8,128)(2,1)} %param.15) | copy-start | bytes 393220
  53.6 11.3 %copy-start.2 = (bf16[256,1024]{1,0:T(8,128)(2,1)S(1)}, bf16[256,1024]{1,0:T(8,128)(2,1)}, u32[]{:S(2)}) copy-start(bf16[256,1024]{1,0:T(8,128)(2,1)} %copy-done.1) | copy-start | bytes 1572868
  56.6 17.4 %collective-permute-start.12 = (f32[512,128]{1,0:T(8,128)S(1)}, f32[512,128]{1,0:T(8,128)S(1)}, u32[]{:S(2)}, u32[]{:S(2)}) collective-permute-start(f32[512,128]{1,0:T(8,128)S(1)} %get-tuple-element.64), channel_id=1, source_target_pairs={{0,16},{16,0},{1,17},{17,1},{2,18},{18,2},{3,19},{19,3},{4,20},{20... | collective-permute-start | bytes 786440 | tf_op jit(solution)/shard_map/key_x/ppermute | solution.py:295
  58.1 16.9 %collective-permute-start.11 = (f32[520,128]{1,0:T(8,128)S(1)}, f32[520,128]{1,0:T(8,128)S(1)}, u32[]{:S(2)}, u32[]{:S(2)}) collective-permute-start(f32[520,128]{1,0:T(8,128)S(1)} %get-tuple-element.63), channel_id=1, source_target_pairs={{0,2},{2,0},{4,6},{6,4},{8,10},{10,8},{12,14},{14,12},{1,3},{3,1},... | collective-permute-start | bytes 798728 | tf_op jit(solution)/shard_map/key_y/ppermute | solution.py:287
  58.7 16.3 %collective-permute-start.13 = (f32[512,128]{1,0:T(8,128)S(1)}, f32[512,128]{1,0:T(8,128)S(1)}, u32[]{:S(2)}, u32[]{:S(2)}) collective-permute-start(f32[512,128]{1,0:T(8,128)S(1)} %get-tuple-element.65), channel_id=1, source_target_pairs={{0,18},{2,16},{4,22},{6,20},{8,26},{10,24},{12,30},{14,28},{16,2},... | collective-permute-start | bytes 786440 | tf_op jit(solution)/shard_map/key_xy/ppermute | solution.py:300
  60.2 7.6 %collective-permute-start.14 = (bf16[32,1024]{1,0:T(8,128)(2,1)S(1)}, bf16[32,1024]{1,0:T(8,128)(2,1)S(1)}, u32[]{:S(2)}, u32[]{:S(2)}) collective-permute-start(bf16[32,1024]{1,0:T(8,128)(2,1)S(1)} %get-tuple-element.88), channel_id=1, source_target_pairs={{0,0},{1,8},{2,4},{3,12},{4,2},{5,10},{6,6},{7,14},{8,1},{9,9},{10... | collective-permute-start | bytes 196616 | tf_op jit(solution)/shard_map/q_head/ppermute | solution.py:366
  62.4 11.6 %collective-permute-start.15 = (bf16[32,1024]{1,0:T(8,128)(2,1)S(1)}, bf16[32,1024]{1,0:T(8,128)(2,1)S(1)}, u32[]{:S(2)}, u32[]{:S(2)}) collective-permute-start(bf16[32,1024]{1,0:T(8,128)(2,1)S(1)} %get-tuple-element.87), channel_id=1, source_target_pairs={{0,4},{1,12},{2,0},{3,8},{4,6},{5,14},{6,2},{7,10},{8,5},{9,13},{1... | collective-permute-start | bytes 196616 | tf_op jit(solution)/shard_map/q_head/ppermute | solution.py:366
  64.9 10.2 %copy-start.3 = (f32[128]{0:T(128)S(1)}, f32[128]{0:T(128)}, u32[]{:S(2)}) copy-start(f32[128]{0:T(128)} %param.14) | copy-start | bytes 1540
  64.9 23.4 %copy-start.13 = (s32[256]{0:T(256)S(1)}, s32[256]{0:T(256)}, u32[]{:S(2)}) copy-start(s32[256]{0:T(256)} %param.16) | copy-start | bytes 3076
  67.8 15.7 %collective-permute-start.21 = (bf16[512,128]{1,0:T(8,128)(2,1)S(1)}, bf16[512,128]{1,0:T(8,128)(2,1)S(1)}, u32[]{:S(2)}, u32[]{:S(2)}) collective-permute-start(bf16[512,128]{1,0:T(8,128)(2,1)S(1)} %get-tuple-element.78), channel_id=1, source_target_pairs={{0,2},{2,0},{4,6},{6,4},{8,10},{10,8},{12,14},{14,12},{1,3},{3,1},... | collective-permute-start | bytes 393224 | tf_op jit(solution)/shard_map/value_y/ppermute | solution.py:287
  74.0 9.4 %collective-permute-start.22 = (bf16[512,128]{1,0:T(8,128)(2,1)S(1)}, bf16[512,128]{1,0:T(8,128)(2,1)S(1)}, u32[]{:S(2)}, u32[]{:S(2)}) collective-permute-start(bf16[512,128]{1,0:T(8,128)(2,1)S(1)} %get-tuple-element.79), channel_id=1, source_target_pairs={{0,16},{16,0},{1,17},{17,1},{2,18},{18,2},{3,19},{19,3},{4,20},{20... | collective-permute-start | bytes 393224 | tf_op jit(solution)/shard_map/value_x/ppermute | solution.py:295
  74.0 9.4 %collective-permute-start.23 = (bf16[512,128]{1,0:T(8,128)(2,1)S(1)}, bf16[512,128]{1,0:T(8,128)(2,1)S(1)}, u32[]{:S(2)}, u32[]{:S(2)}) collective-permute-start(bf16[512,128]{1,0:T(8,128)(2,1)S(1)} %get-tuple-element.80), channel_id=1, source_target_pairs={{0,18},{2,16},{4,22},{6,20},{8,26},{10,24},{12,30},{14,28},{16,2},... | collective-permute-start | bytes 393224 | tf_op jit(solution)/shard_map/value_xy/ppermute | solution.py:300
  75.2 13.3 %collective-permute-start.16 = (bf16[528,128]{1,0:T(8,128)(2,1)S(1)}, bf16[528,128]{1,0:T(8,128)(2,1)S(1)}, u32[]{:S(2)}, u32[]{:S(2)}) collective-permute-start(bf16[528,128]{1,0:T(8,128)(2,1)S(1)} %shard_map.104), channel_id=1, source_target_pairs={{0,0},{1,8},{2,4},{3,12},{4,2},{5,10},{6,6},{7,14},{8,1},{9,9},{10... | collective-permute-start | bytes 405512 | tf_op jit(solution)/shard_map/key_head/ppermute | solution.py:358
  75.9 19.4 %collective-permute-start.17 = (bf16[528,128]{1,0:T(8,128)(2,1)S(1)}, bf16[528,128]{1,0:T(8,128)(2,1)S(1)}, u32[]{:S(2)}, u32[]{:S(2)}) collective-permute-start(bf16[528,128]{1,0:T(8,128)(2,1)S(1)} %shard_map.104), channel_id=1, source_target_pairs={{0,2},{1,10},{2,6},{3,14},{4,0},{5,8},{6,4},{7,12},{8,3},{9,11},{1... | collective-permute-start | bytes 405512 | tf_op jit(solution)/shard_map/key_head/ppermute | solution.py:358
  83.5 11.8 %collective-permute-start.24 = (bf16[512,128]{1,0:T(8,128)(2,1)S(1)}, bf16[512,128]{1,0:T(8,128)(2,1)S(1)}, u32[]{:S(2)}, u32[]{:S(2)}) collective-permute-start(bf16[512,128]{1,0:T(8,128)(2,1)S(1)} %add_convert_fusion.1), channel_id=1, source_target_pairs={{0,0},{1,8},{2,4},{3,12},{4,2},{5,10},{6,6},{7,14},{8,1},{9,9},{10... | collective-permute-start | bytes 393224 | tf_op jit(solution)/shard_map/value_head/ppermute | solution.py:358
  84.2 13.9 %collective-permute-start.25 = (bf16[512,128]{1,0:T(8,128)(2,1)S(1)}, bf16[512,128]{1,0:T(8,128)(2,1)S(1)}, u32[]{:S(2)}, u32[]{:S(2)}) collective-permute-start(bf16[512,128]{1,0:T(8,128)(2,1)S(1)} %add_convert_fusion.1), channel_id=1, source_target_pairs={{0,2},{1,10},{2,6},{3,14},{4,0},{5,8},{6,4},{7,12},{8,3},{9,11},{1... | collective-permute-start | bytes 393224 | tf_op jit(solution)/shard_map/value_head/ppermute | solution.py:358
  88.5 9.7 %collective-permute-start.18 = (bf16[528,128]{1,0:T(8,128)(2,1)S(1)}, bf16[528,128]{1,0:T(8,128)(2,1)S(1)}, u32[]{:S(2)}, u32[]{:S(2)}) collective-permute-start(bf16[528,128]{1,0:T(8,128)(2,1)S(1)} %collective-permute-done.16.refs_0_), channel_id=1, source_target_pairs={{0,1},{1,0},{2,3},{3,2},{4,5},{5,4},{6,7},{7,6},{8,9},{9,8},{10,11... | collective-permute-start | bytes 405512 | tf_op jit(solution)/shard_map/key_tile_core/ppermute | solution.py:291
  95.3 2.9 %collective-permute-start.19 = (bf16[528,128]{1,0:T(8,128)(2,1)S(1)}, bf16[528,128]{1,0:T(8,128)(2,1)S(1)}, u32[]{:S(2)}, u32[]{:S(2)}) collective-permute-start(bf16[528,128]{1,0:T(8,128)(2,1)S(1)} %collective-permute-done.17.refs_1_), channel_id=1, source_target_pairs={{0,1},{1,0},{2,3},{3,2},{4,5},{5,4},{6,7},{7,6},{8,9},{9,8},{10,11... | collective-permute-start | bytes 405512 | tf_op jit(solution)/shard_map/key_tile_core/ppermute | solution.py:291
  95.3 4.7 %collective-permute-start.26 = (bf16[512,128]{1,0:T(8,128)(2,1)S(1)}, bf16[512,128]{1,0:T(8,128)(2,1)S(1)}, u32[]{:S(2)}, u32[]{:S(2)}) collective-permute-start(bf16[512,128]{1,0:T(8,128)(2,1)S(1)} %collective-permute-done.24.refs_0_), channel_id=1, source_target_pairs={{0,1},{1,0},{2,3},{3,2},{4,5},{5,4},{6,7},{7,6},{8,9},{9,8},{10,11... | collective-permute-start | bytes 393224 | tf_op jit(solution)/shard_map/value_tile_core/ppermute | solution.py:291
  98.1 1.9 %collective-permute-start.27 = (bf16[512,128]{1,0:T(8,128)(2,1)S(1)}, bf16[512,128]{1,0:T(8,128)(2,1)S(1)}, u32[]{:S(2)}, u32[]{:S(2)}) collective-permute-start(bf16[512,128]{1,0:T(8,128)(2,1)S(1)} %collective-permute-done.25.refs_1_), channel_id=1, source_target_pairs={{0,1},{1,0},{2,3},{3,2},{4,5},{5,4},{6,7},{7,6},{8,9},{9,8},{10,11... | collective-permute-start | bytes 393224 | tf_op jit(solution)/shard_map/value_tile_core/ppermute | solution.py:291
  100.0 30.0 %copy-start.10 = (bf16[128,1024]{1,0:T(8,128)(2,1)S(1)}, bf16[128,1024]{1,0:T(8,128)(2,1)}, u32[]{:S(2)}) copy-start(bf16[128,1024]{1,0:T(8,128)(2,1)} %param.17) | copy-start | bytes 786436
  100.8 7.9 %collective-permute-start.28 = (bf16[64,1024]{1,0:T(8,128)(2,1)S(1)}, bf16[64,1024]{1,0:T(8,128)(2,1)S(1)}, u32[]{:S(2)}, u32[]{:S(2)}) collective-permute-start(bf16[64,1024]{1,0:T(8,128)(2,1)S(1)} %shard_map.107), channel_id=1, source_target_pairs={{0,0},{1,4},{2,2},{3,6},{4,8},{5,12},{6,10},{7,14},{8,1},{9,5},{10... | collective-permute-start | bytes 393224 | tf_op jit(solution)/shard_map/attn_out0/ppermute | solution.py:505
  101.4 7.4 %collective-permute-start.29 = (bf16[64,1024]{1,0:T(8,128)(2,1)S(1)}, bf16[64,1024]{1,0:T(8,128)(2,1)S(1)}, u32[]{:S(2)}, u32[]{:S(2)}) collective-permute-start(bf16[64,1024]{1,0:T(8,128)(2,1)S(1)} %shard_map.107), channel_id=1, source_target_pairs={{0,4},{1,0},{2,6},{3,2},{4,12},{5,8},{6,14},{7,10},{8,5},{9,1},{10... | collective-permute-start | bytes 393224 | tf_op jit(solution)/shard_map/attn_out1/ppermute | solution.py:505
  102.3 8.5 %collective-permute-start.30 = (bf16[64,1024]{1,0:T(8,128)(2,1)S(1)}, bf16[64,1024]{1,0:T(8,128)(2,1)S(1)}, u32[]{:S(2)}, u32[]{:S(2)}) collective-permute-start(bf16[64,1024]{1,0:T(8,128)(2,1)S(1)} %shard_map.107), channel_id=1, source_target_pairs={{0,8},{1,12},{2,10},{3,14},{4,0},{5,4},{6,2},{7,6},{8,9},{9,13},{1... | collective-permute-start | bytes 393224 | tf_op jit(solution)/shard_map/attn_out2/ppermute | solution.py:505
  105.9 7.8 %collective-permute-start.31 = (bf16[64,1024]{1,0:T(8,128)(2,1)S(1)}, bf16[64,1024]{1,0:T(8,128)(2,1)S(1)}, u32[]{:S(2)}, u32[]{:S(2)}) collective-permute-start(bf16[64,1024]{1,0:T(8,128)(2,1)S(1)} %shard_map.107), channel_id=1, source_target_pairs={{0,12},{1,8},{2,14},{3,10},{4,4},{5,0},{6,6},{7,2},{8,13},{9,9},{1... | collective-permute-start | bytes 393224 | tf_op jit(solution)/shard_map/attn_out3/ppermute | solution.py:505
  108.7 5.1 %collective-permute-start.32 = (bf16[64,1024]{1,0:T(8,128)(2,1)S(1)}, bf16[64,1024]{1,0:T(8,128)(2,1)S(1)}, u32[]{:S(2)}, u32[]{:S(2)}) collective-permute-start(bf16[64,1024]{1,0:T(8,128)(2,1)S(1)} %collective-permute-done.28.refs_0_), channel_id=1, source_target_pairs={{0,2},{2,0},{4,6},{6,4},{8,10},{10,8},{12,14},{14,12},{1,3},{3,1},... | collective-permute-start | bytes 393224 | tf_op jit(solution)/shard_map/attn0_y/ppermute | solution.py:287
  108.8 6.3 %collective-permute-start.33 = (bf16[64,1024]{1,0:T(8,128)(2,1)S(1)}, bf16[64,1024]{1,0:T(8,128)(2,1)S(1)}, u32[]{:S(2)}, u32[]{:S(2)}) collective-permute-start(bf16[64,1024]{1,0:T(8,128)(2,1)S(1)} %collective-permute-done.29.refs_1_), channel_id=1, source_target_pairs={{0,2},{2,0},{4,6},{6,4},{8,10},{10,8},{12,14},{14,12},{1,3},{3,1},... | collective-permute-start | bytes 393224 | tf_op jit(solution)/shard_map/attn1_y/ppermute | solution.py:287
  110.8 5.7 %collective-permute-start.34 = (bf16[64,1024]{1,0:T(8,128)(2,1)S(1)}, bf16[64,1024]{1,0:T(8,128)(2,1)S(1)}, u32[]{:S(2)}, u32[]{:S(2)}) collective-permute-start(bf16[64,1024]{1,0:T(8,128)(2,1)S(1)} %collective-permute-done.30.refs_2_), channel_id=1, source_target_pairs={{0,2},{2,0},{4,6},{6,4},{8,10},{10,8},{12,14},{14,12},{1,3},{3,1},... | collective-permute-start | bytes 393224 | tf_op jit(solution)/shard_map/attn2_y/ppermute | solution.py:287
  113.6 6.0 %collective-permute-start.35 = (bf16[64,1024]{1,0:T(8,128)(2,1)S(1)}, bf16[64,1024]{1,0:T(8,128)(2,1)S(1)}, u32[]{:S(2)}, u32[]{:S(2)}) collective-permute-start(bf16[64,1024]{1,0:T(8,128)(2,1)S(1)} %collective-permute-done.31.refs_3_), channel_id=1, source_target_pairs={{0,2},{2,0},{4,6},{6,4},{8,10},{10,8},{12,14},{14,12},{1,3},{3,1},... | collective-permute-start | bytes 393224 | tf_op jit(solution)/shard_map/attn3_y/ppermute | solution.py:287
  124.4 5.7 %collective-permute-start.36 = (bf16[128,1024]{1,0:T(8,128)(2,1)S(1)}, bf16[128,1024]{1,0:T(8,128)(2,1)S(1)}, u32[]{:S(2)}, u32[]{:S(2)}) collective-permute-start(bf16[128,1024]{1,0:T(8,128)(2,1)S(1)} %get-tuple-element.82), channel_id=1, source_target_pairs={{0,1},{1,0},{2,3},{3,2},{4,5},{5,4},{6,7},{7,6},{8,9},{9,8},{10,11... | collective-permute-start | bytes 786440 | tf_op jit(solution)/shard_map/proj_core/ppermute | solution.py:291

commit v4 on v3

v4 whole, which is shorter than its diff:
```python
import functools
import math

import jax
import jax.numpy as jnp
from jax import lax
from jax.experimental import pallas as pl
from jax.experimental.pallas import tpu as pltpu
from jax.sharding import PartitionSpec as P

HD = 128
F32 = jnp.float32
BF16 = jnp.bfloat16
VMEM_BYTES = 20 * 1024 * 1024
PARAMS = pltpu.CompilerParams(vmem_limit_bytes=VMEM_BYTES)
BIG = pltpu.CompilerParams(vmem_limit_bytes=52 * 1024 * 1024)
WHOLE = pl.BlockSpec(memory_space=pltpu.VMEM)
FREE = pl.BlockSpec(memory_space=pltpu.HBM)


def dot(a, b):
    return jnp.dot(a, b, preferred_element_type=F32)


def dot_nt(a, b):
    return lax.dot_general(a, b, (((1,), (1,)), ((), ())), preferred_element_type=F32)


def share_kernel(flips, half_lines, image, *refs):
    par, core, y = lax.axis_index("groups") % 2, lax.axis_index("heads"), lax.axis_index("blk") % 2
    n = len(flips)
    n_weights = (len(refs) - n - 1) // 2
    weights, outs, sems = refs[:n_weights], refs[n_weights:-1], refs[-1]
    copies = []
    for weight, own in zip(weights, outs[n:]):
        half = own.shape[0]
        copies.append((weight.at[pl.ds(pl.multiple_of(par * half, half), half), :], own))
    for (flip_x, flip_y), out in zip(flips, outs):
        half = out.shape[1] // half_lines
        to_par = 1 - par if flip_x else par
        to_y = 1 - y if flip_y else y
        for l in range(half_lines):
            at = pl.multiple_of(((2 * (core * half_lines + l) + to_y) * 2 + to_par) * half, half)
            copies.append((image.at[:, pl.ds(at, half)], out.at[:, pl.ds(l * half, half)]))
    copies = [pltpu.make_async_copy(src, dst, sems.at[i]) for i, (src, dst) in enumerate(copies)]
    for c in copies:
        c.start()
    for c in copies:
        c.wait()


def load_shards(first, sources, idx_ref, image, got, weights, x_ref, w_ref, sems):
    par, core, y, inner = idx_ref[0], idx_ref[1], idx_ref[2], idx_ref[3]
    rows = image.shape[0]
    half = x_ref.shape[2]
    half_lines = got[0].shape[1] // half
    cols = weights[0].shape[1]

    def copy(src, dst, k, i):
        return pltpu.make_async_copy(src, dst, sems.at[k, i])

    waits = []
    for k, projections in enumerate(sources):
        line = idx_ref[4 + first + k]
        own_at = pl.multiple_of(((2 * line + y) * 2 + par) * half, half)
        here = line // half_lines == core
        got_at = pl.multiple_of(lax.rem(line, half_lines) * half, half)
        own = copy(image.at[:, pl.ds(own_at, half)], x_ref.at[k, pl.ds(0, rows), :], k, 0)
        own.start()

        def from_core(which, k=k, got_at=got_at):
            return [
                copy(
                    got[2 * i + which].at[:, pl.ds(got_at, half)],
                    x_ref.at[k, pl.ds((i + 1) * rows, rows), :],
                    k,
                    1 + i,
                )
                for i in range(3)
            ]

        mine = from_core(0)

        @pl.when(here)
        def _(mine=mine):
            for c in mine:
                c.start()

        @pl.when(jnp.logical_not(here))
        def _(from_core=from_core):
            for c in from_core(1):
                c.start()

        waits.append([own] + mine)
        for p, (in_src, out_src) in enumerate(projections):

            def from_weight(src, k=k, p=p):
                return copy(
                    weights[src[0]].at[pl.ds(src[1], half), :], w_ref.at[k, :, pl.ds(p * cols, cols)], k, 4 + p
                )

            weight = from_weight(in_src)
            if in_src == out_src:
                weight.start()
            else:

                @pl.when(inner > 0)
                def _(weight=weight):
                    weight.start()

                @pl.when(inner <= 0)
                def _(from_weight=from_weight, out_src=out_src):
                    from_weight(out_src).start()

            waits[-1].append(weight)
    return waits


def project_kernel(sources, extra, idx_ref, slots, image, *refs):
    got, weights = refs[:6], refs[6:-8]
    (keep, to_y, to_x, to_both), (x_ref, w_ref, acc_ref, sems) = refs[-8:-4], refs[-4:]
    y = idx_ref[2]
    rows = image.shape[0]
    cols = keep.shape[1]
    kind = to_y.dtype
    waits = load_shards(0, tuple((s,) for s in sources), idx_ref, image, got, weights, x_ref, w_ref, sems)
    for k, copies in enumerate(waits):
        for c in copies:
            c.wait()
        part = dot(x_ref[k], w_ref[k])
        if k == 0:
            acc_ref[...] = part
        elif k < len(waits) - 1:
            acc_ref[...] += part
    total = acc_ref[...] + part
    low = y == 0
    mine = jnp.where(low, total[:, :cols], total[:, cols:])
    other = jnp.where(low, total[:, cols:], total[:, :cols]).astype(kind)
    keep[...] = mine[: 2 * rows]
    to_y[:rows, :] = other[rows : 2 * rows]
    to_y[rows : 2 * rows, :] = other[:rows]
    to_x[...] = mine[2 * rows :].astype(kind)
    to_both[:rows, :] = other[3 * rows :]
    to_both[rows:, :] = other[2 * rows : 3 * rows]
    if extra:
        n = slots.shape[0]
        to_y[2 * rows : 2 * rows + n, :HD] = slots[...]
        to_y[2 * rows + n :, :] = jnp.zeros((extra - n, cols), kind)
        if cols > HD:
            to_y[2 * rows : 2 * rows + n, HD:] = jnp.zeros((n, cols - HD), kind)


def key_kernel(keep, got_y, got_x, got_both, gain, slots, out):
    rows = keep.shape[0]
    n = slots.shape[0]
    raw = (keep[...] + got_y[:rows, :]) + (got_x[...] + got_both[...])
    for c in range(0, raw.shape[1], HD):
        part = raw[:, c : c + HD]
        scale = lax.rsqrt(jnp.mean(part * part, axis=-1, keepdims=True) + 1e-05)
        out[:rows, c : c + HD] = (part * scale * gain[...]).astype(BF16)
    pad = jnp.zeros((out.shape[0] - rows - 2 * n, HD), F32)
    out[rows:, :HD] = jnp.concatenate([slots[...], got_y[rows : rows + n, :HD], pad], 0).astype(BF16)


def score_kernel(n, heads, limit_ref, keys_ref, *refs):
    queries = refs[:n]
    expo_ref, figures_ref, q_ref = refs[n:]
    rows = queries[0].shape[0]
    tokens = expo_ref.shape[1]
    scale = 1.0 / math.sqrt(HD)
    slots = keys_ref[tokens : tokens + 16 * (-(-tokens // HD) // 16 + (-(-tokens // HD) % 16 > 0)), :].astype(F32)
    lane = lax.broadcasted_iota(jnp.int32, (rows, HD), 1)
    for i in range(n):
        limit = limit_ref[i * rows : (i + 1) * rows, :]
        seen = []
        for c in range(tokens // HD):
            slot = slots[c : c + 1, :]
            seen.append(jnp.where((slot >= 0.0) & (slot <= limit), 1.0, 0.0))
        seen = jnp.concatenate(seen, 1)
        for j in range(heads):
            q_ref[j * rows : (j + 1) * rows, :] = queries[i][:, j * HD : (j + 1) * HD]
        s = dot_nt(q_ref[...], keys_ref[:tokens, :]) * scale
        s = jnp.where(seen[None] > 0.5, s.reshape(heads, rows, tokens), -1e30).reshape(heads * rows, tokens)
        top = jnp.max(s, axis=1, keepdims=True).astype(BF16).astype(F32)
        e = jnp.where(s > -1e29, jnp.exp(s - top), 0.0)
        total = jnp.sum(e, axis=1, keepdims=True)
        expo_ref[i * heads * rows : (i + 1) * heads * rows, :] = e.astype(BF16)
        high = total.astype(BF16).astype(F32)
        figures = jnp.zeros((rows, HD), F32)
        for j in range(heads):
            part = slice(j * rows, (j + 1) * rows)
            figures = jnp.where(lane == j, top[part], figures)
            figures = jnp.where(lane == heads + j, high[part], figures)
            figures = jnp.where(lane == 2 * heads + j, total[part] - high[part], figures)
        figures_ref[i * rows : (i + 1) * rows, :] = figures.astype(BF16)


def value_kernel(n, heads, expo_ref, figures_ref, values_ref, *outs):
    rows = figures_ref.shape[0] // n
    for i in range(n):
        acc = dot(expo_ref[i * heads * rows : (i + 1) * heads * rows, :], values_ref[...]).astype(BF16)
        for j in range(heads):
            outs[i][:, j * HD : (j + 1) * HD] = acc[j * rows : (j + 1) * rows, :]
        outs[i][:, heads * HD :] = figures_ref[i * rows : (i + 1) * rows, :]


def combine_kernel(n, heads, *refs):
    parts, out_ref = refs[:n], refs[n]
    rows = out_ref.shape[0]
    lane = lax.broadcasted_iota(jnp.int32, (rows, HD), 1)
    figures = [part[:, heads * HD :].astype(F32) for part in parts]

    def column(figure, at):
        return jnp.sum(jnp.where(lane == at, figure, 0.0), axis=1, keepdims=True)

    for j in range(heads):
        tops = [column(f, j) for f in figures]
        top = functools.reduce(jnp.maximum, tops)
        total = jnp.zeros((rows, 1), F32)
        acc = jnp.zeros((rows, HD), F32)
        for part, figure, own_top in zip(parts, figures, tops):
            weight = jnp.exp(own_top - top)
            total = total + weight * (column(figure, heads + j) + column(figure, 2 * heads + j))
            acc = acc + weight * part[:, j * HD : (j + 1) * HD].astype(F32)
        out_ref[:, j * HD : (j + 1) * HD] = (acc / total).astype(BF16)


def proj_kernel(n, idx_ref, *refs):
    pieces = refs[:n]
    w_ref, keep_ref, send_ref, a_ref, p_ref = refs[n:]
    rows, width = pieces[0].shape
    for k in range(n):
        at_row = pl.multiple_of(idx_ref[1 + 2 * k] * rows, rows)
        at_col = pl.multiple_of(idx_ref[2 + 2 * k] * width, width)
        a_ref[pl.ds(at_row, rows), pl.ds(at_col, width)] = pieces[k][...]
    p_ref[...] = dot(a_ref[...], w_ref[...])
    size = keep_ref.shape[0]
    core = idx_ref[0]
    keep_ref[...] = p_ref[pl.ds(pl.multiple_of(core * size, size), size), :]
    send_ref[...] = p_ref[pl.ds(pl.multiple_of((1 - core) * size, size), size), :].astype(BF16)


def body(
    image_feats,
    slot_image,
    key_weight,
    value_weight,
    key_gain,
    queries,
    text_image,
    text_hidden,
    out_weight,
    attn_gate,
):
    groups, nblk, cores = (lax.axis_size(a) for a in ("groups", "blk", "heads"))
    lines = nblk // 2
    tok = image_feats.shape[0]
    depth = key_weight.shape[0]
    kv_cols = key_weight.shape[1]
    mine_cols = kv_cols // 2
    text_rows = queries.shape[0]
    q_half = queries.shape[1] // 2
    per_kv = q_half // mine_cols
    grp, blk, core = (lax.axis_index(a) for a in ("groups", "blk", "heads"))
    par = grp % 2
    y = blk % 2
    line = blk // 2

    swap_y = [(b, b ^ 1) for b in range(nblk)]
    swap_core = [(c, c ^ 1) for c in range(cores)]
    half = depth // 2
    fast = lines == 4 and cores == 2 and kv_cols == 2 * HD

    def along(name, array, d, ok=lambda l: True):
        with jax.named_scope(f"{name}_z{d}"):
            return lax.ppermute(array, "blk", [(b, b ^ (2 * d)) for b in range(nblk) if ok(b // 2)])

    def over_y(name, array):
        with jax.named_scope(name + "_y"):
            return lax.ppermute(array, "blk", swap_y)

    def over_core(name, array):
        with jax.named_scope(name + "_core"):
            return lax.ppermute(array, "heads", swap_core)

    def over_x(name, array):
        with jax.named_scope(name + "_x"):
            return lax.ppermute(array, "groups", [(g, g ^ 1) for g in range(groups)])

    def over_both(name, array):
        pairs = [(g * nblk + b, (g ^ 1) * nblk + (b ^ 1)) for g in range(groups) for b in range(nblk)]
        with jax.named_scope(name + "_xy"):
            return lax.ppermute(array, ("groups", "blk"), pairs)

    def hold(*arrays):
        return lax.optimization_barrier(arrays)

    def take_y(array, size, which):
        return lax.dynamic_slice_in_dim(array, which * size, size, 1)

    def middle(l):
        return l in (1, 2)

    half_lines = lines // 2

    def share(to_x, to_y):
        return jnp.concatenate(
            [
                lax.dynamic_slice_in_dim(
                    image_feats, ((2 * (core * half_lines + l) + to_y) * 2 + to_x) * half, half, 1
                )
                for l in range(half_lines)
            ],
            1,
        )

    half_lines = lines // 2
    scalars = pl.BlockSpec(memory_space=pltpu.SMEM)
    share = jax.ShapeDtypeStruct((tok, half_lines * half), BF16)

    def shares(flips, *weights):
        out_shape = [share] * len(flips) + [jax.ShapeDtypeStruct((half, kv_cols), BF16)] * len(weights)
        return pl.pallas_call(
            functools.partial(share_kernel, flips, half_lines),
            out_shape=tuple(out_shape),
            in_specs=[FREE] + [FREE] * len(weights),
            out_specs=(WHOLE,) * len(out_shape),
            scratch_shapes=[pltpu.SemaphoreType.DMA((2 + len(flips) * half_lines,))],
            compiler_params=pltpu.CompilerParams(vmem_limit_bytes=56 * 1024 * 1024),
        )(image_feats, *weights)

    share_x, share_y, key_own = shares(((1, 0), (0, 1)), key_weight)
    share_both, value_own = shares(((1, 1),), value_weight)
    if fast:
        def devices(route):
            pairs = []
            for l in range(lines):
                for yy in range(2):
                    for c in range(cores):
                        to_l, to_y, to_c = route(l, yy, c)
                        pairs.append(((2 * l + yy) * cores + c, (2 * to_l + to_y) * cores + to_c))
            return pairs

        def to_head(name, tile):
            tiles = []
            for r in range(2):
                with jax.named_scope(name + "_head"):
                    tiles.append(
                        lax.ppermute(
                            tile, ("blk", "heads"), devices(lambda l, yy, c: (2 * c + yy, (l % 2) ^ r, l // 2))
                        )
                    )
            return tiles + [over_core(name + "_tile", t) for t in tiles]

        k1, km = along("wk", key_own, 1), along("wk", key_own, 3, middle)
        img_y, img_x = over_y("image", share_y), over_x("image", share_x)
        kb, ka = along("wk_across", k1, 3, middle), along("wk_out", km, 1, middle)
        kb, ka, img_y, img_x, share_both, value_own = hold(kb, ka, img_y, img_x, share_both, value_own)
        img_both = over_both("image", share_both)
        ke = along("wk_end", kb, 1, middle)
        v1, vm = along("wv", value_own, 1), along("wv", value_own, 3, middle)
        core_y, core_x = over_core("image", img_y), over_core("image", img_x)
        v1, vm, ke, img_both, core_y, core_x = hold(v1, vm, ke, img_both, core_y, core_x)
        core_both = over_core("image", img_both)
        vb, va = along("wv_across", v1, 3, middle), along("wv_out", vm, 1, middle)
        pass
        key_refs, value_refs = [key_own, k1, kb, ka, km, ke], [value_own, v1, vb, va, vm]
        pair = lambda i, o: ((i, 0), (o, 0))
        sources = (pair(0, 0), pair(1, 1), pair(2, 3), pair(4, 5))
    else:
        img_y, img_x, img_both = over_y("image", share_y), over_x("image", share_x), over_both("image", share_both)
        core_y, core_x, core_both = (over_core("image", i) for i in (img_y, img_x, img_both))
        key_refs = [key_own] + [along("wk", key_own, d) for d in range(1, lines)]
        value_refs = [value_own] + [along("wv", value_own, d) for d in range(1, lines)]
        sources = tuple(((d, 0), (d, 0)) for d in range(lines))
    pieces = [img_y, core_y, img_x, core_x, img_both, core_both]
    slots = slot_image.astype(F32).reshape(tok // HD, HD)
    extra = 8 * (-(-(tok // HD) // 8))

    idx = jnp.stack([par, core, y, ((line == 1) | (line == 2)).astype(jnp.int32)] + [line ^ d for d in range(lines)])
    macs = 4 * tok * half * kv_cols

    def project(weights, extra, kind):
        out = lambda rows, dtype: jax.ShapeDtypeStruct((rows, mine_cols), dtype)
        return pl.pallas_call(
            functools.partial(project_kernel, sources, extra),
            out_shape=(out(2 * tok, F32), out(2 * tok + extra, kind), out(2 * tok, kind), out(2 * tok, kind)),
            in_specs=[scalars, WHOLE] + [FREE] * (7 + len(weights)),
            out_specs=(WHOLE,) * 4,
            scratch_shapes=[
                pltpu.VMEM((lines, 4 * tok, half), BF16),
                pltpu.VMEM((lines, half, kv_cols), BF16),
                pltpu.VMEM((4 * tok, kv_cols), F32),
                pltpu.SemaphoreType.DMA((lines, 5)),
            ],
            compiler_params=BIG,
            cost_estimate=pl.CostEstimate(
                flops=2 * macs * lines, bytes_accessed=macs * lines // 32, transcendentals=0
            ),
        )(idx, slots, image_feats, *pieces, *weights)

    rows = 2 * text_rows
    q_mine, q_got = take_y(queries, q_half, y), over_y("q", take_y(queries, q_half, 1 - y))
    low_y = y == 0
    q_rows = jnp.concatenate([jnp.where(low_y, q_mine, q_got), jnp.where(low_y, q_got, q_mine)], 0)
    keep, to_y, to_x, to_both = project(key_refs, extra, F32)
    if fast:
        vb, to_y, to_x, to_both = hold(vb, to_y, to_x, to_both)
    key_parts = [over_y("key", to_y), over_x("key", to_x), over_both("key", to_both)]
    q_pieces = [q_rows if d == 0 else along("q", q_rows, d) for d in range(lines)]
    if fast:
        value_refs.append(along("wv_end", vb, 1, middle))
    slot_rows = 2 * tok // HD
    packed = pl.pallas_call(
        key_kernel,
        out_shape=jax.ShapeDtypeStruct((2 * tok + slot_rows + (-slot_rows % 16), mine_cols), BF16),
        in_specs=[WHOLE] * 6,
        out_specs=WHOLE,
        compiler_params=PARAMS,
    )(keep, *key_parts, key_gain.reshape(1, HD), slots)

    keep, to_y, to_x, to_both = project(value_refs, 0, BF16)
    if fast:
        to_y, to_x, to_both, *q_pieces = hold(to_y, to_x, to_both, *q_pieces)
    value_parts = [over_y("value", to_y), over_x("value", to_x), over_both("value", to_both)]
    limits = text_image.astype(F32).reshape(lines, rows)
    limits = jnp.concatenate([lax.dynamic_slice_in_dim(limits, line ^ d, 1, 0) for d in range(lines)], 0)
    limits = limits.reshape(lines * rows, 1)
    all_rows = lines * rows * per_kv
    expo, figures = pl.pallas_call(
        functools.partial(score_kernel, lines, per_kv),
        out_shape=(
            jax.ShapeDtypeStruct((all_rows, 2 * tok), BF16),
            jax.ShapeDtypeStruct((lines * rows, HD), BF16),
        ),
        in_specs=[WHOLE] * (2 + lines),
        out_specs=(WHOLE, WHOLE),
        scratch_shapes=[pltpu.VMEM((per_kv * rows, HD), BF16)],
        compiler_params=PARAMS,
    )(limits, packed, *q_pieces)
    value_y, value_x, value_both = (part.astype(F32) for part in value_parts)
    values = ((keep + value_y) + (value_x + value_both)).astype(BF16)
    sums = pl.pallas_call(
        functools.partial(value_kernel, lines, per_kv),
        out_shape=(jax.ShapeDtypeStruct((rows, q_half + HD), BF16),) * lines,
        in_specs=[WHOLE] * 3,
        out_specs=(WHOLE,) * lines,
        compiler_params=PARAMS,
    )(expo, figures, values)
    sums = [sums[0]] + [along("sums", sums[d], d) for d in range(1, lines)]
    attn = pl.pallas_call(
        functools.partial(combine_kernel, lines, per_kv),
        out_shape=jax.ShapeDtypeStruct((rows, q_half), BF16),
        in_specs=[WHOLE] * lines,
        out_specs=WHOLE,
        compiler_params=PARAMS,
    )(*sums)
    mine = [attn if d == 0 else along("attn", attn, d) for d in range(lines)]
    where = [(line ^ d, y) for d in range(lines)] + [(line ^ d, 1 - y) for d in range(lines)]
    other = [over_y(f"attn{d}", m) for d, m in enumerate(mine)]

    out_rows = lines * rows
    out_cols = out_weight.shape[1]
    keep, send = pl.pallas_call(
        functools.partial(proj_kernel, 2 * lines),
        out_shape=(
            jax.ShapeDtypeStruct((out_rows // 2, out_cols), F32),
            jax.ShapeDtypeStruct((out_rows // 2, out_cols), BF16),
        ),
        in_specs=[scalars] + [WHOLE] * (2 * lines + 1),
        out_specs=(WHOLE, WHOLE),
        scratch_shapes=[pltpu.VMEM((out_rows, 2 * q_half), BF16), pltpu.VMEM((out_rows, out_cols), F32)],
        compiler_params=PARAMS,
    )(jnp.stack([core] + [i for pair in where for i in pair]), *mine, *other, out_weight)
    head_total = keep + over_core("proj", send).astype(F32)
    return (text_hidden.astype(F32) + jnp.tanh(attn_gate[0]) * head_total).astype(BF16)


def solution(mesh):
    placed = (
        P(("groups", "blk"), None),
        P(("groups", "blk")),
        P("blk", "heads"),
        P("blk", "heads"),
        P(),
        P(("groups", "blk"), "heads"),
        P("groups"),
        P(("groups", "heads"), "blk"),
        P("heads", "blk"),
        P(),
    )
    return jax.shard_map(
        body, mesh=mesh, in_specs=placed, out_specs=P(("groups", "heads"), "blk"), check_vma=False
    )
```

time: 131 us -> 127 us (0.969)
  starting transfers between devices: 52.1 us -> 44.8 us
  waiting for transfers between devices: 50.7 us -> 56 us
  Pallas kernels: 24.3 us -> 20.6 us
  local copies, waits for them, and re-layouts: 1.08 us -> 3.36 us
    ppermute x10 -> x0, starting transfers between devices: 24 us -> none  [the longest x4 13 us: to_head(): lax.ppermute(tile, ('blk', 'heads'), devices(lambda l, yy, c: (2 * c + yy...]
    ppermute x6 -> x19, starting transfers between devices: 8.32 us -> 25.6 us  [along(): lax.ppermute(array, 'blk', [(b, b ^ 2 * d) for b in range(nblk) if ok(b /...]
    ppermute x6 -> x19, waiting for transfers between devices: 25.7 us -> 42.5 us  [along(): lax.ppermute(array, 'blk', [(b, b ^ 2 * d) for b in range(nblk) if ok(b /...]
    ppermute x10 -> x0, waiting for transfers between devices: 15.3 us -> none  [the longest x4 9.04 us: to_head(): lax.ppermute(tile, ('blk', 'heads'), devices(lambda l, yy, c: (2 * c + yy...]
    ppermute x8 -> x4, starting transfers between devices: 5.67 us -> 0.58 us  [over_core(): return lax.ppermute(array, 'heads', swap_core)]
    ppermute x7 -> x8, starting transfers between devices: 7.14 us -> 10.1 us  [over_y(): return lax.ppermute(array, 'blk', swap_y)]
    ppermute x7 -> x8, waiting for transfers between devices: 8.02 us -> 10.9 us  [over_y(): return lax.ppermute(array, 'blk', swap_y)]
    pallas_call x1, Pallas kernels: 4.83 us -> 1.92 us  [body(): pl.pallas_call(functools.partial(proj_kernel, 2 * lines), out_shape=(jax....]
  transfers between devices with their start and end apart: 37 -> 37, of which waited for: 14 -> 16; matrix products, arithmetic and copies ran while one was open for 1% -> 0% of each run, Pallas kernels for 12% -> 12%
where the time goes in v4:
time: 127 us
  waiting for transfers between devices  56 us (44%)
  starting transfers between devices  44.8 us (35%)
  Pallas kernels  20.6 us (16%)
  local copies, waits for them, and re-layouts  3.36 us (3%)
    ppermute x19, waiting for transfers between devices, along(): lax.ppermute(array, 'blk', [(b, b ^ 2 * d) for b in range(nblk) if ok(b /...  42.5 us
    ppermute x19, starting transfers between devices, along(): lax.ppermute(array, 'blk', [(b, b ^ 2 * d) for b in range(nblk) if ok(b /...  25.6 us
    ppermute x8, waiting for transfers between devices, over_y(): return lax.ppermute(array, 'blk', swap_y)  10.9 us
    pallas_call x2, Pallas kernels, project(): pl.pallas_call(functools.partial(project_kernel, sources, extra), out_sha...  10.4 us
    ppermute x8, starting transfers between devices, over_y(): return lax.ppermute(array, 'blk', swap_y)  10.1 us
    ppermute x3, starting transfers between devices, over_both(): return lax.ppermute(array, ('groups', 'blk'), pairs)  4.98 us
    pallas_call x2, Pallas kernels, shares(): pl.pallas_call(functools.partial(share_kernel, flips, half_lines), out_sh...  4.44 us
    ppermute x3, starting transfers between devices, over_x(): return lax.ppermute(array, 'groups', [(g, g ^ 1) for g in range(groups)])  3.5 us
  transfers between devices with their start and end apart: 37, of which 16 were waited for; matrix products, arithmetic and copies ran while one was open for 0% of the time, Pallas kernels for 12%

profile of v4, /device:TPU:0, one launch (start us, length us, event | category | flops | bytes accessed | tf_op | source)
XLA Modules:
  0.0 126.6 jit_solution(3601495260765821550)
XLA Ops:
  0.0 2.4 %shard_map.100 = (bf16[256,1024]{1,0:T(8,128)(2,1)}, bf16[256,1024]{1,0:T(8,128)(2,1)}, bf16[512,256]{1,0:T(8,128)(2,1)}) custom-call(bf16[256,8192]{1,0:T(8,128)(2,1)} %image.7, bf16[1024,256]{1,0:T(8,128)(2,1)} %refs_0_.2), custom_call_target="tpu_custom_call" | custom-call | tf_op jit(solution)/shard_map/pallas_call | solution.py:323
  2.4 3.1 %collective-permute-start = (bf16[512,256]{1,0:T(8,128)(2,1)}, bf16[512,256]{1,0:T(8,128)(2,1)S(1)}, u32[]{:S(2)}, u32[]{:S(2)}) collective-permute-start(bf16[512,256]{1,0:T(8,128)(2,1)} %get-tuple-element.49.refs_6_), channel_id=1, source_target_pairs={{0,4},{2,6},{4,0},{6,2},{8,12},{10,14},{12,8},{14,10},{1,5},{3,7},... | collective-permute-start | bytes 786440 | tf_op jit(solution)/shard_map/wk_z1/ppermute | solution.py:276
  5.5 0.7 collective-permute-start.2
  6.2 1.6 %collective-permute-start.4 = (bf16[256,1024]{1,0:T(8,128)(2,1)}, bf16[256,1024]{1,0:T(8,128)(2,1)S(1)}, u32[]{:S(2)}, u32[]{:S(2)}) collective-permute-start(bf16[256,1024]{1,0:T(8,128)(2,1)} %get-tuple-element.50), channel_id=1, source_target_pairs={{0,2},{2,0},{4,6},{6,4},{8,10},{10,8},{12,14},{14,12},{1,3},{3,1},... | collective-permute-start | bytes 1572872 | tf_op jit(solution)/shard_map/image_y/ppermute | solution.py:280
  7.8 1.5 %collective-permute-start.5 = (bf16[256,1024]{1,0:T(8,128)(2,1)}, bf16[256,1024]{1,0:T(8,128)(2,1)S(1)}, u32[]{:S(2)}, u32[]{:S(2)}) collective-permute-start(bf16[256,1024]{1,0:T(8,128)(2,1)} %get-tuple-element.51), channel_id=1, source_target_pairs={{0,16},{16,0},{1,17},{17,1},{2,18},{18,2},{3,19},{19,3},{4,20},{20... | collective-permute-start | bytes 1572872 | tf_op jit(solution)/shard_map/image_x/ppermute | solution.py:288
  9.3 2.8 %collective-permute-done.refs_7_ = bf16[512,256]{1,0:T(8,128)(2,1)S(1)} collective-permute-done((bf16[512,256]{1,0:T(8,128)(2,1)}, bf16[512,256]{1,0:T(8,128)(2,1)S(1)}, u32[]{:S(2)}, u32[]{:S(2)}) %collective-permute-start) | collective-permute-done | bytes 262176 | tf_op jit(solution)/shard_map/wk_z1/ppermute | solution.py:276
  12.0 0.7 collective-permute-start.1
  12.7 1.3 %collective-permute-start.3 = (bf16[512,256]{1,0:T(8,128)(2,1)S(1)}, bf16[512,256]{1,0:T(8,128)(2,1)S(1)}, u32[]{:S(2)}, u32[]{:S(2)}) collective-permute-start(bf16[512,256]{1,0:T(8,128)(2,1)S(1)} %collective-permute-done.2.refs_10_), channel_id=1, source_target_pairs={{4,0},{6,2},{8,12},{10,14},{5,1},{7,3},{9,13},{11,15},{20,16},{22,... | collective-permute-start | bytes 786440 | tf_op jit(solution)/shard_map/wk_out_z1/ppermute | solution.py:276
  14.0 2.0 %shard_map.101 = (bf16[256,1024]{1,0:T(8,128)(2,1)}, bf16[512,256]{1,0:T(8,128)(2,1)}) custom-call(bf16[256,8192]{1,0:T(8,128)(2,1)} %image.7, bf16[1024,256]{1,0:T(8,128)(2,1)} %refs_0_.3), custom_call_target="tpu_custom_call" | custom-call | tf_op jit(solution)/shard_map/pallas_call | solution.py:323
  16.1 7.6 %collective-permute-done.3.refs_9_ = bf16[512,256]{1,0:T(8,128)(2,1)S(1)} collective-permute-done((bf16[512,256]{1,0:T(8,128)(2,1)S(1)}, bf16[512,256]{1,0:T(8,128)(2,1)S(1)}, u32[]{:S(2)}, u32[]{:S(2)}) %collective-permute-start.3) | collective-permute-done | bytes 262176 | tf_op jit(solution)/shard_map/wk_out_z1/ppermute | solution.py:276
  23.7 1.5 %collective-permute-start.6 = (bf16[512,256]{1,0:T(8,128)(2,1)}, bf16[512,256]{1,0:T(8,128)(2,1)S(1)}, u32[]{:S(2)}, u32[]{:S(2)}) collective-permute-start(bf16[512,256]{1,0:T(8,128)(2,1)} %get-tuple-element.55.refs_6_), channel_id=1, source_target_pairs={{0,4},{2,6},{4,0},{6,2},{8,12},{10,14},{12,8},{14,10},{1,5},{3,7},... | collective-permute-start | bytes 786440 | tf_op jit(solution)/shard_map/wv_z1/ppermute | solution.py:276
  25.2 0.5 collective-permute-start.11
  25.7 1.4 %collective-permute-start.9 = (bf16[256,1024]{1,0:T(8,128)(2,1)}, bf16[256,1024]{1,0:T(8,128)(2,1)}, u32[]{:S(2)}, u32[]{:S(2)}) collective-permute-start(bf16[256,1024]{1,0:T(8,128)(2,1)} %get-tuple-element.57), channel_id=1, source_target_pairs={{0,18},{2,16},{4,22},{6,20},{8,26},{10,24},{12,30},{14,28},{16,2},... | collective-permute-start | bytes 1572872 | tf_op jit(solution)/shard_map/image_xy/ppermute | solution.py:293
  27.2 0.7 collective-permute-start.7
  27.8 2.6 %collective-permute-done.6.refs_7_ = bf16[512,256]{1,0:T(8,128)(2,1)S(1)} collective-permute-done((bf16[512,256]{1,0:T(8,128)(2,1)}, bf16[512,256]{1,0:T(8,128)(2,1)S(1)}, u32[]{:S(2)}, u32[]{:S(2)}) %collective-permute-start.6) | collective-permute-done | bytes 262176 | tf_op jit(solution)/shard_map/wv_z1/ppermute | solution.py:276
  30.4 1.3 %collective-permute-start.8 = (bf16[512,256]{1,0:T(8,128)(2,1)S(1)}, bf16[512,256]{1,0:T(8,128)(2,1)S(1)}, u32[]{:S(2)}, u32[]{:S(2)}) collective-permute-start(bf16[512,256]{1,0:T(8,128)(2,1)S(1)} %collective-permute-done.1.refs_8_), channel_id=1, source_target_pairs={{4,0},{6,2},{8,12},{10,14},{5,1},{7,3},{9,13},{11,15},{20,16},{22,... | collective-permute-start | bytes 786440 | tf_op jit(solution)/shard_map/wk_end_z1/ppermute | solution.py:276
  31.7 7.4 %collective-permute-done.8.refs_11_ = bf16[512,256]{1,0:T(8,128)(2,1)S(1)} collective-permute-done((bf16[512,256]{1,0:T(8,128)(2,1)S(1)}, bf16[512,256]{1,0:T(8,128)(2,1)S(1)}, u32[]{:S(2)}, u32[]{:S(2)}) %collective-permute-start.8) | collective-permute-done | bytes 262176 | tf_op jit(solution)/shard_map/wk_end_z1/ppermute | solution.py:276
  39.1 1.7 %collective-permute-done.9.refs_4_ = bf16[256,1024]{1,0:T(8,128)(2,1)} collective-permute-done((bf16[256,1024]{1,0:T(8,128)(2,1)}, bf16[256,1024]{1,0:T(8,128)(2,1)}, u32[]{:S(2)}, u32[]{:S(2)}) %collective-permute-start.9) | collective-permute-done | bytes 524320 | tf_op jit(solution)/shard_map/image_xy/ppermute | solution.py:293
  40.8 0.6 collective-permute-start.19
  41.4 0.1 stack.63.idx_ref
  41.4 0.7 collective-permute-start.13
  42.1 3.2 %collective-permute-done.19 = bf16[32,1024]{1,0:T(8,128)(2,1)S(1)} collective-permute-done((bf16[32,1024]{1,0:T(8,128)(2,1)S(1)}, bf16[32,1024]{1,0:T(8,128)(2,1)S(1)}, u32[]{:S(2)}, u32[]{:S(2)}) %collective-permute-start.19) | collective-permute-done | bytes 65568 | tf_op jit(solution)/shard_map/q_y/ppermute | solution.py:280
  45.4 1.4 %collective-permute-start.17 = (bf16[512,256]{1,0:T(8,128)(2,1)S(1)}, bf16[512,256]{1,0:T(8,128)(2,1)S(1)}, u32[]{:S(2)}, u32[]{:S(2)}) collective-permute-start(bf16[512,256]{1,0:T(8,128)(2,1)S(1)} %collective-permute-done.7.refs_10_), channel_id=1, source_target_pairs={{4,0},{6,2},{8,12},{10,14},{5,1},{7,3},{9,13},{11,15},{20,16},{22,... | collective-permute-start | bytes 786440 | tf_op jit(solution)/shard_map/wv_out_z1/ppermute | solution.py:276
  46.9 5.2 %shard_map.102 = (f32[512,128]{1,0:T(8,128)S(1)}, f32[520,128]{1,0:T(8,128)}, f32[512,128]{1,0:T(8,128)}, f32[512,128]{1,0:T(8,128)S(1)}) custom-call(s32[8]{0:T(128)S(1)} %stack.63.idx_ref, f32[2,128]{1,0:T(2,128)S(1)} %convert_bitcast_fusion.slots, bf16[256,8192]{1,0:T(8,128)(2,1)} %image.7, bf16[256,1024]{1,0:T(8,128)(2,1)} %copy-done.4, ...), custom_call_target="tpu_custom_call" | custom-call | flops 1073741824 | bytes 16777216 | tf_op jit(solution)/shard_map/pallas_call | solution.py:385
  52.1 1.3 %collective-permute-start.18 = (bf16[512,256]{1,0:T(8,128)(2,1)S(1)}, bf16[512,256]{1,0:T(8,128)(2,1)S(1)}, u32[]{:S(2)}, u32[]{:S(2)}) collective-permute-start(bf16[512,256]{1,0:T(8,128)(2,1)S(1)} %collective-permute-done.13.refs_8_), channel_id=1, source_target_pairs={{4,0},{6,2},{8,12},{10,14},{5,1},{7,3},{9,13},{11,15},{20,16},{22,... | collective-permute-start | bytes 786440 | tf_op jit(solution)/shard_map/wv_end_z1/ppermute | solution.py:276
  53.4 2.7 %collective-permute-start.20 = (bf16[64,1024]{1,0:T(8,128)(2,1)S(1)}, bf16[64,1024]{1,0:T(8,128)(2,1)S(1)}, u32[]{:S(2)}, u32[]{:S(2)}) collective-permute-start(bf16[64,1024]{1,0:T(8,128)(2,1)S(1)} %pad_maximum_fusion.refs_0_), channel_id=1, source_target_pairs={{0,4},{2,6},{4,0},{6,2},{8,12},{10,14},{12,8},{14,10},{1,5},{3,7},... | collective-permute-start | bytes 393224 | tf_op jit(solution)/shard_map/q_z1/ppermute | solution.py:276
  56.1 1.5 %collective-permute-start.15 = (f32[512,128]{1,0:T(8,128)}, f32[512,128]{1,0:T(8,128)S(1)}, u32[]{:S(2)}, u32[]{:S(2)}) collective-permute-start(f32[512,128]{1,0:T(8,128)} %get-tuple-element.70), channel_id=1, source_target_pairs={{0,16},{16,0},{1,17},{17,1},{2,18},{18,2},{3,19},{19,3},{4,20},{20... | collective-permute-start | bytes 786440 | tf_op jit(solution)/shard_map/key_x/ppermute | solution.py:288
  57.6 9.9 %collective-permute-done.20.refs_1_ = bf16[64,1024]{1,0:T(8,128)(2,1)S(1)} collective-permute-done((bf16[64,1024]{1,0:T(8,128)(2,1)S(1)}, bf16[64,1024]{1,0:T(8,128)(2,1)S(1)}, u32[]{:S(2)}, u32[]{:S(2)}) %collective-permute-start.20) | collective-permute-done | bytes 131104 | tf_op jit(solution)/shard_map/q_z1/ppermute | solution.py:276
  67.5 1.2 collective-permute-start.22
  68.7 0.1 reshape.13
  68.8 1.2 collective-permute-start.14
  70.0 0.7 copy-done.9
  70.7 1.8 %collective-permute-start.16 = (f32[512,128]{1,0:T(8,128)S(1)}, f32[512,128]{1,0:T(8,128)S(1)}, u32[]{:S(2)}, u32[]{:S(2)}) collective-permute-start(f32[512,128]{1,0:T(8,128)S(1)} %get-tuple-element.71), channel_id=1, source_target_pairs={{0,18},{2,16},{4,22},{6,20},{8,26},{10,24},{12,30},{14,28},{16,2},... | collective-permute-start | bytes 786440 | tf_op jit(solution)/shard_map/key_xy/ppermute | solution.py:293
  72.5 5.2 %shard_map.104 = (f32[512,128]{1,0:T(8,128)S(1)}, bf16[512,128]{1,0:T(8,128)(2,1)}, bf16[512,128]{1,0:T(8,128)(2,1)}, bf16[512,128]{1,0:T(8,128)(2,1)}) custom-call(s32[8]{0:T(128)S(1)} %stack.63.idx_ref, f32[2,128]{1,0:T(2,128)S(1)} %convert_bitcast_fusion.slots, bf16[256,8192]{1,0:T(8,128)(2,1)} %image.7, bf16[256,1024]{1,0:T(8,128)(2,1)} %copy-done.4, ...), custom_call_target="tpu_custom_call" | custom-call | flops 1073741824 | bytes 16777216 | tf_op jit(solution)/shard_map/pallas_call | solution.py:385
  77.7 1.3 collective-permute-start.23
  79.0 0.5 collective-permute-start.24
  79.5 1.8 %collective-permute-start.25 = (bf16[512,128]{1,0:T(8,128)(2,1)}, bf16[512,128]{1,0:T(8,128)(2,1)S(1)}, u32[]{:S(2)}, u32[]{:S(2)}) collective-permute-start(bf16[512,128]{1,0:T(8,128)(2,1)} %get-tuple-element.86), channel_id=1, source_target_pairs={{0,18},{2,16},{4,22},{6,20},{8,26},{10,24},{12,30},{14,28},{16,2},... | collective-permute-start | bytes 393224 | tf_op jit(solution)/shard_map/value_xy/ppermute | solution.py:293
  81.3 0.1 reshape.18.limit_ref
  81.5 2.9 %collective-permute-done.14.got_y = f32[520,128]{1,0:T(8,128)S(1)} collective-permute-done((f32[520,128]{1,0:T(8,128)}, f32[520,128]{1,0:T(8,128)S(1)}, u32[]{:S(2)}, u32[]{:S(2)}) %collective-permute-start.14) | collective-permute-done | bytes 266272 | tf_op jit(solution)/shard_map/key_y/ppermute | solution.py:280
  84.3 0.2 shard_map.103.keys_ref
  84.5 2.0 %shard_map.105 = (bf16[2048,512]{1,0:T(8,128)(2,1)S(1)}, bf16[256,128]{1,0:T(8,128)(2,1)S(1)}) custom-call(f32[256,1]{1,0:T(8,128)S(1)} %reshape.18.limit_ref, bf16[528,128]{1,0:T(8,128)(2,1)S(1)} %shard_map.103.keys_ref, bf16[64,1024]{1,0:T(8,128)(2,1)S(1)} %pad_maximum_fusion.refs_0_, bf16[64,1024]{1,0:T(8,128)(2,1)S(1)} %collective-permute-done.20.refs_1_, ...), custom_call_target="tpu_custom_call" | custom-call | tf_op jit(solution)/shard_map/pallas_call | solution.py:430
  86.6 0.6 collective-permute-done.23
  87.2 0.7 shard_map.106
  88.0 3.2 %collective-permute-start.27 = (bf16[64,1152]{1,0:T(8,128)(2,1)S(1)}, bf16[64,1152]{1,0:T(8,128)(2,1)S(1)}, u32[]{:S(2)}, u32[]{:S(2)}) collective-permute-start(bf16[64,1152]{1,0:T(8,128)(2,1)S(1)} %get-tuple-element.89), channel_id=1, source_target_pairs={{0,8},{2,10},{4,12},{6,14},{8,0},{10,2},{12,4},{14,6},{1,9},{3,11}... | collective-permute-start | bytes 442376 | tf_op jit(solution)/shard_map/sums_z2/ppermute | solution.py:276
  91.2 1.2 collective-permute-start.28
  92.4 3.1 %collective-permute-done.26.refs_1_ = bf16[64,1152]{1,0:T(8,128)(2,1)S(1)} collective-permute-done((bf16[64,1152]{1,0:T(8,128)(2,1)S(1)}, bf16[64,1152]{1,0:T(8,128)(2,1)S(1)}, u32[]{:S(2)}, u32[]{:S(2)}) %collective-permute-start.26) | collective-permute-done | bytes 147488 | tf_op jit(solution)/shard_map/sums_z1/ppermute | solution.py:276
  95.5 4.2 %collective-permute-done.27.refs_2_ = bf16[64,1152]{1,0:T(8,128)(2,1)S(1)} collective-permute-done((bf16[64,1152]{1,0:T(8,128)(2,1)S(1)}, bf16[64,1152]{1,0:T(8,128)(2,1)S(1)}, u32[]{:S(2)}, u32[]{:S(2)}) %collective-permute-start.27) | collective-permute-done | bytes 147488 | tf_op jit(solution)/shard_map/sums_z2/ppermute | solution.py:276
  99.8 0.9 shard_map.107.refs_0_
  100.7 2.2 %collective-permute-start.29 = (bf16[64,1024]{1,0:T(8,128)(2,1)S(1)}, bf16[64,1024]{1,0:T(8,128)(2,1)S(1)}, u32[]{:S(2)}, u32[]{:S(2)}) collective-permute-start(bf16[64,1024]{1,0:T(8,128)(2,1)S(1)} %shard_map.107.refs_0_), channel_id=1, source_target_pairs={{0,4},{2,6},{4,0},{6,2},{8,12},{10,14},{12,8},{14,10},{1,5},{3,7},... | collective-permute-start | bytes 393224 | tf_op jit(solution)/shard_map/attn_z1/ppermute | solution.py:276
  102.9 1.1 collective-permute-start.30
  104.0 1.4 %collective-permute-start.31 = (bf16[64,1024]{1,0:T(8,128)(2,1)S(1)}, bf16[64,1024]{1,0:T(8,128)(2,1)S(1)}, u32[]{:S(2)}, u32[]{:S(2)}) collective-permute-start(bf16[64,1024]{1,0:T(8,128)(2,1)S(1)} %shard_map.107.refs_0_), channel_id=1, source_target_pairs={{0,12},{2,14},{4,8},{6,10},{8,4},{10,6},{12,0},{14,2},{1,13},{3,15... | collective-permute-start | bytes 393224 | tf_op jit(solution)/shard_map/attn_z3/ppermute | solution.py:276
  105.4 0.6 collective-permute-start.32
  106.0 0.6 collective-permute-done.29.refs_1_
  106.6 2.8 %collective-permute-start.33 = (bf16[64,1024]{1,0:T(8,128)(2,1)S(1)}, bf16[64,1024]{1,0:T(8,128)(2,1)S(1)}, u32[]{:S(2)}, u32[]{:S(2)}) collective-permute-start(bf16[64,1024]{1,0:T(8,128)(2,1)S(1)} %collective-permute-done.29.refs_1_), channel_id=1, source_target_pairs={{0,2},{2,0},{4,6},{6,4},{8,10},{10,8},{12,14},{14,12},{1,3},{3,1},... | collective-permute-start | bytes 393224 | tf_op jit(solution)/shard_map/attn1_y/ppermute | solution.py:280
  109.4 4.3 %collective-permute-done.30.refs_2_ = bf16[64,1024]{1,0:T(8,128)(2,1)S(1)} collective-permute-done((bf16[64,1024]{1,0:T(8,128)(2,1)S(1)}, bf16[64,1024]{1,0:T(8,128)(2,1)S(1)}, u32[]{:S(2)}, u32[]{:S(2)}) %collective-permute-start.30) | collective-permute-done | bytes 131104 | tf_op jit(solution)/shard_map/attn_z2/ppermute | solution.py:276
  113.7 0.3 collective-permute-start.34
  114.1 1.7 %collective-permute-start.35 = (bf16[64,1024]{1,0:T(8,128)(2,1)S(1)}, bf16[64,1024]{1,0:T(8,128)(2,1)S(1)}, u32[]{:S(2)}, u32[]{:S(2)}) collective-permute-start(bf16[64,1024]{1,0:T(8,128)(2,1)S(1)} %collective-permute-done.31.refs_3_), channel_id=1, source_target_pairs={{0,2},{2,0},{4,6},{6,4},{8,10},{10,8},{12,14},{14,12},{1,3},{3,1},... | collective-permute-start | bytes 393224 | tf_op jit(solution)/shard_map/attn3_y/ppermute | solution.py:280
  115.8 0.1 stack.59.idx_ref
  115.9 2.8 %collective-permute-done.34.refs_6_ = bf16[64,1024]{1,0:T(8,128)(2,1)S(1)} collective-permute-done((bf16[64,1024]{1,0:T(8,128)(2,1)S(1)}, bf16[64,1024]{1,0:T(8,128)(2,1)S(1)}, u32[]{:S(2)}, u32[]{:S(2)}) %collective-permute-start.34) | collective-permute-done | bytes 131104 | tf_op jit(solution)/shard_map/attn2_y/ppermute | solution.py:280
  118.7 1.4 %collective-permute-done.35.refs_7_ = bf16[64,1024]{1,0:T(8,128)(2,1)S(1)} collective-permute-done((bf16[64,1024]{1,0:T(8,128)(2,1)S(1)}, bf16[64,1024]{1,0:T(8,128)(2,1)S(1)}, u32[]{:S(2)}, u32[]{:S(2)}) %collective-permute-start.35) | collective-permute-done | bytes 131104 | tf_op jit(solution)/shard_map/attn3_y/ppermute | solution.py:280
  120.1 2.2 %copy-done = bf16[2048,1024]{1,0:T(8,128)(2,1)S(1)} copy-done((bf16[2048,1024]{1,0:T(8,128)(2,1)S(1)}, bf16[2048,1024]{1,0:T(8,128)(2,1)}, u32[]{:S(2)}) %copy-start) | copy-done | bytes 4194328
  122.3 1.9 %shard_map.108 = (f32[128,1024]{1,0:T(8,128)S(1)}, bf16[128,1024]{1,0:T(8,128)(2,1)S(1)}) custom-call(s32[17]{0:T(128)S(1)} %stack.59.idx_ref, bf16[64,1024]{1,0:T(8,128)(2,1)S(1)} %shard_map.107.refs_0_, bf16[64,1024]{1,0:T(8,128)(2,1)S(1)} %collective-permute-done.29.refs_1_, bf16[64,1024]{1,0:T(8,128)(2,1)S(1)} %collective-permute-done.30.refs_2_, ...), custom_call_target="tpu_custom_call" | custom-call | tf_op jit(solution)/shard_map/pallas_call | solution.py:464
  125.0 0.8 collective-permute-done.36
  125.8 0.8 add_convert_fusion
  (58 shorter events, 0.4 us)
Async XLA Ops:
  0.0 40.8 %copy-start.10 = (bf16[32,2048]{1,0:T(8,128)(2,1)S(1)}, bf16[32,2048]{1,0:T(8,128)(2,1)}, u32[]{:S(2)}) copy-start(bf16[32,2048]{1,0:T(8,128)(2,1)} %param.15) | copy-start | bytes 393220
  0.0 41.4 %copy-start.11 = (s32[256]{0:T(256)S(1)}, s32[256]{0:T(256)}, u32[]{:S(2)}) copy-start(s32[256]{0:T(256)} %param.11) | copy-start | bytes 3076
  2.4 44.4 %copy-start.2 = (bf16[512,256]{1,0:T(8,128)(2,1)S(1)}, bf16[512,256]{1,0:T(8,128)(2,1)}, u32[]{:S(2)}) copy-start(bf16[512,256]{1,0:T(8,128)(2,1)} %get-tuple-element.49.refs_6_) | copy-start | bytes 786436
  2.4 9.6 %collective-permute-start = (bf16[512,256]{1,0:T(8,128)(2,1)}, bf16[512,256]{1,0:T(8,128)(2,1)S(1)}, u32[]{:S(2)}, u32[]{:S(2)}) collective-permute-start(bf16[512,256]{1,0:T(8,128)(2,1)} %get-tuple-element.49.refs_6_), channel_id=1, source_target_pairs={{0,4},{2,6},{4,0},{6,2},{8,12},{10,14},{12,8},{14,10},{1,5},{3,7},... | collective-permute-start | bytes 786440 | tf_op jit(solution)/shard_map/wk_z1/ppermute | solution.py:276
  5.5 7.2 %collective-permute-start.2 = (bf16[512,256]{1,0:T(8,128)(2,1)}, bf16[512,256]{1,0:T(8,128)(2,1)S(1)}, u32[]{:S(2)}, u32[]{:S(2)}) collective-permute-start(bf16[512,256]{1,0:T(8,128)(2,1)} %get-tuple-element.49.refs_6_), channel_id=1, source_target_pairs={{4,8},{6,10},{8,4},{10,6},{5,9},{7,11},{9,5},{11,7},{20,24},{22,26... | collective-permute-start | bytes 786440 | tf_op jit(solution)/shard_map/wk_z3/ppermute | solution.py:276
  6.2 17.5 %collective-permute-start.4 = (bf16[256,1024]{1,0:T(8,128)(2,1)}, bf16[256,1024]{1,0:T(8,128)(2,1)S(1)}, u32[]{:S(2)}, u32[]{:S(2)}) collective-permute-start(bf16[256,1024]{1,0:T(8,128)(2,1)} %get-tuple-element.50), channel_id=1, source_target_pairs={{0,2},{2,0},{4,6},{6,4},{8,10},{10,8},{12,14},{14,12},{1,3},{3,1},... | collective-permute-start | bytes 1572872 | tf_op jit(solution)/shard_map/image_y/ppermute | solution.py:280
  7.8 15.9 %collective-permute-start.5 = (bf16[256,1024]{1,0:T(8,128)(2,1)}, bf16[256,1024]{1,0:T(8,128)(2,1)S(1)}, u32[]{:S(2)}, u32[]{:S(2)}) collective-permute-start(bf16[256,1024]{1,0:T(8,128)(2,1)} %get-tuple-element.51), channel_id=1, source_target_pairs={{0,16},{16,0},{1,17},{17,1},{2,18},{18,2},{3,19},{19,3},{4,20},{20... | collective-permute-start | bytes 1572872 | tf_op jit(solution)/shard_map/image_x/ppermute | solution.py:288
  12.0 4.0 %collective-permute-start.1 = (bf16[512,256]{1,0:T(8,128)(2,1)S(1)}, bf16[512,256]{1,0:T(8,128)(2,1)S(1)}, u32[]{:S(2)}, u32[]{:S(2)}) collective-permute-start(bf16[512,256]{1,0:T(8,128)(2,1)S(1)} %collective-permute-done.refs_7_), channel_id=1, source_target_pairs={{4,8},{6,10},{8,4},{10,6},{5,9},{7,11},{9,5},{11,7},{20,24},{22,26... | collective-permute-start | bytes 786440 | tf_op jit(solution)/shard_map/wk_across_z3/ppermute | solution.py:276
  12.7 32.6 %copy-start.7 = (bf16[512,256]{1,0:T(8,128)(2,1)}, bf16[512,256]{1,0:T(8,128)(2,1)S(1)}, u32[]{:S(2)}) copy-start(bf16[512,256]{1,0:T(8,128)(2,1)S(1)} %collective-permute-done.2.refs_10_) | copy-start | bytes 786436
  12.7 11.0 %collective-permute-start.3 = (bf16[512,256]{1,0:T(8,128)(2,1)S(1)}, bf16[512,256]{1,0:T(8,128)(2,1)S(1)}, u32[]{:S(2)}, u32[]{:S(2)}) collective-permute-start(bf16[512,256]{1,0:T(8,128)(2,1)S(1)} %collective-permute-done.2.refs_10_), channel_id=1, source_target_pairs={{4,0},{6,2},{8,12},{10,14},{5,1},{7,3},{9,13},{11,15},{20,16},{22,... | collective-permute-start | bytes 786440 | tf_op jit(solution)/shard_map/wk_out_z1/ppermute | solution.py:276
  23.7 23.1 %copy-start.4 = (bf16[256,1024]{1,0:T(8,128)(2,1)}, bf16[256,1024]{1,0:T(8,128)(2,1)S(1)}, u32[]{:S(2)}) copy-start(bf16[256,1024]{1,0:T(8,128)(2,1)S(1)} %collective-permute-done.4.refs_0_) | copy-start | bytes 1572868
  23.7 17.6 %copy-start.5 = (bf16[256,1024]{1,0:T(8,128)(2,1)}, bf16[256,1024]{1,0:T(8,128)(2,1)S(1)}, u32[]{:S(2)}) copy-start(bf16[256,1024]{1,0:T(8,128)(2,1)S(1)} %collective-permute-done.5.refs_2_) | copy-start | bytes 1572868
  23.7 6.6 %collective-permute-start.6 = (bf16[512,256]{1,0:T(8,128)(2,1)}, bf16[512,256]{1,0:T(8,128)(2,1)S(1)}, u32[]{:S(2)}, u32[]{:S(2)}) collective-permute-start(bf16[512,256]{1,0:T(8,128)(2,1)} %get-tuple-element.55.refs_6_), channel_id=1, source_target_pairs={{0,4},{2,6},{4,0},{6,2},{8,12},{10,14},{12,8},{14,10},{1,5},{3,7},... | collective-permute-start | bytes 786440 | tf_op jit(solution)/shard_map/wv_z1/ppermute | solution.py:276
  25.2 13.9 %collective-permute-start.10 = (bf16[256,1024]{1,0:T(8,128)(2,1)S(1)}, bf16[256,1024]{1,0:T(8,128)(2,1)}, u32[]{:S(2)}, u32[]{:S(2)}) collective-permute-start(bf16[256,1024]{1,0:T(8,128)(2,1)S(1)} %collective-permute-done.4.refs_0_), channel_id=1, source_target_pairs={{0,1},{1,0},{2,3},{3,2},{4,5},{5,4},{6,7},{7,6},{8,9},{9,8},{10,11... | collective-permute-start | bytes 1572872 | tf_op jit(solution)/shard_map/image_core/ppermute | solution.py:284
  25.2 13.9 %collective-permute-start.11 = (bf16[256,1024]{1,0:T(8,128)(2,1)S(1)}, bf16[256,1024]{1,0:T(8,128)(2,1)}, u32[]{:S(2)}, u32[]{:S(2)}) collective-permute-start(bf16[256,1024]{1,0:T(8,128)(2,1)S(1)} %collective-permute-done.5.refs_2_), channel_id=1, source_target_pairs={{0,1},{1,0},{2,3},{3,2},{4,5},{5,4},{6,7},{7,6},{8,9},{9,8},{10,11... | collective-permute-start | bytes 1572872 | tf_op jit(solution)/shard_map/image_core/ppermute | solution.py:284
  25.7 15.0 %collective-permute-start.9 = (bf16[256,1024]{1,0:T(8,128)(2,1)}, bf16[256,1024]{1,0:T(8,128)(2,1)}, u32[]{:S(2)}, u32[]{:S(2)}) collective-permute-start(bf16[256,1024]{1,0:T(8,128)(2,1)} %get-tuple-element.57), channel_id=1, source_target_pairs={{0,18},{2,16},{4,22},{6,20},{8,26},{10,24},{12,30},{14,28},{16,2},... | collective-permute-start | bytes 1572872 | tf_op jit(solution)/shard_map/image_xy/ppermute | solution.py:293
  27.2 4.5 %collective-permute-start.7 = (bf16[512,256]{1,0:T(8,128)(2,1)}, bf16[512,256]{1,0:T(8,128)(2,1)S(1)}, u32[]{:S(2)}, u32[]{:S(2)}) collective-permute-start(bf16[512,256]{1,0:T(8,128)(2,1)} %get-tuple-element.55.refs_6_), channel_id=1, source_target_pairs={{4,8},{6,10},{8,4},{10,6},{5,9},{7,11},{9,5},{11,7},{20,24},{22,26... | collective-permute-start | bytes 786440 | tf_op jit(solution)/shard_map/wv_z3/ppermute | solution.py:276
  30.4 8.7 %collective-permute-start.8 = (bf16[512,256]{1,0:T(8,128)(2,1)S(1)}, bf16[512,256]{1,0:T(8,128)(2,1)S(1)}, u32[]{:S(2)}, u32[]{:S(2)}) collective-permute-start(bf16[512,256]{1,0:T(8,128)(2,1)S(1)} %collective-permute-done.1.refs_8_), channel_id=1, source_target_pairs={{4,0},{6,2},{8,12},{10,14},{5,1},{7,3},{9,13},{11,15},{20,16},{22,... | collective-permute-start | bytes 786440 | tf_op jit(solution)/shard_map/wk_end_z1/ppermute | solution.py:276
  39.1 6.3 %copy-start.8 = (bf16[512,256]{1,0:T(8,128)(2,1)}, bf16[512,256]{1,0:T(8,128)(2,1)S(1)}, u32[]{:S(2)}) copy-start(bf16[512,256]{1,0:T(8,128)(2,1)S(1)} %collective-permute-done.8.refs_11_) | copy-start | bytes 786436
  40.8 6.1 %collective-permute-start.12 = (bf16[256,1024]{1,0:T(8,128)(2,1)}, bf16[256,1024]{1,0:T(8,128)(2,1)}, u32[]{:S(2)}, u32[]{:S(2)}) collective-permute-start(bf16[256,1024]{1,0:T(8,128)(2,1)} %collective-permute-done.9.refs_4_), channel_id=1, source_target_pairs={{0,1},{1,0},{2,3},{3,2},{4,5},{5,4},{6,7},{7,6},{8,9},{9,8},{10,11... | collective-permute-start | bytes 1572872 | tf_op jit(solution)/shard_map/image_core/ppermute | solution.py:284
  40.8 4.6 %collective-permute-start.19 = (bf16[32,1024]{1,0:T(8,128)(2,1)S(1)}, bf16[32,1024]{1,0:T(8,128)(2,1)S(1)}, u32[]{:S(2)}, u32[]{:S(2)}) collective-permute-start(bf16[32,1024]{1,0:T(8,128)(2,1)S(1)} %constant_dynamic-slice_fusion), channel_id=1, source_target_pairs={{0,2},{2,0},{4,6},{6,4},{8,10},{10,8},{12,14},{14,12},{1,3},{3,1},... | collective-permute-start | bytes 196616 | tf_op jit(solution)/shard_map/q_y/ppermute | solution.py:280
  41.4 10.6 %collective-permute-start.13 = (bf16[512,256]{1,0:T(8,128)(2,1)S(1)}, bf16[512,256]{1,0:T(8,128)(2,1)S(1)}, u32[]{:S(2)}, u32[]{:S(2)}) collective-permute-start(bf16[512,256]{1,0:T(8,128)(2,1)S(1)} %collective-permute-done.6.refs_7_), channel_id=1, source_target_pairs={{4,8},{6,10},{8,4},{10,6},{5,9},{7,11},{9,5},{11,7},{20,24},{22,26... | collective-permute-start | bytes 786440 | tf_op jit(solution)/shard_map/wv_across_z3/ppermute | solution.py:276
  45.4 23.3 %copy-start.12 = (s32[256]{0:T(256)S(1)}, s32[256]{0:T(256)}, u32[]{:S(2)}) copy-start(s32[256]{0:T(256)} %param.16) | copy-start | bytes 3076
  45.4 27.1 %copy-start.1 = (bf16[512,256]{1,0:T(8,128)(2,1)S(1)}, bf16[512,256]{1,0:T(8,128)(2,1)}, u32[]{:S(2)}) copy-start(bf16[512,256]{1,0:T(8,128)(2,1)} %get-tuple-element.55.refs_6_) | copy-start | bytes 786436
  45.4 23.4 %collective-permute-start.17 = (bf16[512,256]{1,0:T(8,128)(2,1)S(1)}, bf16[512,256]{1,0:T(8,128)(2,1)S(1)}, u32[]{:S(2)}, u32[]{:S(2)}) collective-permute-start(bf16[512,256]{1,0:T(8,128)(2,1)S(1)} %collective-permute-done.7.refs_10_), channel_id=1, source_target_pairs={{4,0},{6,2},{8,12},{10,14},{5,1},{7,3},{9,13},{11,15},{20,16},{22,... | collective-permute-start | bytes 786440 | tf_op jit(solution)/shard_map/wv_out_z1/ppermute | solution.py:276
  52.1 18.0 %collective-permute-start.18 = (bf16[512,256]{1,0:T(8,128)(2,1)S(1)}, bf16[512,256]{1,0:T(8,128)(2,1)S(1)}, u32[]{:S(2)}, u32[]{:S(2)}) collective-permute-start(bf16[512,256]{1,0:T(8,128)(2,1)S(1)} %collective-permute-done.13.refs_8_), channel_id=1, source_target_pairs={{4,0},{6,2},{8,12},{10,14},{5,1},{7,3},{9,13},{11,15},{20,16},{22,... | collective-permute-start | bytes 786440 | tf_op jit(solution)/shard_map/wv_end_z1/ppermute | solution.py:276
  53.4 14.1 %collective-permute-start.20 = (bf16[64,1024]{1,0:T(8,128)(2,1)S(1)}, bf16[64,1024]{1,0:T(8,128)(2,1)S(1)}, u32[]{:S(2)}, u32[]{:S(2)}) collective-permute-start(bf16[64,1024]{1,0:T(8,128)(2,1)S(1)} %pad_maximum_fusion.refs_0_), channel_id=1, source_target_pairs={{0,4},{2,6},{4,0},{6,2},{8,12},{10,14},{12,8},{14,10},{1,5},{3,7},... | collective-permute-start | bytes 393224 | tf_op jit(solution)/shard_map/q_z1/ppermute | solution.py:276
  56.1 23.4 %collective-permute-start.15 = (f32[512,128]{1,0:T(8,128)}, f32[512,128]{1,0:T(8,128)S(1)}, u32[]{:S(2)}, u32[]{:S(2)}) collective-permute-start(f32[512,128]{1,0:T(8,128)} %get-tuple-element.70), channel_id=1, source_target_pairs={{0,16},{16,0},{1,17},{17,1},{2,18},{18,2},{3,19},{19,3},{4,20},{20... | collective-permute-start | bytes 786440 | tf_op jit(solution)/shard_map/key_x/ppermute | solution.py:288
  57.6 20.1 %collective-permute-start.21 = (bf16[64,1024]{1,0:T(8,128)(2,1)S(1)}, bf16[64,1024]{1,0:T(8,128)(2,1)S(1)}, u32[]{:S(2)}, u32[]{:S(2)}) collective-permute-start(bf16[64,1024]{1,0:T(8,128)(2,1)S(1)} %pad_maximum_fusion.refs_0_), channel_id=1, source_target_pairs={{0,8},{2,10},{4,12},{6,14},{8,0},{10,2},{12,4},{14,6},{1,9},{3,11}... | collective-permute-start | bytes 393224 | tf_op jit(solution)/shard_map/q_z2/ppermute | solution.py:276
  67.5 10.2 %collective-permute-start.22 = (bf16[64,1024]{1,0:T(8,128)(2,1)S(1)}, bf16[64,1024]{1,0:T(8,128)(2,1)S(1)}, u32[]{:S(2)}, u32[]{:S(2)}) collective-permute-start(bf16[64,1024]{1,0:T(8,128)(2,1)S(1)} %pad_maximum_fusion.refs_0_), channel_id=1, source_target_pairs={{0,12},{2,14},{4,8},{6,10},{8,4},{10,6},{12,0},{14,2},{1,13},{3,15... | collective-permute-start | bytes 393224 | tf_op jit(solution)/shard_map/q_z3/ppermute | solution.py:276
  68.8 15.5 %copy-start.3 = (f32[128]{0:T(128)S(1)}, f32[128]{0:T(128)}, u32[]{:S(2)}) copy-start(f32[128]{0:T(128)} %param.14) | copy-start | bytes 1540
  68.8 15.5 %collective-permute-start.14 = (f32[520,128]{1,0:T(8,128)}, f32[520,128]{1,0:T(8,128)S(1)}, u32[]{:S(2)}, u32[]{:S(2)}) collective-permute-start(f32[520,128]{1,0:T(8,128)} %get-tuple-element.69), channel_id=1, source_target_pairs={{0,2},{2,0},{4,6},{6,4},{8,10},{10,8},{12,14},{14,12},{1,3},{3,1},... | collective-permute-start | bytes 798728 | tf_op jit(solution)/shard_map/key_y/ppermute | solution.py:280
  70.0 0.7 copy-start.9
  70.7 10.7 %collective-permute-start.16 = (f32[512,128]{1,0:T(8,128)S(1)}, f32[512,128]{1,0:T(8,128)S(1)}, u32[]{:S(2)}, u32[]{:S(2)}) collective-permute-start(f32[512,128]{1,0:T(8,128)S(1)} %get-tuple-element.71), channel_id=1, source_target_pairs={{0,18},{2,16},{4,22},{6,20},{8,26},{10,24},{12,30},{14,28},{16,2},... | collective-permute-start | bytes 786440 | tf_op jit(solution)/shard_map/key_xy/ppermute | solution.py:293
  77.7 9.4 %collective-permute-start.23 = (bf16[512,128]{1,0:T(8,128)(2,1)}, bf16[512,128]{1,0:T(8,128)(2,1)S(1)}, u32[]{:S(2)}, u32[]{:S(2)}) collective-permute-start(bf16[512,128]{1,0:T(8,128)(2,1)} %get-tuple-element.84), channel_id=1, source_target_pairs={{0,2},{2,0},{4,6},{6,4},{8,10},{10,8},{12,14},{14,12},{1,3},{3,1},... | collective-permute-start | bytes 393224 | tf_op jit(solution)/shard_map/value_y/ppermute | solution.py:280
  79.0 8.2 %collective-permute-start.24 = (bf16[512,128]{1,0:T(8,128)(2,1)}, bf16[512,128]{1,0:T(8,128)(2,1)S(1)}, u32[]{:S(2)}, u32[]{:S(2)}) collective-permute-start(bf16[512,128]{1,0:T(8,128)(2,1)} %get-tuple-element.85), channel_id=1, source_target_pairs={{0,16},{16,0},{1,17},{17,1},{2,18},{18,2},{3,19},{19,3},{4,20},{20... | collective-permute-start | bytes 393224 | tf_op jit(solution)/shard_map/value_x/ppermute | solution.py:288
  79.5 7.6 %collective-permute-start.25 = (bf16[512,128]{1,0:T(8,128)(2,1)}, bf16[512,128]{1,0:T(8,128)(2,1)S(1)}, u32[]{:S(2)}, u32[]{:S(2)}) collective-permute-start(bf16[512,128]{1,0:T(8,128)(2,1)} %get-tuple-element.86), channel_id=1, source_target_pairs={{0,18},{2,16},{4,22},{6,20},{8,26},{10,24},{12,30},{14,28},{16,2},... | collective-permute-start | bytes 393224 | tf_op jit(solution)/shard_map/value_xy/ppermute | solution.py:293
  87.2 38.6 %copy-start.6 = (bf16[128,1024]{1,0:T(8,128)(2,1)S(1)}, bf16[128,1024]{1,0:T(8,128)(2,1)}, u32[]{:S(2)}) copy-start(bf16[128,1024]{1,0:T(8,128)(2,1)} %param.17) | copy-start | bytes 786436
  88.0 7.6 %collective-permute-start.26 = (bf16[64,1152]{1,0:T(8,128)(2,1)S(1)}, bf16[64,1152]{1,0:T(8,128)(2,1)S(1)}, u32[]{:S(2)}, u32[]{:S(2)}) collective-permute-start(bf16[64,1152]{1,0:T(8,128)(2,1)S(1)} %get-tuple-element.88), channel_id=1, source_target_pairs={{0,4},{2,6},{4,0},{6,2},{8,12},{10,14},{12,8},{14,10},{1,5},{3,7},... | collective-permute-start | bytes 442376 | tf_op jit(solution)/shard_map/sums_z1/ppermute | solution.py:276
  88.0 11.7 %collective-permute-start.27 = (bf16[64,1152]{1,0:T(8,128)(2,1)S(1)}, bf16[64,1152]{1,0:T(8,128)(2,1)S(1)}, u32[]{:S(2)}, u32[]{:S(2)}) collective-permute-start(bf16[64,1152]{1,0:T(8,128)(2,1)S(1)} %get-tuple-element.89), channel_id=1, source_target_pairs={{0,8},{2,10},{4,12},{6,14},{8,0},{10,2},{12,4},{14,6},{1,9},{3,11}... | collective-permute-start | bytes 442376 | tf_op jit(solution)/shard_map/sums_z2/ppermute | solution.py:276
  91.2 8.6 %collective-permute-start.28 = (bf16[64,1152]{1,0:T(8,128)(2,1)S(1)}, bf16[64,1152]{1,0:T(8,128)(2,1)S(1)}, u32[]{:S(2)}, u32[]{:S(2)}) collective-permute-start(bf16[64,1152]{1,0:T(8,128)(2,1)S(1)} %get-tuple-element.90), channel_id=1, source_target_pairs={{0,12},{2,14},{4,8},{6,10},{8,4},{10,6},{12,0},{14,2},{1,13},{3,15... | collective-permute-start | bytes 442376 | tf_op jit(solution)/shard_map/sums_z3/ppermute | solution.py:276
  100.7 5.9 %collective-permute-start.29 = (bf16[64,1024]{1,0:T(8,128)(2,1)S(1)}, bf16[64,1024]{1,0:T(8,128)(2,1)S(1)}, u32[]{:S(2)}, u32[]{:S(2)}) collective-permute-start(bf16[64,1024]{1,0:T(8,128)(2,1)S(1)} %shard_map.107.refs_0_), channel_id=1, source_target_pairs={{0,4},{2,6},{4,0},{6,2},{8,12},{10,14},{12,8},{14,10},{1,5},{3,7},... | collective-permute-start | bytes 393224 | tf_op jit(solution)/shard_map/attn_z1/ppermute | solution.py:276
  102.9 10.8 %collective-permute-start.30 = (bf16[64,1024]{1,0:T(8,128)(2,1)S(1)}, bf16[64,1024]{1,0:T(8,128)(2,1)S(1)}, u32[]{:S(2)}, u32[]{:S(2)}) collective-permute-start(bf16[64,1024]{1,0:T(8,128)(2,1)S(1)} %shard_map.107.refs_0_), channel_id=1, source_target_pairs={{0,8},{2,10},{4,12},{6,14},{8,0},{10,2},{12,4},{14,6},{1,9},{3,11}... | collective-permute-start | bytes 393224 | tf_op jit(solution)/shard_map/attn_z2/ppermute | solution.py:276
  104.0 10.1 %collective-permute-start.31 = (bf16[64,1024]{1,0:T(8,128)(2,1)S(1)}, bf16[64,1024]{1,0:T(8,128)(2,1)S(1)}, u32[]{:S(2)}, u32[]{:S(2)}) collective-permute-start(bf16[64,1024]{1,0:T(8,128)(2,1)S(1)} %shard_map.107.refs_0_), channel_id=1, source_target_pairs={{0,12},{2,14},{4,8},{6,10},{8,4},{10,6},{12,0},{14,2},{1,13},{3,15... | collective-permute-start | bytes 393224 | tf_op jit(solution)/shard_map/attn_z3/ppermute | solution.py:276
  105.4 10.5 %collective-permute-start.32 = (bf16[64,1024]{1,0:T(8,128)(2,1)S(1)}, bf16[64,1024]{1,0:T(8,128)(2,1)S(1)}, u32[]{:S(2)}, u32[]{:S(2)}) collective-permute-start(bf16[64,1024]{1,0:T(8,128)(2,1)S(1)} %shard_map.107.refs_0_), channel_id=1, source_target_pairs={{0,2},{2,0},{4,6},{6,4},{8,10},{10,8},{12,14},{14,12},{1,3},{3,1},... | collective-permute-start | bytes 393224 | tf_op jit(solution)/shard_map/attn0_y/ppermute | solution.py:280
  106.6 9.3 %collective-permute-start.33 = (bf16[64,1024]{1,0:T(8,128)(2,1)S(1)}, bf16[64,1024]{1,0:T(8,128)(2,1)S(1)}, u32[]{:S(2)}, u32[]{:S(2)}) collective-permute-start(bf16[64,1024]{1,0:T(8,128)(2,1)S(1)} %collective-permute-done.29.refs_1_), channel_id=1, source_target_pairs={{0,2},{2,0},{4,6},{6,4},{8,10},{10,8},{12,14},{14,12},{1,3},{3,1},... | collective-permute-start | bytes 393224 | tf_op jit(solution)/shard_map/attn1_y/ppermute | solution.py:280
  113.7 5.0 %collective-permute-start.34 = (bf16[64,1024]{1,0:T(8,128)(2,1)S(1)}, bf16[64,1024]{1,0:T(8,128)(2,1)S(1)}, u32[]{:S(2)}, u32[]{:S(2)}) collective-permute-start(bf16[64,1024]{1,0:T(8,128)(2,1)S(1)} %collective-permute-done.30.refs_2_), channel_id=1, source_target_pairs={{0,2},{2,0},{4,6},{6,4},{8,10},{10,8},{12,14},{14,12},{1,3},{3,1},... | collective-permute-start | bytes 393224 | tf_op jit(solution)/shard_map/attn2_y/ppermute | solution.py:280
  114.1 6.0 %collective-permute-start.35 = (bf16[64,1024]{1,0:T(8,128)(2,1)S(1)}, bf16[64,1024]{1,0:T(8,128)(2,1)S(1)}, u32[]{:S(2)}, u32[]{:S(2)}) collective-permute-start(bf16[64,1024]{1,0:T(8,128)(2,1)S(1)} %collective-permute-done.31.refs_3_), channel_id=1, source_target_pairs={{0,2},{2,0},{4,6},{6,4},{8,10},{10,8},{12,14},{14,12},{1,3},{3,1},... | collective-permute-start | bytes 393224 | tf_op jit(solution)/shard_map/attn3_y/ppermute | solution.py:280
  120.1 2.2 %copy-start = (bf16[2048,1024]{1,0:T(8,128)(2,1)S(1)}, bf16[2048,1024]{1,0:T(8,128)(2,1)}, u32[]{:S(2)}) copy-start(bf16[2048,1024]{1,0:T(8,128)(2,1)} %refs_8_.1) | copy-start | bytes 12582916
  124.2 1.6 %collective-permute-start.36 = (bf16[128,1024]{1,0:T(8,128)(2,1)S(1)}, bf16[128,1024]{1,0:T(8,128)(2,1)S(1)}, u32[]{:S(2)}, u32[]{:S(2)}) collective-permute-start(bf16[128,1024]{1,0:T(8,128)(2,1)S(1)} %get-tuple-element.92), channel_id=1, source_target_pairs={{0,1},{1,0},{2,3},{3,2},{4,5},{5,4},{6,7},{7,6},{8,9},{9,8},{10,11... | collective-permute-start | bytes 786440 | tf_op jit(solution)/shard_map/proj_core/ppermute | solution.py:284

commit v5 on v4

--- a/solution.py
+++ b/solution.py
@@ -163,9 +163,9 @@
 
 
 def score_kernel(n, heads, limit_ref, keys_ref, *refs):
-    queries = refs[:n]
-    expo_ref, figures_ref, q_ref = refs[n:]
-    rows = queries[0].shape[0]
+    *queries, expo_ref, figures_ref, q_ref = refs
+    rows = limit_ref.shape[0] // n
+    each = n // len(queries)
     tokens = expo_ref.shape[1]
     scale = 1.0 / math.sqrt(HD)
     slots = keys_ref[tokens : tokens + 16 * (-(-tokens // HD) // 16 + (-(-tokens // HD) % 16 > 0)), :].astype(F32)
@@ -178,7 +178,8 @@
             seen.append(jnp.where((slot >= 0.0) & (slot <= limit), 1.0, 0.0))
         seen = jnp.concatenate(seen, 1)
         for j in range(heads):
-            q_ref[j * rows : (j + 1) * rows, :] = queries[i][:, j * HD : (j + 1) * HD]
+            at = i % each * rows
+            q_ref[j * rows : (j + 1) * rows, :] = queries[i // each][at : at + rows, j * HD : (j + 1) * HD]
         s = dot_nt(q_ref[...], keys_ref[:tokens, :]) * scale
         s = jnp.where(seen[None] > 0.5, s.reshape(heads, rows, tokens), -1e30).reshape(heads * rows, tokens)
         top = jnp.max(s, axis=1, keepdims=True).astype(BF16).astype(F32)
@@ -331,6 +332,9 @@
 
     share_x, share_y, key_own = shares(((1, 0), (0, 1)), key_weight)
     share_both, value_own = shares(((1, 1),), value_weight)
+    q_mine, q_got = take_y(queries, q_half, y), over_y("q", take_y(queries, q_half, 1 - y))
+    low_y = y == 0
+    q_rows = jnp.concatenate([jnp.where(low_y, q_mine, q_got), jnp.where(low_y, q_got, q_mine)], 0)
     if fast:
         def devices(route):
             pairs = []
@@ -355,12 +359,15 @@
         k1, km = along("wk", key_own, 1), along("wk", key_own, 3, middle)
         img_y, img_x = over_y("image", share_y), over_x("image", share_x)
         kb, ka = along("wk_across", k1, 3, middle), along("wk_out", km, 1, middle)
-        kb, ka, img_y, img_x, share_both, value_own = hold(kb, ka, img_y, img_x, share_both, value_own)
+        kb, ka, img_y, img_x, share_both, value_own, q_rows = hold(kb, ka, img_y, img_x, share_both, value_own, q_rows)
         img_both = over_both("image", share_both)
         ke = along("wk_end", kb, 1, middle)
         v1, vm = along("wv", value_own, 1), along("wv", value_own, 3, middle)
         core_y, core_x = over_core("image", img_y), over_core("image", img_x)
-        v1, vm, ke, img_both, core_y, core_x = hold(v1, vm, ke, img_both, core_y, core_x)
+        q_1 = along("q", q_rows, 1)
+        v1, vm, ke, img_both, core_y, core_x, q_1 = hold(v1, vm, ke, img_both, core_y, core_x, q_1)
+        q_near = jnp.concatenate([q_rows, q_1], 0)
+        q_far = along("q", q_near, 2)
         core_both = over_core("image", img_both)
         vb, va = along("wv_across", v1, 3, middle), along("wv_out", vm, 1, middle)
         pass
@@ -368,6 +375,7 @@
         pair = lambda i, o: ((i, 0), (o, 0))
         sources = (pair(0, 0), pair(1, 1), pair(2, 3), pair(4, 5))
     else:
+        q_pieces = [q_rows if d == 0 else along("q", q_rows, d) for d in range(lines)]
         img_y, img_x, img_both = over_y("image", share_y), over_x("image", share_x), over_both("image", share_both)
         core_y, core_x, core_both = (over_core("image", i) for i in (img_y, img_x, img_both))
         key_refs = [key_own] + [along("wk", key_own, d) for d in range(1, lines)]
@@ -400,14 +408,10 @@
         )(idx, slots, image_feats, *pieces, *weights)
 
     rows = 2 * text_rows
-    q_mine, q_got = take_y(queries, q_half, y), over_y("q", take_y(queries, q_half, 1 - y))
-    low_y = y == 0
-    q_rows = jnp.concatenate([jnp.where(low_y, q_mine, q_got), jnp.where(low_y, q_got, q_mine)], 0)
     keep, to_y, to_x, to_both = project(key_refs, extra, F32)
     if fast:
-        vb, to_y, to_x, to_both = hold(vb, to_y, to_x, to_both)
+        vb, keep = hold(vb, keep)
     key_parts = [over_y("key", to_y), over_x("key", to_x), over_both("key", to_both)]
-    q_pieces = [q_rows if d == 0 else along("q", q_rows, d) for d in range(lines)]
     if fast:
         value_refs.append(along("wv_end", vb, 1, middle))
     slot_rows = 2 * tok // HD
@@ -421,7 +425,8 @@
 
     keep, to_y, to_x, to_both = project(value_refs, 0, BF16)
     if fast:
-        to_y, to_x, to_both, *q_pieces = hold(to_y, to_x, to_both, *q_pieces)
+        to_y, to_x, to_both, q_far = hold(to_y, to_x, to_both, q_far)
+        q_pieces = [q_near, q_far]
     value_parts = [over_y("value", to_y), over_x("value", to_x), over_both("value", to_both)]
     limits = text_image.astype(F32).reshape(lines, rows)
     limits = jnp.concatenate([lax.dynamic_slice_in_dim(limits, line ^ d, 1, 0) for d in range(lines)], 0)
@@ -433,7 +438,7 @@
             jax.ShapeDtypeStruct((all_rows, 2 * tok), BF16),
             jax.ShapeDtypeStruct((lines * rows, HD), BF16),
         ),
-        in_specs=[WHOLE] * (2 + lines),
+        in_specs=[WHOLE] * (2 + len(q_pieces)),
         out_specs=(WHOLE, WHOLE),
         scratch_shapes=[pltpu.VMEM((per_kv * rows, HD), BF16)],
         compiler_params=PARAMS,

time: 127 us -> 122 us (0.961)
  waiting for transfers between devices: 56 us -> 48.4 us
    ppermute x19 -> x18, waiting for transfers between devices: 42.5 us -> 32.8 us  [along(): lax.ppermute(array, 'blk', [(b, b ^ 2 * d) for b in range(nblk) if ok(b /...]
    ppermute x8, waiting for transfers between devices: 10.9 us -> 13.2 us  [over_y(): return lax.ppermute(array, 'blk', swap_y)]
    ppermute x19 -> x18, starting transfers between devices: 25.6 us -> 25.9 us  [along(): lax.ppermute(array, 'blk', [(b, b ^ 2 * d) for b in range(nblk) if ok(b /...]
    unnamed x26 -> x29, local copies, waits for them, and re-layouts: 2.95 us -> 3.15 us
  transfers between devices with their start and end apart: 37 -> 36, of which waited for: 16 -> 16; matrix products, arithmetic and copies ran while one was open for 0% -> 1% of each run, Pallas kernels for 12% -> 12%
where the time goes in v5:
time: 122 us; the launch traced here: 121 us
  waiting for transfers between devices  48.4 us (40%)
  starting transfers between devices  45.7 us (37%)
  Pallas kernels  20.5 us (17%)
  local copies, waits for them, and re-layouts  4.47 us (4%)
    ppermute x18, waiting for transfers between devices, along(): lax.ppermute(array, 'blk', [(b, b ^ 2 * d) for b in range(nblk) if ok(b /...  32.8 us
    ppermute x18, starting transfers between devices, along(): lax.ppermute(array, 'blk', [(b, b ^ 2 * d) for b in range(nblk) if ok(b /...  25.9 us
    ppermute x8, waiting for transfers between devices, over_y(): return lax.ppermute(array, 'blk', swap_y)  13.2 us
    pallas_call x2, Pallas kernels, project(): pl.pallas_call(functools.partial(project_kernel, sources, extra), out_sha...  10.4 us
    ppermute x8, starting transfers between devices, over_y(): return lax.ppermute(array, 'blk', swap_y)  9.71 us
    ppermute x3, starting transfers between devices, over_both(): return lax.ppermute(array, ('groups', 'blk'), pairs)  5.3 us
    pallas_call x2, Pallas kernels, shares(): pl.pallas_call(functools.partial(share_kernel, flips, half_lines), out_sh...  4.46 us
    ppermute x3, starting transfers between devices, over_x(): return lax.ppermute(array, 'groups', [(g, g ^ 1) for g in range(groups)])  4.17 us
  transfers between devices with their start and end apart: 36, of which 16 were waited for; matrix products, arithmetic and copies ran while one was open for 1% of the time, Pallas kernels for 12%

profile of v5, /device:TPU:0, one launch (start us, length us, event | category | flops | bytes accessed | tf_op | source)
XLA Modules:
  0.0 121.3 jit_solution(8788494695769794836)
XLA Ops:
  0.0 2.4 %shard_map.100 = (bf16[256,1024]{1,0:T(8,128)(2,1)}, bf16[256,1024]{1,0:T(8,128)(2,1)}, bf16[512,256]{1,0:T(8,128)(2,1)}) custom-call(bf16[256,8192]{1,0:T(8,128)(2,1)} %image.7, bf16[1024,256]{1,0:T(8,128)(2,1)} %refs_0_.2), custom_call_target="tpu_custom_call" | custom-call | tf_op jit(solution)/shard_map/pallas_call | solution.py:324
  2.4 3.1 %collective-permute-start = (bf16[512,256]{1,0:T(8,128)(2,1)}, bf16[512,256]{1,0:T(8,128)(2,1)S(1)}, u32[]{:S(2)}, u32[]{:S(2)}) collective-permute-start(bf16[512,256]{1,0:T(8,128)(2,1)} %get-tuple-element.46.refs_6_), channel_id=1, source_target_pairs={{0,4},{2,6},{4,0},{6,2},{8,12},{10,14},{12,8},{14,10},{1,5},{3,7},... | collective-permute-start | bytes 786440 | tf_op jit(solution)/shard_map/wk_z1/ppermute | solution.py:277
  5.5 0.7 collective-permute-start.2
  6.2 1.6 %collective-permute-start.4 = (bf16[256,1024]{1,0:T(8,128)(2,1)}, bf16[256,1024]{1,0:T(8,128)(2,1)S(1)}, u32[]{:S(2)}, u32[]{:S(2)}) collective-permute-start(bf16[256,1024]{1,0:T(8,128)(2,1)} %get-tuple-element.47), channel_id=1, source_target_pairs={{0,2},{2,0},{4,6},{6,4},{8,10},{10,8},{12,14},{14,12},{1,3},{3,1},... | collective-permute-start | bytes 1572872 | tf_op jit(solution)/shard_map/image_y/ppermute | solution.py:281
  7.8 1.5 %collective-permute-start.5 = (bf16[256,1024]{1,0:T(8,128)(2,1)}, bf16[256,1024]{1,0:T(8,128)(2,1)S(1)}, u32[]{:S(2)}, u32[]{:S(2)}) collective-permute-start(bf16[256,1024]{1,0:T(8,128)(2,1)} %get-tuple-element.48), channel_id=1, source_target_pairs={{0,16},{16,0},{1,17},{17,1},{2,18},{18,2},{3,19},{19,3},{4,20},{20... | collective-permute-start | bytes 1572872 | tf_op jit(solution)/shard_map/image_x/ppermute | solution.py:289
  9.3 0.6 collective-permute-start.6
  9.9 2.1 %shard_map.101 = (bf16[256,1024]{1,0:T(8,128)(2,1)}, bf16[512,256]{1,0:T(8,128)(2,1)}) custom-call(bf16[256,8192]{1,0:T(8,128)(2,1)} %image.7, bf16[1024,256]{1,0:T(8,128)(2,1)} %refs_0_.3), custom_call_target="tpu_custom_call" | custom-call | tf_op jit(solution)/shard_map/pallas_call | solution.py:324
  11.9 0.1 collective-permute-done.refs_7_
  12.0 0.7 collective-permute-start.1
  12.7 1.3 %collective-permute-start.3 = (bf16[512,256]{1,0:T(8,128)(2,1)S(1)}, bf16[512,256]{1,0:T(8,128)(2,1)S(1)}, u32[]{:S(2)}, u32[]{:S(2)}) collective-permute-start(bf16[512,256]{1,0:T(8,128)(2,1)S(1)} %collective-permute-done.2.refs_10_), channel_id=1, source_target_pairs={{4,0},{6,2},{8,12},{10,14},{5,1},{7,3},{9,13},{11,15},{20,16},{22,... | collective-permute-start | bytes 786440 | tf_op jit(solution)/shard_map/wk_out_z1/ppermute | solution.py:277
  14.0 7.2 %collective-permute-done.6 = bf16[32,1024]{1,0:T(8,128)(2,1)S(1)} collective-permute-done((bf16[32,1024]{1,0:T(8,128)(2,1)S(1)}, bf16[32,1024]{1,0:T(8,128)(2,1)S(1)}, u32[]{:S(2)}, u32[]{:S(2)}) %collective-permute-start.6) | collective-permute-done | bytes 65568 | tf_op jit(solution)/shard_map/q_y/ppermute | solution.py:281
  21.3 3.1 %collective-permute-done.3.refs_9_ = bf16[512,256]{1,0:T(8,128)(2,1)S(1)} collective-permute-done((bf16[512,256]{1,0:T(8,128)(2,1)S(1)}, bf16[512,256]{1,0:T(8,128)(2,1)S(1)}, u32[]{:S(2)}, u32[]{:S(2)}) %collective-permute-start.3) | collective-permute-done | bytes 262176 | tf_op jit(solution)/shard_map/wk_out_z1/ppermute | solution.py:277
  24.5 1.1 collective-permute-start.7
  25.5 2.4 %collective-permute-start.10 = (bf16[256,1024]{1,0:T(8,128)(2,1)}, bf16[256,1024]{1,0:T(8,128)(2,1)}, u32[]{:S(2)}, u32[]{:S(2)}) collective-permute-start(bf16[256,1024]{1,0:T(8,128)(2,1)} %get-tuple-element.53), channel_id=1, source_target_pairs={{0,18},{2,16},{4,22},{6,20},{8,26},{10,24},{12,30},{14,28},{16,2},... | collective-permute-start | bytes 1572872 | tf_op jit(solution)/shard_map/image_xy/ppermute | solution.py:294
  28.0 0.5 collective-permute-start.12
  28.5 0.3 collective-permute-start.13
  28.8 5.3 %collective-permute-done.13 = bf16[64,1024]{1,0:T(8,128)(2,1)} collective-permute-done((bf16[64,1024]{1,0:T(8,128)(2,1)S(1)}, bf16[64,1024]{1,0:T(8,128)(2,1)}, u32[]{:S(2)}, u32[]{:S(2)}) %collective-permute-start.13) | collective-permute-done | bytes 131104 | tf_op jit(solution)/shard_map/q_z1/ppermute | solution.py:277
  34.0 0.7 collective-permute-start.8
  34.7 1.3 %collective-permute-start.9 = (bf16[512,256]{1,0:T(8,128)(2,1)S(1)}, bf16[512,256]{1,0:T(8,128)(2,1)S(1)}, u32[]{:S(2)}, u32[]{:S(2)}) collective-permute-start(bf16[512,256]{1,0:T(8,128)(2,1)S(1)} %collective-permute-done.1.refs_8_), channel_id=1, source_target_pairs={{4,0},{6,2},{8,12},{10,14},{5,1},{7,3},{9,13},{11,15},{20,16},{22,... | collective-permute-start | bytes 786440 | tf_op jit(solution)/shard_map/wk_end_z1/ppermute | solution.py:277
  36.0 8.3 %collective-permute-done.9.refs_11_ = bf16[512,256]{1,0:T(8,128)(2,1)S(1)} collective-permute-done((bf16[512,256]{1,0:T(8,128)(2,1)S(1)}, bf16[512,256]{1,0:T(8,128)(2,1)S(1)}, u32[]{:S(2)}, u32[]{:S(2)}) %collective-permute-start.9) | collective-permute-done | bytes 262176 | tf_op jit(solution)/shard_map/wk_end_z1/ppermute | solution.py:277
  44.5 0.7 copy-done.6
  45.2 0.2 copy-done.7
  45.4 0.7 collective-permute-start.14
  46.1 0.1 stack.63.idx_ref
  46.3 1.4 %collective-permute-start.19 = (bf16[512,256]{1,0:T(8,128)(2,1)S(1)}, bf16[512,256]{1,0:T(8,128)(2,1)S(1)}, u32[]{:S(2)}, u32[]{:S(2)}) collective-permute-start(bf16[512,256]{1,0:T(8,128)(2,1)S(1)} %collective-permute-done.8.refs_10_), channel_id=1, source_target_pairs={{4,0},{6,2},{8,12},{10,14},{5,1},{7,3},{9,13},{11,15},{20,16},{22,... | collective-permute-start | bytes 786440 | tf_op jit(solution)/shard_map/wv_out_z1/ppermute | solution.py:277
  47.7 5.2 %shard_map.102 = (f32[512,128]{1,0:T(8,128)S(1)}, f32[520,128]{1,0:T(8,128)}, f32[512,128]{1,0:T(8,128)}, f32[512,128]{1,0:T(8,128)S(1)}) custom-call(s32[8]{0:T(128)S(1)} %stack.63.idx_ref, f32[2,128]{1,0:T(2,128)S(1)} %convert_bitcast_fusion.slots, bf16[256,8192]{1,0:T(8,128)(2,1)} %image.7, bf16[256,1024]{1,0:T(8,128)(2,1)} %copy-done.4, ...), custom_call_target="tpu_custom_call" | custom-call | flops 1073741824 | bytes 16777216 | tf_op jit(solution)/shard_map/pallas_call | solution.py:393
  52.9 1.3 %collective-permute-start.20 = (bf16[512,256]{1,0:T(8,128)(2,1)S(1)}, bf16[512,256]{1,0:T(8,128)(2,1)}, u32[]{:S(2)}, u32[]{:S(2)}) collective-permute-start(bf16[512,256]{1,0:T(8,128)(2,1)S(1)} %collective-permute-done.14.refs_8_), channel_id=1, source_target_pairs={{4,0},{6,2},{8,12},{10,14},{5,1},{7,3},{9,13},{11,15},{20,16},{22,... | collective-permute-start | bytes 786440 | tf_op jit(solution)/shard_map/wv_end_z1/ppermute | solution.py:277
  54.2 0.9 constant_dynamic-update-slice_fusion.refs_0_
  55.1 4.4 %collective-permute-start.21 = (bf16[128,1024]{1,0:T(8,128)(2,1)S(1)}, bf16[128,1024]{1,0:T(8,128)(2,1)S(1)}, u32[]{:S(2)}, u32[]{:S(2)}) collective-permute-start(bf16[128,1024]{1,0:T(8,128)(2,1)S(1)} %constant_dynamic-update-slice_fusion.refs_0_), channel_id=1, source_target_pairs={{0,8},{2,10},{4,12},{6,14},{8,0},{10,2},{12,4},{14,6},{1,9},{3,11}... | collective-permute-start | bytes 786440 | tf_op jit(solution)/shard_map/q_z2/ppermute | solution.py:277
  59.5 1.3 %collective-permute-start.17 = (f32[512,128]{1,0:T(8,128)}, f32[512,128]{1,0:T(8,128)S(1)}, u32[]{:S(2)}, u32[]{:S(2)}) collective-permute-start(f32[512,128]{1,0:T(8,128)} %get-tuple-element.66), channel_id=1, source_target_pairs={{0,16},{16,0},{1,17},{17,1},{2,18},{18,2},{3,19},{19,3},{4,20},{20... | collective-permute-start | bytes 786440 | tf_op jit(solution)/shard_map/key_x/ppermute | solution.py:289
  60.9 0.7 collective-permute-start.16
  61.6 1.6 %collective-permute-start.18 = (f32[512,128]{1,0:T(8,128)S(1)}, f32[512,128]{1,0:T(8,128)S(1)}, u32[]{:S(2)}, u32[]{:S(2)}) collective-permute-start(f32[512,128]{1,0:T(8,128)S(1)} %get-tuple-element.67), channel_id=1, source_target_pairs={{0,18},{2,16},{4,22},{6,20},{8,26},{10,24},{12,30},{14,28},{16,2},... | collective-permute-start | bytes 786440 | tf_op jit(solution)/shard_map/key_xy/ppermute | solution.py:294
  63.1 0.8 collective-permute-done.20.refs_11_
  63.9 5.2 %shard_map.104 = (f32[512,128]{1,0:T(8,128)S(1)}, bf16[512,128]{1,0:T(8,128)(2,1)}, bf16[512,128]{1,0:T(8,128)(2,1)}, bf16[512,128]{1,0:T(8,128)(2,1)}) custom-call(s32[8]{0:T(128)S(1)} %stack.63.idx_ref, f32[2,128]{1,0:T(2,128)S(1)} %convert_bitcast_fusion.slots, bf16[256,8192]{1,0:T(8,128)(2,1)} %image.7, bf16[256,1024]{1,0:T(8,128)(2,1)} %copy-done.4, ...), custom_call_target="tpu_custom_call" | custom-call | flops 1073741824 | bytes 16777216 | tf_op jit(solution)/shard_map/pallas_call | solution.py:393
  69.1 1.9 %collective-permute-done.21.refs_1_ = bf16[128,1024]{1,0:T(8,128)(2,1)S(1)} collective-permute-done((bf16[128,1024]{1,0:T(8,128)(2,1)S(1)}, bf16[128,1024]{1,0:T(8,128)(2,1)S(1)}, u32[]{:S(2)}, u32[]{:S(2)}) %collective-permute-start.21) | collective-permute-done | bytes 262176 | tf_op jit(solution)/shard_map/q_z2/ppermute | solution.py:277
  71.0 0.8 collective-permute-start.22
  71.8 1.4 %collective-permute-start.23 = (bf16[512,128]{1,0:T(8,128)(2,1)}, bf16[512,128]{1,0:T(8,128)(2,1)S(1)}, u32[]{:S(2)}, u32[]{:S(2)}) collective-permute-start(bf16[512,128]{1,0:T(8,128)(2,1)} %get-tuple-element.79), channel_id=1, source_target_pairs={{0,16},{16,0},{1,17},{17,1},{2,18},{18,2},{3,19},{19,3},{4,20},{20... | collective-permute-start | bytes 393224 | tf_op jit(solution)/shard_map/value_x/ppermute | solution.py:289
  73.2 1.3 %collective-permute-start.24 = (bf16[512,128]{1,0:T(8,128)(2,1)}, bf16[512,128]{1,0:T(8,128)(2,1)S(1)}, u32[]{:S(2)}, u32[]{:S(2)}) collective-permute-start(bf16[512,128]{1,0:T(8,128)(2,1)} %get-tuple-element.80), channel_id=1, source_target_pairs={{0,18},{2,16},{4,22},{6,20},{8,26},{10,24},{12,30},{14,28},{16,2},... | collective-permute-start | bytes 393224 | tf_op jit(solution)/shard_map/value_xy/ppermute | solution.py:294
  74.5 0.1 reshape.18.limit_ref
  74.7 0.2 collective-permute-done.16.got_y
  74.8 0.2 shard_map.103.keys_ref
  75.0 2.0 %shard_map.105 = (bf16[2048,512]{1,0:T(8,128)(2,1)S(1)}, bf16[256,128]{1,0:T(8,128)(2,1)S(1)}) custom-call(f32[256,1]{1,0:T(8,128)S(1)} %reshape.18.limit_ref, bf16[528,128]{1,0:T(8,128)(2,1)S(1)} %shard_map.103.keys_ref, bf16[128,1024]{1,0:T(8,128)(2,1)S(1)} %constant_dynamic-update-slice_fusion.refs_0_, bf16[128,1024]{1,0:T(8,128)(2,1)S(1)} %collective-permute-done.21.refs_1_), custom_call_target="tpu_custom_call" | custom-call | tf_op jit(solution)/shard_map/pallas_call | solution.py:435
  77.0 1.0 collective-permute-done.22
  78.0 1.5 %collective-permute-done.24 = bf16[512,128]{1,0:T(8,128)(2,1)S(1)} collective-permute-done((bf16[512,128]{1,0:T(8,128)(2,1)}, bf16[512,128]{1,0:T(8,128)(2,1)S(1)}, u32[]{:S(2)}, u32[]{:S(2)}) %collective-permute-start.24) | collective-permute-done | bytes 131104 | tf_op jit(solution)/shard_map/value_xy/ppermute | solution.py:294
  79.6 0.7 shard_map.106
  80.4 2.6 %collective-permute-start.26 = (bf16[64,1152]{1,0:T(8,128)(2,1)S(1)}, bf16[64,1152]{1,0:T(8,128)(2,1)S(1)}, u32[]{:S(2)}, u32[]{:S(2)}) collective-permute-start(bf16[64,1152]{1,0:T(8,128)(2,1)S(1)} %get-tuple-element.83), channel_id=1, source_target_pairs={{0,8},{2,10},{4,12},{6,14},{8,0},{10,2},{12,4},{14,6},{1,9},{3,11}... | collective-permute-start | bytes 442376 | tf_op jit(solution)/shard_map/sums_z2/ppermute | solution.py:277
  83.1 1.7 %collective-permute-start.27 = (bf16[64,1152]{1,0:T(8,128)(2,1)S(1)}, bf16[64,1152]{1,0:T(8,128)(2,1)S(1)}, u32[]{:S(2)}, u32[]{:S(2)}) collective-permute-start(bf16[64,1152]{1,0:T(8,128)(2,1)S(1)} %get-tuple-element.84), channel_id=1, source_target_pairs={{0,12},{2,14},{4,8},{6,10},{8,4},{10,6},{12,0},{14,2},{1,13},{3,15... | collective-permute-start | bytes 442376 | tf_op jit(solution)/shard_map/sums_z3/ppermute | solution.py:277
  84.8 2.7 %collective-permute-done.25.refs_1_ = bf16[64,1152]{1,0:T(8,128)(2,1)S(1)} collective-permute-done((bf16[64,1152]{1,0:T(8,128)(2,1)S(1)}, bf16[64,1152]{1,0:T(8,128)(2,1)S(1)}, u32[]{:S(2)}, u32[]{:S(2)}) %collective-permute-start.25) | collective-permute-done | bytes 147488 | tf_op jit(solution)/shard_map/sums_z1/ppermute | solution.py:277
  87.5 5.3 %collective-permute-done.26.refs_2_ = bf16[64,1152]{1,0:T(8,128)(2,1)S(1)} collective-permute-done((bf16[64,1152]{1,0:T(8,128)(2,1)S(1)}, bf16[64,1152]{1,0:T(8,128)(2,1)S(1)}, u32[]{:S(2)}, u32[]{:S(2)}) %collective-permute-start.26) | collective-permute-done | bytes 147488 | tf_op jit(solution)/shard_map/sums_z2/ppermute | solution.py:277
  92.8 0.9 shard_map.107.refs_0_
  93.7 2.2 %collective-permute-start.28 = (bf16[64,1024]{1,0:T(8,128)(2,1)S(1)}, bf16[64,1024]{1,0:T(8,128)(2,1)S(1)}, u32[]{:S(2)}, u32[]{:S(2)}) collective-permute-start(bf16[64,1024]{1,0:T(8,128)(2,1)S(1)} %shard_map.107.refs_0_), channel_id=1, source_target_pairs={{0,4},{2,6},{4,0},{6,2},{8,12},{10,14},{12,8},{14,10},{1,5},{3,7},... | collective-permute-start | bytes 393224 | tf_op jit(solution)/shard_map/attn_z1/ppermute | solution.py:277
  95.9 1.1 collective-permute-start.29
  97.0 1.4 %collective-permute-start.30 = (bf16[64,1024]{1,0:T(8,128)(2,1)S(1)}, bf16[64,1024]{1,0:T(8,128)(2,1)S(1)}, u32[]{:S(2)}, u32[]{:S(2)}) collective-permute-start(bf16[64,1024]{1,0:T(8,128)(2,1)S(1)} %shard_map.107.refs_0_), channel_id=1, source_target_pairs={{0,12},{2,14},{4,8},{6,10},{8,4},{10,6},{12,0},{14,2},{1,13},{3,15... | collective-permute-start | bytes 393224 | tf_op jit(solution)/shard_map/attn_z3/ppermute | solution.py:277
  98.4 1.5 %collective-permute-start.31 = (bf16[64,1024]{1,0:T(8,128)(2,1)S(1)}, bf16[64,1024]{1,0:T(8,128)(2,1)S(1)}, u32[]{:S(2)}, u32[]{:S(2)}) collective-permute-start(bf16[64,1024]{1,0:T(8,128)(2,1)S(1)} %shard_map.107.refs_0_), channel_id=1, source_target_pairs={{0,2},{2,0},{4,6},{6,4},{8,10},{10,8},{12,14},{14,12},{1,3},{3,1},... | collective-permute-start | bytes 393224 | tf_op jit(solution)/shard_map/attn0_y/ppermute | solution.py:281
  99.9 1.7 %collective-permute-start.32 = (bf16[64,1024]{1,0:T(8,128)(2,1)S(1)}, bf16[64,1024]{1,0:T(8,128)(2,1)S(1)}, u32[]{:S(2)}, u32[]{:S(2)}) collective-permute-start(bf16[64,1024]{1,0:T(8,128)(2,1)S(1)} %collective-permute-done.28.refs_1_), channel_id=1, source_target_pairs={{0,2},{2,0},{4,6},{6,4},{8,10},{10,8},{12,14},{14,12},{1,3},{3,1},... | collective-permute-start | bytes 393224 | tf_op jit(solution)/shard_map/attn1_y/ppermute | solution.py:281
  101.7 5.3 %collective-permute-done.29.refs_2_ = bf16[64,1024]{1,0:T(8,128)(2,1)S(1)} collective-permute-done((bf16[64,1024]{1,0:T(8,128)(2,1)S(1)}, bf16[64,1024]{1,0:T(8,128)(2,1)S(1)}, u32[]{:S(2)}, u32[]{:S(2)}) %collective-permute-start.29) | collective-permute-done | bytes 131104 | tf_op jit(solution)/shard_map/attn_z2/ppermute | solution.py:277
  107.0 2.8 %collective-permute-start.33 = (bf16[64,1024]{1,0:T(8,128)(2,1)S(1)}, bf16[64,1024]{1,0:T(8,128)(2,1)S(1)}, u32[]{:S(2)}, u32[]{:S(2)}) collective-permute-start(bf16[64,1024]{1,0:T(8,128)(2,1)S(1)} %collective-permute-done.29.refs_2_), channel_id=1, source_target_pairs={{0,2},{2,0},{4,6},{6,4},{8,10},{10,8},{12,14},{14,12},{1,3},{3,1},... | collective-permute-start | bytes 393224 | tf_op jit(solution)/shard_map/attn2_y/ppermute | solution.py:281
  109.8 0.1 stack.59.idx_ref
  109.9 2.8 %collective-permute-done.33.refs_6_ = bf16[64,1024]{1,0:T(8,128)(2,1)S(1)} collective-permute-done((bf16[64,1024]{1,0:T(8,128)(2,1)S(1)}, bf16[64,1024]{1,0:T(8,128)(2,1)S(1)}, u32[]{:S(2)}, u32[]{:S(2)}) %collective-permute-start.33) | collective-permute-done | bytes 131104 | tf_op jit(solution)/shard_map/attn2_y/ppermute | solution.py:281
  112.7 2.0 %collective-permute-done.34.refs_7_ = bf16[64,1024]{1,0:T(8,128)(2,1)S(1)} collective-permute-done((bf16[64,1024]{1,0:T(8,128)(2,1)S(1)}, bf16[64,1024]{1,0:T(8,128)(2,1)S(1)}, u32[]{:S(2)}, u32[]{:S(2)}) %collective-permute-start.34) | collective-permute-done | bytes 131104 | tf_op jit(solution)/shard_map/attn3_y/ppermute | solution.py:281
  114.7 2.2 %copy-done = bf16[2048,1024]{1,0:T(8,128)(2,1)S(1)} copy-done((bf16[2048,1024]{1,0:T(8,128)(2,1)S(1)}, bf16[2048,1024]{1,0:T(8,128)(2,1)}, u32[]{:S(2)}) %copy-start) | copy-done | bytes 4194328
  116.9 1.9 %shard_map.108 = (f32[128,1024]{1,0:T(8,128)S(1)}, bf16[128,1024]{1,0:T(8,128)(2,1)S(1)}) custom-call(s32[17]{0:T(128)S(1)} %stack.59.idx_ref, bf16[64,1024]{1,0:T(8,128)(2,1)S(1)} %shard_map.107.refs_0_, bf16[64,1024]{1,0:T(8,128)(2,1)S(1)} %collective-permute-done.28.refs_1_, bf16[64,1024]{1,0:T(8,128)(2,1)S(1)} %collective-permute-done.29.refs_2_, ...), custom_call_target="tpu_custom_call" | custom-call | tf_op jit(solution)/shard_map/pallas_call | solution.py:469
  119.6 0.8 collective-permute-done.35
  120.4 0.8 add_convert_fusion
  (60 shorter events, 0.6 us)
Async XLA Ops:
  0.0 9.3 %copy-start.11 = (bf16[32,2048]{1,0:T(8,128)(2,1)S(1)}, bf16[32,2048]{1,0:T(8,128)(2,1)}, u32[]{:S(2)}) copy-start(bf16[32,2048]{1,0:T(8,128)(2,1)} %param.15) | copy-start | bytes 393220
  0.0 46.1 %copy-start.12 = (s32[256]{0:T(256)S(1)}, s32[256]{0:T(256)}, u32[]{:S(2)}) copy-start(s32[256]{0:T(256)} %param.11) | copy-start | bytes 3076
  2.4 45.3 %copy-start.2 = (bf16[512,256]{1,0:T(8,128)(2,1)S(1)}, bf16[512,256]{1,0:T(8,128)(2,1)}, u32[]{:S(2)}) copy-start(bf16[512,256]{1,0:T(8,128)(2,1)} %get-tuple-element.46.refs_6_) | copy-start | bytes 786436
  2.4 9.6 %collective-permute-start = (bf16[512,256]{1,0:T(8,128)(2,1)}, bf16[512,256]{1,0:T(8,128)(2,1)S(1)}, u32[]{:S(2)}, u32[]{:S(2)}) collective-permute-start(bf16[512,256]{1,0:T(8,128)(2,1)} %get-tuple-element.46.refs_6_), channel_id=1, source_target_pairs={{0,4},{2,6},{4,0},{6,2},{8,12},{10,14},{12,8},{14,10},{1,5},{3,7},... | collective-permute-start | bytes 786440 | tf_op jit(solution)/shard_map/wk_z1/ppermute | solution.py:277
  5.5 7.2 %collective-permute-start.2 = (bf16[512,256]{1,0:T(8,128)(2,1)}, bf16[512,256]{1,0:T(8,128)(2,1)S(1)}, u32[]{:S(2)}, u32[]{:S(2)}) collective-permute-start(bf16[512,256]{1,0:T(8,128)(2,1)} %get-tuple-element.46.refs_6_), channel_id=1, source_target_pairs={{4,8},{6,10},{8,4},{10,6},{5,9},{7,11},{9,5},{11,7},{20,24},{22,26... | collective-permute-start | bytes 786440 | tf_op jit(solution)/shard_map/wk_z3/ppermute | solution.py:277
  6.2 18.3 %collective-permute-start.4 = (bf16[256,1024]{1,0:T(8,128)(2,1)}, bf16[256,1024]{1,0:T(8,128)(2,1)S(1)}, u32[]{:S(2)}, u32[]{:S(2)}) collective-permute-start(bf16[256,1024]{1,0:T(8,128)(2,1)} %get-tuple-element.47), channel_id=1, source_target_pairs={{0,2},{2,0},{4,6},{6,4},{8,10},{10,8},{12,14},{14,12},{1,3},{3,1},... | collective-permute-start | bytes 1572872 | tf_op jit(solution)/shard_map/image_y/ppermute | solution.py:281
  7.8 16.7 %collective-permute-start.5 = (bf16[256,1024]{1,0:T(8,128)(2,1)}, bf16[256,1024]{1,0:T(8,128)(2,1)S(1)}, u32[]{:S(2)}, u32[]{:S(2)}) collective-permute-start(bf16[256,1024]{1,0:T(8,128)(2,1)} %get-tuple-element.48), channel_id=1, source_target_pairs={{0,16},{16,0},{1,17},{17,1},{2,18},{18,2},{3,19},{19,3},{4,20},{20... | collective-permute-start | bytes 1572872 | tf_op jit(solution)/shard_map/image_x/ppermute | solution.py:289
  9.3 12.0 %collective-permute-start.6 = (bf16[32,1024]{1,0:T(8,128)(2,1)S(1)}, bf16[32,1024]{1,0:T(8,128)(2,1)S(1)}, u32[]{:S(2)}, u32[]{:S(2)}) collective-permute-start(bf16[32,1024]{1,0:T(8,128)(2,1)S(1)} %constant_dynamic-slice_fusion), channel_id=1, source_target_pairs={{0,2},{2,0},{4,6},{6,4},{8,10},{10,8},{12,14},{14,12},{1,3},{3,1},... | collective-permute-start | bytes 196616 | tf_op jit(solution)/shard_map/q_y/ppermute | solution.py:281
  12.0 9.3 %collective-permute-start.1 = (bf16[512,256]{1,0:T(8,128)(2,1)S(1)}, bf16[512,256]{1,0:T(8,128)(2,1)S(1)}, u32[]{:S(2)}, u32[]{:S(2)}) collective-permute-start(bf16[512,256]{1,0:T(8,128)(2,1)S(1)} %collective-permute-done.refs_7_), channel_id=1, source_target_pairs={{4,8},{6,10},{8,4},{10,6},{5,9},{7,11},{9,5},{11,7},{20,24},{22,26... | collective-permute-start | bytes 786440 | tf_op jit(solution)/shard_map/wk_across_z3/ppermute | solution.py:277
  12.7 33.4 %copy-start.9 = (bf16[512,256]{1,0:T(8,128)(2,1)}, bf16[512,256]{1,0:T(8,128)(2,1)S(1)}, u32[]{:S(2)}) copy-start(bf16[512,256]{1,0:T(8,128)(2,1)S(1)} %collective-permute-done.2.refs_10_) | copy-start | bytes 786436
  12.7 11.7 %collective-permute-start.3 = (bf16[512,256]{1,0:T(8,128)(2,1)S(1)}, bf16[512,256]{1,0:T(8,128)(2,1)S(1)}, u32[]{:S(2)}, u32[]{:S(2)}) collective-permute-start(bf16[512,256]{1,0:T(8,128)(2,1)S(1)} %collective-permute-done.2.refs_10_), channel_id=1, source_target_pairs={{4,0},{6,2},{8,12},{10,14},{5,1},{7,3},{9,13},{11,15},{20,16},{22,... | collective-permute-start | bytes 786440 | tf_op jit(solution)/shard_map/wk_out_z1/ppermute | solution.py:277
  24.5 19.9 %copy-start.4 = (bf16[256,1024]{1,0:T(8,128)(2,1)}, bf16[256,1024]{1,0:T(8,128)(2,1)S(1)}, u32[]{:S(2)}) copy-start(bf16[256,1024]{1,0:T(8,128)(2,1)S(1)} %collective-permute-done.4.refs_0_) | copy-start | bytes 1572868
  24.5 21.7 %copy-start.5 = (bf16[256,1024]{1,0:T(8,128)(2,1)}, bf16[256,1024]{1,0:T(8,128)(2,1)S(1)}, u32[]{:S(2)}) copy-start(bf16[256,1024]{1,0:T(8,128)(2,1)S(1)} %collective-permute-done.5.refs_2_) | copy-start | bytes 1572868
  24.5 10.2 %collective-permute-start.7 = (bf16[512,256]{1,0:T(8,128)(2,1)}, bf16[512,256]{1,0:T(8,128)(2,1)S(1)}, u32[]{:S(2)}, u32[]{:S(2)}) collective-permute-start(bf16[512,256]{1,0:T(8,128)(2,1)} %get-tuple-element.51.refs_6_), channel_id=1, source_target_pairs={{0,4},{2,6},{4,0},{6,2},{8,12},{10,14},{12,8},{14,10},{1,5},{3,7},... | collective-permute-start | bytes 786440 | tf_op jit(solution)/shard_map/wv_z1/ppermute | solution.py:277
  25.5 18.8 %collective-permute-start.10 = (bf16[256,1024]{1,0:T(8,128)(2,1)}, bf16[256,1024]{1,0:T(8,128)(2,1)}, u32[]{:S(2)}, u32[]{:S(2)}) collective-permute-start(bf16[256,1024]{1,0:T(8,128)(2,1)} %get-tuple-element.53), channel_id=1, source_target_pairs={{0,18},{2,16},{4,22},{6,20},{8,26},{10,24},{12,30},{14,28},{16,2},... | collective-permute-start | bytes 1572872 | tf_op jit(solution)/shard_map/image_xy/ppermute | solution.py:294
  28.0 16.4 %collective-permute-start.11 = (bf16[256,1024]{1,0:T(8,128)(2,1)S(1)}, bf16[256,1024]{1,0:T(8,128)(2,1)S(1)}, u32[]{:S(2)}, u32[]{:S(2)}) collective-permute-start(bf16[256,1024]{1,0:T(8,128)(2,1)S(1)} %collective-permute-done.4.refs_0_), channel_id=1, source_target_pairs={{0,1},{1,0},{2,3},{3,2},{4,5},{5,4},{6,7},{7,6},{8,9},{9,8},{10,11... | collective-permute-start | bytes 1572872 | tf_op jit(solution)/shard_map/image_core/ppermute | solution.py:285
  28.0 16.4 %collective-permute-start.12 = (bf16[256,1024]{1,0:T(8,128)(2,1)S(1)}, bf16[256,1024]{1,0:T(8,128)(2,1)S(1)}, u32[]{:S(2)}, u32[]{:S(2)}) collective-permute-start(bf16[256,1024]{1,0:T(8,128)(2,1)S(1)} %collective-permute-done.5.refs_2_), channel_id=1, source_target_pairs={{0,1},{1,0},{2,3},{3,2},{4,5},{5,4},{6,7},{7,6},{8,9},{9,8},{10,11... | collective-permute-start | bytes 1572872 | tf_op jit(solution)/shard_map/image_core/ppermute | solution.py:285
  28.5 5.5 %collective-permute-start.13 = (bf16[64,1024]{1,0:T(8,128)(2,1)S(1)}, bf16[64,1024]{1,0:T(8,128)(2,1)}, u32[]{:S(2)}, u32[]{:S(2)}) collective-permute-start(bf16[64,1024]{1,0:T(8,128)(2,1)S(1)} %pad_maximum_fusion), channel_id=1, source_target_pairs={{0,4},{2,6},{4,0},{6,2},{8,12},{10,14},{12,8},{14,10},{1,5},{3,7},... | collective-permute-start | bytes 393224 | tf_op jit(solution)/shard_map/q_z1/ppermute | solution.py:277
  34.0 2.0 %collective-permute-start.8 = (bf16[512,256]{1,0:T(8,128)(2,1)}, bf16[512,256]{1,0:T(8,128)(2,1)S(1)}, u32[]{:S(2)}, u32[]{:S(2)}) collective-permute-start(bf16[512,256]{1,0:T(8,128)(2,1)} %get-tuple-element.51.refs_6_), channel_id=1, source_target_pairs={{4,8},{6,10},{8,4},{10,6},{5,9},{7,11},{9,5},{11,7},{20,24},{22,26... | collective-permute-start | bytes 786440 | tf_op jit(solution)/shard_map/wv_z3/ppermute | solution.py:277
  34.7 9.6 %collective-permute-start.9 = (bf16[512,256]{1,0:T(8,128)(2,1)S(1)}, bf16[512,256]{1,0:T(8,128)(2,1)S(1)}, u32[]{:S(2)}, u32[]{:S(2)}) collective-permute-start(bf16[512,256]{1,0:T(8,128)(2,1)S(1)} %collective-permute-done.1.refs_8_), channel_id=1, source_target_pairs={{4,0},{6,2},{8,12},{10,14},{5,1},{7,3},{9,13},{11,15},{20,16},{22,... | collective-permute-start | bytes 786440 | tf_op jit(solution)/shard_map/wk_end_z1/ppermute | solution.py:277
  44.4 1.9 %copy-start.10 = (bf16[512,256]{1,0:T(8,128)(2,1)}, bf16[512,256]{1,0:T(8,128)(2,1)S(1)}, u32[]{:S(2)}) copy-start(bf16[512,256]{1,0:T(8,128)(2,1)S(1)} %collective-permute-done.9.refs_11_) | copy-start | bytes 786436
  44.4 0.8 copy-start.6
  44.4 1.0 copy-start.7
  44.4 3.3 %collective-permute-start.15 = (bf16[256,1024]{1,0:T(8,128)(2,1)}, bf16[256,1024]{1,0:T(8,128)(2,1)}, u32[]{:S(2)}, u32[]{:S(2)}) collective-permute-start(bf16[256,1024]{1,0:T(8,128)(2,1)} %collective-permute-done.10.refs_4_), channel_id=1, source_target_pairs={{0,1},{1,0},{2,3},{3,2},{4,5},{5,4},{6,7},{7,6},{8,9},{9,8},{10,11... | collective-permute-start | bytes 1572872 | tf_op jit(solution)/shard_map/image_core/ppermute | solution.py:285
  45.4 7.5 %collective-permute-start.14 = (bf16[512,256]{1,0:T(8,128)(2,1)S(1)}, bf16[512,256]{1,0:T(8,128)(2,1)S(1)}, u32[]{:S(2)}, u32[]{:S(2)}) collective-permute-start(bf16[512,256]{1,0:T(8,128)(2,1)S(1)} %collective-permute-done.7.refs_7_), channel_id=1, source_target_pairs={{4,8},{6,10},{8,4},{10,6},{5,9},{7,11},{9,5},{11,7},{20,24},{22,26... | collective-permute-start | bytes 786440 | tf_op jit(solution)/shard_map/wv_across_z3/ppermute | solution.py:277
  46.2 14.6 %copy-start.13 = (s32[256]{0:T(256)S(1)}, s32[256]{0:T(256)}, u32[]{:S(2)}) copy-start(s32[256]{0:T(256)} %param.16) | copy-start | bytes 3076
  46.2 17.7 %copy-start.1 = (bf16[512,256]{1,0:T(8,128)(2,1)S(1)}, bf16[512,256]{1,0:T(8,128)(2,1)}, u32[]{:S(2)}) copy-start(bf16[512,256]{1,0:T(8,128)(2,1)} %get-tuple-element.51.refs_6_) | copy-start | bytes 786436
  46.3 15.3 %collective-permute-start.19 = (bf16[512,256]{1,0:T(8,128)(2,1)S(1)}, bf16[512,256]{1,0:T(8,128)(2,1)S(1)}, u32[]{:S(2)}, u32[]{:S(2)}) collective-permute-start(bf16[512,256]{1,0:T(8,128)(2,1)S(1)} %collective-permute-done.8.refs_10_), channel_id=1, source_target_pairs={{4,0},{6,2},{8,12},{10,14},{5,1},{7,3},{9,13},{11,15},{20,16},{22,... | collective-permute-start | bytes 786440 | tf_op jit(solution)/shard_map/wv_out_z1/ppermute | solution.py:277
  52.9 11.0 %collective-permute-start.20 = (bf16[512,256]{1,0:T(8,128)(2,1)S(1)}, bf16[512,256]{1,0:T(8,128)(2,1)}, u32[]{:S(2)}, u32[]{:S(2)}) collective-permute-start(bf16[512,256]{1,0:T(8,128)(2,1)S(1)} %collective-permute-done.14.refs_8_), channel_id=1, source_target_pairs={{4,0},{6,2},{8,12},{10,14},{5,1},{7,3},{9,13},{11,15},{20,16},{22,... | collective-permute-start | bytes 786440 | tf_op jit(solution)/shard_map/wv_end_z1/ppermute | solution.py:277
  55.1 15.9 %collective-permute-start.21 = (bf16[128,1024]{1,0:T(8,128)(2,1)S(1)}, bf16[128,1024]{1,0:T(8,128)(2,1)S(1)}, u32[]{:S(2)}, u32[]{:S(2)}) collective-permute-start(bf16[128,1024]{1,0:T(8,128)(2,1)S(1)} %constant_dynamic-update-slice_fusion.refs_0_), channel_id=1, source_target_pairs={{0,8},{2,10},{4,12},{6,14},{8,0},{10,2},{12,4},{14,6},{1,9},{3,11}... | collective-permute-start | bytes 786440 | tf_op jit(solution)/shard_map/q_z2/ppermute | solution.py:277
  59.5 13.7 %collective-permute-start.17 = (f32[512,128]{1,0:T(8,128)}, f32[512,128]{1,0:T(8,128)S(1)}, u32[]{:S(2)}, u32[]{:S(2)}) collective-permute-start(f32[512,128]{1,0:T(8,128)} %get-tuple-element.66), channel_id=1, source_target_pairs={{0,16},{16,0},{1,17},{17,1},{2,18},{18,2},{3,19},{19,3},{4,20},{20... | collective-permute-start | bytes 786440 | tf_op jit(solution)/shard_map/key_x/ppermute | solution.py:289
  60.9 13.9 %collective-permute-start.16 = (f32[520,128]{1,0:T(8,128)}, f32[520,128]{1,0:T(8,128)S(1)}, u32[]{:S(2)}, u32[]{:S(2)}) collective-permute-start(f32[520,128]{1,0:T(8,128)} %get-tuple-element.65), channel_id=1, source_target_pairs={{0,2},{2,0},{4,6},{6,4},{8,10},{10,8},{12,14},{14,12},{1,3},{3,1},... | collective-permute-start | bytes 798728 | tf_op jit(solution)/shard_map/key_y/ppermute | solution.py:281
  61.6 13.3 %copy-start.3 = (f32[128]{0:T(128)S(1)}, f32[128]{0:T(128)}, u32[]{:S(2)}) copy-start(f32[128]{0:T(128)} %param.14) | copy-start | bytes 1540
  61.6 13.1 %collective-permute-start.18 = (f32[512,128]{1,0:T(8,128)S(1)}, f32[512,128]{1,0:T(8,128)S(1)}, u32[]{:S(2)}, u32[]{:S(2)}) collective-permute-start(f32[512,128]{1,0:T(8,128)S(1)} %get-tuple-element.67), channel_id=1, source_target_pairs={{0,18},{2,16},{4,22},{6,20},{8,26},{10,24},{12,30},{14,28},{16,2},... | collective-permute-start | bytes 786440 | tf_op jit(solution)/shard_map/key_xy/ppermute | solution.py:294
  71.0 7.0 %collective-permute-start.22 = (bf16[512,128]{1,0:T(8,128)(2,1)}, bf16[512,128]{1,0:T(8,128)(2,1)S(1)}, u32[]{:S(2)}, u32[]{:S(2)}) collective-permute-start(bf16[512,128]{1,0:T(8,128)(2,1)} %get-tuple-element.78), channel_id=1, source_target_pairs={{0,2},{2,0},{4,6},{6,4},{8,10},{10,8},{12,14},{14,12},{1,3},{3,1},... | collective-permute-start | bytes 393224 | tf_op jit(solution)/shard_map/value_y/ppermute | solution.py:281
  71.8 6.2 %collective-permute-start.23 = (bf16[512,128]{1,0:T(8,128)(2,1)}, bf16[512,128]{1,0:T(8,128)(2,1)S(1)}, u32[]{:S(2)}, u32[]{:S(2)}) collective-permute-start(bf16[512,128]{1,0:T(8,128)(2,1)} %get-tuple-element.79), channel_id=1, source_target_pairs={{0,16},{16,0},{1,17},{17,1},{2,18},{18,2},{3,19},{19,3},{4,20},{20... | collective-permute-start | bytes 393224 | tf_op jit(solution)/shard_map/value_x/ppermute | solution.py:289
  73.2 6.3 %collective-permute-start.24 = (bf16[512,128]{1,0:T(8,128)(2,1)}, bf16[512,128]{1,0:T(8,128)(2,1)S(1)}, u32[]{:S(2)}, u32[]{:S(2)}) collective-permute-start(bf16[512,128]{1,0:T(8,128)(2,1)} %get-tuple-element.80), channel_id=1, source_target_pairs={{0,18},{2,16},{4,22},{6,20},{8,26},{10,24},{12,30},{14,28},{16,2},... | collective-permute-start | bytes 393224 | tf_op jit(solution)/shard_map/value_xy/ppermute | solution.py:294
  79.6 40.8 %copy-start.8 = (bf16[128,1024]{1,0:T(8,128)(2,1)S(1)}, bf16[128,1024]{1,0:T(8,128)(2,1)}, u32[]{:S(2)}) copy-start(bf16[128,1024]{1,0:T(8,128)(2,1)} %param.17) | copy-start | bytes 786436
  80.3 7.2 %collective-permute-start.25 = (bf16[64,1152]{1,0:T(8,128)(2,1)S(1)}, bf16[64,1152]{1,0:T(8,128)(2,1)S(1)}, u32[]{:S(2)}, u32[]{:S(2)}) collective-permute-start(bf16[64,1152]{1,0:T(8,128)(2,1)S(1)} %get-tuple-element.82), channel_id=1, source_target_pairs={{0,4},{2,6},{4,0},{6,2},{8,12},{10,14},{12,8},{14,10},{1,5},{3,7},... | collective-permute-start | bytes 442376 | tf_op jit(solution)/shard_map/sums_z1/ppermute | solution.py:277
  80.4 12.4 %collective-permute-start.26 = (bf16[64,1152]{1,0:T(8,128)(2,1)S(1)}, bf16[64,1152]{1,0:T(8,128)(2,1)S(1)}, u32[]{:S(2)}, u32[]{:S(2)}) collective-permute-start(bf16[64,1152]{1,0:T(8,128)(2,1)S(1)} %get-tuple-element.83), channel_id=1, source_target_pairs={{0,8},{2,10},{4,12},{6,14},{8,0},{10,2},{12,4},{14,6},{1,9},{3,11}... | collective-permute-start | bytes 442376 | tf_op jit(solution)/shard_map/sums_z2/ppermute | solution.py:277
  83.1 9.7 %collective-permute-start.27 = (bf16[64,1152]{1,0:T(8,128)(2,1)S(1)}, bf16[64,1152]{1,0:T(8,128)(2,1)S(1)}, u32[]{:S(2)}, u32[]{:S(2)}) collective-permute-start(bf16[64,1152]{1,0:T(8,128)(2,1)S(1)} %get-tuple-element.84), channel_id=1, source_target_pairs={{0,12},{2,14},{4,8},{6,10},{8,4},{10,6},{12,0},{14,2},{1,13},{3,15... | collective-permute-start | bytes 442376 | tf_op jit(solution)/shard_map/sums_z3/ppermute | solution.py:277
  93.7 6.2 %collective-permute-start.28 = (bf16[64,1024]{1,0:T(8,128)(2,1)S(1)}, bf16[64,1024]{1,0:T(8,128)(2,1)S(1)}, u32[]{:S(2)}, u32[]{:S(2)}) collective-permute-start(bf16[64,1024]{1,0:T(8,128)(2,1)S(1)} %shard_map.107.refs_0_), channel_id=1, source_target_pairs={{0,4},{2,6},{4,0},{6,2},{8,12},{10,14},{12,8},{14,10},{1,5},{3,7},... | collective-permute-start | bytes 393224 | tf_op jit(solution)/shard_map/attn_z1/ppermute | solution.py:277
  95.9 11.1 %collective-permute-start.29 = (bf16[64,1024]{1,0:T(8,128)(2,1)S(1)}, bf16[64,1024]{1,0:T(8,128)(2,1)S(1)}, u32[]{:S(2)}, u32[]{:S(2)}) collective-permute-start(bf16[64,1024]{1,0:T(8,128)(2,1)S(1)} %shard_map.107.refs_0_), channel_id=1, source_target_pairs={{0,8},{2,10},{4,12},{6,14},{8,0},{10,2},{12,4},{14,6},{1,9},{3,11}... | collective-permute-start | bytes 393224 | tf_op jit(solution)/shard_map/attn_z2/ppermute | solution.py:277
  97.0 12.8 %collective-permute-start.30 = (bf16[64,1024]{1,0:T(8,128)(2,1)S(1)}, bf16[64,1024]{1,0:T(8,128)(2,1)S(1)}, u32[]{:S(2)}, u32[]{:S(2)}) collective-permute-start(bf16[64,1024]{1,0:T(8,128)(2,1)S(1)} %shard_map.107.refs_0_), channel_id=1, source_target_pairs={{0,12},{2,14},{4,8},{6,10},{8,4},{10,6},{12,0},{14,2},{1,13},{3,15... | collective-permute-start | bytes 393224 | tf_op jit(solution)/shard_map/attn_z3/ppermute | solution.py:277
  98.4 11.5 %collective-permute-start.31 = (bf16[64,1024]{1,0:T(8,128)(2,1)S(1)}, bf16[64,1024]{1,0:T(8,128)(2,1)S(1)}, u32[]{:S(2)}, u32[]{:S(2)}) collective-permute-start(bf16[64,1024]{1,0:T(8,128)(2,1)S(1)} %shard_map.107.refs_0_), channel_id=1, source_target_pairs={{0,2},{2,0},{4,6},{6,4},{8,10},{10,8},{12,14},{14,12},{1,3},{3,1},... | collective-permute-start | bytes 393224 | tf_op jit(solution)/shard_map/attn0_y/ppermute | solution.py:281
  99.9 10.0 %collective-permute-start.32 = (bf16[64,1024]{1,0:T(8,128)(2,1)S(1)}, bf16[64,1024]{1,0:T(8,128)(2,1)S(1)}, u32[]{:S(2)}, u32[]{:S(2)}) collective-permute-start(bf16[64,1024]{1,0:T(8,128)(2,1)S(1)} %collective-permute-done.28.refs_1_), channel_id=1, source_target_pairs={{0,2},{2,0},{4,6},{6,4},{8,10},{10,8},{12,14},{14,12},{1,3},{3,1},... | collective-permute-start | bytes 393224 | tf_op jit(solution)/shard_map/attn1_y/ppermute | solution.py:281
  107.0 5.7 %collective-permute-start.33 = (bf16[64,1024]{1,0:T(8,128)(2,1)S(1)}, bf16[64,1024]{1,0:T(8,128)(2,1)S(1)}, u32[]{:S(2)}, u32[]{:S(2)}) collective-permute-start(bf16[64,1024]{1,0:T(8,128)(2,1)S(1)} %collective-permute-done.29.refs_2_), channel_id=1, source_target_pairs={{0,2},{2,0},{4,6},{6,4},{8,10},{10,8},{12,14},{14,12},{1,3},{3,1},... | collective-permute-start | bytes 393224 | tf_op jit(solution)/shard_map/attn2_y/ppermute | solution.py:281
  109.8 5.0 %collective-permute-start.34 = (bf16[64,1024]{1,0:T(8,128)(2,1)S(1)}, bf16[64,1024]{1,0:T(8,128)(2,1)S(1)}, u32[]{:S(2)}, u32[]{:S(2)}) collective-permute-start(bf16[64,1024]{1,0:T(8,128)(2,1)S(1)} %collective-permute-done.30.refs_3_), channel_id=1, source_target_pairs={{0,2},{2,0},{4,6},{6,4},{8,10},{10,8},{12,14},{14,12},{1,3},{3,1},... | collective-permute-start | bytes 393224 | tf_op jit(solution)/shard_map/attn3_y/ppermute | solution.py:281
  114.7 2.2 %copy-start = (bf16[2048,1024]{1,0:T(8,128)(2,1)S(1)}, bf16[2048,1024]{1,0:T(8,128)(2,1)}, u32[]{:S(2)}) copy-start(bf16[2048,1024]{1,0:T(8,128)(2,1)} %refs_8_.1) | copy-start | bytes 12582916
  118.8 1.6 %collective-permute-start.35 = (bf16[128,1024]{1,0:T(8,128)(2,1)S(1)}, bf16[128,1024]{1,0:T(8,128)(2,1)S(1)}, u32[]{:S(2)}, u32[]{:S(2)}) collective-permute-start(bf16[128,1024]{1,0:T(8,128)(2,1)S(1)} %get-tuple-element.86), channel_id=1, source_target_pairs={{0,1},{1,0},{2,3},{3,2},{4,5},{5,4},{6,7},{7,6},{8,9},{9,8},{10,11... | collective-permute-start | bytes 786440 | tf_op jit(solution)/shard_map/proj_core/ppermute | solution.py:285

commit v6 on v5

--- a/solution.py
+++ b/solution.py
@@ -364,10 +364,8 @@
         ke = along("wk_end", kb, 1, middle)
         v1, vm = along("wv", value_own, 1), along("wv", value_own, 3, middle)
         core_y, core_x = over_core("image", img_y), over_core("image", img_x)
+        v1, vm, ke, img_both, core_y, core_x = hold(v1, vm, ke, img_both, core_y, core_x)
         q_1 = along("q", q_rows, 1)
-        v1, vm, ke, img_both, core_y, core_x, q_1 = hold(v1, vm, ke, img_both, core_y, core_x, q_1)
-        q_near = jnp.concatenate([q_rows, q_1], 0)
-        q_far = along("q", q_near, 2)
         core_both = over_core("image", img_both)
         vb, va = along("wv_across", v1, 3, middle), along("wv_out", vm, 1, middle)
         pass
@@ -410,7 +408,9 @@
     rows = 2 * text_rows
     keep, to_y, to_x, to_both = project(key_refs, extra, F32)
     if fast:
-        vb, keep = hold(vb, keep)
+        vb, keep, q_1 = hold(vb, keep, q_1)
+        q_near = jnp.concatenate([q_rows, q_1], 0)
+        q_far = along("q", q_near, 2)
     key_parts = [over_y("key", to_y), over_x("key", to_x), over_both("key", to_both)]
     if fast:
         value_refs.append(along("wv_end", vb, 1, middle))

time: 122 us -> 117 us (0.959)
  waiting for transfers between devices: 48.4 us -> 45.3 us
    ppermute x18, waiting for transfers between devices: 32.8 us -> 30.1 us  [along(): lax.ppermute(array, 'blk', [(b, b ^ 2 * d) for b in range(nblk) if ok(b /...]
  transfers between devices with their start and end apart: 36 -> 36, of which waited for: 16 -> 16; matrix products, arithmetic and copies ran while one was open for 1% -> 0% of each run, Pallas kernels for 12% -> 13%
where the time goes in v6:
time: 117 us
  waiting for transfers between devices  45.3 us (39%)
  starting transfers between devices  45 us (38%)
  Pallas kernels  20.5 us (18%)
  local copies, waits for them, and re-layouts  3.57 us (3%)
    ppermute x18, waiting for transfers between devices, along(): lax.ppermute(array, 'blk', [(b, b ^ 2 * d) for b in range(nblk) if ok(b /...  30.1 us
    ppermute x18, starting transfers between devices, along(): lax.ppermute(array, 'blk', [(b, b ^ 2 * d) for b in range(nblk) if ok(b /...  26.9 us
    ppermute x8, waiting for transfers between devices, over_y(): return lax.ppermute(array, 'blk', swap_y)  12 us
    pallas_call x2, Pallas kernels, project(): pl.pallas_call(functools.partial(project_kernel, sources, extra), out_sha...  10.4 us
    ppermute x8, starting transfers between devices, over_y(): return lax.ppermute(array, 'blk', swap_y)  9.45 us
    ppermute x3, starting transfers between devices, over_both(): return lax.ppermute(array, ('groups', 'blk'), pairs)  4.75 us
    pallas_call x2, Pallas kernels, shares(): pl.pallas_call(functools.partial(share_kernel, flips, half_lines), out_sh...  4.46 us
    ppermute x3, starting transfers between devices, over_x(): return lax.ppermute(array, 'groups', [(g, g ^ 1) for g in range(groups)])  3.26 us
  transfers between devices with their start and end apart: 36, of which 16 were waited for; matrix products, arithmetic and copies ran while one was open for 0% of the time, Pallas kernels for 13%

profile of v6, /device:TPU:0, one launch (start us, length us, event | category | flops | bytes accessed | tf_op | source)
XLA Modules:
  0.0 116.5 jit_solution(17750721907328062377)
XLA Ops:
  0.0 2.4 %shard_map.100 = (bf16[256,1024]{1,0:T(8,128)(2,1)}, bf16[256,1024]{1,0:T(8,128)(2,1)}, bf16[512,256]{1,0:T(8,128)(2,1)}) custom-call(bf16[256,8192]{1,0:T(8,128)(2,1)} %image.7, bf16[1024,256]{1,0:T(8,128)(2,1)} %refs_0_.2), custom_call_target="tpu_custom_call" | custom-call | tf_op jit(solution)/shard_map/pallas_call | solution.py:324
  2.4 3.1 %collective-permute-start = (bf16[512,256]{1,0:T(8,128)(2,1)}, bf16[512,256]{1,0:T(8,128)(2,1)S(1)}, u32[]{:S(2)}, u32[]{:S(2)}) collective-permute-start(bf16[512,256]{1,0:T(8,128)(2,1)} %get-tuple-element.46.refs_6_), channel_id=1, source_target_pairs={{0,4},{2,6},{4,0},{6,2},{8,12},{10,14},{12,8},{14,10},{1,5},{3,7},... | collective-permute-start | bytes 786440 | tf_op jit(solution)/shard_map/wk_z1/ppermute | solution.py:277
  5.5 0.7 collective-permute-start.2
  6.2 1.6 %collective-permute-start.4 = (bf16[256,1024]{1,0:T(8,128)(2,1)}, bf16[256,1024]{1,0:T(8,128)(2,1)S(1)}, u32[]{:S(2)}, u32[]{:S(2)}) collective-permute-start(bf16[256,1024]{1,0:T(8,128)(2,1)} %get-tuple-element.47), channel_id=1, source_target_pairs={{0,2},{2,0},{4,6},{6,4},{8,10},{10,8},{12,14},{14,12},{1,3},{3,1},... | collective-permute-start | bytes 1572872 | tf_op jit(solution)/shard_map/image_y/ppermute | solution.py:281
  7.8 1.5 %collective-permute-start.5 = (bf16[256,1024]{1,0:T(8,128)(2,1)}, bf16[256,1024]{1,0:T(8,128)(2,1)S(1)}, u32[]{:S(2)}, u32[]{:S(2)}) collective-permute-start(bf16[256,1024]{1,0:T(8,128)(2,1)} %get-tuple-element.48), channel_id=1, source_target_pairs={{0,16},{16,0},{1,17},{17,1},{2,18},{18,2},{3,19},{19,3},{4,20},{20... | collective-permute-start | bytes 1572872 | tf_op jit(solution)/shard_map/image_x/ppermute | solution.py:289
  9.3 0.6 collective-permute-start.6
  9.9 2.1 %shard_map.101 = (bf16[256,1024]{1,0:T(8,128)(2,1)}, bf16[512,256]{1,0:T(8,128)(2,1)}) custom-call(bf16[256,8192]{1,0:T(8,128)(2,1)} %image.7, bf16[1024,256]{1,0:T(8,128)(2,1)} %refs_0_.3), custom_call_target="tpu_custom_call" | custom-call | tf_op jit(solution)/shard_map/pallas_call | solution.py:324
  11.9 0.1 collective-permute-done.refs_7_
  12.0 0.7 collective-permute-start.1
  12.7 1.3 %collective-permute-start.3 = (bf16[512,256]{1,0:T(8,128)(2,1)S(1)}, bf16[512,256]{1,0:T(8,128)(2,1)S(1)}, u32[]{:S(2)}, u32[]{:S(2)}) collective-permute-start(bf16[512,256]{1,0:T(8,128)(2,1)S(1)} %collective-permute-done.2.refs_10_), channel_id=1, source_target_pairs={{4,0},{6,2},{8,12},{10,14},{5,1},{7,3},{9,13},{11,15},{20,16},{22,... | collective-permute-start | bytes 786440 | tf_op jit(solution)/shard_map/wk_out_z1/ppermute | solution.py:277
  14.0 7.2 %collective-permute-done.6 = bf16[32,1024]{1,0:T(8,128)(2,1)S(1)} collective-permute-done((bf16[32,1024]{1,0:T(8,128)(2,1)S(1)}, bf16[32,1024]{1,0:T(8,128)(2,1)S(1)}, u32[]{:S(2)}, u32[]{:S(2)}) %collective-permute-start.6) | collective-permute-done | bytes 65568 | tf_op jit(solution)/shard_map/q_y/ppermute | solution.py:281
  21.3 3.1 %collective-permute-done.3.refs_9_ = bf16[512,256]{1,0:T(8,128)(2,1)S(1)} collective-permute-done((bf16[512,256]{1,0:T(8,128)(2,1)S(1)}, bf16[512,256]{1,0:T(8,128)(2,1)S(1)}, u32[]{:S(2)}, u32[]{:S(2)}) %collective-permute-start.3) | collective-permute-done | bytes 262176 | tf_op jit(solution)/shard_map/wk_out_z1/ppermute | solution.py:277
  24.5 1.1 collective-permute-start.7
  25.5 2.4 %collective-permute-start.10 = (bf16[256,1024]{1,0:T(8,128)(2,1)}, bf16[256,1024]{1,0:T(8,128)(2,1)}, u32[]{:S(2)}, u32[]{:S(2)}) collective-permute-start(bf16[256,1024]{1,0:T(8,128)(2,1)} %get-tuple-element.53), channel_id=1, source_target_pairs={{0,18},{2,16},{4,22},{6,20},{8,26},{10,24},{12,30},{14,28},{16,2},... | collective-permute-start | bytes 1572872 | tf_op jit(solution)/shard_map/image_xy/ppermute | solution.py:294
  28.0 0.5 collective-permute-start.12
  28.5 0.7 collective-permute-start.8
  29.2 1.9 %collective-permute-done.7.refs_7_ = bf16[512,256]{1,0:T(8,128)(2,1)S(1)} collective-permute-done((bf16[512,256]{1,0:T(8,128)(2,1)}, bf16[512,256]{1,0:T(8,128)(2,1)S(1)}, u32[]{:S(2)}, u32[]{:S(2)}) %collective-permute-start.7) | collective-permute-done | bytes 262176 | tf_op jit(solution)/shard_map/wv_z1/ppermute | solution.py:277
  31.1 1.3 %collective-permute-start.9 = (bf16[512,256]{1,0:T(8,128)(2,1)S(1)}, bf16[512,256]{1,0:T(8,128)(2,1)S(1)}, u32[]{:S(2)}, u32[]{:S(2)}) collective-permute-start(bf16[512,256]{1,0:T(8,128)(2,1)S(1)} %collective-permute-done.1.refs_8_), channel_id=1, source_target_pairs={{4,0},{6,2},{8,12},{10,14},{5,1},{7,3},{9,13},{11,15},{20,16},{22,... | collective-permute-start | bytes 786440 | tf_op jit(solution)/shard_map/wk_end_z1/ppermute | solution.py:277
  32.4 7.3 %collective-permute-done.9.refs_11_ = bf16[512,256]{1,0:T(8,128)(2,1)S(1)} collective-permute-done((bf16[512,256]{1,0:T(8,128)(2,1)S(1)}, bf16[512,256]{1,0:T(8,128)(2,1)S(1)}, u32[]{:S(2)}, u32[]{:S(2)}) %collective-permute-start.9) | collective-permute-done | bytes 262176 | tf_op jit(solution)/shard_map/wk_end_z1/ppermute | solution.py:277
  39.8 0.7 copy-done.6
  40.5 0.2 copy-done.7
  40.7 0.7 collective-permute-start.13
  41.4 0.1 stack.63.idx_ref
  41.5 2.3 %collective-permute-start.15 = (bf16[64,1024]{1,0:T(8,128)(2,1)S(1)}, bf16[64,1024]{1,0:T(8,128)(2,1)S(1)}, u32[]{:S(2)}, u32[]{:S(2)}) collective-permute-start(bf16[64,1024]{1,0:T(8,128)(2,1)S(1)} %pad_maximum_fusion), channel_id=1, source_target_pairs={{0,4},{2,6},{4,0},{6,2},{8,12},{10,14},{12,8},{14,10},{1,5},{3,7},... | collective-permute-start | bytes 393224 | tf_op jit(solution)/shard_map/q_z1/ppermute | solution.py:277
  43.8 1.4 %collective-permute-start.19 = (bf16[512,256]{1,0:T(8,128)(2,1)S(1)}, bf16[512,256]{1,0:T(8,128)(2,1)S(1)}, u32[]{:S(2)}, u32[]{:S(2)}) collective-permute-start(bf16[512,256]{1,0:T(8,128)(2,1)S(1)} %collective-permute-done.8.refs_10_), channel_id=1, source_target_pairs={{4,0},{6,2},{8,12},{10,14},{5,1},{7,3},{9,13},{11,15},{20,16},{22,... | collective-permute-start | bytes 786440 | tf_op jit(solution)/shard_map/wv_out_z1/ppermute | solution.py:277
  45.3 5.2 %shard_map.102 = (f32[512,128]{1,0:T(8,128)S(1)}, f32[520,128]{1,0:T(8,128)}, f32[512,128]{1,0:T(8,128)}, f32[512,128]{1,0:T(8,128)S(1)}) custom-call(s32[8]{0:T(128)S(1)} %stack.63.idx_ref, f32[2,128]{1,0:T(2,128)S(1)} %convert_bitcast_fusion.slots, bf16[256,8192]{1,0:T(8,128)(2,1)} %image.7, bf16[256,1024]{1,0:T(8,128)(2,1)} %copy-done.4, ...), custom_call_target="tpu_custom_call" | custom-call | flops 1073741824 | bytes 16777216 | tf_op jit(solution)/shard_map/pallas_call | solution.py:391
  50.5 1.3 %collective-permute-start.20 = (bf16[512,256]{1,0:T(8,128)(2,1)S(1)}, bf16[512,256]{1,0:T(8,128)(2,1)}, u32[]{:S(2)}, u32[]{:S(2)}) collective-permute-start(bf16[512,256]{1,0:T(8,128)(2,1)S(1)} %collective-permute-done.13.refs_8_), channel_id=1, source_target_pairs={{4,0},{6,2},{8,12},{10,14},{5,1},{7,3},{9,13},{11,15},{20,16},{22,... | collective-permute-start | bytes 786440 | tf_op jit(solution)/shard_map/wv_end_z1/ppermute | solution.py:277
  51.8 3.5 %collective-permute-start.21 = (bf16[128,1024]{1,0:T(8,128)(2,1)S(1)}, bf16[128,1024]{1,0:T(8,128)(2,1)S(1)}, u32[]{:S(2)}, u32[]{:S(2)}) collective-permute-start(bf16[128,1024]{1,0:T(8,128)(2,1)S(1)} %constant_dynamic-update-slice_fusion.refs_0_), channel_id=1, source_target_pairs={{0,8},{2,10},{4,12},{6,14},{8,0},{10,2},{12,4},{14,6},{1,9},{3,11}... | collective-permute-start | bytes 786440 | tf_op jit(solution)/shard_map/q_z2/ppermute | solution.py:277
  55.3 1.5 %collective-permute-start.17 = (f32[512,128]{1,0:T(8,128)}, f32[512,128]{1,0:T(8,128)S(1)}, u32[]{:S(2)}, u32[]{:S(2)}) collective-permute-start(f32[512,128]{1,0:T(8,128)} %get-tuple-element.66), channel_id=1, source_target_pairs={{0,16},{16,0},{1,17},{17,1},{2,18},{18,2},{3,19},{19,3},{4,20},{20... | collective-permute-start | bytes 786440 | tf_op jit(solution)/shard_map/key_x/ppermute | solution.py:289
  56.9 1.3 %collective-permute-start.16 = (f32[520,128]{1,0:T(8,128)}, f32[520,128]{1,0:T(8,128)S(1)}, u32[]{:S(2)}, u32[]{:S(2)}) collective-permute-start(f32[520,128]{1,0:T(8,128)} %get-tuple-element.65), channel_id=1, source_target_pairs={{0,2},{2,0},{4,6},{6,4},{8,10},{10,8},{12,14},{14,12},{1,3},{3,1},... | collective-permute-start | bytes 798728 | tf_op jit(solution)/shard_map/key_y/ppermute | solution.py:281
  58.1 0.7 collective-permute-start.18
  58.9 3.0 %collective-permute-done.20.refs_11_ = bf16[512,256]{1,0:T(8,128)(2,1)} collective-permute-done((bf16[512,256]{1,0:T(8,128)(2,1)S(1)}, bf16[512,256]{1,0:T(8,128)(2,1)}, u32[]{:S(2)}, u32[]{:S(2)}) %collective-permute-start.20) | collective-permute-done | bytes 262176 | tf_op jit(solution)/shard_map/wv_end_z1/ppermute | solution.py:277
  61.9 5.2 %shard_map.104 = (f32[512,128]{1,0:T(8,128)S(1)}, bf16[512,128]{1,0:T(8,128)(2,1)}, bf16[512,128]{1,0:T(8,128)(2,1)}, bf16[512,128]{1,0:T(8,128)(2,1)}) custom-call(s32[8]{0:T(128)S(1)} %stack.63.idx_ref, f32[2,128]{1,0:T(2,128)S(1)} %convert_bitcast_fusion.slots, bf16[256,8192]{1,0:T(8,128)(2,1)} %image.7, bf16[256,1024]{1,0:T(8,128)(2,1)} %copy-done.4, ...), custom_call_target="tpu_custom_call" | custom-call | flops 1073741824 | bytes 16777216 | tf_op jit(solution)/shard_map/pallas_call | solution.py:391
  67.1 1.7 %collective-permute-start.22 = (bf16[512,128]{1,0:T(8,128)(2,1)}, bf16[512,128]{1,0:T(8,128)(2,1)S(1)}, u32[]{:S(2)}, u32[]{:S(2)}) collective-permute-start(bf16[512,128]{1,0:T(8,128)(2,1)} %get-tuple-element.78), channel_id=1, source_target_pairs={{0,2},{2,0},{4,6},{6,4},{8,10},{10,8},{12,14},{14,12},{1,3},{3,1},... | collective-permute-start | bytes 393224 | tf_op jit(solution)/shard_map/value_y/ppermute | solution.py:281
  68.8 0.3 collective-permute-start.23
  69.0 1.6 %collective-permute-start.24 = (bf16[512,128]{1,0:T(8,128)(2,1)}, bf16[512,128]{1,0:T(8,128)(2,1)S(1)}, u32[]{:S(2)}, u32[]{:S(2)}) collective-permute-start(bf16[512,128]{1,0:T(8,128)(2,1)} %get-tuple-element.80), channel_id=1, source_target_pairs={{0,18},{2,16},{4,22},{6,20},{8,26},{10,24},{12,30},{14,28},{16,2},... | collective-permute-start | bytes 393224 | tf_op jit(solution)/shard_map/value_xy/ppermute | solution.py:294
  70.6 0.1 reshape.18.limit_ref
  70.8 0.2 shard_map.103.keys_ref
  71.0 2.0 %shard_map.105 = (bf16[2048,512]{1,0:T(8,128)(2,1)S(1)}, bf16[256,128]{1,0:T(8,128)(2,1)S(1)}) custom-call(f32[256,1]{1,0:T(8,128)S(1)} %reshape.18.limit_ref, bf16[528,128]{1,0:T(8,128)(2,1)S(1)} %shard_map.103.keys_ref, bf16[128,1024]{1,0:T(8,128)(2,1)S(1)} %constant_dynamic-update-slice_fusion.refs_0_, bf16[128,1024]{1,0:T(8,128)(2,1)S(1)} %collective-permute-done.21.refs_1_), custom_call_target="tpu_custom_call" | custom-call | tf_op jit(solution)/shard_map/pallas_call | solution.py:435
  73.0 0.6 collective-permute-done.22
  73.6 1.1 collective-permute-done.23
  74.7 1.2 %collective-permute-done.24 = bf16[512,128]{1,0:T(8,128)(2,1)S(1)} collective-permute-done((bf16[512,128]{1,0:T(8,128)(2,1)}, bf16[512,128]{1,0:T(8,128)(2,1)S(1)}, u32[]{:S(2)}, u32[]{:S(2)}) %collective-permute-start.24) | collective-permute-done | bytes 131104 | tf_op jit(solution)/shard_map/value_xy/ppermute | solution.py:294
  76.0 0.7 shard_map.106
  76.8 2.6 %collective-permute-start.26 = (bf16[64,1152]{1,0:T(8,128)(2,1)S(1)}, bf16[64,1152]{1,0:T(8,128)(2,1)S(1)}, u32[]{:S(2)}, u32[]{:S(2)}) collective-permute-start(bf16[64,1152]{1,0:T(8,128)(2,1)S(1)} %get-tuple-element.83), channel_id=1, source_target_pairs={{0,8},{2,10},{4,12},{6,14},{8,0},{10,2},{12,4},{14,6},{1,9},{3,11}... | collective-permute-start | bytes 442376 | tf_op jit(solution)/shard_map/sums_z2/ppermute | solution.py:277
  79.4 1.8 %collective-permute-start.27 = (bf16[64,1152]{1,0:T(8,128)(2,1)S(1)}, bf16[64,1152]{1,0:T(8,128)(2,1)S(1)}, u32[]{:S(2)}, u32[]{:S(2)}) collective-permute-start(bf16[64,1152]{1,0:T(8,128)(2,1)S(1)} %get-tuple-element.84), channel_id=1, source_target_pairs={{0,12},{2,14},{4,8},{6,10},{8,4},{10,6},{12,0},{14,2},{1,13},{3,15... | collective-permute-start | bytes 442376 | tf_op jit(solution)/shard_map/sums_z3/ppermute | solution.py:277
  81.2 1.9 %collective-permute-done.25.refs_1_ = bf16[64,1152]{1,0:T(8,128)(2,1)S(1)} collective-permute-done((bf16[64,1152]{1,0:T(8,128)(2,1)S(1)}, bf16[64,1152]{1,0:T(8,128)(2,1)S(1)}, u32[]{:S(2)}, u32[]{:S(2)}) %collective-permute-start.25) | collective-permute-done | bytes 147488 | tf_op jit(solution)/shard_map/sums_z1/ppermute | solution.py:277
  83.1 6.3 %collective-permute-done.26.refs_2_ = bf16[64,1152]{1,0:T(8,128)(2,1)S(1)} collective-permute-done((bf16[64,1152]{1,0:T(8,128)(2,1)S(1)}, bf16[64,1152]{1,0:T(8,128)(2,1)S(1)}, u32[]{:S(2)}, u32[]{:S(2)}) %collective-permute-start.26) | collective-permute-done | bytes 147488 | tf_op jit(solution)/shard_map/sums_z2/ppermute | solution.py:277
  89.4 0.9 shard_map.107.refs_0_
  90.4 2.2 %collective-permute-start.28 = (bf16[64,1024]{1,0:T(8,128)(2,1)S(1)}, bf16[64,1024]{1,0:T(8,128)(2,1)S(1)}, u32[]{:S(2)}, u32[]{:S(2)}) collective-permute-start(bf16[64,1024]{1,0:T(8,128)(2,1)S(1)} %shard_map.107.refs_0_), channel_id=1, source_target_pairs={{0,4},{2,6},{4,0},{6,2},{8,12},{10,14},{12,8},{14,10},{1,5},{3,7},... | collective-permute-start | bytes 393224 | tf_op jit(solution)/shard_map/attn_z1/ppermute | solution.py:277
  92.6 1.1 collective-permute-start.29
  93.6 1.4 %collective-permute-start.30 = (bf16[64,1024]{1,0:T(8,128)(2,1)S(1)}, bf16[64,1024]{1,0:T(8,128)(2,1)S(1)}, u32[]{:S(2)}, u32[]{:S(2)}) collective-permute-start(bf16[64,1024]{1,0:T(8,128)(2,1)S(1)} %shard_map.107.refs_0_), channel_id=1, source_target_pairs={{0,12},{2,14},{4,8},{6,10},{8,4},{10,6},{12,0},{14,2},{1,13},{3,15... | collective-permute-start | bytes 393224 | tf_op jit(solution)/shard_map/attn_z3/ppermute | solution.py:277
  95.0 1.4 %collective-permute-start.31 = (bf16[64,1024]{1,0:T(8,128)(2,1)S(1)}, bf16[64,1024]{1,0:T(8,128)(2,1)S(1)}, u32[]{:S(2)}, u32[]{:S(2)}) collective-permute-start(bf16[64,1024]{1,0:T(8,128)(2,1)S(1)} %shard_map.107.refs_0_), channel_id=1, source_target_pairs={{0,2},{2,0},{4,6},{6,4},{8,10},{10,8},{12,14},{14,12},{1,3},{3,1},... | collective-permute-start | bytes 393224 | tf_op jit(solution)/shard_map/attn0_y/ppermute | solution.py:281
  96.4 0.2 collective-permute-done.28.refs_1_
  96.6 0.9 collective-permute-start.32
  97.5 6.2 %collective-permute-done.29.refs_2_ = bf16[64,1024]{1,0:T(8,128)(2,1)S(1)} collective-permute-done((bf16[64,1024]{1,0:T(8,128)(2,1)S(1)}, bf16[64,1024]{1,0:T(8,128)(2,1)S(1)}, u32[]{:S(2)}, u32[]{:S(2)}) %collective-permute-start.29) | collective-permute-done | bytes 131104 | tf_op jit(solution)/shard_map/attn_z2/ppermute | solution.py:277
  103.6 1.0 collective-permute-start.33
  104.7 1.0 collective-permute-start.34
  105.7 0.1 stack.59.idx_ref
  105.8 2.8 %collective-permute-done.33.refs_6_ = bf16[64,1024]{1,0:T(8,128)(2,1)S(1)} collective-permute-done((bf16[64,1024]{1,0:T(8,128)(2,1)S(1)}, bf16[64,1024]{1,0:T(8,128)(2,1)S(1)}, u32[]{:S(2)}, u32[]{:S(2)}) %collective-permute-start.33) | collective-permute-done | bytes 131104 | tf_op jit(solution)/shard_map/attn2_y/ppermute | solution.py:281
  108.6 1.4 %collective-permute-done.34.refs_7_ = bf16[64,1024]{1,0:T(8,128)(2,1)S(1)} collective-permute-done((bf16[64,1024]{1,0:T(8,128)(2,1)S(1)}, bf16[64,1024]{1,0:T(8,128)(2,1)S(1)}, u32[]{:S(2)}, u32[]{:S(2)}) %collective-permute-start.34) | collective-permute-done | bytes 131104 | tf_op jit(solution)/shard_map/attn3_y/ppermute | solution.py:281
  110.0 2.2 %copy-done = bf16[2048,1024]{1,0:T(8,128)(2,1)S(1)} copy-done((bf16[2048,1024]{1,0:T(8,128)(2,1)S(1)}, bf16[2048,1024]{1,0:T(8,128)(2,1)}, u32[]{:S(2)}) %copy-start) | copy-done | bytes 4194328
  112.2 1.9 %shard_map.108 = (f32[128,1024]{1,0:T(8,128)S(1)}, bf16[128,1024]{1,0:T(8,128)(2,1)S(1)}) custom-call(s32[17]{0:T(128)S(1)} %stack.59.idx_ref, bf16[64,1024]{1,0:T(8,128)(2,1)S(1)} %shard_map.107.refs_0_, bf16[64,1024]{1,0:T(8,128)(2,1)S(1)} %collective-permute-done.28.refs_1_, bf16[64,1024]{1,0:T(8,128)(2,1)S(1)} %collective-permute-done.29.refs_2_, ...), custom_call_target="tpu_custom_call" | custom-call | tf_op jit(solution)/shard_map/pallas_call | solution.py:469
  114.9 0.8 collective-permute-done.35
  115.7 0.8 add_convert_fusion
  (60 shorter events, 0.6 us)
Async XLA Ops:
  0.0 9.3 %copy-start.11 = (bf16[32,2048]{1,0:T(8,128)(2,1)S(1)}, bf16[32,2048]{1,0:T(8,128)(2,1)}, u32[]{:S(2)}) copy-start(bf16[32,2048]{1,0:T(8,128)(2,1)} %param.15) | copy-start | bytes 393220
  0.0 41.4 %copy-start.12 = (s32[256]{0:T(256)S(1)}, s32[256]{0:T(256)}, u32[]{:S(2)}) copy-start(s32[256]{0:T(256)} %param.11) | copy-start | bytes 3076
  2.4 42.9 %copy-start.2 = (bf16[512,256]{1,0:T(8,128)(2,1)S(1)}, bf16[512,256]{1,0:T(8,128)(2,1)}, u32[]{:S(2)}) copy-start(bf16[512,256]{1,0:T(8,128)(2,1)} %get-tuple-element.46.refs_6_) | copy-start | bytes 786436
  2.4 9.6 %collective-permute-start = (bf16[512,256]{1,0:T(8,128)(2,1)}, bf16[512,256]{1,0:T(8,128)(2,1)S(1)}, u32[]{:S(2)}, u32[]{:S(2)}) collective-permute-start(bf16[512,256]{1,0:T(8,128)(2,1)} %get-tuple-element.46.refs_6_), channel_id=1, source_target_pairs={{0,4},{2,6},{4,0},{6,2},{8,12},{10,14},{12,8},{14,10},{1,5},{3,7},... | collective-permute-start | bytes 786440 | tf_op jit(solution)/shard_map/wk_z1/ppermute | solution.py:277
  5.5 7.2 %collective-permute-start.2 = (bf16[512,256]{1,0:T(8,128)(2,1)}, bf16[512,256]{1,0:T(8,128)(2,1)S(1)}, u32[]{:S(2)}, u32[]{:S(2)}) collective-permute-start(bf16[512,256]{1,0:T(8,128)(2,1)} %get-tuple-element.46.refs_6_), channel_id=1, source_target_pairs={{4,8},{6,10},{8,4},{10,6},{5,9},{7,11},{9,5},{11,7},{20,24},{22,26... | collective-permute-start | bytes 786440 | tf_op jit(solution)/shard_map/wk_z3/ppermute | solution.py:277
  6.2 18.3 %collective-permute-start.4 = (bf16[256,1024]{1,0:T(8,128)(2,1)}, bf16[256,1024]{1,0:T(8,128)(2,1)S(1)}, u32[]{:S(2)}, u32[]{:S(2)}) collective-permute-start(bf16[256,1024]{1,0:T(8,128)(2,1)} %get-tuple-element.47), channel_id=1, source_target_pairs={{0,2},{2,0},{4,6},{6,4},{8,10},{10,8},{12,14},{14,12},{1,3},{3,1},... | collective-permute-start | bytes 1572872 | tf_op jit(solution)/shard_map/image_y/ppermute | solution.py:281
  7.8 16.7 %collective-permute-start.5 = (bf16[256,1024]{1,0:T(8,128)(2,1)}, bf16[256,1024]{1,0:T(8,128)(2,1)S(1)}, u32[]{:S(2)}, u32[]{:S(2)}) collective-permute-start(bf16[256,1024]{1,0:T(8,128)(2,1)} %get-tuple-element.48), channel_id=1, source_target_pairs={{0,16},{16,0},{1,17},{17,1},{2,18},{18,2},{3,19},{19,3},{4,20},{20... | collective-permute-start | bytes 1572872 | tf_op jit(solution)/shard_map/image_x/ppermute | solution.py:289
  9.3 12.0 %collective-permute-start.6 = (bf16[32,1024]{1,0:T(8,128)(2,1)S(1)}, bf16[32,1024]{1,0:T(8,128)(2,1)S(1)}, u32[]{:S(2)}, u32[]{:S(2)}) collective-permute-start(bf16[32,1024]{1,0:T(8,128)(2,1)S(1)} %constant_dynamic-slice_fusion), channel_id=1, source_target_pairs={{0,2},{2,0},{4,6},{6,4},{8,10},{10,8},{12,14},{14,12},{1,3},{3,1},... | collective-permute-start | bytes 196616 | tf_op jit(solution)/shard_map/q_y/ppermute | solution.py:281
  12.0 9.3 %collective-permute-start.1 = (bf16[512,256]{1,0:T(8,128)(2,1)S(1)}, bf16[512,256]{1,0:T(8,128)(2,1)S(1)}, u32[]{:S(2)}, u32[]{:S(2)}) collective-permute-start(bf16[512,256]{1,0:T(8,128)(2,1)S(1)} %collective-permute-done.refs_7_), channel_id=1, source_target_pairs={{4,8},{6,10},{8,4},{10,6},{5,9},{7,11},{9,5},{11,7},{20,24},{22,26... | collective-permute-start | bytes 786440 | tf_op jit(solution)/shard_map/wk_across_z3/ppermute | solution.py:277
  12.7 28.8 %copy-start.9 = (bf16[512,256]{1,0:T(8,128)(2,1)}, bf16[512,256]{1,0:T(8,128)(2,1)S(1)}, u32[]{:S(2)}) copy-start(bf16[512,256]{1,0:T(8,128)(2,1)S(1)} %collective-permute-done.2.refs_10_) | copy-start | bytes 786436
  12.7 11.7 %collective-permute-start.3 = (bf16[512,256]{1,0:T(8,128)(2,1)S(1)}, bf16[512,256]{1,0:T(8,128)(2,1)S(1)}, u32[]{:S(2)}, u32[]{:S(2)}) collective-permute-start(bf16[512,256]{1,0:T(8,128)(2,1)S(1)} %collective-permute-done.2.refs_10_), channel_id=1, source_target_pairs={{4,0},{6,2},{8,12},{10,14},{5,1},{7,3},{9,13},{11,15},{20,16},{22,... | collective-permute-start | bytes 786440 | tf_op jit(solution)/shard_map/wk_out_z1/ppermute | solution.py:277
  24.5 15.3 %copy-start.4 = (bf16[256,1024]{1,0:T(8,128)(2,1)}, bf16[256,1024]{1,0:T(8,128)(2,1)S(1)}, u32[]{:S(2)}) copy-start(bf16[256,1024]{1,0:T(8,128)(2,1)S(1)} %collective-permute-done.4.refs_0_) | copy-start | bytes 1572868
  24.5 19.3 %copy-start.5 = (bf16[256,1024]{1,0:T(8,128)(2,1)}, bf16[256,1024]{1,0:T(8,128)(2,1)S(1)}, u32[]{:S(2)}) copy-start(bf16[256,1024]{1,0:T(8,128)(2,1)S(1)} %collective-permute-done.5.refs_2_) | copy-start | bytes 1572868
  24.5 6.6 %collective-permute-start.7 = (bf16[512,256]{1,0:T(8,128)(2,1)}, bf16[512,256]{1,0:T(8,128)(2,1)S(1)}, u32[]{:S(2)}, u32[]{:S(2)}) collective-permute-start(bf16[512,256]{1,0:T(8,128)(2,1)} %get-tuple-element.51.refs_6_), channel_id=1, source_target_pairs={{0,4},{2,6},{4,0},{6,2},{8,12},{10,14},{12,8},{14,10},{1,5},{3,7},... | collective-permute-start | bytes 786440 | tf_op jit(solution)/shard_map/wv_z1/ppermute | solution.py:277
  25.5 14.1 %collective-permute-start.10 = (bf16[256,1024]{1,0:T(8,128)(2,1)}, bf16[256,1024]{1,0:T(8,128)(2,1)}, u32[]{:S(2)}, u32[]{:S(2)}) collective-permute-start(bf16[256,1024]{1,0:T(8,128)(2,1)} %get-tuple-element.53), channel_id=1, source_target_pairs={{0,18},{2,16},{4,22},{6,20},{8,26},{10,24},{12,30},{14,28},{16,2},... | collective-permute-start | bytes 1572872 | tf_op jit(solution)/shard_map/image_xy/ppermute | solution.py:294
  28.0 11.7 %collective-permute-start.11 = (bf16[256,1024]{1,0:T(8,128)(2,1)S(1)}, bf16[256,1024]{1,0:T(8,128)(2,1)S(1)}, u32[]{:S(2)}, u32[]{:S(2)}) collective-permute-start(bf16[256,1024]{1,0:T(8,128)(2,1)S(1)} %collective-permute-done.4.refs_0_), channel_id=1, source_target_pairs={{0,1},{1,0},{2,3},{3,2},{4,5},{5,4},{6,7},{7,6},{8,9},{9,8},{10,11... | collective-permute-start | bytes 1572872 | tf_op jit(solution)/shard_map/image_core/ppermute | solution.py:285
  28.0 11.7 %collective-permute-start.12 = (bf16[256,1024]{1,0:T(8,128)(2,1)S(1)}, bf16[256,1024]{1,0:T(8,128)(2,1)S(1)}, u32[]{:S(2)}, u32[]{:S(2)}) collective-permute-start(bf16[256,1024]{1,0:T(8,128)(2,1)S(1)} %collective-permute-done.5.refs_2_), channel_id=1, source_target_pairs={{0,1},{1,0},{2,3},{3,2},{4,5},{5,4},{6,7},{7,6},{8,9},{9,8},{10,11... | collective-permute-start | bytes 1572872 | tf_op jit(solution)/shard_map/image_core/ppermute | solution.py:285
  28.5 3.9 %collective-permute-start.8 = (bf16[512,256]{1,0:T(8,128)(2,1)}, bf16[512,256]{1,0:T(8,128)(2,1)S(1)}, u32[]{:S(2)}, u32[]{:S(2)}) collective-permute-start(bf16[512,256]{1,0:T(8,128)(2,1)} %get-tuple-element.51.refs_6_), channel_id=1, source_target_pairs={{4,8},{6,10},{8,4},{10,6},{5,9},{7,11},{9,5},{11,7},{20,24},{22,26... | collective-permute-start | bytes 786440 | tf_op jit(solution)/shard_map/wv_z3/ppermute | solution.py:277
  31.1 8.6 %collective-permute-start.9 = (bf16[512,256]{1,0:T(8,128)(2,1)S(1)}, bf16[512,256]{1,0:T(8,128)(2,1)S(1)}, u32[]{:S(2)}, u32[]{:S(2)}) collective-permute-start(bf16[512,256]{1,0:T(8,128)(2,1)S(1)} %collective-permute-done.1.refs_8_), channel_id=1, source_target_pairs={{4,0},{6,2},{8,12},{10,14},{5,1},{7,3},{9,13},{11,15},{20,16},{22,... | collective-permute-start | bytes 786440 | tf_op jit(solution)/shard_map/wk_end_z1/ppermute | solution.py:277
  39.7 4.1 %copy-start.10 = (bf16[512,256]{1,0:T(8,128)(2,1)}, bf16[512,256]{1,0:T(8,128)(2,1)S(1)}, u32[]{:S(2)}) copy-start(bf16[512,256]{1,0:T(8,128)(2,1)S(1)} %collective-permute-done.9.refs_11_) | copy-start | bytes 786436
  39.7 0.8 copy-start.6
  39.7 1.0 copy-start.7
  39.7 5.5 %collective-permute-start.14 = (bf16[256,1024]{1,0:T(8,128)(2,1)}, bf16[256,1024]{1,0:T(8,128)(2,1)}, u32[]{:S(2)}, u32[]{:S(2)}) collective-permute-start(bf16[256,1024]{1,0:T(8,128)(2,1)} %collective-permute-done.10.refs_4_), channel_id=1, source_target_pairs={{0,1},{1,0},{2,3},{3,2},{4,5},{5,4},{6,7},{7,6},{8,9},{9,8},{10,11... | collective-permute-start | bytes 1572872 | tf_op jit(solution)/shard_map/image_core/ppermute | solution.py:285
  40.7 9.8 %collective-permute-start.13 = (bf16[512,256]{1,0:T(8,128)(2,1)S(1)}, bf16[512,256]{1,0:T(8,128)(2,1)S(1)}, u32[]{:S(2)}, u32[]{:S(2)}) collective-permute-start(bf16[512,256]{1,0:T(8,128)(2,1)S(1)} %collective-permute-done.7.refs_7_), channel_id=1, source_target_pairs={{4,8},{6,10},{8,4},{10,6},{5,9},{7,11},{9,5},{11,7},{20,24},{22,26... | collective-permute-start | bytes 786440 | tf_op jit(solution)/shard_map/wv_across_z3/ppermute | solution.py:277
  41.5 9.0 %collective-permute-start.15 = (bf16[64,1024]{1,0:T(8,128)(2,1)S(1)}, bf16[64,1024]{1,0:T(8,128)(2,1)S(1)}, u32[]{:S(2)}, u32[]{:S(2)}) collective-permute-start(bf16[64,1024]{1,0:T(8,128)(2,1)S(1)} %pad_maximum_fusion), channel_id=1, source_target_pairs={{0,4},{2,6},{4,0},{6,2},{8,12},{10,14},{12,8},{14,10},{1,5},{3,7},... | collective-permute-start | bytes 393224 | tf_op jit(solution)/shard_map/q_z1/ppermute | solution.py:277
  43.8 13.0 %copy-start.13 = (s32[256]{0:T(256)S(1)}, s32[256]{0:T(256)}, u32[]{:S(2)}) copy-start(s32[256]{0:T(256)} %param.16) | copy-start | bytes 3076
  43.8 18.0 %copy-start.1 = (bf16[512,256]{1,0:T(8,128)(2,1)S(1)}, bf16[512,256]{1,0:T(8,128)(2,1)}, u32[]{:S(2)}) copy-start(bf16[512,256]{1,0:T(8,128)(2,1)} %get-tuple-element.51.refs_6_) | copy-start | bytes 786436
  43.8 14.3 %collective-permute-start.19 = (bf16[512,256]{1,0:T(8,128)(2,1)S(1)}, bf16[512,256]{1,0:T(8,128)(2,1)S(1)}, u32[]{:S(2)}, u32[]{:S(2)}) collective-permute-start(bf16[512,256]{1,0:T(8,128)(2,1)S(1)} %collective-permute-done.8.refs_10_), channel_id=1, source_target_pairs={{4,0},{6,2},{8,12},{10,14},{5,1},{7,3},{9,13},{11,15},{20,16},{22,... | collective-permute-start | bytes 786440 | tf_op jit(solution)/shard_map/wv_out_z1/ppermute | solution.py:277
  50.5 11.4 %collective-permute-start.20 = (bf16[512,256]{1,0:T(8,128)(2,1)S(1)}, bf16[512,256]{1,0:T(8,128)(2,1)}, u32[]{:S(2)}, u32[]{:S(2)}) collective-permute-start(bf16[512,256]{1,0:T(8,128)(2,1)S(1)} %collective-permute-done.13.refs_8_), channel_id=1, source_target_pairs={{4,0},{6,2},{8,12},{10,14},{5,1},{7,3},{9,13},{11,15},{20,16},{22,... | collective-permute-start | bytes 786440 | tf_op jit(solution)/shard_map/wv_end_z1/ppermute | solution.py:277
  51.8 15.2 %collective-permute-start.21 = (bf16[128,1024]{1,0:T(8,128)(2,1)S(1)}, bf16[128,1024]{1,0:T(8,128)(2,1)S(1)}, u32[]{:S(2)}, u32[]{:S(2)}) collective-permute-start(bf16[128,1024]{1,0:T(8,128)(2,1)S(1)} %constant_dynamic-update-slice_fusion.refs_0_), channel_id=1, source_target_pairs={{0,8},{2,10},{4,12},{6,14},{8,0},{10,2},{12,4},{14,6},{1,9},{3,11}... | collective-permute-start | bytes 786440 | tf_op jit(solution)/shard_map/q_z2/ppermute | solution.py:277
  55.3 13.8 %collective-permute-start.17 = (f32[512,128]{1,0:T(8,128)}, f32[512,128]{1,0:T(8,128)S(1)}, u32[]{:S(2)}, u32[]{:S(2)}) collective-permute-start(f32[512,128]{1,0:T(8,128)} %get-tuple-element.66), channel_id=1, source_target_pairs={{0,16},{16,0},{1,17},{17,1},{2,18},{18,2},{3,19},{19,3},{4,20},{20... | collective-permute-start | bytes 786440 | tf_op jit(solution)/shard_map/key_x/ppermute | solution.py:289
  56.9 13.9 %collective-permute-start.16 = (f32[520,128]{1,0:T(8,128)}, f32[520,128]{1,0:T(8,128)S(1)}, u32[]{:S(2)}, u32[]{:S(2)}) collective-permute-start(f32[520,128]{1,0:T(8,128)} %get-tuple-element.65), channel_id=1, source_target_pairs={{0,2},{2,0},{4,6},{6,4},{8,10},{10,8},{12,14},{14,12},{1,3},{3,1},... | collective-permute-start | bytes 798728 | tf_op jit(solution)/shard_map/key_y/ppermute | solution.py:281
  58.1 12.7 %copy-start.3 = (f32[128]{0:T(128)S(1)}, f32[128]{0:T(128)}, u32[]{:S(2)}) copy-start(f32[128]{0:T(128)} %param.14) | copy-start | bytes 1540
  58.1 12.7 %collective-permute-start.18 = (f32[512,128]{1,0:T(8,128)S(1)}, f32[512,128]{1,0:T(8,128)S(1)}, u32[]{:S(2)}, u32[]{:S(2)}) collective-permute-start(f32[512,128]{1,0:T(8,128)S(1)} %get-tuple-element.67), channel_id=1, source_target_pairs={{0,18},{2,16},{4,22},{6,20},{8,26},{10,24},{12,30},{14,28},{16,2},... | collective-permute-start | bytes 786440 | tf_op jit(solution)/shard_map/key_xy/ppermute | solution.py:294
  67.1 6.5 %collective-permute-start.22 = (bf16[512,128]{1,0:T(8,128)(2,1)}, bf16[512,128]{1,0:T(8,128)(2,1)S(1)}, u32[]{:S(2)}, u32[]{:S(2)}) collective-permute-start(bf16[512,128]{1,0:T(8,128)(2,1)} %get-tuple-element.78), channel_id=1, source_target_pairs={{0,2},{2,0},{4,6},{6,4},{8,10},{10,8},{12,14},{14,12},{1,3},{3,1},... | collective-permute-start | bytes 393224 | tf_op jit(solution)/shard_map/value_y/ppermute | solution.py:281
  68.8 6.0 %collective-permute-start.23 = (bf16[512,128]{1,0:T(8,128)(2,1)}, bf16[512,128]{1,0:T(8,128)(2,1)S(1)}, u32[]{:S(2)}, u32[]{:S(2)}) collective-permute-start(bf16[512,128]{1,0:T(8,128)(2,1)} %get-tuple-element.79), channel_id=1, source_target_pairs={{0,16},{16,0},{1,17},{17,1},{2,18},{18,2},{3,19},{19,3},{4,20},{20... | collective-permute-start | bytes 393224 | tf_op jit(solution)/shard_map/value_x/ppermute | solution.py:289
  69.0 6.9 %collective-permute-start.24 = (bf16[512,128]{1,0:T(8,128)(2,1)}, bf16[512,128]{1,0:T(8,128)(2,1)S(1)}, u32[]{:S(2)}, u32[]{:S(2)}) collective-permute-start(bf16[512,128]{1,0:T(8,128)(2,1)} %get-tuple-element.80), channel_id=1, source_target_pairs={{0,18},{2,16},{4,22},{6,20},{8,26},{10,24},{12,30},{14,28},{16,2},... | collective-permute-start | bytes 393224 | tf_op jit(solution)/shard_map/value_xy/ppermute | solution.py:294
  76.0 39.7 %copy-start.8 = (bf16[128,1024]{1,0:T(8,128)(2,1)S(1)}, bf16[128,1024]{1,0:T(8,128)(2,1)}, u32[]{:S(2)}) copy-start(bf16[128,1024]{1,0:T(8,128)(2,1)} %param.17) | copy-start | bytes 786436
  76.7 6.4 %collective-permute-start.25 = (bf16[64,1152]{1,0:T(8,128)(2,1)S(1)}, bf16[64,1152]{1,0:T(8,128)(2,1)S(1)}, u32[]{:S(2)}, u32[]{:S(2)}) collective-permute-start(bf16[64,1152]{1,0:T(8,128)(2,1)S(1)} %get-tuple-element.82), channel_id=1, source_target_pairs={{0,4},{2,6},{4,0},{6,2},{8,12},{10,14},{12,8},{14,10},{1,5},{3,7},... | collective-permute-start | bytes 442376 | tf_op jit(solution)/shard_map/sums_z1/ppermute | solution.py:277
  76.8 12.6 %collective-permute-start.26 = (bf16[64,1152]{1,0:T(8,128)(2,1)S(1)}, bf16[64,1152]{1,0:T(8,128)(2,1)S(1)}, u32[]{:S(2)}, u32[]{:S(2)}) collective-permute-start(bf16[64,1152]{1,0:T(8,128)(2,1)S(1)} %get-tuple-element.83), channel_id=1, source_target_pairs={{0,8},{2,10},{4,12},{6,14},{8,0},{10,2},{12,4},{14,6},{1,9},{3,11}... | collective-permute-start | bytes 442376 | tf_op jit(solution)/shard_map/sums_z2/ppermute | solution.py:277
  79.4 10.1 %collective-permute-start.27 = (bf16[64,1152]{1,0:T(8,128)(2,1)S(1)}, bf16[64,1152]{1,0:T(8,128)(2,1)S(1)}, u32[]{:S(2)}, u32[]{:S(2)}) collective-permute-start(bf16[64,1152]{1,0:T(8,128)(2,1)S(1)} %get-tuple-element.84), channel_id=1, source_target_pairs={{0,12},{2,14},{4,8},{6,10},{8,4},{10,6},{12,0},{14,2},{1,13},{3,15... | collective-permute-start | bytes 442376 | tf_op jit(solution)/shard_map/sums_z3/ppermute | solution.py:277
  90.4 6.2 %collective-permute-start.28 = (bf16[64,1024]{1,0:T(8,128)(2,1)S(1)}, bf16[64,1024]{1,0:T(8,128)(2,1)S(1)}, u32[]{:S(2)}, u32[]{:S(2)}) collective-permute-start(bf16[64,1024]{1,0:T(8,128)(2,1)S(1)} %shard_map.107.refs_0_), channel_id=1, source_target_pairs={{0,4},{2,6},{4,0},{6,2},{8,12},{10,14},{12,8},{14,10},{1,5},{3,7},... | collective-permute-start | bytes 393224 | tf_op jit(solution)/shard_map/attn_z1/ppermute | solution.py:277
  92.6 11.1 %collective-permute-start.29 = (bf16[64,1024]{1,0:T(8,128)(2,1)S(1)}, bf16[64,1024]{1,0:T(8,128)(2,1)S(1)}, u32[]{:S(2)}, u32[]{:S(2)}) collective-permute-start(bf16[64,1024]{1,0:T(8,128)(2,1)S(1)} %shard_map.107.refs_0_), channel_id=1, source_target_pairs={{0,8},{2,10},{4,12},{6,14},{8,0},{10,2},{12,4},{14,6},{1,9},{3,11}... | collective-permute-start | bytes 393224 | tf_op jit(solution)/shard_map/attn_z2/ppermute | solution.py:277
  93.6 11.1 %collective-permute-start.30 = (bf16[64,1024]{1,0:T(8,128)(2,1)S(1)}, bf16[64,1024]{1,0:T(8,128)(2,1)S(1)}, u32[]{:S(2)}, u32[]{:S(2)}) collective-permute-start(bf16[64,1024]{1,0:T(8,128)(2,1)S(1)} %shard_map.107.refs_0_), channel_id=1, source_target_pairs={{0,12},{2,14},{4,8},{6,10},{8,4},{10,6},{12,0},{14,2},{1,13},{3,15... | collective-permute-start | bytes 393224 | tf_op jit(solution)/shard_map/attn_z3/ppermute | solution.py:277
  95.0 10.8 %collective-permute-start.31 = (bf16[64,1024]{1,0:T(8,128)(2,1)S(1)}, bf16[64,1024]{1,0:T(8,128)(2,1)S(1)}, u32[]{:S(2)}, u32[]{:S(2)}) collective-permute-start(bf16[64,1024]{1,0:T(8,128)(2,1)S(1)} %shard_map.107.refs_0_), channel_id=1, source_target_pairs={{0,2},{2,0},{4,6},{6,4},{8,10},{10,8},{12,14},{14,12},{1,3},{3,1},... | collective-permute-start | bytes 393224 | tf_op jit(solution)/shard_map/attn0_y/ppermute | solution.py:281
  96.6 9.2 %collective-permute-start.32 = (bf16[64,1024]{1,0:T(8,128)(2,1)S(1)}, bf16[64,1024]{1,0:T(8,128)(2,1)S(1)}, u32[]{:S(2)}, u32[]{:S(2)}) collective-permute-start(bf16[64,1024]{1,0:T(8,128)(2,1)S(1)} %collective-permute-done.28.refs_1_), channel_id=1, source_target_pairs={{0,2},{2,0},{4,6},{6,4},{8,10},{10,8},{12,14},{14,12},{1,3},{3,1},... | collective-permute-start | bytes 393224 | tf_op jit(solution)/shard_map/attn1_y/ppermute | solution.py:281
  103.6 5.0 %collective-permute-start.33 = (bf16[64,1024]{1,0:T(8,128)(2,1)S(1)}, bf16[64,1024]{1,0:T(8,128)(2,1)S(1)}, u32[]{:S(2)}, u32[]{:S(2)}) collective-permute-start(bf16[64,1024]{1,0:T(8,128)(2,1)S(1)} %collective-permute-done.29.refs_2_), channel_id=1, source_target_pairs={{0,2},{2,0},{4,6},{6,4},{8,10},{10,8},{12,14},{14,12},{1,3},{3,1},... | collective-permute-start | bytes 393224 | tf_op jit(solution)/shard_map/attn2_y/ppermute | solution.py:281
  104.7 5.3 %collective-permute-start.34 = (bf16[64,1024]{1,0:T(8,128)(2,1)S(1)}, bf16[64,1024]{1,0:T(8,128)(2,1)S(1)}, u32[]{:S(2)}, u32[]{:S(2)}) collective-permute-start(bf16[64,1024]{1,0:T(8,128)(2,1)S(1)} %collective-permute-done.30.refs_3_), channel_id=1, source_target_pairs={{0,2},{2,0},{4,6},{6,4},{8,10},{10,8},{12,14},{14,12},{1,3},{3,1},... | collective-permute-start | bytes 393224 | tf_op jit(solution)/shard_map/attn3_y/ppermute | solution.py:281
  110.0 2.2 %copy-start = (bf16[2048,1024]{1,0:T(8,128)(2,1)S(1)}, bf16[2048,1024]{1,0:T(8,128)(2,1)}, u32[]{:S(2)}) copy-start(bf16[2048,1024]{1,0:T(8,128)(2,1)} %refs_8_.1) | copy-start | bytes 12582916
  114.1 1.6 %collective-permute-start.35 = (bf16[128,1024]{1,0:T(8,128)(2,1)S(1)}, bf16[128,1024]{1,0:T(8,128)(2,1)S(1)}, u32[]{:S(2)}, u32[]{:S(2)}) collective-permute-start(bf16[128,1024]{1,0:T(8,128)(2,1)S(1)} %get-tuple-element.86), channel_id=1, source_target_pairs={{0,1},{1,0},{2,3},{3,2},{4,5},{5,4},{6,7},{7,6},{8,9},{9,8},{10,11... | collective-permute-start | bytes 786440 | tf_op jit(solution)/shard_map/proj_core/ppermute | solution.py:285

commit v7 on v6

--- a/solution.py
+++ b/solution.py
@@ -196,10 +196,11 @@
         figures_ref[i * rows : (i + 1) * rows, :] = figures.astype(BF16)
 
 
-def value_kernel(n, heads, expo_ref, figures_ref, values_ref, *outs):
+def value_kernel(n, heads, expo_ref, figures_ref, keep, got_y, got_x, got_both, *outs):
     rows = figures_ref.shape[0] // n
+    values = ((keep[...] + got_y[...].astype(F32)) + (got_x[...].astype(F32) + got_both[...].astype(F32))).astype(BF16)
     for i in range(n):
-        acc = dot(expo_ref[i * heads * rows : (i + 1) * heads * rows, :], values_ref[...]).astype(BF16)
+        acc = dot(expo_ref[i * heads * rows : (i + 1) * heads * rows, :], values).astype(BF16)
         for j in range(heads):
             outs[i][:, j * HD : (j + 1) * HD] = acc[j * rows : (j + 1) * rows, :]
         outs[i][:, heads * HD :] = figures_ref[i * rows : (i + 1) * rows, :]
@@ -228,13 +229,25 @@
 
 def proj_kernel(n, idx_ref, *refs):
     pieces = refs[:n]
-    w_ref, keep_ref, send_ref, a_ref, p_ref = refs[n:]
+    far_ref, keep_ref, send_ref, a_ref, p_ref, w_ref, sems = refs[n:]
     rows, width = pieces[0].shape
+    steps, depth = w_ref.shape[:2]
+    copies = [
+        pltpu.make_async_copy(far_ref.at[pl.ds(i * depth, depth), :], w_ref.at[i], sems.at[i]) for i in range(steps)
+    ]
+    for c in copies:
+        c.start()
     for k in range(n):
         at_row = pl.multiple_of(idx_ref[1 + 2 * k] * rows, rows)
         at_col = pl.multiple_of(idx_ref[2 + 2 * k] * width, width)
         a_ref[pl.ds(at_row, rows), pl.ds(at_col, width)] = pieces[k][...]
-    p_ref[...] = dot(a_ref[...], w_ref[...])
+    for i, c in enumerate(copies):
+        c.wait()
+        part = dot(a_ref[:, i * depth : (i + 1) * depth], w_ref[i])
+        if i == 0:
+            p_ref[...] = part
+        else:
+            p_ref[...] += part
     size = keep_ref.shape[0]
     core = idx_ref[0]
     keep_ref[...] = p_ref[pl.ds(pl.multiple_of(core * size, size), size), :]
@@ -443,15 +456,13 @@
         scratch_shapes=[pltpu.VMEM((per_kv * rows, HD), BF16)],
         compiler_params=PARAMS,
     )(limits, packed, *q_pieces)
-    value_y, value_x, value_both = (part.astype(F32) for part in value_parts)
-    values = ((keep + value_y) + (value_x + value_both)).astype(BF16)
     sums = pl.pallas_call(
         functools.partial(value_kernel, lines, per_kv),
         out_shape=(jax.ShapeDtypeStruct((rows, q_half + HD), BF16),) * lines,
-        in_specs=[WHOLE] * 3,
+        in_specs=[WHOLE] * 6,
         out_specs=(WHOLE,) * lines,
         compiler_params=PARAMS,
-    )(expo, figures, values)
+    )(expo, figures, keep, *value_parts)
     sums = [sums[0]] + [along("sums", sums[d], d) for d in range(1, lines)]
     attn = pl.pallas_call(
         functools.partial(combine_kernel, lines, per_kv),
@@ -472,10 +483,15 @@
             jax.ShapeDtypeStruct((out_rows // 2, out_cols), F32),
             jax.ShapeDtypeStruct((out_rows // 2, out_cols), BF16),
         ),
-        in_specs=[scalars] + [WHOLE] * (2 * lines + 1),
+        in_specs=[scalars] + [WHOLE] * (2 * lines) + [FREE],
         out_specs=(WHOLE, WHOLE),
-        scratch_shapes=[pltpu.VMEM((out_rows, 2 * q_half), BF16), pltpu.VMEM((out_rows, out_cols), F32)],
-        compiler_params=PARAMS,
+        scratch_shapes=[
+            pltpu.VMEM((out_rows, 2 * q_half), BF16),
+            pltpu.VMEM((out_rows, out_cols), F32),
+            pltpu.VMEM((4, q_half // 2, out_cols), BF16),
+            pltpu.SemaphoreType.DMA((4,)),
+        ],
+        compiler_params=BIG,
     )(jnp.stack([core] + [i for pair in where for i in pair]), *mine, *other, out_weight)
     head_total = keep + over_core("proj", send).astype(F32)
     return (text_hidden.astype(F32) + jnp.tanh(attn_gate[0]) * head_total).astype(BF16)

time: 117 us -> 116 us (level)
  local copies, waits for them, and re-layouts: 3.57 us -> 1.39 us
  Pallas kernels: 20.5 us -> 21.9 us
    unnamed x29 -> x27, local copies, waits for them, and re-layouts: 3.15 us -> 0.97 us
    pallas_call x1, Pallas kernels: 1.89 us -> 3.28 us  [body(): pl.pallas_call(functools.partial(proj_kernel, 2 * lines), out_shape=(jax....]
where the time goes in v7:
time: 116 us
  waiting for transfers between devices  46.1 us (40%)
  starting transfers between devices  44.5 us (38%)
  Pallas kernels  21.9 us (19%)
  local copies, waits for them, and re-layouts  1.39 us (1%)
    ppermute x18, waiting for transfers between devices, along(): lax.ppermute(array, 'blk', [(b, b ^ 2 * d) for b in range(nblk) if ok(b /...  30.9 us
    ppermute x18, starting transfers between devices, along(): lax.ppermute(array, 'blk', [(b, b ^ 2 * d) for b in range(nblk) if ok(b /...  27 us
    ppermute x8, waiting for transfers between devices, over_y(): return lax.ppermute(array, 'blk', swap_y)  12 us
    pallas_call x2, Pallas kernels, project(): pl.pallas_call(functools.partial(project_kernel, sources, extra), out_sha...  10.4 us
    ppermute x8, starting transfers between devices, over_y(): return lax.ppermute(array, 'blk', swap_y)  8.83 us
    ppermute x3, starting transfers between devices, over_both(): return lax.ppermute(array, ('groups', 'blk'), pairs)  4.74 us
    pallas_call x2, Pallas kernels, shares(): pl.pallas_call(functools.partial(share_kernel, flips, half_lines), out_sh...  4.45 us
    pallas_call x1, Pallas kernels, body(): pl.pallas_call(functools.partial(proj_kernel, 2 * lines), out_shape=(jax....  3.28 us
  transfers between devices with their start and end apart: 36, of which 16 were waited for; matrix products, arithmetic and copies ran while one was open for 0% of the time, Pallas kernels for 13%

profile of v7, /device:TPU:0, one launch (start us, length us, event | category | flops | bytes accessed | tf_op | source)
XLA Modules:
  0.0 115.9 jit_solution(2519095111009216575)
XLA Ops:
  0.0 2.4 %shard_map.100 = (bf16[256,1024]{1,0:T(8,128)(2,1)}, bf16[256,1024]{1,0:T(8,128)(2,1)}, bf16[512,256]{1,0:T(8,128)(2,1)}) custom-call(bf16[256,8192]{1,0:T(8,128)(2,1)} %image.7, bf16[1024,256]{1,0:T(8,128)(2,1)} %refs_0_.2), custom_call_target="tpu_custom_call" | custom-call | tf_op jit(solution)/shard_map/pallas_call | solution.py:337
  2.4 3.1 %collective-permute-start = (bf16[512,256]{1,0:T(8,128)(2,1)}, bf16[512,256]{1,0:T(8,128)(2,1)S(1)}, u32[]{:S(2)}, u32[]{:S(2)}) collective-permute-start(bf16[512,256]{1,0:T(8,128)(2,1)} %get-tuple-element.46.refs_6_), channel_id=1, source_target_pairs={{0,4},{2,6},{4,0},{6,2},{8,12},{10,14},{12,8},{14,10},{1,5},{3,7},... | collective-permute-start | bytes 786440 | tf_op jit(solution)/shard_map/wk_z1/ppermute | solution.py:290
  5.5 0.7 collective-permute-start.2
  6.2 1.6 %collective-permute-start.4 = (bf16[256,1024]{1,0:T(8,128)(2,1)}, bf16[256,1024]{1,0:T(8,128)(2,1)S(1)}, u32[]{:S(2)}, u32[]{:S(2)}) collective-permute-start(bf16[256,1024]{1,0:T(8,128)(2,1)} %get-tuple-element.47), channel_id=1, source_target_pairs={{0,2},{2,0},{4,6},{6,4},{8,10},{10,8},{12,14},{14,12},{1,3},{3,1},... | collective-permute-start | bytes 1572872 | tf_op jit(solution)/shard_map/image_y/ppermute | solution.py:294
  7.8 1.5 %collective-permute-start.5 = (bf16[256,1024]{1,0:T(8,128)(2,1)}, bf16[256,1024]{1,0:T(8,128)(2,1)S(1)}, u32[]{:S(2)}, u32[]{:S(2)}) collective-permute-start(bf16[256,1024]{1,0:T(8,128)(2,1)} %get-tuple-element.48), channel_id=1, source_target_pairs={{0,16},{16,0},{1,17},{17,1},{2,18},{18,2},{3,19},{19,3},{4,20},{20... | collective-permute-start | bytes 1572872 | tf_op jit(solution)/shard_map/image_x/ppermute | solution.py:302
  9.3 0.6 collective-permute-start.6
  9.9 2.0 %shard_map.101 = (bf16[256,1024]{1,0:T(8,128)(2,1)}, bf16[512,256]{1,0:T(8,128)(2,1)}) custom-call(bf16[256,8192]{1,0:T(8,128)(2,1)} %image.7, bf16[1024,256]{1,0:T(8,128)(2,1)} %refs_0_.3), custom_call_target="tpu_custom_call" | custom-call | tf_op jit(solution)/shard_map/pallas_call | solution.py:337
  11.9 0.1 collective-permute-done.refs_7_
  12.0 0.7 collective-permute-start.1
  12.7 1.3 %collective-permute-start.3 = (bf16[512,256]{1,0:T(8,128)(2,1)S(1)}, bf16[512,256]{1,0:T(8,128)(2,1)S(1)}, u32[]{:S(2)}, u32[]{:S(2)}) collective-permute-start(bf16[512,256]{1,0:T(8,128)(2,1)S(1)} %collective-permute-done.2.refs_10_), channel_id=1, source_target_pairs={{4,0},{6,2},{8,12},{10,14},{5,1},{7,3},{9,13},{11,15},{20,16},{22,... | collective-permute-start | bytes 786440 | tf_op jit(solution)/shard_map/wk_out_z1/ppermute | solution.py:290
  14.0 7.2 %collective-permute-done.6 = bf16[32,1024]{1,0:T(8,128)(2,1)S(1)} collective-permute-done((bf16[32,1024]{1,0:T(8,128)(2,1)S(1)}, bf16[32,1024]{1,0:T(8,128)(2,1)S(1)}, u32[]{:S(2)}, u32[]{:S(2)}) %collective-permute-start.6) | collective-permute-done | bytes 65568 | tf_op jit(solution)/shard_map/q_y/ppermute | solution.py:294
  21.3 3.1 %collective-permute-done.3.refs_9_ = bf16[512,256]{1,0:T(8,128)(2,1)S(1)} collective-permute-done((bf16[512,256]{1,0:T(8,128)(2,1)S(1)}, bf16[512,256]{1,0:T(8,128)(2,1)S(1)}, u32[]{:S(2)}, u32[]{:S(2)}) %collective-permute-start.3) | collective-permute-done | bytes 262176 | tf_op jit(solution)/shard_map/wk_out_z1/ppermute | solution.py:290
  24.5 1.1 collective-permute-start.7
  25.5 2.4 %collective-permute-start.10 = (bf16[256,1024]{1,0:T(8,128)(2,1)}, bf16[256,1024]{1,0:T(8,128)(2,1)}, u32[]{:S(2)}, u32[]{:S(2)}) collective-permute-start(bf16[256,1024]{1,0:T(8,128)(2,1)} %get-tuple-element.53), channel_id=1, source_target_pairs={{0,18},{2,16},{4,22},{6,20},{8,26},{10,24},{12,30},{14,28},{16,2},... | collective-permute-start | bytes 1572872 | tf_op jit(solution)/shard_map/image_xy/ppermute | solution.py:307
  28.0 0.5 collective-permute-start.12
  28.5 0.7 collective-permute-start.8
  29.2 1.9 %collective-permute-done.7.refs_7_ = bf16[512,256]{1,0:T(8,128)(2,1)S(1)} collective-permute-done((bf16[512,256]{1,0:T(8,128)(2,1)}, bf16[512,256]{1,0:T(8,128)(2,1)S(1)}, u32[]{:S(2)}, u32[]{:S(2)}) %collective-permute-start.7) | collective-permute-done | bytes 262176 | tf_op jit(solution)/shard_map/wv_z1/ppermute | solution.py:290
  31.1 1.3 %collective-permute-start.9 = (bf16[512,256]{1,0:T(8,128)(2,1)S(1)}, bf16[512,256]{1,0:T(8,128)(2,1)S(1)}, u32[]{:S(2)}, u32[]{:S(2)}) collective-permute-start(bf16[512,256]{1,0:T(8,128)(2,1)S(1)} %collective-permute-done.1.refs_8_), channel_id=1, source_target_pairs={{4,0},{6,2},{8,12},{10,14},{5,1},{7,3},{9,13},{11,15},{20,16},{22,... | collective-permute-start | bytes 786440 | tf_op jit(solution)/shard_map/wk_end_z1/ppermute | solution.py:290
  32.4 7.3 %collective-permute-done.9.refs_11_ = bf16[512,256]{1,0:T(8,128)(2,1)S(1)} collective-permute-done((bf16[512,256]{1,0:T(8,128)(2,1)S(1)}, bf16[512,256]{1,0:T(8,128)(2,1)S(1)}, u32[]{:S(2)}, u32[]{:S(2)}) %collective-permute-start.9) | collective-permute-done | bytes 262176 | tf_op jit(solution)/shard_map/wk_end_z1/ppermute | solution.py:290
  39.8 0.7 copy-done.5
  40.5 0.2 copy-done.6
  40.7 0.7 collective-permute-start.13
  41.4 0.1 stack.63.idx_ref
  41.5 2.3 %collective-permute-start.15 = (bf16[64,1024]{1,0:T(8,128)(2,1)S(1)}, bf16[64,1024]{1,0:T(8,128)(2,1)S(1)}, u32[]{:S(2)}, u32[]{:S(2)}) collective-permute-start(bf16[64,1024]{1,0:T(8,128)(2,1)S(1)} %pad_maximum_fusion), channel_id=1, source_target_pairs={{0,4},{2,6},{4,0},{6,2},{8,12},{10,14},{12,8},{14,10},{1,5},{3,7},... | collective-permute-start | bytes 393224 | tf_op jit(solution)/shard_map/q_z1/ppermute | solution.py:290
  43.8 1.4 %collective-permute-start.19 = (bf16[512,256]{1,0:T(8,128)(2,1)S(1)}, bf16[512,256]{1,0:T(8,128)(2,1)S(1)}, u32[]{:S(2)}, u32[]{:S(2)}) collective-permute-start(bf16[512,256]{1,0:T(8,128)(2,1)S(1)} %collective-permute-done.8.refs_10_), channel_id=1, source_target_pairs={{4,0},{6,2},{8,12},{10,14},{5,1},{7,3},{9,13},{11,15},{20,16},{22,... | collective-permute-start | bytes 786440 | tf_op jit(solution)/shard_map/wv_out_z1/ppermute | solution.py:290
  45.3 5.2 %shard_map.102 = (f32[512,128]{1,0:T(8,128)S(1)}, f32[520,128]{1,0:T(8,128)}, f32[512,128]{1,0:T(8,128)}, f32[512,128]{1,0:T(8,128)S(1)}) custom-call(s32[8]{0:T(128)S(1)} %stack.63.idx_ref, f32[2,128]{1,0:T(2,128)S(1)} %convert_bitcast_fusion.slots, bf16[256,8192]{1,0:T(8,128)(2,1)} %image.7, bf16[256,1024]{1,0:T(8,128)(2,1)} %copy-done.3, ...), custom_call_target="tpu_custom_call" | custom-call | flops 1073741824 | bytes 16777216 | tf_op jit(solution)/shard_map/pallas_call | solution.py:404
  50.5 1.3 %collective-permute-start.20 = (bf16[512,256]{1,0:T(8,128)(2,1)S(1)}, bf16[512,256]{1,0:T(8,128)(2,1)}, u32[]{:S(2)}, u32[]{:S(2)}) collective-permute-start(bf16[512,256]{1,0:T(8,128)(2,1)S(1)} %collective-permute-done.13.refs_8_), channel_id=1, source_target_pairs={{4,0},{6,2},{8,12},{10,14},{5,1},{7,3},{9,13},{11,15},{20,16},{22,... | collective-permute-start | bytes 786440 | tf_op jit(solution)/shard_map/wv_end_z1/ppermute | solution.py:290
  51.8 3.5 %collective-permute-start.21 = (bf16[128,1024]{1,0:T(8,128)(2,1)S(1)}, bf16[128,1024]{1,0:T(8,128)(2,1)S(1)}, u32[]{:S(2)}, u32[]{:S(2)}) collective-permute-start(bf16[128,1024]{1,0:T(8,128)(2,1)S(1)} %constant_dynamic-update-slice_fusion.refs_0_), channel_id=1, source_target_pairs={{0,8},{2,10},{4,12},{6,14},{8,0},{10,2},{12,4},{14,6},{1,9},{3,11}... | collective-permute-start | bytes 786440 | tf_op jit(solution)/shard_map/q_z2/ppermute | solution.py:290
  55.3 1.5 %collective-permute-start.17 = (f32[512,128]{1,0:T(8,128)}, f32[512,128]{1,0:T(8,128)S(1)}, u32[]{:S(2)}, u32[]{:S(2)}) collective-permute-start(f32[512,128]{1,0:T(8,128)} %get-tuple-element.66), channel_id=1, source_target_pairs={{0,16},{16,0},{1,17},{17,1},{2,18},{18,2},{3,19},{19,3},{4,20},{20... | collective-permute-start | bytes 786440 | tf_op jit(solution)/shard_map/key_x/ppermute | solution.py:302
  56.8 0.1 reshape.13
  56.9 1.3 %collective-permute-start.16 = (f32[520,128]{1,0:T(8,128)}, f32[520,128]{1,0:T(8,128)S(1)}, u32[]{:S(2)}, u32[]{:S(2)}) collective-permute-start(f32[520,128]{1,0:T(8,128)} %get-tuple-element.65), channel_id=1, source_target_pairs={{0,2},{2,0},{4,6},{6,4},{8,10},{10,8},{12,14},{14,12},{1,3},{3,1},... | collective-permute-start | bytes 798728 | tf_op jit(solution)/shard_map/key_y/ppermute | solution.py:294
  58.2 0.7 collective-permute-start.18
  58.9 3.0 %collective-permute-done.20.refs_11_ = bf16[512,256]{1,0:T(8,128)(2,1)} collective-permute-done((bf16[512,256]{1,0:T(8,128)(2,1)S(1)}, bf16[512,256]{1,0:T(8,128)(2,1)}, u32[]{:S(2)}, u32[]{:S(2)}) %collective-permute-start.20) | collective-permute-done | bytes 262176 | tf_op jit(solution)/shard_map/wv_end_z1/ppermute | solution.py:290
  61.9 5.2 %shard_map.104 = (f32[512,128]{1,0:T(8,128)S(1)}, bf16[512,128]{1,0:T(8,128)(2,1)}, bf16[512,128]{1,0:T(8,128)(2,1)}, bf16[512,128]{1,0:T(8,128)(2,1)}) custom-call(s32[8]{0:T(128)S(1)} %stack.63.idx_ref, f32[2,128]{1,0:T(2,128)S(1)} %convert_bitcast_fusion.slots, bf16[256,8192]{1,0:T(8,128)(2,1)} %image.7, bf16[256,1024]{1,0:T(8,128)(2,1)} %copy-done.3, ...), custom_call_target="tpu_custom_call" | custom-call | flops 1073741824 | bytes 16777216 | tf_op jit(solution)/shard_map/pallas_call | solution.py:404
  67.1 1.7 %collective-permute-start.22 = (bf16[512,128]{1,0:T(8,128)(2,1)}, bf16[512,128]{1,0:T(8,128)(2,1)S(1)}, u32[]{:S(2)}, u32[]{:S(2)}) collective-permute-start(bf16[512,128]{1,0:T(8,128)(2,1)} %get-tuple-element.78), channel_id=1, source_target_pairs={{0,2},{2,0},{4,6},{6,4},{8,10},{10,8},{12,14},{14,12},{1,3},{3,1},... | collective-permute-start | bytes 393224 | tf_op jit(solution)/shard_map/value_y/ppermute | solution.py:294
  68.8 0.3 collective-permute-start.23
  69.1 1.6 %collective-permute-start.24 = (bf16[512,128]{1,0:T(8,128)(2,1)}, bf16[512,128]{1,0:T(8,128)(2,1)S(1)}, u32[]{:S(2)}, u32[]{:S(2)}) collective-permute-start(bf16[512,128]{1,0:T(8,128)(2,1)} %get-tuple-element.80), channel_id=1, source_target_pairs={{0,18},{2,16},{4,22},{6,20},{8,26},{10,24},{12,30},{14,28},{16,2},... | collective-permute-start | bytes 393224 | tf_op jit(solution)/shard_map/value_xy/ppermute | solution.py:307
  70.6 0.1 reshape.18.limit_ref
  70.8 0.2 shard_map.103.keys_ref
  71.0 2.0 %shard_map.105 = (bf16[2048,512]{1,0:T(8,128)(2,1)S(1)}, bf16[256,128]{1,0:T(8,128)(2,1)S(1)}) custom-call(f32[256,1]{1,0:T(8,128)S(1)} %reshape.18.limit_ref, bf16[528,128]{1,0:T(8,128)(2,1)S(1)} %shard_map.103.keys_ref, bf16[128,1024]{1,0:T(8,128)(2,1)S(1)} %constant_dynamic-update-slice_fusion.refs_0_, bf16[128,1024]{1,0:T(8,128)(2,1)S(1)} %collective-permute-done.21.refs_1_), custom_call_target="tpu_custom_call" | custom-call | tf_op jit(solution)/shard_map/pallas_call | solution.py:448
  73.0 0.6 collective-permute-done.22.got_y
  73.6 1.1 collective-permute-done.23.got_x
  74.7 1.2 %collective-permute-done.24.got_both = bf16[512,128]{1,0:T(8,128)(2,1)S(1)} collective-permute-done((bf16[512,128]{1,0:T(8,128)(2,1)}, bf16[512,128]{1,0:T(8,128)(2,1)S(1)}, u32[]{:S(2)}, u32[]{:S(2)}) %collective-permute-start.24) | collective-permute-done | bytes 131104 | tf_op jit(solution)/shard_map/value_xy/ppermute | solution.py:307
  75.9 0.7 shard_map.106
  76.7 2.6 %collective-permute-start.26 = (bf16[64,1152]{1,0:T(8,128)(2,1)S(1)}, bf16[64,1152]{1,0:T(8,128)(2,1)S(1)}, u32[]{:S(2)}, u32[]{:S(2)}) collective-permute-start(bf16[64,1152]{1,0:T(8,128)(2,1)S(1)} %get-tuple-element.83), channel_id=1, source_target_pairs={{0,8},{2,10},{4,12},{6,14},{8,0},{10,2},{12,4},{14,6},{1,9},{3,11}... | collective-permute-start | bytes 442376 | tf_op jit(solution)/shard_map/sums_z2/ppermute | solution.py:290
  79.3 1.8 %collective-permute-start.27 = (bf16[64,1152]{1,0:T(8,128)(2,1)S(1)}, bf16[64,1152]{1,0:T(8,128)(2,1)S(1)}, u32[]{:S(2)}, u32[]{:S(2)}) collective-permute-start(bf16[64,1152]{1,0:T(8,128)(2,1)S(1)} %get-tuple-element.84), channel_id=1, source_target_pairs={{0,12},{2,14},{4,8},{6,10},{8,4},{10,6},{12,0},{14,2},{1,13},{3,15... | collective-permute-start | bytes 442376 | tf_op jit(solution)/shard_map/sums_z3/ppermute | solution.py:290
  81.1 1.2 collective-permute-done.25.refs_1_
  82.3 7.4 %collective-permute-done.26.refs_2_ = bf16[64,1152]{1,0:T(8,128)(2,1)S(1)} collective-permute-done((bf16[64,1152]{1,0:T(8,128)(2,1)S(1)}, bf16[64,1152]{1,0:T(8,128)(2,1)S(1)}, u32[]{:S(2)}, u32[]{:S(2)}) %collective-permute-start.26) | collective-permute-done | bytes 147488 | tf_op jit(solution)/shard_map/sums_z2/ppermute | solution.py:290
  89.7 0.9 shard_map.107.refs_0_
  90.6 2.2 %collective-permute-start.28 = (bf16[64,1024]{1,0:T(8,128)(2,1)S(1)}, bf16[64,1024]{1,0:T(8,128)(2,1)S(1)}, u32[]{:S(2)}, u32[]{:S(2)}) collective-permute-start(bf16[64,1024]{1,0:T(8,128)(2,1)S(1)} %shard_map.107.refs_0_), channel_id=1, source_target_pairs={{0,4},{2,6},{4,0},{6,2},{8,12},{10,14},{12,8},{14,10},{1,5},{3,7},... | collective-permute-start | bytes 393224 | tf_op jit(solution)/shard_map/attn_z1/ppermute | solution.py:290
  92.8 1.1 collective-permute-start.29
  93.9 1.4 %collective-permute-start.30 = (bf16[64,1024]{1,0:T(8,128)(2,1)S(1)}, bf16[64,1024]{1,0:T(8,128)(2,1)S(1)}, u32[]{:S(2)}, u32[]{:S(2)}) collective-permute-start(bf16[64,1024]{1,0:T(8,128)(2,1)S(1)} %shard_map.107.refs_0_), channel_id=1, source_target_pairs={{0,12},{2,14},{4,8},{6,10},{8,4},{10,6},{12,0},{14,2},{1,13},{3,15... | collective-permute-start | bytes 393224 | tf_op jit(solution)/shard_map/attn_z3/ppermute | solution.py:290
  95.3 1.1 collective-permute-start.31
  96.4 0.4 collective-permute-done.28.refs_1_
  96.8 0.6 collective-permute-start.32
  97.4 6.4 %collective-permute-done.29.refs_2_ = bf16[64,1024]{1,0:T(8,128)(2,1)S(1)} collective-permute-done((bf16[64,1024]{1,0:T(8,128)(2,1)S(1)}, bf16[64,1024]{1,0:T(8,128)(2,1)S(1)}, u32[]{:S(2)}, u32[]{:S(2)}) %collective-permute-start.29) | collective-permute-done | bytes 131104 | tf_op jit(solution)/shard_map/attn_z2/ppermute | solution.py:290
  103.8 0.8 collective-permute-start.33
  104.6 1.2 %collective-permute-start.34 = (bf16[64,1024]{1,0:T(8,128)(2,1)S(1)}, bf16[64,1024]{1,0:T(8,128)(2,1)S(1)}, u32[]{:S(2)}, u32[]{:S(2)}) collective-permute-start(bf16[64,1024]{1,0:T(8,128)(2,1)S(1)} %collective-permute-done.30.refs_3_), channel_id=1, source_target_pairs={{0,2},{2,0},{4,6},{6,4},{8,10},{10,8},{12,14},{14,12},{1,3},{3,1},... | collective-permute-start | bytes 393224 | tf_op jit(solution)/shard_map/attn3_y/ppermute | solution.py:294
  105.9 0.1 stack.59.idx_ref
  106.0 2.8 %collective-permute-done.33.refs_6_ = bf16[64,1024]{1,0:T(8,128)(2,1)S(1)} collective-permute-done((bf16[64,1024]{1,0:T(8,128)(2,1)S(1)}, bf16[64,1024]{1,0:T(8,128)(2,1)S(1)}, u32[]{:S(2)}, u32[]{:S(2)}) %collective-permute-start.33) | collective-permute-done | bytes 131104 | tf_op jit(solution)/shard_map/attn2_y/ppermute | solution.py:294
  108.8 1.4 %collective-permute-done.34.refs_7_ = bf16[64,1024]{1,0:T(8,128)(2,1)S(1)} collective-permute-done((bf16[64,1024]{1,0:T(8,128)(2,1)S(1)}, bf16[64,1024]{1,0:T(8,128)(2,1)S(1)}, u32[]{:S(2)}, u32[]{:S(2)}) %collective-permute-start.34) | collective-permute-done | bytes 131104 | tf_op jit(solution)/shard_map/attn3_y/ppermute | solution.py:294
  110.2 3.3 %shard_map.108 = (f32[128,1024]{1,0:T(8,128)S(1)}, bf16[128,1024]{1,0:T(8,128)(2,1)S(1)}) custom-call(s32[17]{0:T(128)S(1)} %stack.59.idx_ref, bf16[64,1024]{1,0:T(8,128)(2,1)S(1)} %shard_map.107.refs_0_, bf16[64,1024]{1,0:T(8,128)(2,1)S(1)} %collective-permute-done.28.refs_1_, bf16[64,1024]{1,0:T(8,128)(2,1)S(1)} %collective-permute-done.29.refs_2_, ...), custom_call_target="tpu_custom_call" | custom-call | tf_op jit(solution)/shard_map/pallas_call | solution.py:480
  114.3 0.8 collective-permute-done.35
  115.1 0.8 add_convert_fusion
  (57 shorter events, 0.4 us)
Async XLA Ops:
  0.0 9.3 %copy-start.10 = (bf16[32,2048]{1,0:T(8,128)(2,1)S(1)}, bf16[32,2048]{1,0:T(8,128)(2,1)}, u32[]{:S(2)}) copy-start(bf16[32,2048]{1,0:T(8,128)(2,1)} %param.15) | copy-start | bytes 393220
  0.0 41.4 %copy-start.11 = (s32[256]{0:T(256)S(1)}, s32[256]{0:T(256)}, u32[]{:S(2)}) copy-start(s32[256]{0:T(256)} %param.11) | copy-start | bytes 3076
  2.4 42.9 %copy-start.1 = (bf16[512,256]{1,0:T(8,128)(2,1)S(1)}, bf16[512,256]{1,0:T(8,128)(2,1)}, u32[]{:S(2)}) copy-start(bf16[512,256]{1,0:T(8,128)(2,1)} %get-tuple-element.46.refs_6_) | copy-start | bytes 786436
  2.4 9.6 %collective-permute-start = (bf16[512,256]{1,0:T(8,128)(2,1)}, bf16[512,256]{1,0:T(8,128)(2,1)S(1)}, u32[]{:S(2)}, u32[]{:S(2)}) collective-permute-start(bf16[512,256]{1,0:T(8,128)(2,1)} %get-tuple-element.46.refs_6_), channel_id=1, source_target_pairs={{0,4},{2,6},{4,0},{6,2},{8,12},{10,14},{12,8},{14,10},{1,5},{3,7},... | collective-permute-start | bytes 786440 | tf_op jit(solution)/shard_map/wk_z1/ppermute | solution.py:290
  5.5 7.2 %collective-permute-start.2 = (bf16[512,256]{1,0:T(8,128)(2,1)}, bf16[512,256]{1,0:T(8,128)(2,1)S(1)}, u32[]{:S(2)}, u32[]{:S(2)}) collective-permute-start(bf16[512,256]{1,0:T(8,128)(2,1)} %get-tuple-element.46.refs_6_), channel_id=1, source_target_pairs={{4,8},{6,10},{8,4},{10,6},{5,9},{7,11},{9,5},{11,7},{20,24},{22,26... | collective-permute-start | bytes 786440 | tf_op jit(solution)/shard_map/wk_z3/ppermute | solution.py:290
  6.2 18.2 %collective-permute-start.4 = (bf16[256,1024]{1,0:T(8,128)(2,1)}, bf16[256,1024]{1,0:T(8,128)(2,1)S(1)}, u32[]{:S(2)}, u32[]{:S(2)}) collective-permute-start(bf16[256,1024]{1,0:T(8,128)(2,1)} %get-tuple-element.47), channel_id=1, source_target_pairs={{0,2},{2,0},{4,6},{6,4},{8,10},{10,8},{12,14},{14,12},{1,3},{3,1},... | collective-permute-start | bytes 1572872 | tf_op jit(solution)/shard_map/image_y/ppermute | solution.py:294
  7.8 16.7 %collective-permute-start.5 = (bf16[256,1024]{1,0:T(8,128)(2,1)}, bf16[256,1024]{1,0:T(8,128)(2,1)S(1)}, u32[]{:S(2)}, u32[]{:S(2)}) collective-permute-start(bf16[256,1024]{1,0:T(8,128)(2,1)} %get-tuple-element.48), channel_id=1, source_target_pairs={{0,16},{16,0},{1,17},{17,1},{2,18},{18,2},{3,19},{19,3},{4,20},{20... | collective-permute-start | bytes 1572872 | tf_op jit(solution)/shard_map/image_x/ppermute | solution.py:302
  9.3 12.0 %collective-permute-start.6 = (bf16[32,1024]{1,0:T(8,128)(2,1)S(1)}, bf16[32,1024]{1,0:T(8,128)(2,1)S(1)}, u32[]{:S(2)}, u32[]{:S(2)}) collective-permute-start(bf16[32,1024]{1,0:T(8,128)(2,1)S(1)} %constant_dynamic-slice_fusion), channel_id=1, source_target_pairs={{0,2},{2,0},{4,6},{6,4},{8,10},{10,8},{12,14},{14,12},{1,3},{3,1},... | collective-permute-start | bytes 196616 | tf_op jit(solution)/shard_map/q_y/ppermute | solution.py:294
  12.0 9.3 %collective-permute-start.1 = (bf16[512,256]{1,0:T(8,128)(2,1)S(1)}, bf16[512,256]{1,0:T(8,128)(2,1)S(1)}, u32[]{:S(2)}, u32[]{:S(2)}) collective-permute-start(bf16[512,256]{1,0:T(8,128)(2,1)S(1)} %collective-permute-done.refs_7_), channel_id=1, source_target_pairs={{4,8},{6,10},{8,4},{10,6},{5,9},{7,11},{9,5},{11,7},{20,24},{22,26... | collective-permute-start | bytes 786440 | tf_op jit(solution)/shard_map/wk_across_z3/ppermute | solution.py:290
  12.7 28.8 %copy-start.8 = (bf16[512,256]{1,0:T(8,128)(2,1)}, bf16[512,256]{1,0:T(8,128)(2,1)S(1)}, u32[]{:S(2)}) copy-start(bf16[512,256]{1,0:T(8,128)(2,1)S(1)} %collective-permute-done.2.refs_10_) | copy-start | bytes 786436
  12.7 11.7 %collective-permute-start.3 = (bf16[512,256]{1,0:T(8,128)(2,1)S(1)}, bf16[512,256]{1,0:T(8,128)(2,1)S(1)}, u32[]{:S(2)}, u32[]{:S(2)}) collective-permute-start(bf16[512,256]{1,0:T(8,128)(2,1)S(1)} %collective-permute-done.2.refs_10_), channel_id=1, source_target_pairs={{4,0},{6,2},{8,12},{10,14},{5,1},{7,3},{9,13},{11,15},{20,16},{22,... | collective-permute-start | bytes 786440 | tf_op jit(solution)/shard_map/wk_out_z1/ppermute | solution.py:290
  24.4 15.3 %copy-start.3 = (bf16[256,1024]{1,0:T(8,128)(2,1)}, bf16[256,1024]{1,0:T(8,128)(2,1)S(1)}, u32[]{:S(2)}) copy-start(bf16[256,1024]{1,0:T(8,128)(2,1)S(1)} %collective-permute-done.4.refs_0_) | copy-start | bytes 1572868
  24.5 19.3 %copy-start.4 = (bf16[256,1024]{1,0:T(8,128)(2,1)}, bf16[256,1024]{1,0:T(8,128)(2,1)S(1)}, u32[]{:S(2)}) copy-start(bf16[256,1024]{1,0:T(8,128)(2,1)S(1)} %collective-permute-done.5.refs_2_) | copy-start | bytes 1572868
  24.5 6.6 %collective-permute-start.7 = (bf16[512,256]{1,0:T(8,128)(2,1)}, bf16[512,256]{1,0:T(8,128)(2,1)S(1)}, u32[]{:S(2)}, u32[]{:S(2)}) collective-permute-start(bf16[512,256]{1,0:T(8,128)(2,1)} %get-tuple-element.51.refs_6_), channel_id=1, source_target_pairs={{0,4},{2,6},{4,0},{6,2},{8,12},{10,14},{12,8},{14,10},{1,5},{3,7},... | collective-permute-start | bytes 786440 | tf_op jit(solution)/shard_map/wv_z1/ppermute | solution.py:290
  25.5 14.1 %collective-permute-start.10 = (bf16[256,1024]{1,0:T(8,128)(2,1)}, bf16[256,1024]{1,0:T(8,128)(2,1)}, u32[]{:S(2)}, u32[]{:S(2)}) collective-permute-start(bf16[256,1024]{1,0:T(8,128)(2,1)} %get-tuple-element.53), channel_id=1, source_target_pairs={{0,18},{2,16},{4,22},{6,20},{8,26},{10,24},{12,30},{14,28},{16,2},... | collective-permute-start | bytes 1572872 | tf_op jit(solution)/shard_map/image_xy/ppermute | solution.py:307
  28.0 11.7 %collective-permute-start.11 = (bf16[256,1024]{1,0:T(8,128)(2,1)S(1)}, bf16[256,1024]{1,0:T(8,128)(2,1)S(1)}, u32[]{:S(2)}, u32[]{:S(2)}) collective-permute-start(bf16[256,1024]{1,0:T(8,128)(2,1)S(1)} %collective-permute-done.4.refs_0_), channel_id=1, source_target_pairs={{0,1},{1,0},{2,3},{3,2},{4,5},{5,4},{6,7},{7,6},{8,9},{9,8},{10,11... | collective-permute-start | bytes 1572872 | tf_op jit(solution)/shard_map/image_core/ppermute | solution.py:298
  28.0 11.7 %collective-permute-start.12 = (bf16[256,1024]{1,0:T(8,128)(2,1)S(1)}, bf16[256,1024]{1,0:T(8,128)(2,1)S(1)}, u32[]{:S(2)}, u32[]{:S(2)}) collective-permute-start(bf16[256,1024]{1,0:T(8,128)(2,1)S(1)} %collective-permute-done.5.refs_2_), channel_id=1, source_target_pairs={{0,1},{1,0},{2,3},{3,2},{4,5},{5,4},{6,7},{7,6},{8,9},{9,8},{10,11... | collective-permute-start | bytes 1572872 | tf_op jit(solution)/shard_map/image_core/ppermute | solution.py:298
  28.5 3.9 %collective-permute-start.8 = (bf16[512,256]{1,0:T(8,128)(2,1)}, bf16[512,256]{1,0:T(8,128)(2,1)S(1)}, u32[]{:S(2)}, u32[]{:S(2)}) collective-permute-start(bf16[512,256]{1,0:T(8,128)(2,1)} %get-tuple-element.51.refs_6_), channel_id=1, source_target_pairs={{4,8},{6,10},{8,4},{10,6},{5,9},{7,11},{9,5},{11,7},{20,24},{22,26... | collective-permute-start | bytes 786440 | tf_op jit(solution)/shard_map/wv_z3/ppermute | solution.py:290
  31.1 8.6 %collective-permute-start.9 = (bf16[512,256]{1,0:T(8,128)(2,1)S(1)}, bf16[512,256]{1,0:T(8,128)(2,1)S(1)}, u32[]{:S(2)}, u32[]{:S(2)}) collective-permute-start(bf16[512,256]{1,0:T(8,128)(2,1)S(1)} %collective-permute-done.1.refs_8_), channel_id=1, source_target_pairs={{4,0},{6,2},{8,12},{10,14},{5,1},{7,3},{9,13},{11,15},{20,16},{22,... | collective-permute-start | bytes 786440 | tf_op jit(solution)/shard_map/wk_end_z1/ppermute | solution.py:290
  39.7 4.1 %copy-start.9 = (bf16[512,256]{1,0:T(8,128)(2,1)}, bf16[512,256]{1,0:T(8,128)(2,1)S(1)}, u32[]{:S(2)}) copy-start(bf16[512,256]{1,0:T(8,128)(2,1)S(1)} %collective-permute-done.9.refs_11_) | copy-start | bytes 786436
  39.7 0.8 copy-start.5
  39.7 1.0 copy-start.6
  39.7 5.5 %collective-permute-start.14 = (bf16[256,1024]{1,0:T(8,128)(2,1)}, bf16[256,1024]{1,0:T(8,128)(2,1)}, u32[]{:S(2)}, u32[]{:S(2)}) collective-permute-start(bf16[256,1024]{1,0:T(8,128)(2,1)} %collective-permute-done.10.refs_4_), channel_id=1, source_target_pairs={{0,1},{1,0},{2,3},{3,2},{4,5},{5,4},{6,7},{7,6},{8,9},{9,8},{10,11... | collective-permute-start | bytes 1572872 | tf_op jit(solution)/shard_map/image_core/ppermute | solution.py:298
  40.7 9.8 %collective-permute-start.13 = (bf16[512,256]{1,0:T(8,128)(2,1)S(1)}, bf16[512,256]{1,0:T(8,128)(2,1)S(1)}, u32[]{:S(2)}, u32[]{:S(2)}) collective-permute-start(bf16[512,256]{1,0:T(8,128)(2,1)S(1)} %collective-permute-done.7.refs_7_), channel_id=1, source_target_pairs={{4,8},{6,10},{8,4},{10,6},{5,9},{7,11},{9,5},{11,7},{20,24},{22,26... | collective-permute-start | bytes 786440 | tf_op jit(solution)/shard_map/wv_across_z3/ppermute | solution.py:290
  41.5 9.0 %collective-permute-start.15 = (bf16[64,1024]{1,0:T(8,128)(2,1)S(1)}, bf16[64,1024]{1,0:T(8,128)(2,1)S(1)}, u32[]{:S(2)}, u32[]{:S(2)}) collective-permute-start(bf16[64,1024]{1,0:T(8,128)(2,1)S(1)} %pad_maximum_fusion), channel_id=1, source_target_pairs={{0,4},{2,6},{4,0},{6,2},{8,12},{10,14},{12,8},{14,10},{1,5},{3,7},... | collective-permute-start | bytes 393224 | tf_op jit(solution)/shard_map/q_z1/ppermute | solution.py:290
  43.8 13.0 %copy-start.12 = (s32[256]{0:T(256)S(1)}, s32[256]{0:T(256)}, u32[]{:S(2)}) copy-start(s32[256]{0:T(256)} %param.16) | copy-start | bytes 3076
  43.8 18.0 %copy-start = (bf16[512,256]{1,0:T(8,128)(2,1)S(1)}, bf16[512,256]{1,0:T(8,128)(2,1)}, u32[]{:S(2)}) copy-start(bf16[512,256]{1,0:T(8,128)(2,1)} %get-tuple-element.51.refs_6_) | copy-start | bytes 786436
  43.8 14.3 %collective-permute-start.19 = (bf16[512,256]{1,0:T(8,128)(2,1)S(1)}, bf16[512,256]{1,0:T(8,128)(2,1)S(1)}, u32[]{:S(2)}, u32[]{:S(2)}) collective-permute-start(bf16[512,256]{1,0:T(8,128)(2,1)S(1)} %collective-permute-done.8.refs_10_), channel_id=1, source_target_pairs={{4,0},{6,2},{8,12},{10,14},{5,1},{7,3},{9,13},{11,15},{20,16},{22,... | collective-permute-start | bytes 786440 | tf_op jit(solution)/shard_map/wv_out_z1/ppermute | solution.py:290
  50.5 11.4 %collective-permute-start.20 = (bf16[512,256]{1,0:T(8,128)(2,1)S(1)}, bf16[512,256]{1,0:T(8,128)(2,1)}, u32[]{:S(2)}, u32[]{:S(2)}) collective-permute-start(bf16[512,256]{1,0:T(8,128)(2,1)S(1)} %collective-permute-done.13.refs_8_), channel_id=1, source_target_pairs={{4,0},{6,2},{8,12},{10,14},{5,1},{7,3},{9,13},{11,15},{20,16},{22,... | collective-permute-start | bytes 786440 | tf_op jit(solution)/shard_map/wv_end_z1/ppermute | solution.py:290
  51.8 15.2 %collective-permute-start.21 = (bf16[128,1024]{1,0:T(8,128)(2,1)S(1)}, bf16[128,1024]{1,0:T(8,128)(2,1)S(1)}, u32[]{:S(2)}, u32[]{:S(2)}) collective-permute-start(bf16[128,1024]{1,0:T(8,128)(2,1)S(1)} %constant_dynamic-update-slice_fusion.refs_0_), channel_id=1, source_target_pairs={{0,8},{2,10},{4,12},{6,14},{8,0},{10,2},{12,4},{14,6},{1,9},{3,11}... | collective-permute-start | bytes 786440 | tf_op jit(solution)/shard_map/q_z2/ppermute | solution.py:290
  55.3 13.8 %collective-permute-start.17 = (f32[512,128]{1,0:T(8,128)}, f32[512,128]{1,0:T(8,128)S(1)}, u32[]{:S(2)}, u32[]{:S(2)}) collective-permute-start(f32[512,128]{1,0:T(8,128)} %get-tuple-element.66), channel_id=1, source_target_pairs={{0,16},{16,0},{1,17},{17,1},{2,18},{18,2},{3,19},{19,3},{4,20},{20... | collective-permute-start | bytes 786440 | tf_op jit(solution)/shard_map/key_x/ppermute | solution.py:302
  56.9 13.9 %collective-permute-start.16 = (f32[520,128]{1,0:T(8,128)}, f32[520,128]{1,0:T(8,128)S(1)}, u32[]{:S(2)}, u32[]{:S(2)}) collective-permute-start(f32[520,128]{1,0:T(8,128)} %get-tuple-element.65), channel_id=1, source_target_pairs={{0,2},{2,0},{4,6},{6,4},{8,10},{10,8},{12,14},{14,12},{1,3},{3,1},... | collective-permute-start | bytes 798728 | tf_op jit(solution)/shard_map/key_y/ppermute | solution.py:294
  58.2 12.7 %copy-start.2 = (f32[128]{0:T(128)S(1)}, f32[128]{0:T(128)}, u32[]{:S(2)}) copy-start(f32[128]{0:T(128)} %param.14) | copy-start | bytes 1540
  58.2 12.6 %collective-permute-start.18 = (f32[512,128]{1,0:T(8,128)S(1)}, f32[512,128]{1,0:T(8,128)S(1)}, u32[]{:S(2)}, u32[]{:S(2)}) collective-permute-start(f32[512,128]{1,0:T(8,128)S(1)} %get-tuple-element.67), channel_id=1, source_target_pairs={{0,18},{2,16},{4,22},{6,20},{8,26},{10,24},{12,30},{14,28},{16,2},... | collective-permute-start | bytes 786440 | tf_op jit(solution)/shard_map/key_xy/ppermute | solution.py:307
  67.1 6.5 %collective-permute-start.22 = (bf16[512,128]{1,0:T(8,128)(2,1)}, bf16[512,128]{1,0:T(8,128)(2,1)S(1)}, u32[]{:S(2)}, u32[]{:S(2)}) collective-permute-start(bf16[512,128]{1,0:T(8,128)(2,1)} %get-tuple-element.78), channel_id=1, source_target_pairs={{0,2},{2,0},{4,6},{6,4},{8,10},{10,8},{12,14},{14,12},{1,3},{3,1},... | collective-permute-start | bytes 393224 | tf_op jit(solution)/shard_map/value_y/ppermute | solution.py:294
  68.8 6.0 %collective-permute-start.23 = (bf16[512,128]{1,0:T(8,128)(2,1)}, bf16[512,128]{1,0:T(8,128)(2,1)S(1)}, u32[]{:S(2)}, u32[]{:S(2)}) collective-permute-start(bf16[512,128]{1,0:T(8,128)(2,1)} %get-tuple-element.79), channel_id=1, source_target_pairs={{0,16},{16,0},{1,17},{17,1},{2,18},{18,2},{3,19},{19,3},{4,20},{20... | collective-permute-start | bytes 393224 | tf_op jit(solution)/shard_map/value_x/ppermute | solution.py:302
  69.1 6.9 %collective-permute-start.24 = (bf16[512,128]{1,0:T(8,128)(2,1)}, bf16[512,128]{1,0:T(8,128)(2,1)S(1)}, u32[]{:S(2)}, u32[]{:S(2)}) collective-permute-start(bf16[512,128]{1,0:T(8,128)(2,1)} %get-tuple-element.80), channel_id=1, source_target_pairs={{0,18},{2,16},{4,22},{6,20},{8,26},{10,24},{12,30},{14,28},{16,2},... | collective-permute-start | bytes 393224 | tf_op jit(solution)/shard_map/value_xy/ppermute | solution.py:307
  75.9 39.2 %copy-start.7 = (bf16[128,1024]{1,0:T(8,128)(2,1)S(1)}, bf16[128,1024]{1,0:T(8,128)(2,1)}, u32[]{:S(2)}) copy-start(bf16[128,1024]{1,0:T(8,128)(2,1)} %param.17) | copy-start | bytes 786436
  76.7 5.6 %collective-permute-start.25 = (bf16[64,1152]{1,0:T(8,128)(2,1)S(1)}, bf16[64,1152]{1,0:T(8,128)(2,1)S(1)}, u32[]{:S(2)}, u32[]{:S(2)}) collective-permute-start(bf16[64,1152]{1,0:T(8,128)(2,1)S(1)} %get-tuple-element.82), channel_id=1, source_target_pairs={{0,4},{2,6},{4,0},{6,2},{8,12},{10,14},{12,8},{14,10},{1,5},{3,7},... | collective-permute-start | bytes 442376 | tf_op jit(solution)/shard_map/sums_z1/ppermute | solution.py:290
  76.7 12.9 %collective-permute-start.26 = (bf16[64,1152]{1,0:T(8,128)(2,1)S(1)}, bf16[64,1152]{1,0:T(8,128)(2,1)S(1)}, u32[]{:S(2)}, u32[]{:S(2)}) collective-permute-start(bf16[64,1152]{1,0:T(8,128)(2,1)S(1)} %get-tuple-element.83), channel_id=1, source_target_pairs={{0,8},{2,10},{4,12},{6,14},{8,0},{10,2},{12,4},{14,6},{1,9},{3,11}... | collective-permute-start | bytes 442376 | tf_op jit(solution)/shard_map/sums_z2/ppermute | solution.py:290
  79.3 10.4 %collective-permute-start.27 = (bf16[64,1152]{1,0:T(8,128)(2,1)S(1)}, bf16[64,1152]{1,0:T(8,128)(2,1)S(1)}, u32[]{:S(2)}, u32[]{:S(2)}) collective-permute-start(bf16[64,1152]{1,0:T(8,128)(2,1)S(1)} %get-tuple-element.84), channel_id=1, source_target_pairs={{0,12},{2,14},{4,8},{6,10},{8,4},{10,6},{12,0},{14,2},{1,13},{3,15... | collective-permute-start | bytes 442376 | tf_op jit(solution)/shard_map/sums_z3/ppermute | solution.py:290
  90.6 6.2 %collective-permute-start.28 = (bf16[64,1024]{1,0:T(8,128)(2,1)S(1)}, bf16[64,1024]{1,0:T(8,128)(2,1)S(1)}, u32[]{:S(2)}, u32[]{:S(2)}) collective-permute-start(bf16[64,1024]{1,0:T(8,128)(2,1)S(1)} %shard_map.107.refs_0_), channel_id=1, source_target_pairs={{0,4},{2,6},{4,0},{6,2},{8,12},{10,14},{12,8},{14,10},{1,5},{3,7},... | collective-permute-start | bytes 393224 | tf_op jit(solution)/shard_map/attn_z1/ppermute | solution.py:290
  92.8 11.0 %collective-permute-start.29 = (bf16[64,1024]{1,0:T(8,128)(2,1)S(1)}, bf16[64,1024]{1,0:T(8,128)(2,1)S(1)}, u32[]{:S(2)}, u32[]{:S(2)}) collective-permute-start(bf16[64,1024]{1,0:T(8,128)(2,1)S(1)} %shard_map.107.refs_0_), channel_id=1, source_target_pairs={{0,8},{2,10},{4,12},{6,14},{8,0},{10,2},{12,4},{14,6},{1,9},{3,11}... | collective-permute-start | bytes 393224 | tf_op jit(solution)/shard_map/attn_z2/ppermute | solution.py:290
  93.9 10.7 %collective-permute-start.30 = (bf16[64,1024]{1,0:T(8,128)(2,1)S(1)}, bf16[64,1024]{1,0:T(8,128)(2,1)S(1)}, u32[]{:S(2)}, u32[]{:S(2)}) collective-permute-start(bf16[64,1024]{1,0:T(8,128)(2,1)S(1)} %shard_map.107.refs_0_), channel_id=1, source_target_pairs={{0,12},{2,14},{4,8},{6,10},{8,4},{10,6},{12,0},{14,2},{1,13},{3,15... | collective-permute-start | bytes 393224 | tf_op jit(solution)/shard_map/attn_z3/ppermute | solution.py:290
  95.3 10.7 %collective-permute-start.31 = (bf16[64,1024]{1,0:T(8,128)(2,1)S(1)}, bf16[64,1024]{1,0:T(8,128)(2,1)S(1)}, u32[]{:S(2)}, u32[]{:S(2)}) collective-permute-start(bf16[64,1024]{1,0:T(8,128)(2,1)S(1)} %shard_map.107.refs_0_), channel_id=1, source_target_pairs={{0,2},{2,0},{4,6},{6,4},{8,10},{10,8},{12,14},{14,12},{1,3},{3,1},... | collective-permute-start | bytes 393224 | tf_op jit(solution)/shard_map/attn0_y/ppermute | solution.py:294
  96.8 9.2 %collective-permute-start.32 = (bf16[64,1024]{1,0:T(8,128)(2,1)S(1)}, bf16[64,1024]{1,0:T(8,128)(2,1)S(1)}, u32[]{:S(2)}, u32[]{:S(2)}) collective-permute-start(bf16[64,1024]{1,0:T(8,128)(2,1)S(1)} %collective-permute-done.28.refs_1_), channel_id=1, source_target_pairs={{0,2},{2,0},{4,6},{6,4},{8,10},{10,8},{12,14},{14,12},{1,3},{3,1},... | collective-permute-start | bytes 393224 | tf_op jit(solution)/shard_map/attn1_y/ppermute | solution.py:294
  103.8 5.0 %collective-permute-start.33 = (bf16[64,1024]{1,0:T(8,128)(2,1)S(1)}, bf16[64,1024]{1,0:T(8,128)(2,1)S(1)}, u32[]{:S(2)}, u32[]{:S(2)}) collective-permute-start(bf16[64,1024]{1,0:T(8,128)(2,1)S(1)} %collective-permute-done.29.refs_2_), channel_id=1, source_target_pairs={{0,2},{2,0},{4,6},{6,4},{8,10},{10,8},{12,14},{14,12},{1,3},{3,1},... | collective-permute-start | bytes 393224 | tf_op jit(solution)/shard_map/attn2_y/ppermute | solution.py:294
  104.6 5.6 %collective-permute-start.34 = (bf16[64,1024]{1,0:T(8,128)(2,1)S(1)}, bf16[64,1024]{1,0:T(8,128)(2,1)S(1)}, u32[]{:S(2)}, u32[]{:S(2)}) collective-permute-start(bf16[64,1024]{1,0:T(8,128)(2,1)S(1)} %collective-permute-done.30.refs_3_), channel_id=1, source_target_pairs={{0,2},{2,0},{4,6},{6,4},{8,10},{10,8},{12,14},{14,12},{1,3},{3,1},... | collective-permute-start | bytes 393224 | tf_op jit(solution)/shard_map/attn3_y/ppermute | solution.py:294
  113.5 1.6 %collective-permute-start.35 = (bf16[128,1024]{1,0:T(8,128)(2,1)S(1)}, bf16[128,1024]{1,0:T(8,128)(2,1)S(1)}, u32[]{:S(2)}, u32[]{:S(2)}) collective-permute-start(bf16[128,1024]{1,0:T(8,128)(2,1)S(1)} %get-tuple-element.86), channel_id=1, source_target_pairs={{0,1},{1,0},{2,3},{3,2},{4,5},{5,4},{6,7},{7,6},{8,9},{9,8},{10,11... | collective-permute-start | bytes 786440 | tf_op jit(solution)/shard_map/proj_core/ppermute | solution.py:298

commit v8 on v7

--- a/solution.py
+++ b/solution.py
@@ -463,16 +463,20 @@
         out_specs=(WHOLE,) * lines,
         compiler_params=PARAMS,
     )(expo, figures, keep, *value_parts)
-    sums = [sums[0]] + [along("sums", sums[d], d) for d in range(1, lines)]
+    far_first = sorted(range(1, lines), key=lambda d: (d < 2, d))
+    moved = {d: along("sums", sums[d], d) for d in far_first}
+    sums = [sums[0]] + [moved[d] for d in range(1, lines)]
     attn = pl.pallas_call(
         functools.partial(combine_kernel, lines, per_kv),
         out_shape=jax.ShapeDtypeStruct((rows, q_half), BF16),
         in_specs=[WHOLE] * lines,
         out_specs=WHOLE,
         compiler_params=PARAMS,
-    )(*sums)
-    mine = [attn if d == 0 else along("attn", attn, d) for d in range(lines)]
-    where = [(line ^ d, y) for d in range(lines)] + [(line ^ d, 1 - y) for d in range(lines)]
+    )(sums[0], *(sums[d] for d in far_first))
+    moved = {d: along("attn", attn, d) for d in far_first}
+    order = [0] + far_first
+    mine = [attn if d == 0 else moved[d] for d in order]
+    where = [(line ^ d, y) for d in order] + [(line ^ d, 1 - y) for d in order]
     other = [over_y(f"attn{d}", m) for d, m in enumerate(mine)]
 
     out_rows = lines * rows

time: 116 us -> 116 us (level)
  no operation moved by 1% of the time
where the time goes in v8:
time: 116 us
  waiting for transfers between devices  46.9 us (40%)
  starting transfers between devices  43.5 us (38%)
  Pallas kernels  21.9 us (19%)
  local copies, waits for them, and re-layouts  1.39 us (1%)
    ppermute x18, waiting for transfers between devices, along(): lax.ppermute(array, 'blk', [(b, b ^ 2 * d) for b in range(nblk) if ok(b /...  31.2 us
    ppermute x18, starting transfers between devices, along(): lax.ppermute(array, 'blk', [(b, b ^ 2 * d) for b in range(nblk) if ok(b /...  26.1 us
    ppermute x8, waiting for transfers between devices, over_y(): return lax.ppermute(array, 'blk', swap_y)  12.5 us
    pallas_call x2, Pallas kernels, project(): pl.pallas_call(functools.partial(project_kernel, sources, extra), out_sha...  10.4 us
    ppermute x8, starting transfers between devices, over_y(): return lax.ppermute(array, 'blk', swap_y)  8.7 us
    ppermute x3, starting transfers between devices, over_both(): return lax.ppermute(array, ('groups', 'blk'), pairs)  4.74 us
    pallas_call x2, Pallas kernels, shares(): pl.pallas_call(functools.partial(share_kernel, flips, half_lines), out_sh...  4.45 us
    pallas_call x1, Pallas kernels, body(): pl.pallas_call(functools.partial(proj_kernel, 2 * lines), out_shape=(jax....  3.28 us
  transfers between devices with their start and end apart: 36, of which 16 were waited for; matrix products, arithmetic and copies ran while one was open for 0% of the time, Pallas kernels for 13%

profile of v8, /device:TPU:0, one launch (start us, length us, event | category | flops | bytes accessed | tf_op | source)
XLA Modules:
  0.0 115.7 jit_solution(8147083609466432383)
XLA Ops:
  0.0 2.4 %shard_map.100 = (bf16[256,1024]{1,0:T(8,128)(2,1)}, bf16[256,1024]{1,0:T(8,128)(2,1)}, bf16[512,256]{1,0:T(8,128)(2,1)}) custom-call(bf16[256,8192]{1,0:T(8,128)(2,1)} %image.7, bf16[1024,256]{1,0:T(8,128)(2,1)} %refs_0_.2), custom_call_target="tpu_custom_call" | custom-call | tf_op jit(solution)/shard_map/pallas_call | solution.py:337
  2.4 3.1 %collective-permute-start = (bf16[512,256]{1,0:T(8,128)(2,1)}, bf16[512,256]{1,0:T(8,128)(2,1)S(1)}, u32[]{:S(2)}, u32[]{:S(2)}) collective-permute-start(bf16[512,256]{1,0:T(8,128)(2,1)} %get-tuple-element.46.refs_6_), channel_id=1, source_target_pairs={{0,4},{2,6},{4,0},{6,2},{8,12},{10,14},{12,8},{14,10},{1,5},{3,7},... | collective-permute-start | bytes 786440 | tf_op jit(solution)/shard_map/wk_z1/ppermute | solution.py:290
  5.5 0.7 collective-permute-start.2
  6.2 1.6 %collective-permute-start.4 = (bf16[256,1024]{1,0:T(8,128)(2,1)}, bf16[256,1024]{1,0:T(8,128)(2,1)S(1)}, u32[]{:S(2)}, u32[]{:S(2)}) collective-permute-start(bf16[256,1024]{1,0:T(8,128)(2,1)} %get-tuple-element.47), channel_id=1, source_target_pairs={{0,2},{2,0},{4,6},{6,4},{8,10},{10,8},{12,14},{14,12},{1,3},{3,1},... | collective-permute-start | bytes 1572872 | tf_op jit(solution)/shard_map/image_y/ppermute | solution.py:294
  7.8 1.5 %collective-permute-start.5 = (bf16[256,1024]{1,0:T(8,128)(2,1)}, bf16[256,1024]{1,0:T(8,128)(2,1)S(1)}, u32[]{:S(2)}, u32[]{:S(2)}) collective-permute-start(bf16[256,1024]{1,0:T(8,128)(2,1)} %get-tuple-element.48), channel_id=1, source_target_pairs={{0,16},{16,0},{1,17},{17,1},{2,18},{18,2},{3,19},{19,3},{4,20},{20... | collective-permute-start | bytes 1572872 | tf_op jit(solution)/shard_map/image_x/ppermute | solution.py:302
  9.3 0.6 collective-permute-start.6
  9.9 2.0 %shard_map.101 = (bf16[256,1024]{1,0:T(8,128)(2,1)}, bf16[512,256]{1,0:T(8,128)(2,1)}) custom-call(bf16[256,8192]{1,0:T(8,128)(2,1)} %image.7, bf16[1024,256]{1,0:T(8,128)(2,1)} %refs_0_.3), custom_call_target="tpu_custom_call" | custom-call | tf_op jit(solution)/shard_map/pallas_call | solution.py:337
  11.9 0.1 collective-permute-done.refs_7_
  12.0 0.7 collective-permute-start.1
  12.7 1.3 %collective-permute-start.3 = (bf16[512,256]{1,0:T(8,128)(2,1)S(1)}, bf16[512,256]{1,0:T(8,128)(2,1)S(1)}, u32[]{:S(2)}, u32[]{:S(2)}) collective-permute-start(bf16[512,256]{1,0:T(8,128)(2,1)S(1)} %collective-permute-done.2.refs_10_), channel_id=1, source_target_pairs={{4,0},{6,2},{8,12},{10,14},{5,1},{7,3},{9,13},{11,15},{20,16},{22,... | collective-permute-start | bytes 786440 | tf_op jit(solution)/shard_map/wk_out_z1/ppermute | solution.py:290
  14.0 7.2 %collective-permute-done.6 = bf16[32,1024]{1,0:T(8,128)(2,1)S(1)} collective-permute-done((bf16[32,1024]{1,0:T(8,128)(2,1)S(1)}, bf16[32,1024]{1,0:T(8,128)(2,1)S(1)}, u32[]{:S(2)}, u32[]{:S(2)}) %collective-permute-start.6) | collective-permute-done | bytes 65568 | tf_op jit(solution)/shard_map/q_y/ppermute | solution.py:294
  21.3 3.1 %collective-permute-done.3.refs_9_ = bf16[512,256]{1,0:T(8,128)(2,1)S(1)} collective-permute-done((bf16[512,256]{1,0:T(8,128)(2,1)S(1)}, bf16[512,256]{1,0:T(8,128)(2,1)S(1)}, u32[]{:S(2)}, u32[]{:S(2)}) %collective-permute-start.3) | collective-permute-done | bytes 262176 | tf_op jit(solution)/shard_map/wk_out_z1/ppermute | solution.py:290
  24.5 1.1 collective-permute-start.7
  25.5 2.4 %collective-permute-start.10 = (bf16[256,1024]{1,0:T(8,128)(2,1)}, bf16[256,1024]{1,0:T(8,128)(2,1)}, u32[]{:S(2)}, u32[]{:S(2)}) collective-permute-start(bf16[256,1024]{1,0:T(8,128)(2,1)} %get-tuple-element.53), channel_id=1, source_target_pairs={{0,18},{2,16},{4,22},{6,20},{8,26},{10,24},{12,30},{14,28},{16,2},... | collective-permute-start | bytes 1572872 | tf_op jit(solution)/shard_map/image_xy/ppermute | solution.py:307
  28.0 0.5 collective-permute-start.12
  28.5 0.7 collective-permute-start.8
  29.2 1.9 %collective-permute-done.7.refs_7_ = bf16[512,256]{1,0:T(8,128)(2,1)S(1)} collective-permute-done((bf16[512,256]{1,0:T(8,128)(2,1)}, bf16[512,256]{1,0:T(8,128)(2,1)S(1)}, u32[]{:S(2)}, u32[]{:S(2)}) %collective-permute-start.7) | collective-permute-done | bytes 262176 | tf_op jit(solution)/shard_map/wv_z1/ppermute | solution.py:290
  31.1 1.3 %collective-permute-start.9 = (bf16[512,256]{1,0:T(8,128)(2,1)S(1)}, bf16[512,256]{1,0:T(8,128)(2,1)S(1)}, u32[]{:S(2)}, u32[]{:S(2)}) collective-permute-start(bf16[512,256]{1,0:T(8,128)(2,1)S(1)} %collective-permute-done.1.refs_8_), channel_id=1, source_target_pairs={{4,0},{6,2},{8,12},{10,14},{5,1},{7,3},{9,13},{11,15},{20,16},{22,... | collective-permute-start | bytes 786440 | tf_op jit(solution)/shard_map/wk_end_z1/ppermute | solution.py:290
  32.4 7.3 %collective-permute-done.9.refs_11_ = bf16[512,256]{1,0:T(8,128)(2,1)S(1)} collective-permute-done((bf16[512,256]{1,0:T(8,128)(2,1)S(1)}, bf16[512,256]{1,0:T(8,128)(2,1)S(1)}, u32[]{:S(2)}, u32[]{:S(2)}) %collective-permute-start.9) | collective-permute-done | bytes 262176 | tf_op jit(solution)/shard_map/wk_end_z1/ppermute | solution.py:290
  39.7 0.1 collective-permute-start.14
  39.8 0.7 copy-done.5
  40.5 0.2 copy-done.6
  40.7 0.7 collective-permute-start.13
  41.4 0.1 stack.63.idx_ref
  41.5 2.3 %collective-permute-start.15 = (bf16[64,1024]{1,0:T(8,128)(2,1)S(1)}, bf16[64,1024]{1,0:T(8,128)(2,1)S(1)}, u32[]{:S(2)}, u32[]{:S(2)}) collective-permute-start(bf16[64,1024]{1,0:T(8,128)(2,1)S(1)} %pad_maximum_fusion), channel_id=1, source_target_pairs={{0,4},{2,6},{4,0},{6,2},{8,12},{10,14},{12,8},{14,10},{1,5},{3,7},... | collective-permute-start | bytes 393224 | tf_op jit(solution)/shard_map/q_z1/ppermute | solution.py:290
  43.8 1.4 %collective-permute-start.19 = (bf16[512,256]{1,0:T(8,128)(2,1)S(1)}, bf16[512,256]{1,0:T(8,128)(2,1)S(1)}, u32[]{:S(2)}, u32[]{:S(2)}) collective-permute-start(bf16[512,256]{1,0:T(8,128)(2,1)S(1)} %collective-permute-done.8.refs_10_), channel_id=1, source_target_pairs={{4,0},{6,2},{8,12},{10,14},{5,1},{7,3},{9,13},{11,15},{20,16},{22,... | collective-permute-start | bytes 786440 | tf_op jit(solution)/shard_map/wv_out_z1/ppermute | solution.py:290
  45.3 5.2 %shard_map.102 = (f32[512,128]{1,0:T(8,128)S(1)}, f32[520,128]{1,0:T(8,128)}, f32[512,128]{1,0:T(8,128)}, f32[512,128]{1,0:T(8,128)S(1)}) custom-call(s32[8]{0:T(128)S(1)} %stack.63.idx_ref, f32[2,128]{1,0:T(2,128)S(1)} %convert_bitcast_fusion.slots, bf16[256,8192]{1,0:T(8,128)(2,1)} %image.7, bf16[256,1024]{1,0:T(8,128)(2,1)} %copy-done.3, ...), custom_call_target="tpu_custom_call" | custom-call | flops 1073741824 | bytes 16777216 | tf_op jit(solution)/shard_map/pallas_call | solution.py:404
  50.5 1.3 %collective-permute-start.20 = (bf16[512,256]{1,0:T(8,128)(2,1)S(1)}, bf16[512,256]{1,0:T(8,128)(2,1)}, u32[]{:S(2)}, u32[]{:S(2)}) collective-permute-start(bf16[512,256]{1,0:T(8,128)(2,1)S(1)} %collective-permute-done.13.refs_8_), channel_id=1, source_target_pairs={{4,0},{6,2},{8,12},{10,14},{5,1},{7,3},{9,13},{11,15},{20,16},{22,... | collective-permute-start | bytes 786440 | tf_op jit(solution)/shard_map/wv_end_z1/ppermute | solution.py:290
  51.8 3.5 %collective-permute-start.21 = (bf16[128,1024]{1,0:T(8,128)(2,1)S(1)}, bf16[128,1024]{1,0:T(8,128)(2,1)S(1)}, u32[]{:S(2)}, u32[]{:S(2)}) collective-permute-start(bf16[128,1024]{1,0:T(8,128)(2,1)S(1)} %constant_dynamic-update-slice_fusion.refs_0_), channel_id=1, source_target_pairs={{0,8},{2,10},{4,12},{6,14},{8,0},{10,2},{12,4},{14,6},{1,9},{3,11}... | collective-permute-start | bytes 786440 | tf_op jit(solution)/shard_map/q_z2/ppermute | solution.py:290
  55.3 1.5 %collective-permute-start.17 = (f32[512,128]{1,0:T(8,128)}, f32[512,128]{1,0:T(8,128)S(1)}, u32[]{:S(2)}, u32[]{:S(2)}) collective-permute-start(f32[512,128]{1,0:T(8,128)} %get-tuple-element.66), channel_id=1, source_target_pairs={{0,16},{16,0},{1,17},{17,1},{2,18},{18,2},{3,19},{19,3},{4,20},{20... | collective-permute-start | bytes 786440 | tf_op jit(solution)/shard_map/key_x/ppermute | solution.py:302
  56.8 0.1 reshape.13
  56.9 1.3 %collective-permute-start.16 = (f32[520,128]{1,0:T(8,128)}, f32[520,128]{1,0:T(8,128)S(1)}, u32[]{:S(2)}, u32[]{:S(2)}) collective-permute-start(f32[520,128]{1,0:T(8,128)} %get-tuple-element.65), channel_id=1, source_target_pairs={{0,2},{2,0},{4,6},{6,4},{8,10},{10,8},{12,14},{14,12},{1,3},{3,1},... | collective-permute-start | bytes 798728 | tf_op jit(solution)/shard_map/key_y/ppermute | solution.py:294
  58.2 0.7 collective-permute-start.18
  58.9 3.0 %collective-permute-done.20.refs_11_ = bf16[512,256]{1,0:T(8,128)(2,1)} collective-permute-done((bf16[512,256]{1,0:T(8,128)(2,1)S(1)}, bf16[512,256]{1,0:T(8,128)(2,1)}, u32[]{:S(2)}, u32[]{:S(2)}) %collective-permute-start.20) | collective-permute-done | bytes 262176 | tf_op jit(solution)/shard_map/wv_end_z1/ppermute | solution.py:290
  61.9 5.2 %shard_map.104 = (f32[512,128]{1,0:T(8,128)S(1)}, bf16[512,128]{1,0:T(8,128)(2,1)}, bf16[512,128]{1,0:T(8,128)(2,1)}, bf16[512,128]{1,0:T(8,128)(2,1)}) custom-call(s32[8]{0:T(128)S(1)} %stack.63.idx_ref, f32[2,128]{1,0:T(2,128)S(1)} %convert_bitcast_fusion.slots, bf16[256,8192]{1,0:T(8,128)(2,1)} %image.7, bf16[256,1024]{1,0:T(8,128)(2,1)} %copy-done.3, ...), custom_call_target="tpu_custom_call" | custom-call | flops 1073741824 | bytes 16777216 | tf_op jit(solution)/shard_map/pallas_call | solution.py:404
  67.1 1.7 %collective-permute-start.22 = (bf16[512,128]{1,0:T(8,128)(2,1)}, bf16[512,128]{1,0:T(8,128)(2,1)S(1)}, u32[]{:S(2)}, u32[]{:S(2)}) collective-permute-start(bf16[512,128]{1,0:T(8,128)(2,1)} %get-tuple-element.78), channel_id=1, source_target_pairs={{0,2},{2,0},{4,6},{6,4},{8,10},{10,8},{12,14},{14,12},{1,3},{3,1},... | collective-permute-start | bytes 393224 | tf_op jit(solution)/shard_map/value_y/ppermute | solution.py:294
  68.8 0.3 collective-permute-start.23
  69.1 1.6 %collective-permute-start.24 = (bf16[512,128]{1,0:T(8,128)(2,1)}, bf16[512,128]{1,0:T(8,128)(2,1)S(1)}, u32[]{:S(2)}, u32[]{:S(2)}) collective-permute-start(bf16[512,128]{1,0:T(8,128)(2,1)} %get-tuple-element.80), channel_id=1, source_target_pairs={{0,18},{2,16},{4,22},{6,20},{8,26},{10,24},{12,30},{14,28},{16,2},... | collective-permute-start | bytes 393224 | tf_op jit(solution)/shard_map/value_xy/ppermute | solution.py:307
  70.6 0.1 reshape.18.limit_ref
  70.8 0.2 shard_map.103.keys_ref
  71.0 2.0 %shard_map.105 = (bf16[2048,512]{1,0:T(8,128)(2,1)S(1)}, bf16[256,128]{1,0:T(8,128)(2,1)S(1)}) custom-call(f32[256,1]{1,0:T(8,128)S(1)} %reshape.18.limit_ref, bf16[528,128]{1,0:T(8,128)(2,1)S(1)} %shard_map.103.keys_ref, bf16[128,1024]{1,0:T(8,128)(2,1)S(1)} %constant_dynamic-update-slice_fusion.refs_0_, bf16[128,1024]{1,0:T(8,128)(2,1)S(1)} %collective-permute-done.21.refs_1_), custom_call_target="tpu_custom_call" | custom-call | tf_op jit(solution)/shard_map/pallas_call | solution.py:448
  73.0 0.6 collective-permute-done.22.got_y
  73.6 1.1 collective-permute-done.23.got_x
  74.7 1.2 %collective-permute-done.24.got_both = bf16[512,128]{1,0:T(8,128)(2,1)S(1)} collective-permute-done((bf16[512,128]{1,0:T(8,128)(2,1)}, bf16[512,128]{1,0:T(8,128)(2,1)S(1)}, u32[]{:S(2)}, u32[]{:S(2)}) %collective-permute-start.24) | collective-permute-done | bytes 131104 | tf_op jit(solution)/shard_map/value_xy/ppermute | solution.py:307
  75.9 0.7 shard_map.106
  76.7 2.1 %collective-permute-start.26 = (bf16[64,1152]{1,0:T(8,128)(2,1)S(1)}, bf16[64,1152]{1,0:T(8,128)(2,1)S(1)}, u32[]{:S(2)}, u32[]{:S(2)}) collective-permute-start(bf16[64,1152]{1,0:T(8,128)(2,1)S(1)} %get-tuple-element.83), channel_id=1, source_target_pairs={{0,12},{2,14},{4,8},{6,10},{8,4},{10,6},{12,0},{14,2},{1,13},{3,15... | collective-permute-start | bytes 442376 | tf_op jit(solution)/shard_map/sums_z3/ppermute | solution.py:290
  78.8 1.4 %collective-permute-start.27 = (bf16[64,1152]{1,0:T(8,128)(2,1)S(1)}, bf16[64,1152]{1,0:T(8,128)(2,1)S(1)}, u32[]{:S(2)}, u32[]{:S(2)}) collective-permute-start(bf16[64,1152]{1,0:T(8,128)(2,1)S(1)} %get-tuple-element.84), channel_id=1, source_target_pairs={{0,4},{2,6},{4,0},{6,2},{8,12},{10,14},{12,8},{14,10},{1,5},{3,7},... | collective-permute-start | bytes 442376 | tf_op jit(solution)/shard_map/sums_z1/ppermute | solution.py:290
  80.2 7.8 %collective-permute-done.25.refs_1_ = bf16[64,1152]{1,0:T(8,128)(2,1)S(1)} collective-permute-done((bf16[64,1152]{1,0:T(8,128)(2,1)S(1)}, bf16[64,1152]{1,0:T(8,128)(2,1)S(1)}, u32[]{:S(2)}, u32[]{:S(2)}) %collective-permute-start.25) | collective-permute-done | bytes 147488 | tf_op jit(solution)/shard_map/sums_z2/ppermute | solution.py:290
  88.0 0.9 collective-permute-done.27.refs_3_
  88.8 0.9 shard_map.107.refs_0_
  89.7 2.4 %collective-permute-start.28 = (bf16[64,1024]{1,0:T(8,128)(2,1)S(1)}, bf16[64,1024]{1,0:T(8,128)(2,1)S(1)}, u32[]{:S(2)}, u32[]{:S(2)}) collective-permute-start(bf16[64,1024]{1,0:T(8,128)(2,1)S(1)} %shard_map.107.refs_0_), channel_id=1, source_target_pairs={{0,8},{2,10},{4,12},{6,14},{8,0},{10,2},{12,4},{14,6},{1,9},{3,11}... | collective-permute-start | bytes 393224 | tf_op jit(solution)/shard_map/attn_z2/ppermute | solution.py:290
  92.1 2.4 %collective-permute-start.29 = (bf16[64,1024]{1,0:T(8,128)(2,1)S(1)}, bf16[64,1024]{1,0:T(8,128)(2,1)S(1)}, u32[]{:S(2)}, u32[]{:S(2)}) collective-permute-start(bf16[64,1024]{1,0:T(8,128)(2,1)S(1)} %shard_map.107.refs_0_), channel_id=1, source_target_pairs={{0,12},{2,14},{4,8},{6,10},{8,4},{10,6},{12,0},{14,2},{1,13},{3,15... | collective-permute-start | bytes 393224 | tf_op jit(solution)/shard_map/attn_z3/ppermute | solution.py:290
  94.5 0.6 collective-permute-start.31
  95.1 7.2 %collective-permute-done.28.refs_1_ = bf16[64,1024]{1,0:T(8,128)(2,1)S(1)} collective-permute-done((bf16[64,1024]{1,0:T(8,128)(2,1)S(1)}, bf16[64,1024]{1,0:T(8,128)(2,1)S(1)}, u32[]{:S(2)}, u32[]{:S(2)}) %collective-permute-start.28) | collective-permute-done | bytes 131104 | tf_op jit(solution)/shard_map/attn_z2/ppermute | solution.py:290
  102.2 0.9 collective-permute-start.32
  103.1 1.1 collective-permute-start.33
  104.3 0.9 collective-permute-start.34
  105.2 0.1 stack.59.idx_ref
  105.3 1.9 %collective-permute-done.32.refs_5_ = bf16[64,1024]{1,0:T(8,128)(2,1)S(1)} collective-permute-done((bf16[64,1024]{1,0:T(8,128)(2,1)S(1)}, bf16[64,1024]{1,0:T(8,128)(2,1)S(1)}, u32[]{:S(2)}, u32[]{:S(2)}) %collective-permute-start.32) | collective-permute-done | bytes 131104 | tf_op jit(solution)/shard_map/attn1_y/ppermute | solution.py:294
  107.2 1.4 %collective-permute-done.33.refs_6_ = bf16[64,1024]{1,0:T(8,128)(2,1)S(1)} collective-permute-done((bf16[64,1024]{1,0:T(8,128)(2,1)S(1)}, bf16[64,1024]{1,0:T(8,128)(2,1)S(1)}, u32[]{:S(2)}, u32[]{:S(2)}) %collective-permute-start.33) | collective-permute-done | bytes 131104 | tf_op jit(solution)/shard_map/attn2_y/ppermute | solution.py:294
  108.6 1.4 %collective-permute-done.34.refs_7_ = bf16[64,1024]{1,0:T(8,128)(2,1)S(1)} collective-permute-done((bf16[64,1024]{1,0:T(8,128)(2,1)S(1)}, bf16[64,1024]{1,0:T(8,128)(2,1)S(1)}, u32[]{:S(2)}, u32[]{:S(2)}) %collective-permute-start.34) | collective-permute-done | bytes 131104 | tf_op jit(solution)/shard_map/attn3_y/ppermute | solution.py:294
  110.0 3.3 %shard_map.108 = (f32[128,1024]{1,0:T(8,128)S(1)}, bf16[128,1024]{1,0:T(8,128)(2,1)S(1)}) custom-call(s32[17]{0:T(128)S(1)} %stack.59.idx_ref, bf16[64,1024]{1,0:T(8,128)(2,1)S(1)} %shard_map.107.refs_0_, bf16[64,1024]{1,0:T(8,128)(2,1)S(1)} %collective-permute-done.28.refs_1_, bf16[64,1024]{1,0:T(8,128)(2,1)S(1)} %collective-permute-done.29.refs_2_, ...), custom_call_target="tpu_custom_call" | custom-call | tf_op jit(solution)/shard_map/pallas_call | solution.py:484
  114.1 0.8 collective-permute-done.35
  114.9 0.8 add_convert_fusion
  (57 shorter events, 0.3 us)
Async XLA Ops:
  0.0 9.3 %copy-start.10 = (bf16[32,2048]{1,0:T(8,128)(2,1)S(1)}, bf16[32,2048]{1,0:T(8,128)(2,1)}, u32[]{:S(2)}) copy-start(bf16[32,2048]{1,0:T(8,128)(2,1)} %param.15) | copy-start | bytes 393220
  0.0 41.4 %copy-start.11 = (s32[256]{0:T(256)S(1)}, s32[256]{0:T(256)}, u32[]{:S(2)}) copy-start(s32[256]{0:T(256)} %param.11) | copy-start | bytes 3076
  2.4 42.9 %copy-start.1 = (bf16[512,256]{1,0:T(8,128)(2,1)S(1)}, bf16[512,256]{1,0:T(8,128)(2,1)}, u32[]{:S(2)}) copy-start(bf16[512,256]{1,0:T(8,128)(2,1)} %get-tuple-element.46.refs_6_) | copy-start | bytes 786436
  2.4 9.6 %collective-permute-start = (bf16[512,256]{1,0:T(8,128)(2,1)}, bf16[512,256]{1,0:T(8,128)(2,1)S(1)}, u32[]{:S(2)}, u32[]{:S(2)}) collective-permute-start(bf16[512,256]{1,0:T(8,128)(2,1)} %get-tuple-element.46.refs_6_), channel_id=1, source_target_pairs={{0,4},{2,6},{4,0},{6,2},{8,12},{10,14},{12,8},{14,10},{1,5},{3,7},... | collective-permute-start | bytes 786440 | tf_op jit(solution)/shard_map/wk_z1/ppermute | solution.py:290
  5.5 7.2 %collective-permute-start.2 = (bf16[512,256]{1,0:T(8,128)(2,1)}, bf16[512,256]{1,0:T(8,128)(2,1)S(1)}, u32[]{:S(2)}, u32[]{:S(2)}) collective-permute-start(bf16[512,256]{1,0:T(8,128)(2,1)} %get-tuple-element.46.refs_6_), channel_id=1, source_target_pairs={{4,8},{6,10},{8,4},{10,6},{5,9},{7,11},{9,5},{11,7},{20,24},{22,26... | collective-permute-start | bytes 786440 | tf_op jit(solution)/shard_map/wk_z3/ppermute | solution.py:290
  6.2 18.2 %collective-permute-start.4 = (bf16[256,1024]{1,0:T(8,128)(2,1)}, bf16[256,1024]{1,0:T(8,128)(2,1)S(1)}, u32[]{:S(2)}, u32[]{:S(2)}) collective-permute-start(bf16[256,1024]{1,0:T(8,128)(2,1)} %get-tuple-element.47), channel_id=1, source_target_pairs={{0,2},{2,0},{4,6},{6,4},{8,10},{10,8},{12,14},{14,12},{1,3},{3,1},... | collective-permute-start | bytes 1572872 | tf_op jit(solution)/shard_map/image_y/ppermute | solution.py:294
  7.8 16.7 %collective-permute-start.5 = (bf16[256,1024]{1,0:T(8,128)(2,1)}, bf16[256,1024]{1,0:T(8,128)(2,1)S(1)}, u32[]{:S(2)}, u32[]{:S(2)}) collective-permute-start(bf16[256,1024]{1,0:T(8,128)(2,1)} %get-tuple-element.48), channel_id=1, source_target_pairs={{0,16},{16,0},{1,17},{17,1},{2,18},{18,2},{3,19},{19,3},{4,20},{20... | collective-permute-start | bytes 1572872 | tf_op jit(solution)/shard_map/image_x/ppermute | solution.py:302
  9.3 12.0 %collective-permute-start.6 = (bf16[32,1024]{1,0:T(8,128)(2,1)S(1)}, bf16[32,1024]{1,0:T(8,128)(2,1)S(1)}, u32[]{:S(2)}, u32[]{:S(2)}) collective-permute-start(bf16[32,1024]{1,0:T(8,128)(2,1)S(1)} %constant_dynamic-slice_fusion), channel_id=1, source_target_pairs={{0,2},{2,0},{4,6},{6,4},{8,10},{10,8},{12,14},{14,12},{1,3},{3,1},... | collective-permute-start | bytes 196616 | tf_op jit(solution)/shard_map/q_y/ppermute | solution.py:294
  12.0 9.3 %collective-permute-start.1 = (bf16[512,256]{1,0:T(8,128)(2,1)S(1)}, bf16[512,256]{1,0:T(8,128)(2,1)S(1)}, u32[]{:S(2)}, u32[]{:S(2)}) collective-permute-start(bf16[512,256]{1,0:T(8,128)(2,1)S(1)} %collective-permute-done.refs_7_), channel_id=1, source_target_pairs={{4,8},{6,10},{8,4},{10,6},{5,9},{7,11},{9,5},{11,7},{20,24},{22,26... | collective-permute-start | bytes 786440 | tf_op jit(solution)/shard_map/wk_across_z3/ppermute | solution.py:290
  12.7 28.8 %copy-start.8 = (bf16[512,256]{1,0:T(8,128)(2,1)}, bf16[512,256]{1,0:T(8,128)(2,1)S(1)}, u32[]{:S(2)}) copy-start(bf16[512,256]{1,0:T(8,128)(2,1)S(1)} %collective-permute-done.2.refs_10_) | copy-start | bytes 786436
  12.7 11.7 %collective-permute-start.3 = (bf16[512,256]{1,0:T(8,128)(2,1)S(1)}, bf16[512,256]{1,0:T(8,128)(2,1)S(1)}, u32[]{:S(2)}, u32[]{:S(2)}) collective-permute-start(bf16[512,256]{1,0:T(8,128)(2,1)S(1)} %collective-permute-done.2.refs_10_), channel_id=1, source_target_pairs={{4,0},{6,2},{8,12},{10,14},{5,1},{7,3},{9,13},{11,15},{20,16},{22,... | collective-permute-start | bytes 786440 | tf_op jit(solution)/shard_map/wk_out_z1/ppermute | solution.py:290
  24.4 15.3 %copy-start.3 = (bf16[256,1024]{1,0:T(8,128)(2,1)}, bf16[256,1024]{1,0:T(8,128)(2,1)S(1)}, u32[]{:S(2)}) copy-start(bf16[256,1024]{1,0:T(8,128)(2,1)S(1)} %collective-permute-done.4.refs_0_) | copy-start | bytes 1572868
  24.5 19.3 %copy-start.4 = (bf16[256,1024]{1,0:T(8,128)(2,1)}, bf16[256,1024]{1,0:T(8,128)(2,1)S(1)}, u32[]{:S(2)}) copy-start(bf16[256,1024]{1,0:T(8,128)(2,1)S(1)} %collective-permute-done.5.refs_2_) | copy-start | bytes 1572868
  24.5 6.6 %collective-permute-start.7 = (bf16[512,256]{1,0:T(8,128)(2,1)}, bf16[512,256]{1,0:T(8,128)(2,1)S(1)}, u32[]{:S(2)}, u32[]{:S(2)}) collective-permute-start(bf16[512,256]{1,0:T(8,128)(2,1)} %get-tuple-element.51.refs_6_), channel_id=1, source_target_pairs={{0,4},{2,6},{4,0},{6,2},{8,12},{10,14},{12,8},{14,10},{1,5},{3,7},... | collective-permute-start | bytes 786440 | tf_op jit(solution)/shard_map/wv_z1/ppermute | solution.py:290
  25.5 14.1 %collective-permute-start.10 = (bf16[256,1024]{1,0:T(8,128)(2,1)}, bf16[256,1024]{1,0:T(8,128)(2,1)}, u32[]{:S(2)}, u32[]{:S(2)}) collective-permute-start(bf16[256,1024]{1,0:T(8,128)(2,1)} %get-tuple-element.53), channel_id=1, source_target_pairs={{0,18},{2,16},{4,22},{6,20},{8,26},{10,24},{12,30},{14,28},{16,2},... | collective-permute-start | bytes 1572872 | tf_op jit(solution)/shard_map/image_xy/ppermute | solution.py:307
  28.0 11.7 %collective-permute-start.11 = (bf16[256,1024]{1,0:T(8,128)(2,1)S(1)}, bf16[256,1024]{1,0:T(8,128)(2,1)S(1)}, u32[]{:S(2)}, u32[]{:S(2)}) collective-permute-start(bf16[256,1024]{1,0:T(8,128)(2,1)S(1)} %collective-permute-done.4.refs_0_), channel_id=1, source_target_pairs={{0,1},{1,0},{2,3},{3,2},{4,5},{5,4},{6,7},{7,6},{8,9},{9,8},{10,11... | collective-permute-start | bytes 1572872 | tf_op jit(solution)/shard_map/image_core/ppermute | solution.py:298
  28.0 11.7 %collective-permute-start.12 = (bf16[256,1024]{1,0:T(8,128)(2,1)S(1)}, bf16[256,1024]{1,0:T(8,128)(2,1)S(1)}, u32[]{:S(2)}, u32[]{:S(2)}) collective-permute-start(bf16[256,1024]{1,0:T(8,128)(2,1)S(1)} %collective-permute-done.5.refs_2_), channel_id=1, source_target_pairs={{0,1},{1,0},{2,3},{3,2},{4,5},{5,4},{6,7},{7,6},{8,9},{9,8},{10,11... | collective-permute-start | bytes 1572872 | tf_op jit(solution)/shard_map/image_core/ppermute | solution.py:298
  28.5 3.9 %collective-permute-start.8 = (bf16[512,256]{1,0:T(8,128)(2,1)}, bf16[512,256]{1,0:T(8,128)(2,1)S(1)}, u32[]{:S(2)}, u32[]{:S(2)}) collective-permute-start(bf16[512,256]{1,0:T(8,128)(2,1)} %get-tuple-element.51.refs_6_), channel_id=1, source_target_pairs={{4,8},{6,10},{8,4},{10,6},{5,9},{7,11},{9,5},{11,7},{20,24},{22,26... | collective-permute-start | bytes 786440 | tf_op jit(solution)/shard_map/wv_z3/ppermute | solution.py:290
  31.1 8.6 %collective-permute-start.9 = (bf16[512,256]{1,0:T(8,128)(2,1)S(1)}, bf16[512,256]{1,0:T(8,128)(2,1)S(1)}, u32[]{:S(2)}, u32[]{:S(2)}) collective-permute-start(bf16[512,256]{1,0:T(8,128)(2,1)S(1)} %collective-permute-done.1.refs_8_), channel_id=1, source_target_pairs={{4,0},{6,2},{8,12},{10,14},{5,1},{7,3},{9,13},{11,15},{20,16},{22,... | collective-permute-start | bytes 786440 | tf_op jit(solution)/shard_map/wk_end_z1/ppermute | solution.py:290
  39.7 4.1 %copy-start.9 = (bf16[512,256]{1,0:T(8,128)(2,1)}, bf16[512,256]{1,0:T(8,128)(2,1)S(1)}, u32[]{:S(2)}) copy-start(bf16[512,256]{1,0:T(8,128)(2,1)S(1)} %collective-permute-done.9.refs_11_) | copy-start | bytes 786436
  39.7 0.8 copy-start.5
  39.7 1.0 copy-start.6
  39.7 5.5 %collective-permute-start.14 = (bf16[256,1024]{1,0:T(8,128)(2,1)}, bf16[256,1024]{1,0:T(8,128)(2,1)}, u32[]{:S(2)}, u32[]{:S(2)}) collective-permute-start(bf16[256,1024]{1,0:T(8,128)(2,1)} %collective-permute-done.10.refs_4_), channel_id=1, source_target_pairs={{0,1},{1,0},{2,3},{3,2},{4,5},{5,4},{6,7},{7,6},{8,9},{9,8},{10,11... | collective-permute-start | bytes 1572872 | tf_op jit(solution)/shard_map/image_core/ppermute | solution.py:298
  40.7 9.8 %collective-permute-start.13 = (bf16[512,256]{1,0:T(8,128)(2,1)S(1)}, bf16[512,256]{1,0:T(8,128)(2,1)S(1)}, u32[]{:S(2)}, u32[]{:S(2)}) collective-permute-start(bf16[512,256]{1,0:T(8,128)(2,1)S(1)} %collective-permute-done.7.refs_7_), channel_id=1, source_target_pairs={{4,8},{6,10},{8,4},{10,6},{5,9},{7,11},{9,5},{11,7},{20,24},{22,26... | collective-permute-start | bytes 786440 | tf_op jit(solution)/shard_map/wv_across_z3/ppermute | solution.py:290
  41.5 9.0 %collective-permute-start.15 = (bf16[64,1024]{1,0:T(8,128)(2,1)S(1)}, bf16[64,1024]{1,0:T(8,128)(2,1)S(1)}, u32[]{:S(2)}, u32[]{:S(2)}) collective-permute-start(bf16[64,1024]{1,0:T(8,128)(2,1)S(1)} %pad_maximum_fusion), channel_id=1, source_target_pairs={{0,4},{2,6},{4,0},{6,2},{8,12},{10,14},{12,8},{14,10},{1,5},{3,7},... | collective-permute-start | bytes 393224 | tf_op jit(solution)/shard_map/q_z1/ppermute | solution.py:290
  43.8 13.0 %copy-start.12 = (s32[256]{0:T(256)S(1)}, s32[256]{0:T(256)}, u32[]{:S(2)}) copy-start(s32[256]{0:T(256)} %param.16) | copy-start | bytes 3076
  43.8 18.0 %copy-start = (bf16[512,256]{1,0:T(8,128)(2,1)S(1)}, bf16[512,256]{1,0:T(8,128)(2,1)}, u32[]{:S(2)}) copy-start(bf16[512,256]{1,0:T(8,128)(2,1)} %get-tuple-element.51.refs_6_) | copy-start | bytes 786436
  43.8 14.3 %collective-permute-start.19 = (bf16[512,256]{1,0:T(8,128)(2,1)S(1)}, bf16[512,256]{1,0:T(8,128)(2,1)S(1)}, u32[]{:S(2)}, u32[]{:S(2)}) collective-permute-start(bf16[512,256]{1,0:T(8,128)(2,1)S(1)} %collective-permute-done.8.refs_10_), channel_id=1, source_target_pairs={{4,0},{6,2},{8,12},{10,14},{5,1},{7,3},{9,13},{11,15},{20,16},{22,... | collective-permute-start | bytes 786440 | tf_op jit(solution)/shard_map/wv_out_z1/ppermute | solution.py:290
  50.5 11.4 %collective-permute-start.20 = (bf16[512,256]{1,0:T(8,128)(2,1)S(1)}, bf16[512,256]{1,0:T(8,128)(2,1)}, u32[]{:S(2)}, u32[]{:S(2)}) collective-permute-start(bf16[512,256]{1,0:T(8,128)(2,1)S(1)} %collective-permute-done.13.refs_8_), channel_id=1, source_target_pairs={{4,0},{6,2},{8,12},{10,14},{5,1},{7,3},{9,13},{11,15},{20,16},{22,... | collective-permute-start | bytes 786440 | tf_op jit(solution)/shard_map/wv_end_z1/ppermute | solution.py:290
  51.8 15.2 %collective-permute-start.21 = (bf16[128,1024]{1,0:T(8,128)(2,1)S(1)}, bf16[128,1024]{1,0:T(8,128)(2,1)S(1)}, u32[]{:S(2)}, u32[]{:S(2)}) collective-permute-start(bf16[128,1024]{1,0:T(8,128)(2,1)S(1)} %constant_dynamic-update-slice_fusion.refs_0_), channel_id=1, source_target_pairs={{0,8},{2,10},{4,12},{6,14},{8,0},{10,2},{12,4},{14,6},{1,9},{3,11}... | collective-permute-start | bytes 786440 | tf_op jit(solution)/shard_map/q_z2/ppermute | solution.py:290
  55.3 13.8 %collective-permute-start.17 = (f32[512,128]{1,0:T(8,128)}, f32[512,128]{1,0:T(8,128)S(1)}, u32[]{:S(2)}, u32[]{:S(2)}) collective-permute-start(f32[512,128]{1,0:T(8,128)} %get-tuple-element.66), channel_id=1, source_target_pairs={{0,16},{16,0},{1,17},{17,1},{2,18},{18,2},{3,19},{19,3},{4,20},{20... | collective-permute-start | bytes 786440 | tf_op jit(solution)/shard_map/key_x/ppermute | solution.py:302
  56.9 13.9 %collective-permute-start.16 = (f32[520,128]{1,0:T(8,128)}, f32[520,128]{1,0:T(8,128)S(1)}, u32[]{:S(2)}, u32[]{:S(2)}) collective-permute-start(f32[520,128]{1,0:T(8,128)} %get-tuple-element.65), channel_id=1, source_target_pairs={{0,2},{2,0},{4,6},{6,4},{8,10},{10,8},{12,14},{14,12},{1,3},{3,1},... | collective-permute-start | bytes 798728 | tf_op jit(solution)/shard_map/key_y/ppermute | solution.py:294
  58.2 12.7 %copy-start.2 = (f32[128]{0:T(128)S(1)}, f32[128]{0:T(128)}, u32[]{:S(2)}) copy-start(f32[128]{0:T(128)} %param.14) | copy-start | bytes 1540
  58.2 12.6 %collective-permute-start.18 = (f32[512,128]{1,0:T(8,128)S(1)}, f32[512,128]{1,0:T(8,128)S(1)}, u32[]{:S(2)}, u32[]{:S(2)}) collective-permute-start(f32[512,128]{1,0:T(8,128)S(1)} %get-tuple-element.67), channel_id=1, source_target_pairs={{0,18},{2,16},{4,22},{6,20},{8,26},{10,24},{12,30},{14,28},{16,2},... | collective-permute-start | bytes 786440 | tf_op jit(solution)/shard_map/key_xy/ppermute | solution.py:307
  67.1 6.5 %collective-permute-start.22 = (bf16[512,128]{1,0:T(8,128)(2,1)}, bf16[512,128]{1,0:T(8,128)(2,1)S(1)}, u32[]{:S(2)}, u32[]{:S(2)}) collective-permute-start(bf16[512,128]{1,0:T(8,128)(2,1)} %get-tuple-element.78), channel_id=1, source_target_pairs={{0,2},{2,0},{4,6},{6,4},{8,10},{10,8},{12,14},{14,12},{1,3},{3,1},... | collective-permute-start | bytes 393224 | tf_op jit(solution)/shard_map/value_y/ppermute | solution.py:294
  68.8 6.0 %collective-permute-start.23 = (bf16[512,128]{1,0:T(8,128)(2,1)}, bf16[512,128]{1,0:T(8,128)(2,1)S(1)}, u32[]{:S(2)}, u32[]{:S(2)}) collective-permute-start(bf16[512,128]{1,0:T(8,128)(2,1)} %get-tuple-element.79), channel_id=1, source_target_pairs={{0,16},{16,0},{1,17},{17,1},{2,18},{18,2},{3,19},{19,3},{4,20},{20... | collective-permute-start | bytes 393224 | tf_op jit(solution)/shard_map/value_x/ppermute | solution.py:302
  69.1 6.9 %collective-permute-start.24 = (bf16[512,128]{1,0:T(8,128)(2,1)}, bf16[512,128]{1,0:T(8,128)(2,1)S(1)}, u32[]{:S(2)}, u32[]{:S(2)}) collective-permute-start(bf16[512,128]{1,0:T(8,128)(2,1)} %get-tuple-element.80), channel_id=1, source_target_pairs={{0,18},{2,16},{4,22},{6,20},{8,26},{10,24},{12,30},{14,28},{16,2},... | collective-permute-start | bytes 393224 | tf_op jit(solution)/shard_map/value_xy/ppermute | solution.py:307
  75.9 39.0 %copy-start.7 = (bf16[128,1024]{1,0:T(8,128)(2,1)S(1)}, bf16[128,1024]{1,0:T(8,128)(2,1)}, u32[]{:S(2)}) copy-start(bf16[128,1024]{1,0:T(8,128)(2,1)} %param.17) | copy-start | bytes 786436
  76.7 11.3 %collective-permute-start.25 = (bf16[64,1152]{1,0:T(8,128)(2,1)S(1)}, bf16[64,1152]{1,0:T(8,128)(2,1)S(1)}, u32[]{:S(2)}, u32[]{:S(2)}) collective-permute-start(bf16[64,1152]{1,0:T(8,128)(2,1)S(1)} %get-tuple-element.82), channel_id=1, source_target_pairs={{0,8},{2,10},{4,12},{6,14},{8,0},{10,2},{12,4},{14,6},{1,9},{3,11}... | collective-permute-start | bytes 442376 | tf_op jit(solution)/shard_map/sums_z2/ppermute | solution.py:290
  76.7 11.2 %collective-permute-start.26 = (bf16[64,1152]{1,0:T(8,128)(2,1)S(1)}, bf16[64,1152]{1,0:T(8,128)(2,1)S(1)}, u32[]{:S(2)}, u32[]{:S(2)}) collective-permute-start(bf16[64,1152]{1,0:T(8,128)(2,1)S(1)} %get-tuple-element.83), channel_id=1, source_target_pairs={{0,12},{2,14},{4,8},{6,10},{8,4},{10,6},{12,0},{14,2},{1,13},{3,15... | collective-permute-start | bytes 442376 | tf_op jit(solution)/shard_map/sums_z3/ppermute | solution.py:290
  78.8 10.0 %collective-permute-start.27 = (bf16[64,1152]{1,0:T(8,128)(2,1)S(1)}, bf16[64,1152]{1,0:T(8,128)(2,1)S(1)}, u32[]{:S(2)}, u32[]{:S(2)}) collective-permute-start(bf16[64,1152]{1,0:T(8,128)(2,1)S(1)} %get-tuple-element.84), channel_id=1, source_target_pairs={{0,4},{2,6},{4,0},{6,2},{8,12},{10,14},{12,8},{14,10},{1,5},{3,7},... | collective-permute-start | bytes 442376 | tf_op jit(solution)/shard_map/sums_z1/ppermute | solution.py:290
  89.7 12.5 %collective-permute-start.28 = (bf16[64,1024]{1,0:T(8,128)(2,1)S(1)}, bf16[64,1024]{1,0:T(8,128)(2,1)S(1)}, u32[]{:S(2)}, u32[]{:S(2)}) collective-permute-start(bf16[64,1024]{1,0:T(8,128)(2,1)S(1)} %shard_map.107.refs_0_), channel_id=1, source_target_pairs={{0,8},{2,10},{4,12},{6,14},{8,0},{10,2},{12,4},{14,6},{1,9},{3,11}... | collective-permute-start | bytes 393224 | tf_op jit(solution)/shard_map/attn_z2/ppermute | solution.py:290
  92.1 11.0 %collective-permute-start.29 = (bf16[64,1024]{1,0:T(8,128)(2,1)S(1)}, bf16[64,1024]{1,0:T(8,128)(2,1)S(1)}, u32[]{:S(2)}, u32[]{:S(2)}) collective-permute-start(bf16[64,1024]{1,0:T(8,128)(2,1)S(1)} %shard_map.107.refs_0_), channel_id=1, source_target_pairs={{0,12},{2,14},{4,8},{6,10},{8,4},{10,6},{12,0},{14,2},{1,13},{3,15... | collective-permute-start | bytes 393224 | tf_op jit(solution)/shard_map/attn_z3/ppermute | solution.py:290
  94.5 9.8 %collective-permute-start.30 = (bf16[64,1024]{1,0:T(8,128)(2,1)S(1)}, bf16[64,1024]{1,0:T(8,128)(2,1)S(1)}, u32[]{:S(2)}, u32[]{:S(2)}) collective-permute-start(bf16[64,1024]{1,0:T(8,128)(2,1)S(1)} %shard_map.107.refs_0_), channel_id=1, source_target_pairs={{0,4},{2,6},{4,0},{6,2},{8,12},{10,14},{12,8},{14,10},{1,5},{3,7},... | collective-permute-start | bytes 393224 | tf_op jit(solution)/shard_map/attn_z1/ppermute | solution.py:290
  94.5 10.8 %collective-permute-start.31 = (bf16[64,1024]{1,0:T(8,128)(2,1)S(1)}, bf16[64,1024]{1,0:T(8,128)(2,1)S(1)}, u32[]{:S(2)}, u32[]{:S(2)}) collective-permute-start(bf16[64,1024]{1,0:T(8,128)(2,1)S(1)} %shard_map.107.refs_0_), channel_id=1, source_target_pairs={{0,2},{2,0},{4,6},{6,4},{8,10},{10,8},{12,14},{14,12},{1,3},{3,1},... | collective-permute-start | bytes 393224 | tf_op jit(solution)/shard_map/attn0_y/ppermute | solution.py:294
  102.2 5.0 %collective-permute-start.32 = (bf16[64,1024]{1,0:T(8,128)(2,1)S(1)}, bf16[64,1024]{1,0:T(8,128)(2,1)S(1)}, u32[]{:S(2)}, u32[]{:S(2)}) collective-permute-start(bf16[64,1024]{1,0:T(8,128)(2,1)S(1)} %collective-permute-done.28.refs_1_), channel_id=1, source_target_pairs={{0,2},{2,0},{4,6},{6,4},{8,10},{10,8},{12,14},{14,12},{1,3},{3,1},... | collective-permute-start | bytes 393224 | tf_op jit(solution)/shard_map/attn1_y/ppermute | solution.py:294
  103.1 5.5 %collective-permute-start.33 = (bf16[64,1024]{1,0:T(8,128)(2,1)S(1)}, bf16[64,1024]{1,0:T(8,128)(2,1)S(1)}, u32[]{:S(2)}, u32[]{:S(2)}) collective-permute-start(bf16[64,1024]{1,0:T(8,128)(2,1)S(1)} %collective-permute-done.29.refs_2_), channel_id=1, source_target_pairs={{0,2},{2,0},{4,6},{6,4},{8,10},{10,8},{12,14},{14,12},{1,3},{3,1},... | collective-permute-start | bytes 393224 | tf_op jit(solution)/shard_map/attn2_y/ppermute | solution.py:294
  104.3 5.7 %collective-permute-start.34 = (bf16[64,1024]{1,0:T(8,128)(2,1)S(1)}, bf16[64,1024]{1,0:T(8,128)(2,1)S(1)}, u32[]{:S(2)}, u32[]{:S(2)}) collective-permute-start(bf16[64,1024]{1,0:T(8,128)(2,1)S(1)} %collective-permute-done.30.refs_3_), channel_id=1, source_target_pairs={{0,2},{2,0},{4,6},{6,4},{8,10},{10,8},{12,14},{14,12},{1,3},{3,1},... | collective-permute-start | bytes 393224 | tf_op jit(solution)/shard_map/attn3_y/ppermute | solution.py:294
  113.3 1.6 %collective-permute-start.35 = (bf16[128,1024]{1,0:T(8,128)(2,1)S(1)}, bf16[128,1024]{1,0:T(8,128)(2,1)S(1)}, u32[]{:S(2)}, u32[]{:S(2)}) collective-permute-start(bf16[128,1024]{1,0:T(8,128)(2,1)S(1)} %get-tuple-element.86), channel_id=1, source_target_pairs={{0,1},{1,0},{2,3},{3,2},{4,5},{5,4},{6,7},{7,6},{8,9},{9,8},{10,11... | collective-permute-start | bytes 786440 | tf_op jit(solution)/shard_map/proj_core/ppermute | solution.py:298
